TPU v7x, 32 devices: a whole 2x2x4 slice. The times are simulated.
32 devices in a mesh: dev: 32 (over z, y, x, core).
Axes of the slice: x: 2, y: 2, z: 4, core: 2. Of those that a mesh axis runs over, the one named last changes fastest.
Arguments:
- tokens: bfloat16 [16384, 768], P('dev'), may hold values from -6 to 6
- cotangent: bfloat16 [16384, 768], P('dev'), may hold values from -6 to 6
- segment_ids: int32 [16384], P('dev'), may hold values from -1 to 127, as said below
- wide_weight: float32 [768, 6144], P('dev')
- wide_moment: float32 [768, 6144], P('dev'), may hold values from -5 to 5
- wide_average: float32 [768, 6144], P('dev'), may hold values from -0.21875 to 0.21875
- down_weight: float32 [3072, 768], P('dev'), may hold values from -0.109375 to 0.109375
- down_moment: float32 [3072, 768], P('dev'), may hold values from -5 to 5
- down_average: float32 [3072, 768], P('dev'), may hold values from -0.109375 to 0.109375
- vector_weight: float32 [12, 768], replicated
- vector_moment: float32 [12, 768], replicated, may hold values from -5 to 5
- vector_average: float32 [12, 768], replicated, may hold values from -3 to 3
Outputs:
- block_output: bfloat16 [16384, 768], P('dev')
- input_grad: bfloat16 [16384, 768], P('dev')
- grad_norm: float32 [], replicated
- wide_new: float32 [768, 6144], P('dev')
- wide_moment_new: float32 [768, 6144], P('dev')
- wide_average_new: float32 [768, 6144], P('dev')
- down_new: float32 [3072, 768], P('dev')
- down_moment_new: float32 [3072, 768], P('dev')
- down_average_new: float32 [3072, 768], P('dev')
- vector_new: float32 [12, 768], replicated
- vector_moment_new: float32 [12, 768], replicated
- vector_average_new: float32 [12, 768], replicated
Inputs may be any that keep to these rules, and one draw needn't show every extreme that they name: `segment_ids`: -1 marks an empty row. Among the rows of one device at most 16 carry ids of one group 4 * r to 4 * r + 3, and in every draw one group gets exactly 16 rows from every device. Each group holds at most 512 rows in all.
All inputs are finite; a program needn't handle non-finite values.
Results may differ from a plain program's by a relative error of at most 0.012.
The roundings to bfloat16 on the way count: a program that leaves them out, or rounds other values in their place, can miss the bound.
Values may be sent and summed in bfloat16 or wider, within the bound.
No kernel may reach another device: no remote copies, remote signals or barrier semaphores. Data moves between devices by JAX's collectives and lax.ppermute only.
A program may use at most 128 MiB of HBM per device.

v0:
```python
import math

import jax
import jax.numpy as jnp
from jax import lax
from jax.sharding import PartitionSpec as P

HEADS = 12
HEAD = 64
FF = 3072
DOCS_DEV = 4


epsilon = 1e-05
masked_value = -1e30
momentum = 0.9
learn_rate = 0.01
decay_rate = 0.0001
average_rate = 0.8
clip_norm = 2048.0


def norm_rows(values, gain_row, shift_row):
    center = values - jnp.mean(values, -1, keepdims=True)
    spread = jnp.mean(center * center, -1, keepdims=True)
    return center * lax.rsqrt(spread + epsilon) * gain_row + shift_row


def gelu_exact(values):
    return jax.nn.gelu(values, approximate=False)


def product(matrix, other):
    return jnp.dot(matrix, other, preferred_element_type=jnp.float32)


def against(matrix, other):
    return lax.dot_general(
        matrix, other, (((1,), (1,)), ((), ())), preferred_element_type=jnp.float32
    )


def inner_rows(matrix, other):
    return lax.dot_general(
        matrix, other, (((0,), (0,)), ((), ())), preferred_element_type=jnp.float32
    )


def advance(weight, moment, average, gradient, factor, decay_term):
    update = factor * gradient + decay_term * weight
    new_moment = momentum * moment + update
    new_weight = weight - learn_rate * (update + momentum * new_moment)
    new_average = average_rate * average + (1.0 - average_rate) * new_weight
    return (new_weight, new_moment, new_average)


def routing(segment_ids, devices, capacity):
    row_count = segment_ids.shape[0]
    is_live = segment_ids >= 0
    target = jnp.where(is_live, segment_ids // DOCS_DEV, devices)
    onehot = (target[:, None] == jnp.arange(devices, dtype=jnp.int32)[None, :]).astype(jnp.int32)
    earlier = jnp.cumsum(onehot, axis=0) - onehot
    within = jnp.sum(earlier * onehot, axis=1)
    slot_of = jnp.where(is_live, target * capacity + within, row_count)
    anchor = (
        jnp.full((row_count,), row_count, jnp.int32)
        .at[slot_of]
        .set(jnp.arange(row_count, dtype=jnp.int32), mode="drop")
    )
    return (is_live, jnp.minimum(slot_of, row_count - 1), anchor)


def body(
    tokens,
    cotangent,
    segment_ids,
    wide_weight,
    wide_moment,
    wide_average,
    down_weight,
    down_moment,
    down_average,
    vector_weight,
    vector_moment,
    vector_average,
):
    wide_full, down_full = (
        lax.all_gather(wide_weight.astype(jnp.bfloat16), "dev", axis=0, tiled=True),
        lax.all_gather(down_weight.astype(jnp.bfloat16), "dev", axis=0, tiled=True),
    )
    devices = lax.axis_size("dev")
    row_count, feature = tokens.shape
    capacity = row_count // devices
    is_live, slot_of, anchor = routing(segment_ids, devices, capacity)
    blank_row = jnp.zeros((1, feature), jnp.bfloat16)
    send_rows = jnp.concatenate([tokens, blank_row], 0)[anchor].reshape(devices, capacity, feature)
    send_grads = jnp.concatenate([cotangent, blank_row], 0)[anchor].reshape(
        devices, capacity, feature
    )
    send_ids = jnp.concatenate([segment_ids, jnp.full((1,), -1, jnp.int32)], 0)[anchor].reshape(
        devices, capacity
    )
    work_rows, work_grads, work_ids = (
        lax.all_to_all(send_rows, "dev", split_axis=0, concat_axis=0, tiled=True),
        lax.all_to_all(send_grads, "dev", split_axis=0, concat_axis=0, tiled=True),
        lax.all_to_all(send_ids, "dev", split_axis=0, concat_axis=0, tiled=True),
    )
    work_rows = work_rows.reshape(row_count, feature)
    work_grads = work_grads.reshape(row_count, feature)
    work_ids = work_ids.reshape(row_count)
    gain_one, shift_one, gain_two, shift_two, bias_query, bias_value, bias_out, bias_down = [
        vector_weight[row_index] for row_index in range(8)
    ]
    bias_up = vector_weight[8:].reshape(FF)
    w_qkv = wide_full[:, : 3 * feature]
    w_out = wide_full[:, 3 * feature : 4 * feature]
    w_up = wide_full[:, 4 * feature :]
    work_float = work_rows.astype(jnp.float32)
    low_one = norm_rows(work_float, gain_one, shift_one).astype(jnp.bfloat16)
    bias_all = jnp.concatenate([bias_query, jnp.zeros_like(bias_query), bias_value])
    projected = (product(low_one, w_qkv) + bias_all).astype(jnp.bfloat16)
    queries = projected[:, :feature].reshape(row_count, HEADS, HEAD)
    key_rows = projected[:, feature : 2 * feature].reshape(row_count, HEADS, HEAD)
    value_rows = projected[:, 2 * feature :].reshape(row_count, HEADS, HEAD)
    same_seg = work_ids[:, None] == work_ids[None, :]
    block_rows = min(512, row_count)
    group_size = math.gcd(HEADS, 4)
    group_count = HEADS // group_size

    def scores_of(offset, first_head):
        query_part = queries[offset : offset + block_rows, first_head : first_head + group_size]
        raw_scores = (
            jnp.einsum(
                "qhd,khd->hqk",
                query_part,
                key_rows[:, first_head : first_head + group_size],
                preferred_element_type=jnp.float32,
            )
            * 0.125
        )
        return jnp.where(same_seg[None], raw_scores, masked_value)

    stored = []
    offset = 0
    head_outs = []
    for group in range(group_count):
        first_head = group * group_size
        scores = scores_of(offset, first_head)
        row_max = jnp.max(scores, -1, keepdims=True)
        powers = jnp.exp(scores - row_max)
        row_sums = jnp.sum(powers, -1, keepdims=True)
        prob_low = (powers / row_sums).astype(jnp.bfloat16)
        head_outs.append(
            jnp.einsum(
                "hqk,khd->qhd",
                prob_low,
                value_rows[:, first_head : first_head + group_size],
                preferred_element_type=jnp.float32,
            )
        )
        stored.append((row_max, row_sums))
    out_blocks = jnp.concatenate(head_outs, 1)
    attended = out_blocks.reshape(row_count, feature).astype(jnp.bfloat16)
    resid = work_float + product(attended, w_out) + bias_out
    low_two = norm_rows(resid, gain_two, shift_two).astype(jnp.bfloat16)
    up_float = product(low_two, w_up) + bias_up
    hidden = gelu_exact(up_float).astype(jnp.bfloat16)
    output_low = (resid + product(hidden, down_full) + bias_down).astype(jnp.bfloat16)
    dy_float = work_grads.astype(jnp.float32)
    dhidden = against(work_grads, down_full)
    gelu_pull = jax.vjp(gelu_exact, up_float)[1]
    dup_low = gelu_pull(dhidden)[0].astype(jnp.bfloat16)
    da_two = against(dup_low, w_up)
    norm_two_pull = jax.vjp(norm_rows, resid, gain_two, shift_two)[1]
    dres_norm, dgain_two, dshift_two = norm_two_pull(da_two)
    dresid = dy_float + dres_norm
    dres_low = dresid.astype(jnp.bfloat16)
    dattended = against(dres_low, w_out).astype(jnp.bfloat16).reshape(row_count, HEADS, HEAD)
    dkey_parts = [
        jnp.zeros((row_count, group_size, HEAD), jnp.float32) for group in range(group_count)
    ]
    dvalue_parts = [
        jnp.zeros((row_count, group_size, HEAD), jnp.float32) for group in range(group_count)
    ]
    position = 0
    offset = 0
    pieces = []
    for group in range(group_count):
        first_head = group * group_size
        scores = scores_of(offset, first_head)
        row_max, row_sums = stored[position]
        position += 1
        prob_float = jnp.exp(scores - row_max) / row_sums
        prob_low = prob_float.astype(jnp.bfloat16)
        dout_part = dattended[offset : offset + block_rows, first_head : first_head + group_size]
        value_part = value_rows[:, first_head : first_head + group_size]
        dvalue_parts[group] = jnp.einsum(
            "hqk,qhd->khd", prob_low, dout_part, preferred_element_type=jnp.float32
        )
        dprob = jnp.einsum(
            "qhd,khd->hqk", dout_part, value_part, preferred_element_type=jnp.float32
        )
        dscore = (prob_float * (dprob - jnp.sum(prob_float * dprob, -1, keepdims=True))).astype(
            jnp.bfloat16
        )
        pieces.append(
            jnp.einsum(
                "hqk,khd->qhd",
                dscore,
                key_rows[:, first_head : first_head + group_size],
                preferred_element_type=jnp.float32,
            )
            * 0.125
        )
        query_part = queries[offset : offset + block_rows, first_head : first_head + group_size]
        dkey_parts[group] = (
            jnp.einsum("hqk,qhd->khd", dscore, query_part, preferred_element_type=jnp.float32)
            * 0.125
        )
    dquery_blocks = jnp.concatenate(pieces, 1)
    dquery_low = dquery_blocks.reshape(row_count, feature).astype(jnp.bfloat16)
    dkey_low = jnp.concatenate(dkey_parts, 1).reshape(row_count, feature).astype(jnp.bfloat16)
    dvalue_low = jnp.concatenate(dvalue_parts, 1).reshape(row_count, feature).astype(jnp.bfloat16)
    dqkv_low = jnp.concatenate([dquery_low, dkey_low, dvalue_low], 1)
    da_one = against(dqkv_low, w_qkv)
    norm_one_pull = jax.vjp(norm_rows, work_float, gain_one, shift_one)[1]
    dinput_norm, dgain_one, dshift_one = norm_one_pull(da_one)
    dinput_low = (dresid + dinput_norm).astype(jnp.bfloat16)
    back_out, back_grad = (
        lax.all_to_all(
            output_low.reshape(devices, capacity, feature),
            "dev",
            split_axis=0,
            concat_axis=0,
            tiled=True,
        ),
        lax.all_to_all(
            dinput_low.reshape(devices, capacity, feature),
            "dev",
            split_axis=0,
            concat_axis=0,
            tiled=True,
        ),
    )
    block_output = jnp.where(
        is_live[:, None], back_out.reshape(row_count, feature)[slot_of], jnp.zeros_like(tokens)
    )
    input_grad = jnp.where(
        is_live[:, None], back_grad.reshape(row_count, feature)[slot_of], jnp.zeros_like(tokens)
    )
    vector_rows = jnp.stack(
        [
            dgain_one,
            dshift_one,
            dgain_two,
            dshift_two,
            jnp.sum(dquery_low.astype(jnp.float32), 0),
            jnp.sum(dvalue_low.astype(jnp.float32), 0),
            jnp.sum(dres_low.astype(jnp.float32), 0),
            jnp.sum(dy_float, 0),
        ],
        0,
    )
    bias_up_grad = jnp.sum(dup_low.astype(jnp.float32), 0).reshape(FF // feature, feature)
    vector_partial = jnp.concatenate([vector_rows, bias_up_grad], 0)
    down_grad = lax.psum_scatter(
        inner_rows(hidden, work_grads), "dev", scatter_dimension=0, tiled=True
    )
    wide_grad = lax.psum_scatter(
        jnp.concatenate(
            [
                inner_rows(low_one, dqkv_low),
                jnp.concatenate([inner_rows(attended, dres_low), inner_rows(low_two, dup_low)], 1),
            ],
            1,
        ),
        "dev",
        scatter_dimension=0,
        tiled=True,
    )
    shard_squares = jnp.sum(wide_grad * wide_grad) + jnp.sum(down_grad * down_grad)
    vector_grad = lax.psum(vector_partial, "dev")
    total = lax.psum(shard_squares, "dev") + jnp.sum(vector_grad * vector_grad)
    grad_norm = jnp.sqrt(total)
    factor = clip_norm / jnp.maximum(grad_norm, clip_norm)
    wide_new, wide_moment_new, wide_average_new = advance(
        wide_weight, wide_moment, wide_average, wide_grad, factor, decay_rate
    )
    down_new, down_moment_new, down_average_new = advance(
        down_weight, down_moment, down_average, down_grad, factor, decay_rate
    )
    vector_new, vector_moment_new, vector_average_new = advance(
        vector_weight, vector_moment, vector_average, vector_grad, factor, 0.0
    )
    return (
        block_output,
        input_grad,
        grad_norm,
        wide_new,
        wide_moment_new,
        wide_average_new,
        down_new,
        down_moment_new,
        down_average_new,
        vector_new,
        vector_moment_new,
        vector_average_new,
    )


def solution(mesh):
    placed = (
        P("dev", None),
        P("dev", None),
        P("dev"),
        P("dev", None),
        P("dev", None),
        P("dev", None),
        P("dev", None),
        P("dev", None),
        P("dev", None),
        P(),
        P(),
        P(),
    )
    return jax.shard_map(
        body,
        mesh=mesh,
        in_specs=placed,
        out_specs=(
            P("dev", None),
            P("dev", None),
            P(),
            P("dev", None),
            P("dev", None),
            P("dev", None),
            P("dev", None),
            P("dev", None),
            P("dev", None),
            P(),
            P(),
            P(),
        ),
        check_vma=False,
    )
```

profile of v0, /device:TPU:0, one launch (start us, length us, event | category | flops | bytes accessed | tf_op | source)
XLA Modules:
  0.0 640.8 jit_solution(7661372956998276552)
XLA Ops:
  7.2 1.9 convert_element_type.119
  9.8 1.2 reduce-window.6
  12.0 2.4 scatter_custom_fusion
  15.1 2.3 gather_fusion.1
  18.1 7.3 %all-to-all-start.1 = ((s32[32,1,16]{2,1,0:T(1,128)}), s32[32,1,16]{2,1,0:T(1,128)S(1)}, u32[]{:S(2)}, u32[]{:S(2)}) async-start(s32[32,1,16]{2,1,0:T(1,128)} %bitcast.5), calls=%async_computation.1 | async-start | bytes 32768 | tf_op jit(solution)/shard_map/all_to_all | solution.py:106
  25.5 2.7 gather_fusion
  28.2 4.3 all-to-all-done.1
  32.5 2.6 all-to-all-start
  36.0 2.7 gather_fusion.3
  40.9 27.4 %all-to-all-done = bf16[32,16,768]{2,1,0:T(8,128)(2,1)S(1)} async-done(((bf16[32,16,768]{2,1,0:T(8,128)(2,1)}), bf16[32,16,768]{2,1,0:T(8,128)(2,1)S(1)}, u32[]{:S(2)}, u32[]{:S(2)}) %all-to-all-start) | async-done | bytes 786464 | tf_op jit(solution)/shard_map/all_to_all | solution.py:104
  68.3 3.7 all-to-all-start.3
  73.7 46.4 %all-gather.3.cloned.1.call-done = bf16[768,6144]{1,0:T(8,128)(2,1)} async-done(((bf16[24,6144]{1,0:T(8,128)(2,1)}), bf16[768,6144]{1,0:T(8,128)(2,1)}) %all-gather.3.cloned.1.call-update) | async-done | bytes 9437200 | tf_op jit(solution)/shard_map/all_gather | solution.py:88
  120.1 4.0 fusion.9
  124.1 1.3 fusion.99
  125.7 1.7 copy.70
  127.4 2.6 copy.68
  132.3 2.6 fusion.100
  134.9 2.1 fusion.101
  137.1 2.1 fusion.102
  140.3 1.0 copy-done.9
  141.9 1.1 slice-done.1
  143.0 1.4 slice-done.2
  144.8 1.0 fusion.103
  146.1 4.8 fusion.12
  150.9 35.3 %all-gather.5.cloned.1.call-done = bf16[3072,768]{1,0:T(8,128)(2,1)} async-done(((bf16[96,768]{1,0:T(8,128)(2,1)}), bf16[3072,768]{1,0:T(8,128)(2,1)}) %all-gather.5.cloned.1.call-update) | async-done | bytes 4718608 | tf_op jit(solution)/shard_map/all_gather | solution.py:89
  186.2 19.6 %convert_reduce_fusion = (f32[3072]{0:T(1024)S(1)}, bf16[512,3072]{1,0:T(8,128)(2,1)}, f32[512,3072]{1,0:T(8,128)S(1)}) fusion(f32[512,3072]{1,0:T(8,128)} %fusion.12, f32[3072]{0:T(1024)S(1)} %add.183, bf16[512,768]{1,0:T(8,128)(2,1)S(1)} %bitcast.139, bf16[3072,768]{1,0:T(8,128)(2,1)} %all-gather.5.cloned.1.call-done), kind=kOutput, calls=%fused_computation.12 | convolution fusion | flops 2533880832 | bytes 21258240 | tf_op jit(solution)/shard_map/dot_general | solution.py:38
  205.8 1.5 multiply_convert_fusion
  207.3 1.7 copy-done.19
  209.1 5.1 fusion.105
  214.4 6.2 multiply_reduce_fusion.3
  220.6 2.1 fusion.98
  223.1 3.0 convolution_convert_fusion
  226.1 1.5 copy.75
  227.6 3.3 convolution_bitcast_fusion
  232.2 1.6 copy-done.10
  234.8 1.4 copy-done.14
  237.3 1.2 multiply_convert_fusion.1
  239.3 0.9 multiply_reduce_fusion.1
  240.1 1.2 multiply_convert_fusion.2
  242.1 0.9 multiply_reduce_fusion.2
  243.0 1.4 multiply_convert_fusion.3
  248.0 2.0 fusion.62
  250.6 2.9 fusion.94
  253.5 6.8 %pad_maximum_fusion = f32[768,6144]{1,0:T(8,128)} fusion(f32[768,3072]{1,0:T(8,128)S(1)} %fusion.94, f32[768,768]{1,0:T(8,128)S(1)} %fusion.104, f32[768,2304]{1,0:T(8,128)S(1)} %fusion.62), kind=kLoop, calls=%fused_computation.9 | loop fusion | flops 9437184 | bytes 37748736 | tf_op jit(solution)/shard_map/concatenate | solution.py:270
  261.1 7.4 %add_convert_fusion.2 = bf16[512,768]{1,0:T(8,128)(2,1)} fusion(f32[512,768]{1,0:T(8,128)} %copy-done.6, bf16[512,3072]{1,0:T(8,128)(2,1)} %copy-done.19, bf16[3072,768]{1,0:T(8,128)(2,1)} %all-gather.5.cloned.1.call-done, f32[768]{0:T(1024)S(1)} %copy-done.46), kind=kOutput, calls=%fused_computation.93 | convolution fusion | flops 2417098752 | bytes 10226688 | tf_op jit(solution)/shard_map/dot_general | solution.py:34
  268.4 3.7 all-to-all-start.2
  272.1 5.1 fusion.95
  278.1 1.6 add_convert_fusion.1
  279.8 30.3 %all-to-all-done.2 = bf16[32,16,768]{2,1,0:T(8,128)(2,1)S(1)} async-done(((bf16[32,16,768]{2,1,0:T(8,128)(2,1)}), bf16[32,16,768]{2,1,0:T(8,128)(2,1)S(1)}, u32[]{:S(2)}, u32[]{:S(2)}) %all-to-all-start.2) | async-done | bytes 786464 | tf_op jit(solution)/shard_map/all_to_all | solution.py:230
  310.1 3.3 all-to-all-start.4
  313.4 1.3 convert_reduce_fusion.2
  314.9 1.3 concatenate.45
  316.2 2.0 gather_fusion.2
  318.2 22.2 %all-to-all-done.4 = bf16[32,16,768]{2,1,0:T(8,128)(2,1)S(1)} async-done(((bf16[32,16,768]{2,1,0:T(8,128)(2,1)}), bf16[32,16,768]{2,1,0:T(8,128)(2,1)S(1)}, u32[]{:S(2)}, u32[]{:S(2)}) %all-to-all-start.4) | async-done | bytes 786464 | tf_op jit(solution)/shard_map/all_to_all | solution.py:237
  340.4 2.0 gather_fusion.4
  342.5 24.6 %reduce-scatter.5.cloned.1.call-done = f32[96,768]{1,0:T(8,128)} async-done(((f32[3072,768]{1,0:T(8,128)}), f32[96,768]{1,0:T(8,128)}) %reduce-scatter.5.cloned.1.call-update) | async-done | bytes 294928 | tf_op jit(solution)/shard_map/reduce_scatter | solution.py:266
  367.0 1.7 multiply_reduce_fusion.7
  368.7 211.7 %reduce-scatter.3.cloned.1.call-done = f32[24,6144]{1,0:T(8,128)} async-done(((f32[768,6144]{1,0:T(8,128)}), f32[24,6144]{1,0:T(8,128)}) %reduce-scatter.3.cloned.1.call-update) | async-done | bytes 589840 | tf_op jit(solution)/shard_map/reduce_scatter | solution.py:269
  580.4 1.9 multiply_reduce_fusion.6
  583.6 1.3 broadcast_select_fusion
  584.9 39.6 %all-reduce.2 = (f32[]{:T(128)}, f32[12,768]{1,0:T(8,128)S(1)}) all-reduce(f32[]{:T(128)S(6)} %add.193, f32[12,768]{1,0:T(8,128)} %concatenate.45), channel_id=1, replica_groups=mesh['dev'=32] {'dev'}, use_global_device_ids=true, to_apply=%region_25.26 | all-reduce | flops 9217 | bytes 73736 | tf_op jit(solution)/shard_map/psum | solution.py:283
  626.5 1.5 multiply_add_fusion.6
  628.0 2.0 multiply_add_fusion.3
  630.1 2.6 multiply_add_fusion
  (184 shorter events, 24.5 us)
Async XLA Ops:
  7.2 18.2 %copy-start.25 = (bf16[512,768]{1,0:T(8,128)(2,1)S(1)}, bf16[512,768]{1,0:T(8,128)(2,1)}, u32[]{:S(2)}) copy-start(bf16[512,768]{1,0:T(8,128)(2,1)} %param.12) | copy-start | bytes 2359300
  7.2 112.9 %all-gather.3.cloned.1.call-start = ((), (), s32[]{:S(2)}) async-start(), calls=%async_computation.7 | async-start | bytes 9732096 | tf_op jit(solution)/shard_map/all_gather | solution.py:88
  9.8 8.3 %copy-start.44 = (pred[512]{0:T(512)(128)(4,1)}, pred[512]{0:T(512)(128)(4,1)S(1)}, u32[]{:S(2)}) copy-start(pred[512]{0:T(512)(128)(4,1)S(1)} %get-tuple-element.50) | copy-start | bytes 1540
  18.1 14.4 %all-to-all-start.1 = ((s32[32,1,16]{2,1,0:T(1,128)}), s32[32,1,16]{2,1,0:T(1,128)S(1)}, u32[]{:S(2)}, u32[]{:S(2)}) async-start(s32[32,1,16]{2,1,0:T(1,128)} %bitcast.5), calls=%async_computation.1 | async-start | bytes 32768 | tf_op jit(solution)/shard_map/all_to_all | solution.py:106
  25.5 9.7 %copy-start.22 = (f32[96,768]{1,0:T(8,128)S(1)}, f32[96,768]{1,0:T(8,128)}, u32[]{:S(2)}) copy-start(f32[96,768]{1,0:T(8,128)} %param.18) | copy-start | bytes 884740
  25.5 10.4 %slice-start = ((f32[12,768]{1,0:T(8,128)}), f32[4,768]{1,0:T(4,128)S(1)}, s32[]{:S(2)}) async-start(f32[12,768]{1,0:T(8,128)} %param.21), calls=%async_computation.11 | async-start | bytes 24576 | tf_op jit(solution)/shard_map/slice | solution.py:114
  25.5 10.4 %copy-start.26 = (bf16[512,768]{1,0:T(8,128)(2,1)S(1)}, bf16[512,768]{1,0:T(8,128)(2,1)}, u32[]{:S(2)}) copy-start(bf16[512,768]{1,0:T(8,128)(2,1)} %param.13) | copy-start | bytes 2359300
  32.5 35.8 %all-to-all-start = ((bf16[32,16,768]{2,1,0:T(8,128)(2,1)}), bf16[32,16,768]{2,1,0:T(8,128)(2,1)S(1)}, u32[]{:S(2)}, u32[]{:S(2)}) async-start(bf16[32,16,768]{2,1,0:T(8,128)(2,1)} %bitcast.2), calls=%async_computation | async-start | bytes 1572864 | tf_op jit(solution)/shard_map/all_to_all | solution.py:104
  35.1 151.0 %all-gather.5.cloned.1.call-start = ((), (), s32[]{:S(2)}) async-start(), calls=%async_computation.8 | async-start | bytes 4866048 | tf_op jit(solution)/shard_map/all_gather | solution.py:89
  35.9 2.8 copy-start.34
  39.4 84.7 %copy-start.35 = (f32[768]{0:T(1024)}, f32[768]{0:T(1024)S(1)}, u32[]{:S(2)}) copy-start(f32[768]{0:T(1024)S(1)} %get-tuple-element.26) | copy-start | bytes 9220
  39.4 106.7 %copy-start.47 = (f32[768]{0:T(1024)}, f32[768]{0:T(1024)S(1)}, u32[]{:S(2)}) copy-start(f32[768]{0:T(1024)S(1)} %get-tuple-element.20) | copy-start | bytes 9220
  68.3 73.6 %copy-start = (bf16[32,16,768]{2,1,0:T(8,128)(2,1)}, bf16[32,16,768]{2,1,0:T(8,128)(2,1)S(1)}, u32[]{:S(2)}) copy-start(bf16[32,16,768]{2,1,0:T(8,128)(2,1)S(1)} %all-to-all-done) | copy-start | bytes 2359300
  68.3 82.6 %all-to-all-start.3 = ((bf16[32,16,768]{2,1,0:T(8,128)(2,1)}), bf16[32,16,768]{2,1,0:T(8,128)(2,1)S(1)}, u32[]{:S(2)}, u32[]{:S(2)}) async-start(bf16[32,16,768]{2,1,0:T(8,128)(2,1)} %bitcast.14), calls=%async_computation.3 | async-start | bytes 1572864 | tf_op jit(solution)/shard_map/all_to_all | solution.py:105
  72.0 295.0 %reduce-scatter.5.cloned.1.call-start = ((), (), s32[]{:S(2)}) async-start(), calls=%async_computation.10 | async-start | bytes 9732096 | tf_op jit(solution)/shard_map/reduce_scatter | solution.py:266
  72.3 51.8 %copy-start.37 = (f32[512]{0:T(512)}, f32[512]{0:T(512)S(1)}, u32[]{:S(2)}) copy-start(f32[512]{0:T(512)S(1)} %div.98) | copy-start | bytes 6148
  72.7 0.6 copy-start.41
  72.7 51.4 %copy-start.39 = (f32[512]{0:T(512)}, f32[512]{0:T(512)S(1)}, u32[]{:S(2)}) copy-start(f32[512]{0:T(512)S(1)} %rsqrt.22) | copy-start | bytes 6148
  73.7 46.4 %copy-start.27 = (bf16[512,768]{1,0:T(8,128)(2,1)}, bf16[512,768]{1,0:T(8,128)(2,1)S(1)}, u32[]{:S(2)}) copy-start(bf16[512,768]{1,0:T(8,128)(2,1)S(1)} %fusion.35) | copy-start | bytes 2359300
  125.7 5.8 copy-start.15
  127.4 4.1 copy-start.2
  134.9 4.3 copy-start.13
  137.0 2.7 copy-start.11
  137.0 2.2 copy-start.29
  139.2 2.1 copy-start.9
  139.7 3.3 slice-start.1
  139.7 4.7 slice-start.2
  141.3 3.5 slice-start.3
  141.9 3.9 copy-start.17
  145.8 68.6 %copy-start.6 = (f32[512,768]{1,0:T(8,128)}, f32[512,768]{1,0:T(8,128)S(1)}, u32[]{:S(2)}) copy-start(f32[512,768]{1,0:T(8,128)S(1)} %get-tuple-element.65) | copy-start | bytes 4718596
  150.9 71.9 %copy-start.4 = (bf16[32,16,768]{2,1,0:T(8,128)(2,1)}, bf16[32,16,768]{2,1,0:T(8,128)(2,1)S(1)}, u32[]{:S(2)}) copy-start(bf16[32,16,768]{2,1,0:T(8,128)(2,1)S(1)} %all-to-all-done.3) | copy-start | bytes 2359300
  186.2 19.6 %copy-start.8 = (f32[512,3072]{1,0:T(8,128)S(1)}, f32[512,3072]{1,0:T(8,128)}, u32[]{:S(2)}) copy-start(f32[512,3072]{1,0:T(8,128)} %fusion.12) | copy-start | bytes 18874372
  207.3 1.7 copy-start.19
  214.2 366.2 %reduce-scatter.3.cloned.1.call-start = ((), (), s32[]{:S(2)}) async-start(), calls=%async_computation.9 | async-start | bytes 19464192 | tf_op jit(solution)/shard_map/reduce_scatter | solution.py:269
  227.6 3.8 copy-start.12
  231.4 2.4 copy-start.10
  233.8 2.4 copy-start.14
  233.8 2.6 copy-start.30
  236.4 11.5 %copy-start.31 = (bf16[512,12,64]{0,2,1:T(8,128)(2,1)}, bf16[512,12,64]{0,2,1:T(8,128)(2,1)S(1)}, u32[]{:S(2)}) copy-start(bf16[512,12,64]{0,2,1:T(8,128)(2,1)S(1)} %get-tuple-element.44) | copy-start | bytes 2359300
  237.3 1.2 copy-start.3
  244.3 1.2 copy-start.16
  245.5 2.5 copy-start.32
  246.0 1.2 copy-start.18
  246.5 1.5 copy-start.28
  247.2 2.9 copy-start.33
  248.0 2.1 copy-start.7
  248.0 2.1 copy-start.48
  248.0 2.6 copy-start.49
  260.4 0.7 copy-start.46
  261.1 11.0 %copy-start.1 = (bf16[32,16,768]{2,1,0:T(8,128)(2,1)S(1)}, bf16[32,16,768]{2,1,0:T(8,128)(2,1)}, u32[]{:S(2)}) copy-start(bf16[32,16,768]{2,1,0:T(8,128)(2,1)} %copy-done) | copy-start | bytes 2359300
  261.1 11.0 %copy-start.36 = (f32[768]{0:T(1024)S(1)}, f32[768]{0:T(1024)}, u32[]{:S(2)}) copy-start(f32[768]{0:T(1024)} %copy-done.35) | copy-start | bytes 9220
  261.1 11.0 %copy-start.38 = (f32[512]{0:T(512)S(1)}, f32[512]{0:T(512)}, u32[]{:S(2)}) copy-start(f32[512]{0:T(512)} %copy-done.37) | copy-start | bytes 6148
  268.4 41.7 %all-to-all-start.2 = ((bf16[32,16,768]{2,1,0:T(8,128)(2,1)}), bf16[32,16,768]{2,1,0:T(8,128)(2,1)S(1)}, u32[]{:S(2)}, u32[]{:S(2)}) async-start(bf16[32,16,768]{2,1,0:T(8,128)(2,1)} %bitcast.162), calls=%async_computation.2 | async-start | bytes 1572864 | tf_op jit(solution)/shard_map/all_to_all | solution.py:230
  272.1 5.2 copy-start.42
  272.1 5.2 copy-start.40
  272.1 6.0 copy-start.5
  277.3 36.1 %copy-start.43 = (s32[512]{0:T(512)S(1)}, s32[512]{0:T(512)}, u32[]{:S(2)}) copy-start(s32[512]{0:T(512)} %get-tuple-element.54) | copy-start | bytes 6148
  310.1 30.4 %all-to-all-start.4 = ((bf16[32,16,768]{2,1,0:T(8,128)(2,1)}), bf16[32,16,768]{2,1,0:T(8,128)(2,1)S(1)}, u32[]{:S(2)}, u32[]{:S(2)}) async-start(bf16[32,16,768]{2,1,0:T(8,128)(2,1)} %bitcast.149), calls=%async_computation.4 | async-start | bytes 1572864 | tf_op jit(solution)/shard_map/all_to_all | solution.py:237
  318.2 265.4 %copy-start.45 = (pred[512]{0:T(512)(128)(4,1)S(1)}, pred[512]{0:T(512)(128)(4,1)}, u32[]{:S(2)}) copy-start(pred[512]{0:T(512)(128)(4,1)} %copy-done.44) | copy-start | bytes 1540
  340.4 287.6 %copy-start.23 = (f32[96,768]{1,0:T(8,128)S(1)}, f32[96,768]{1,0:T(8,128)}, u32[]{:S(2)}) copy-start(f32[96,768]{1,0:T(8,128)} %param.18) | copy-start | bytes 884740
  342.5 287.6 %copy-start.20 = (f32[24,6144]{1,0:T(8,128)S(1)}, f32[24,6144]{1,0:T(8,128)}, u32[]{:S(2)}) copy-start(f32[24,6144]{1,0:T(8,128)} %param.15) | copy-start | bytes 1769476
  367.0 261.0 %copy-start.24 = (f32[96,768]{1,0:T(8,128)S(1)}, f32[96,768]{1,0:T(8,128)}, u32[]{:S(2)}) copy-start(f32[96,768]{1,0:T(8,128)} %reduce-scatter.5.cloned.1.call-done) | copy-start | bytes 884740
  580.4 49.7 %copy-start.21 = (f32[24,6144]{1,0:T(8,128)S(1)}, f32[24,6144]{1,0:T(8,128)}, u32[]{:S(2)}) copy-start(f32[24,6144]{1,0:T(8,128)} %reduce-scatter.3.cloned.1.call-done) | copy-start | bytes 1769476
Sparse Core Ops, SparseCore 0:
  11.5 108.5 all-gather.2
  123.5 62.5 all-gather.4
  214.3 152.6 reduce-scatter.4
  374.4 205.9 reduce-scatter.2
where the time goes:
time: 649 us; the launch traced here: 641 us
  waiting for transfers between devices  402 us (62%)
  matrix products  76.8 us (12%)
  other arithmetic  45.4 us (7%)
  blocking collectives  39.6 us (6%)
  local copies, waits for them, and re-layouts  37.1 us (6%)
  starting transfers between devices  20.9 us (3%)
  between operations  19 us (3%)
    reduce_scatter x1, waiting for transfers between devices, body(): lax.psum_scatter(jnp.concatenate([inner_rows(low_one, dqkv_low), jnp.conc...  212 us
    all_gather x1, waiting for transfers between devices, body(): lax.all_gather(wide_weight.astype(jnp.bfloat16), 'dev', axis=0, tiled=True)  46.4 us
    psum x1, blocking collectives, body(): total = lax.psum(shard_squares, 'dev') + jnp.sum(vector_grad * vector_grad)  39.6 us
    all_gather x1, waiting for transfers between devices, body(): lax.all_gather(down_weight.astype(jnp.bfloat16), 'dev', axis=0, tiled=True)  35.3 us
    dot_general x4, matrix products, against(): lax.dot_general(matrix, other, (((1,), (1,)), ((), ())), preferred_elemen...  34 us
    all_to_all x1, waiting for transfers between devices, body(): lax.all_to_all(output_low.reshape(devices, capacity, feature), 'dev', spl...  30.3 us
    all_to_all x1, waiting for transfers between devices, body(): lax.all_to_all(send_rows, 'dev', split_axis=0, concat_axis=0, tiled=True)  27.4 us
    reduce_scatter x1, waiting for transfers between devices, body(): lax.psum_scatter(inner_rows(hidden, work_grads), 'dev', scatter_dimension...  24.6 us
  transfers between devices with their start and end apart: 9, of which 8 were waited for; matrix products, arithmetic and copies ran while one was open for 17% of the time, Pallas kernels for 0%

commit v1 on v0

--- a/solution.py
+++ b/solution.py
@@ -3,12 +3,16 @@
 import jax
 import jax.numpy as jnp
 from jax import lax
+from jax.experimental import pallas as pl
+from jax.experimental.pallas import tpu as pltpu
 from jax.sharding import PartitionSpec as P
 
 HEADS = 12
 HEAD = 64
 FF = 3072
 DOCS_DEV = 4
+PLANE = 8
+MIB = 1 << 20
 
 
 epsilon = 1e-05
@@ -70,7 +74,7 @@
     return (is_live, jnp.minimum(slot_of, row_count - 1), anchor)
 
 
-def body(
+def plain_body(
     tokens,
     cotangent,
     segment_ids,
@@ -308,6 +312,922 @@
     )
 
 
+def flips(devices, mask):
+    return [(i, i ^ mask) for i in range(devices)]
+
+
+def shifts(devices, step):
+    return [(i, (i + PLANE * step) % devices) for i in range(devices)]
+
+
+def place():
+    me = lax.axis_index("dev")
+    return jnp.stack([me // PLANE, (me // 4) % 2, (me // 2) % 2, me % 2]).astype(jnp.int32)
+
+
+def core_order(core, mine, theirs):
+    first = jnp.where(core == 0, mine, theirs)
+    second = jnp.where(core == 0, theirs, mine)
+    return first, second
+
+
+def stack_along_z(block):
+    devices = lax.axis_size("dev")
+    depth = devices // PLANE
+    return jnp.stack(
+        [block] + [lax.ppermute(block, "dev", shifts(devices, k)) for k in range(1, depth)], 0
+    )
+
+
+def gather_pieces(own):
+    devices = lax.axis_size("dev")
+    half = own.shape[2] // 2
+    from_x = lax.ppermute(own, "dev", flips(devices, 2))
+    from_y = lax.ppermute(own, "dev", flips(devices, 4))
+    diag_a = lax.ppermute(from_x[:, :, :half], "dev", flips(devices, 4))
+    diag_b = lax.ppermute(from_y[:, :, half:], "dev", flips(devices, 2))
+    mine = (own, from_x, from_y, diag_a, diag_b)
+    return mine + tuple(lax.ppermute(piece, "dev", flips(devices, 1)) for piece in mine)
+
+
+def wide_sum(first, second):
+    return (first.astype(jnp.float32) + second.astype(jnp.float32)).astype(jnp.bfloat16)
+
+
+def scatter_blocks(mine, theirs):
+    devices = lax.axis_size("dev")
+    depth = devices // PLANE
+    half = mine.shape[-1] // 2
+    mine = wide_sum(mine, lax.ppermute(theirs, "dev", flips(devices, 1)))
+    got_a = lax.ppermute(mine[3, :, :, :half], "dev", flips(devices, 4))
+    got_b = lax.ppermute(mine[3, :, :, half:], "dev", flips(devices, 2))
+    to_x = jnp.concatenate([wide_sum(mine[1, :, :, :half], got_a), mine[1, :, :, half:]], -1)
+    to_y = jnp.concatenate([mine[2, :, :, :half], wide_sum(mine[2, :, :, half:], got_b)], -1)
+    got_x = lax.ppermute(to_x, "dev", flips(devices, 2)).astype(jnp.float32)
+    got_y = lax.ppermute(to_y, "dev", flips(devices, 4)).astype(jnp.float32)
+    total = mine[0].astype(jnp.float32) + got_x + got_y
+    result = total[0]
+    for k in range(1, depth):
+        result = result + lax.ppermute(
+            total[k].astype(jnp.bfloat16), "dev", shifts(devices, k)
+        ).astype(jnp.float32)
+    return result
+
+
+def join_columns(core, block):
+    devices = lax.axis_size("dev")
+    rows = block.shape[0] // 2
+    keep, give = core_order(core, block[:rows], block[rows:])
+    got = lax.ppermute(give, "dev", flips(devices, 1))
+    return jnp.concatenate(core_order(core, keep, got), 1)
+
+
+def exchange(rows):
+    return lax.all_to_all(rows, "dev", split_axis=0, concat_axis=0, tiled=True)
+
+
+ANYWHERE = pl.BlockSpec(memory_space=pl.ANY)
+SCALARS = pl.BlockSpec(memory_space=pltpu.SMEM)
+
+
+def whole(*shape):
+    return pl.BlockSpec(shape, lambda *_: (0,) * len(shape))
+
+
+def settings(limit):
+    return pltpu.CompilerParams(vmem_limit_bytes=limit * MIB)
+
+
+def cost(flops, moved, exps=0):
+    return pl.CostEstimate(flops=int(flops), bytes_accessed=int(moved), transcendentals=int(exps))
+
+
+def shaped(shape, dtype):
+    return jax.ShapeDtypeStruct(shape, dtype)
+
+
+def by_rows(matrix, other):
+    return lax.dot_general(
+        matrix, other, (((1,), (1,)), ((), ())), preferred_element_type=jnp.float32
+    )
+
+
+def by_columns(matrix, other):
+    return lax.dot_general(
+        matrix, other, (((0,), (0,)), ((), ())), preferred_element_type=jnp.float32
+    )
+
+
+def normed(values):
+    center = values - jnp.mean(values, -1, keepdims=True)
+    scale = lax.rsqrt(jnp.mean(center * center, -1, keepdims=True) + epsilon)
+    return center * scale, scale
+
+
+def norm_back(grad, gain, unit, scale):
+    inner = grad * gain
+    return scale * (
+        inner
+        - jnp.mean(inner, -1, keepdims=True)
+        - unit * jnp.mean(inner * unit, -1, keepdims=True)
+    )
+
+
+def iota(shape, axis):
+    return lax.broadcasted_iota(jnp.int32, shape, axis)
+
+
+def slots_of(ids_row, capacity, groups):
+    count = ids_row.shape[1]
+    square = (count, count)
+    ids = jnp.sum(
+        jnp.where(iota(square, 0) == iota(square, 1), ids_row, 0), axis=1, keepdims=True
+    )
+    group = jnp.right_shift(ids, DOCS_DEV.bit_length() - 1)
+    lanes = max(128, groups)
+    onehot = jnp.where(group == iota((count, lanes), 1), 1.0, 0.0)
+    lower = jnp.where(iota(square, 0) > iota(square, 1), 1.0, 0.0).astype(jnp.bfloat16)
+    earlier = product(lower, onehot.astype(jnp.bfloat16))
+    within = jnp.sum(earlier * onehot, axis=1, keepdims=True).astype(jnp.int32)
+    return jnp.where(ids >= 0, group * capacity + within, -1)
+
+
+def route(ids_row, tokens, cotangent, devices):
+    count, feature = tokens.shape
+
+    def kernel(ids_ref, tokens_ref, cotangent_ref, rows_ref, grads_ref, code_ref, slot_ref):
+        ids = ids_ref[...]
+        slot = slots_of(ids, count // devices, devices)
+        slot_ref[...] = slot
+        move = jnp.where(slot == iota((count, count), 1), 1.0, 0.0).astype(jnp.bfloat16)
+        rows_ref[...] = by_columns(move, tokens_ref[...]).astype(jnp.bfloat16)
+        grads_ref[...] = by_columns(move, cotangent_ref[...]).astype(jnp.bfloat16)
+        code = jnp.where(ids >= 0, jnp.bitwise_and(ids, DOCS_DEV - 1) + 1, 0)
+        code = jnp.broadcast_to(code.astype(jnp.float32), (8, count)).astype(jnp.bfloat16)
+        code_ref[...] = product(code, move)[:1].astype(jnp.int32)
+
+    rows = shaped((count, feature), jnp.bfloat16)
+    return pl.pallas_call(
+        kernel,
+        out_shape=[rows, rows, shaped((1, count), jnp.int32), shaped((count, 1), jnp.int32)],
+        compiler_params=settings(24),
+        cost_estimate=cost(4 * count * count * feature, 8 * count * feature),
+    )(ids_row, tokens, cotangent)
+
+
+def give_back(slot, rows):
+    count, feature = rows.shape
+
+    def kernel(slot_ref, rows_ref, out_ref):
+        move = jnp.where(slot_ref[...] == iota((count, count), 1), 1.0, 0.0).astype(jnp.bfloat16)
+        out_ref[...] = product(move, rows_ref[...]).astype(jnp.bfloat16)
+
+    return pl.pallas_call(
+        kernel,
+        out_shape=shaped((count, feature), jnp.bfloat16),
+        compiler_params=settings(16),
+        cost_estimate=cost(2 * count * count * feature, 4 * count * feature),
+    )(slot, rows)
+
+
+def wide_copies(where_ref, pieces, buffer, sems):
+    z, y, x, core = where_ref[0], where_ref[1], where_ref[2], where_ref[3]
+    copies = []
+    for half_index, (own, from_x, from_y, diag_a, diag_b) in (
+        (core, pieces[:5]),
+        (1 - core, pieces[5:]),
+    ):
+        depth, rows, columns = own.shape
+        half = columns // 2
+        for step in range(depth):
+            zz = lax.rem(z - step + depth, depth)
+            for source, yy, xx, offset, width in (
+                (own, y, x, 0, columns),
+                (from_x, y, 1 - x, 0, columns),
+                (from_y, 1 - y, x, 0, columns),
+                (diag_a, 1 - y, 1 - x, 0, half),
+                (diag_b, 1 - y, 1 - x, half, half),
+            ):
+                row = pl.multiple_of(((zz * 2 + yy) * 2 + xx) * rows, 16)
+                column = pl.multiple_of(half_index * columns + offset, 128)
+                copies.append(
+                    pltpu.make_async_copy(
+                        source.at[step],
+                        buffer.at[pl.ds(row, rows), pl.ds(column, width)],
+                        sems.at[len(copies)],
+                    )
+                )
+    return copies
+
+
+def down_copies(where_ref, pieces, buffer, sems):
+    z, y, x, core = where_ref[0], where_ref[1], where_ref[2], where_ref[3]
+    copies = []
+    for part, (own, from_x, from_y, diag_a, diag_b) in (
+        (core, pieces[:5]),
+        (1 - core, pieces[5:]),
+    ):
+        depth, rows, columns = own.shape
+        half = columns // 2
+        for step in range(depth):
+            zz = lax.rem(z - step + depth, depth)
+            for source, yy, xx, offset, width in (
+                (own, y, x, 0, columns),
+                (from_x, y, 1 - x, 0, columns),
+                (from_y, 1 - y, x, 0, columns),
+                (diag_a, 1 - y, 1 - x, 0, half),
+                (diag_b, 1 - y, 1 - x, half, half),
+            ):
+                row = pl.multiple_of((((zz * 2 + yy) * 2 + xx) * 2 + part) * rows, 16)
+                copies.append(
+                    pltpu.make_async_copy(
+                        source.at[step],
+                        buffer.at[pl.ds(row, rows), pl.ds(offset, width)],
+                        sems.at[len(copies)],
+                    )
+                )
+    return copies
+
+
+def project(where, work, vector, pieces):
+    count, feature = work.shape
+    depth = pieces[0].shape[0]
+    chunk = 2 * pieces[0].shape[2]
+    tile = 256
+
+    def kernel(where_ref, work_ref, vector_ref, *refs):
+        low_ref, out_ref, weights_ref, buffer, sems, out_sem = refs[10:]
+        copies = wide_copies(where_ref, refs[:10], buffer, sems)
+        for copy in copies:
+            copy.start()
+
+        def rows_of(index, carry):
+            rows = pl.ds(pl.multiple_of(index * 64, 64), 64)
+            unit, _ = normed(work_ref[rows, :].astype(jnp.float32))
+            low_ref[rows, :] = (unit * vector_ref[0:1, :] + vector_ref[1:2, :]).astype(
+                jnp.bfloat16
+            )
+            return carry
+
+        lax.fori_loop(0, count // 64, rows_of, 0)
+        for copy in copies:
+            copy.wait()
+        store = pltpu.make_async_copy(buffer, weights_ref, out_sem)
+        store.start()
+        for part, bias in ((0, 4), (1, None), (2, 5)):
+
+            def columns_of(index, carry):
+                inner = pl.ds(pl.multiple_of(index * tile, tile), tile)
+                columns = pl.ds(pl.multiple_of(part * feature + index * tile, tile), tile)
+                value = product(low_ref[...], buffer[:, columns])
+                if bias is not None:
+                    value = value + vector_ref[bias : bias + 1, inner]
+                out_ref[:, columns] = value.astype(jnp.bfloat16)
+                return carry
+
+            lax.fori_loop(0, feature // tile, columns_of, 0)
+        store.wait()
+
+    return pl.pallas_call(
+        kernel,
+        out_shape=[
+            shaped((count, feature), jnp.bfloat16),
+            shaped((count, 3 * feature), jnp.bfloat16),
+            shaped((feature, chunk), jnp.bfloat16),
+        ],
+        in_specs=[SCALARS, whole(*work.shape), whole(*vector.shape)] + [ANYWHERE] * 10,
+        out_specs=[whole(count, feature), whole(count, 3 * feature), ANYWHERE],
+        scratch_shapes=[
+            pltpu.VMEM((feature, chunk), jnp.bfloat16),
+            pltpu.SemaphoreType.DMA((10 * depth,)),
+            pltpu.SemaphoreType.DMA,
+        ],
+        compiler_params=settings(32),
+        cost_estimate=cost(6 * count * feature * feature, 12 * feature * feature),
+    )(where, work, vector, *pieces)
+
+
+def code_column(code_ref):
+    count = code_ref.shape[1]
+    square = (count, count)
+    return jnp.sum(
+        jnp.where(iota(square, 0) == iota(square, 1), code_ref[...], 0.0), axis=1, keepdims=True
+    )
+
+
+def one_head(values, head):
+    lanes = iota(values.shape, 1)
+    inside = (lanes >= head * HEAD) & (lanes < (head + 1) * HEAD)
+    return jnp.where(inside, values, 0.0).astype(jnp.bfloat16)
+
+
+def attend(projected, code, work, vector, weights):
+    count, feature = work.shape
+    pairs = feature // 128
+    tile = 256
+
+    def kernel(
+        q_ref, k_ref, v_ref, weight_ref, code_ref, work_ref, vector_ref,
+        attended_ref, resid_ref, low_ref, stat_ref, total, column,
+    ):
+        pair = pl.program_id(0)
+
+        @pl.when(pair == 0)
+        def _():
+            column[...] = code_column(code_ref)
+            total[...] = jnp.zeros_like(total)
+
+        keys = k_ref[...]
+        values = v_ref[...].astype(jnp.float32).T.astype(jnp.bfloat16)
+        scaled = q_ref[...].astype(jnp.float32) * 0.125
+        heads = []
+        for head in range(2):
+            query = one_head(scaled, head)
+            parts = []
+            for start in range(0, count, tile):
+                span = slice(start, start + tile)
+                scores = by_rows(keys, query[span])
+                same = column[...] == code_ref[:, span]
+                scores = jnp.where(same, scores, masked_value)
+                most = jnp.max(scores, 0, keepdims=True)
+                powers = jnp.exp(scores - most)
+                sums = jnp.sum(powers, 0, keepdims=True)
+                low = (powers * (1.0 / sums)).astype(jnp.bfloat16)
+                stat_ref[0, head : head + 1, span] = most + jnp.log(sums)
+                parts.append(product(values[head * HEAD : (head + 1) * HEAD], low))
+            heads.append(jnp.concatenate(parts, 1))
+        low = jnp.concatenate(heads, 0).T.astype(jnp.bfloat16)
+        attended_ref[...] = low
+        total[...] += product(low, weight_ref[...])
+
+        @pl.when(pair == pairs - 1)
+        def _():
+            def rows_of(index, carry):
+                rows = pl.ds(pl.multiple_of(index * 64, 64), 64)
+                resid = (
+                    work_ref[rows, :].astype(jnp.float32) + total[rows, :] + vector_ref[6:7, :]
+                )
+                resid_ref[rows, :] = resid
+                unit, _ = normed(resid)
+                low_ref[rows, :] = (unit * vector_ref[2:3, :] + vector_ref[3:4, :]).astype(
+                    jnp.bfloat16
+                )
+                return carry
+
+            lax.fori_loop(0, count // 64, rows_of, 0)
+
+    def columns_at(first):
+        return pl.BlockSpec((count, 128), lambda pair: (0, first + pair))
+
+    return pl.pallas_call(
+        kernel,
+        grid=(pairs,),
+        out_shape=[
+            shaped((count, feature), jnp.bfloat16),
+            shaped((count, feature), jnp.float32),
+            shaped((count, feature), jnp.bfloat16),
+            shaped((pairs, 8, count), jnp.float32),
+        ],
+        in_specs=[
+            columns_at(0),
+            columns_at(pairs),
+            columns_at(2 * pairs),
+            pl.BlockSpec((128, feature), lambda pair: (pair, 3)),
+            whole(1, count),
+            whole(count, feature),
+            whole(*vector.shape),
+        ],
+        out_specs=[
+            columns_at(0),
+            whole(count, feature),
+            whole(count, feature),
+            pl.BlockSpec((1, 8, count), lambda pair: (pair, 0, 0)),
+        ],
+        scratch_shapes=[
+            pltpu.VMEM((count, feature), jnp.float32),
+            pltpu.VMEM((count, 1), jnp.float32),
+        ],
+        compiler_params=settings(32),
+        cost_estimate=cost(
+            8 * count * count * feature, 14 * count * feature, HEADS * count * count
+        ),
+    )(projected, projected, projected, weights, code, work, vector)
+
+
+def widen(where, low, bias_row, pieces):
+    count, feature = low.shape
+    depth = pieces[0].shape[0]
+    chunk = 2 * pieces[0].shape[2]
+    tile = 512
+    steps = chunk // tile
+
+    def kernel(where_ref, low_ref, bias_ref, *refs):
+        hidden_ref, slope_ref, weights_ref, buffer, sems, out_sem = refs[10:]
+        step = pl.program_id(0)
+        store = pltpu.make_async_copy(buffer, weights_ref, out_sem)
+
+        @pl.when(step == 0)
+        def _():
+            copies = wide_copies(where_ref, refs[:10], buffer, sems)
+            for copy in copies:
+                copy.start()
+            for copy in copies:
+                copy.wait()
+            store.start()
+
+        columns = pl.ds(pl.multiple_of(step * tile, tile), tile)
+        up = product(low_ref[...], buffer[:, columns]) + bias_ref[...]
+        below = 0.5 * (1.0 + lax.erf(up * (0.5**0.5)))
+        hidden_ref[...] = (up * below).astype(jnp.bfloat16)
+        slope_ref[...] = below + up * (jnp.exp(-0.5 * up * up) * ((2.0 * math.pi) ** -0.5))
+
+        @pl.when(step == steps - 1)
+        def _():
+            store.wait()
+
+    block = pl.BlockSpec((count, tile), lambda step: (0, step))
+    return pl.pallas_call(
+        kernel,
+        grid=(steps,),
+        out_shape=[
+            shaped((count, chunk), jnp.bfloat16),
+            shaped((count, chunk), jnp.float32),
+            shaped((feature, chunk), jnp.bfloat16),
+        ],
+        in_specs=[
+            SCALARS,
+            whole(count, feature),
+            pl.BlockSpec((1, tile), lambda step: (0, step)),
+        ]
+        + [ANYWHERE] * 10,
+        out_specs=[block, block, ANYWHERE],
+        scratch_shapes=[
+            pltpu.VMEM((feature, chunk), jnp.bfloat16),
+            pltpu.SemaphoreType.DMA((10 * depth,)),
+            pltpu.SemaphoreType.DMA,
+        ],
+        compiler_params=settings(32),
+        cost_estimate=cost(
+            2 * count * feature * chunk, 4 * feature * chunk + 6 * count * chunk, count * chunk
+        ),
+    )(where, low, bias_row, *pieces)
+
+
+def down_gradient(where, hidden, grads, depth):
+    count, wide = hidden.shape
+    feature = grads.shape[1]
+    rows = wide // (depth * PLANE)
+    part = wide // depth
+
+    def kernel(where_ref, hidden_ref, grads_ref, mine_ref, theirs_ref, result):
+        y, x, core = where_ref[1], where_ref[2], where_ref[3]
+        result[...] = by_columns(hidden_ref[...], grads_ref[...])
+        for yy in range(2):
+            for xx in range(2):
+                spot = jnp.bitwise_xor(y, yy) * 2 + jnp.bitwise_xor(x, xx)
+                first = (yy * 2 + xx) * 2
+                for target, side in ((mine_ref, core), (theirs_ref, 1 - core)):
+                    row = pl.multiple_of((first + side) * rows, 16)
+                    target[spot, 0] = result[pl.ds(row, rows), :].astype(jnp.bfloat16)
+
+    shape = shaped((4, depth, rows, feature), jnp.bfloat16)
+    block = pl.BlockSpec((4, 1, rows, feature), lambda step, where_ref: (0, step, 0, 0))
+    return pl.pallas_call(
+        kernel,
+        out_shape=[shape, shape],
+        grid_spec=pltpu.PrefetchScalarGridSpec(
+            num_scalar_prefetch=1,
+            grid=(depth,),
+            in_specs=[
+                pl.BlockSpec(
+                    (count, part),
+                    lambda step, where_ref: (0, lax.rem(where_ref[0] + step, depth)),
+                ),
+                whole(count, feature),
+            ],
+            out_specs=[block, block],
+            scratch_shapes=[pltpu.VMEM((part, feature), jnp.float32)],
+        ),
+        compiler_params=settings(24),
+        cost_estimate=cost(2 * count * wide * feature, 2 * wide * (count + feature)),
+    )(where, hidden, grads)
+
+
+def put_wide(where_ref, result, half, offset, mine_ref, theirs_ref):
+    z, y, x, core = where_ref[0], where_ref[1], where_ref[2], where_ref[3]
+    _, depth, rows, _ = mine_ref.shape
+    width = result.shape[1]
+    columns = pl.ds(pl.multiple_of(offset, 128), width)
+    for is_mine, target in ((True, mine_ref), (False, theirs_ref)):
+
+        @pl.when((half == core) == is_mine)
+        def _():
+            for chip in range(4 * depth):
+                zz, yy, xx = chip // 4, (chip // 2) % 2, chip % 2
+                step = lax.rem(zz - z + depth, depth)
+                spot = jnp.bitwise_xor(y, yy) * 2 + jnp.bitwise_xor(x, xx)
+                target[spot, step, :, columns] = result[chip * rows : (chip + 1) * rows].astype(
+                    jnp.bfloat16
+                )
+
+
+def feed_back(where, hidden, slope, low, grads, resid, vector, up_weights, pieces):
+    count, wide = hidden.shape
+    feature = grads.shape[1]
+    depth, rows, _ = pieces[0].shape
+    tile = 512
+    steps = wide // tile
+    chip_rows = feature // (4 * depth)
+
+    def kernel(where_ref, hidden_ref, slope_ref, low_ref, grads_ref, resid_ref, vector_ref, up_ref, *refs):
+        (
+            out_ref, mine_ref, theirs_ref, dresid_ref, dlow_ref, sums_ref, bias_ref,
+            buffer, sems, total, back, flipped, result,
+        ) = refs[10:]
+        step = pl.program_id(0)
+
+        @pl.when(step == 0)
+        def _():
+            copies = down_copies(where_ref, refs[:10], buffer, sems)
+            for copy in copies:
+                copy.start()
+            flipped[...] = low_ref[...].astype(jnp.float32).T.astype(jnp.bfloat16)
+            total[...] = jnp.zeros_like(total)
+            back[...] = jnp.zeros_like(back)
+            for copy in copies:
+                copy.wait()
+
+        weights = buffer[pl.ds(pl.multiple_of(step * tile, tile), tile), :]
+        total[...] += product(hidden_ref[...], weights)
+        dup = (slope_ref[...] * by_rows(grads_ref[...], weights)).astype(jnp.bfloat16)
+        bias_ref[...] = jnp.sum(dup.astype(jnp.float32), 0, keepdims=True)
+        back[...] += by_rows(dup, up_ref[...])
+        result[...] = product(flipped[...], dup)
+        per_half = wide // 2 // tile
+        put_wide(
+            where_ref, result, step // per_half, lax.rem(step, per_half) * tile, mine_ref, theirs_ref
+        )
+
+        @pl.when(step == steps - 1)
+        def _():
+            sums_ref[...] = jnp.zeros_like(sums_ref)
+
+            def rows_of(index, carry):
+                rows = pl.ds(pl.multiple_of(index * 64, 64), 64)
+                resid = resid_ref[rows, :]
+                out_ref[rows, :] = (resid + (total[rows, :] + vector_ref[7:8, :])).astype(
+                    jnp.bfloat16
+                )
+                unit, scale = normed(resid)
+                da = back[rows, :]
+                dy = grads_ref[rows, :].astype(jnp.float32)
+                dresid = dy + norm_back(da, vector_ref[2:3, :], unit, scale)
+                dresid_ref[rows, :] = dresid
+                dlow = dresid.astype(jnp.bfloat16)
+                dlow_ref[rows, :] = dlow
+                for row, value in enumerate((da * unit, da, dlow.astype(jnp.float32), dy)):
+                    sums_ref[row : row + 1, :] += jnp.sum(value, 0, keepdims=True)
+                return carry
+
+            lax.fori_loop(0, count // 64, rows_of, 0)
+
+    block = pl.BlockSpec((count, tile), lambda step: (0, step))
+    split = (4, depth, chip_rows, wide // 2)
+    return pl.pallas_call(
+        kernel,
+        grid=(steps,),
+        out_shape=[
+            shaped((count, feature), jnp.bfloat16),
+            shaped(split, jnp.bfloat16),
+            shaped(split, jnp.bfloat16),
+            shaped((count, feature), jnp.float32),
+            shaped((count, feature), jnp.bfloat16),
+            shaped((8, feature), jnp.float32),
+            shaped((1, wide), jnp.float32),
+        ],
+        in_specs=[
+            SCALARS,
+            block,
+            block,
+            whole(count, feature),
+            whole(count, feature),
+            whole(count, feature),
+            whole(*vector.shape),
+            pl.BlockSpec((feature, tile), lambda step: (0, step)),
+        ]
+        + [ANYWHERE] * 10,
+        out_specs=[
+            whole(count, feature),
+            whole(*split),
+            whole(*split),
+            whole(count, feature),
+            whole(count, feature),
+            whole(8, feature),
+            pl.BlockSpec((1, tile), lambda step: (0, step)),
+        ],
+        scratch_shapes=[
+            pltpu.VMEM((wide, feature), jnp.bfloat16),
+            pltpu.SemaphoreType.DMA((10 * depth,)),
+            pltpu.VMEM((count, feature), jnp.float32),
+            pltpu.VMEM((count, feature), jnp.float32),
+            pltpu.VMEM((feature, count), jnp.bfloat16),
+            pltpu.VMEM((feature, tile), jnp.float32),
+        ],
+        compiler_params=settings(48),
+        cost_estimate=cost(8 * count * wide * feature, 6 * wide * feature + 6 * count * wide),
+    )(where, hidden, slope, low, grads, resid, vector, up_weights, *pieces)
+
+
+def attend_back(projected, code, stats, dlow, weights):
+    count, feature = dlow.shape
+    pairs = feature // 128
+    tile = 256
+
+    def kernel(
+        q_ref, k_ref, v_ref, code_ref, stat_ref, dlow_ref, weight_ref, out_ref, sums_ref, douts, column
+    ):
+        pair = pl.program_id(0)
+
+        @pl.when(pair == 0)
+        def _():
+            column[...] = code_column(code_ref)
+            for start in range(0, feature, tile):
+                span = slice(start, start + tile)
+                douts[:, span] = by_rows(dlow_ref[...], weight_ref[span, :]).astype(jnp.bfloat16)
+
+        keys, values = k_ref[...], v_ref[...]
+        flipped = keys.astype(jnp.float32).T.astype(jnp.bfloat16)
+        scaled = q_ref[...].astype(jnp.float32) * 0.125
+        dout = douts[:, pl.ds(pl.multiple_of(pair * 128, 128), 128)].astype(jnp.float32)
+        dkey = jnp.zeros((count, 128), jnp.float32)
+        dvalue = jnp.zeros((count, 128), jnp.float32)
+        heads = []
+        for head in range(2):
+            query = one_head(scaled, head)
+            dhead = one_head(dout, head)
+            parts = []
+            for start in range(0, count, tile):
+                span = slice(start, start + tile)
+                scores = by_rows(keys, query[span])
+                same = column[...] == code_ref[:, span]
+                probs = jnp.exp(
+                    jnp.where(same, scores, masked_value) - stat_ref[0, head : head + 1, span]
+                )
+                dprob = by_rows(values, dhead[span])
+                inner = jnp.sum(probs * dprob, 0, keepdims=True)
+                dscore = (probs * (dprob - inner)).astype(jnp.bfloat16)
+                dvalue = dvalue + product(probs.astype(jnp.bfloat16), dhead[span])
+                dkey = dkey + product(dscore, query[span])
+                parts.append(product(flipped[head * HEAD : (head + 1) * HEAD], dscore))
+            heads.append(jnp.concatenate(parts, 1))
+        dquery = (jnp.concatenate(heads, 0).T * 0.125).astype(jnp.bfloat16)
+        dvalue = dvalue.astype(jnp.bfloat16)
+        out_ref[0] = dquery
+        out_ref[1] = dkey.astype(jnp.bfloat16)
+        out_ref[2] = dvalue
+        sums_ref[0:1, :] = jnp.sum(dquery.astype(jnp.float32), 0, keepdims=True)
+        sums_ref[1:2, :] = jnp.sum(dvalue.astype(jnp.float32), 0, keepdims=True)
+
+    def columns_at(first):
+        return pl.BlockSpec((count, 128), lambda pair: (0, first + pair))
+
+    return pl.pallas_call(
+        kernel,
+        grid=(pairs,),
+        out_shape=[
+            shaped((3, count, feature), jnp.bfloat16),
+            shaped((8, feature), jnp.float32),
+        ],
+        in_specs=[
+            columns_at(0),
+            columns_at(pairs),
+            columns_at(2 * pairs),
+            whole(1, count),
+            pl.BlockSpec((1, 8, count), lambda pair: (pair, 0, 0)),
+            whole(count, feature),
+            pl.BlockSpec((feature, feature), lambda pair: (0, 3)),
+        ],
+        out_specs=[
+            pl.BlockSpec((3, count, 128), lambda pair: (0, 0, pair)),
+            pl.BlockSpec((8, 128), lambda pair: (0, pair)),
+        ],
+        scratch_shapes=[
+            pltpu.VMEM((count, feature), jnp.bfloat16),
+            pltpu.VMEM((count, 1), jnp.float32),
+        ],
+        compiler_params=settings(32),
+        cost_estimate=cost(
+            14 * count * count * feature, 16 * count * feature, HEADS * count * count
+        ),
+    )(projected, projected, projected, code, stats, dlow, weights)
+
+
+def first_gradient(where, low, dprojected, attended, dlow, depth):
+    count, feature = low.shape
+    split = (4, depth, feature // (4 * depth), 2 * feature)
+
+    def kernel(where_ref, low_ref, dprojected_ref, attended_ref, dlow_ref, mine_ref, theirs_ref, result):
+        step = pl.program_id(0)
+
+        @pl.when(step < 3)
+        def _():
+            result[...] = by_columns(low_ref[...], dprojected_ref[0])
+
+        @pl.when(step == 3)
+        def _():
+            result[...] = by_columns(attended_ref[...], dlow_ref[...])
+
+        put_wide(where_ref, result, step // 2, lax.rem(step, 2) * feature, mine_ref, theirs_ref)
+
+    return pl.pallas_call(
+        kernel,
+        grid=(4,),
+        out_shape=[shaped(split, jnp.bfloat16)] * 2,
+        in_specs=[
+            SCALARS,
+            whole(count, feature),
+            pl.BlockSpec((1, count, feature), lambda step: (jnp.minimum(step, 2), 0, 0)),
+            whole(count, feature),
+            whole(count, feature),
+        ],
+        out_specs=[whole(*split)] * 2,
+        scratch_shapes=[pltpu.VMEM((feature, feature), jnp.float32)],
+        compiler_params=settings(32),
+        cost_estimate=cost(8 * count * feature * feature, 8 * feature * feature),
+    )(where, low, dprojected, attended, dlow)
+
+
+def project_back(work, dprojected, dresid, vector, weights):
+    count, feature = work.shape
+    tile = 128
+
+    def kernel(work_ref, dprojected_ref, dresid_ref, vector_ref, weight_ref, out_ref, sums_ref):
+        sums_ref[...] = jnp.zeros_like(sums_ref)
+
+        def rows_of(index, carry):
+            rows = pl.ds(pl.multiple_of(index * tile, tile), tile)
+            da = by_rows(dprojected_ref[0, rows, :], weight_ref[:, :feature])
+            da += by_rows(dprojected_ref[1, rows, :], weight_ref[:, feature : 2 * feature])
+            da += by_rows(dprojected_ref[2, rows, :], weight_ref[:, 2 * feature :])
+            unit, scale = normed(work_ref[rows, :].astype(jnp.float32))
+            out_ref[rows, :] = (
+                dresid_ref[rows, :] + norm_back(da, vector_ref[0:1, :], unit, scale)
+            ).astype(jnp.bfloat16)
+            sums_ref[0:1, :] += jnp.sum(da * unit, 0, keepdims=True)
+            sums_ref[1:2, :] += jnp.sum(da, 0, keepdims=True)
+            return carry
+
+        lax.fori_loop(0, count // tile, rows_of, 0)
+
+    return pl.pallas_call(
+        kernel,
+        grid=(1,),
+        out_shape=[shaped((count, feature), jnp.bfloat16), shaped((8, feature), jnp.float32)],
+        in_specs=[
+            whole(count, feature),
+            whole(3, count, feature),
+            whole(count, feature),
+            whole(*vector.shape),
+            whole(feature, 3 * feature),
+        ],
+        out_specs=[whole(count, feature), whole(8, feature)],
+        compiler_params=settings(32),
+        cost_estimate=cost(6 * count * feature * feature, 6 * feature * feature),
+    )(work, dprojected, dresid, vector, weights)
+
+
+def structured(devices, feature):
+    rows = feature // devices
+    return devices % PLANE == 0 and feature % devices == 0 and (2 * rows) % 16 == 0
+
+
+def body(
+    tokens,
+    cotangent,
+    segment_ids,
+    wide_weight,
+    wide_moment,
+    wide_average,
+    down_weight,
+    down_moment,
+    down_average,
+    vector_weight,
+    vector_moment,
+    vector_average,
+):
+    devices = lax.axis_size("dev")
+    count, feature = tokens.shape
+    if not structured(devices, feature):
+        return plain_body(
+            tokens,
+            cotangent,
+            segment_ids,
+            wide_weight,
+            wide_moment,
+            wide_average,
+            down_weight,
+            down_moment,
+            down_average,
+            vector_weight,
+            vector_moment,
+            vector_average,
+        )
+    depth = devices // PLANE
+    capacity = count // devices
+    where = place()
+    core = where[3]
+
+    wide_low, down_low = wide_weight.astype(jnp.bfloat16), down_weight.astype(jnp.bfloat16)
+    rows, columns = wide_low.shape
+    parts = wide_low.reshape(rows, 2, 2, columns // 4)
+    keep, give = core_order(core, parts[:, :, 0], parts[:, :, 1])
+    got = lax.ppermute(give, "dev", flips(devices, 1))
+    pair = jnp.concatenate(core_order(core, keep, got), 0)
+
+    send_rows, send_grads, send_code, slot = route(
+        segment_ids.reshape(1, count), tokens, cotangent, devices
+    )
+    work = exchange(send_rows.reshape(devices, capacity, feature)).reshape(count, feature)
+    code = exchange(send_code.reshape(devices, 1, capacity)).reshape(1, count)
+    code = code.astype(jnp.float32)
+
+    first_own = stack_along_z(pair[:, 0])
+    up_block, first_own = lax.optimization_barrier((pair[:, 1], first_own))
+    first_pieces = gather_pieces(first_own)
+    up_own = stack_along_z(up_block)
+    down_block, up_own = lax.optimization_barrier((down_low, up_own))
+    up_pieces = gather_pieces(up_own)
+    down_pieces = gather_pieces(stack_along_z(down_block))
+
+    grads = exchange(send_grads.reshape(devices, capacity, feature)).reshape(count, feature)
+
+    low_one, projected, first_weights = project(where, work, vector_weight, first_pieces)
+    attended, resid, low_two, stats = attend(projected, code, work, vector_weight, first_weights)
+    hidden, slope, up_weights = widen(
+        where, low_two, vector_weight[8:].reshape(1, FF), up_pieces
+    )
+    down_mine, down_theirs = down_gradient(where, hidden, grads, depth)
+    down_grad = scatter_blocks(down_mine, down_theirs)
+    output, up_mine, up_theirs, dresid, dlow, sums_two, bias_up_grad = feed_back(
+        where, hidden, slope, low_two, grads, resid, vector_weight, up_weights, down_pieces
+    )
+    up_grad = join_columns(core, scatter_blocks(up_mine, up_theirs))
+    dprojected, sums_attend = attend_back(projected, code, stats, dlow, first_weights)
+    first_mine, first_theirs = first_gradient(where, low_one, dprojected, attended, dlow, depth)
+    first_grad = join_columns(core, scatter_blocks(first_mine, first_theirs))
+    dinput, sums_one = project_back(work, dprojected, dresid, vector_weight, first_weights)
+
+    back_out = exchange(output.reshape(devices, capacity, feature)).reshape(count, feature)
+    back_grad = exchange(dinput.reshape(devices, capacity, feature)).reshape(count, feature)
+    block_output = give_back(slot, back_out)
+    input_grad = give_back(slot, back_grad)
+
+    vector_partial = jnp.concatenate(
+        [
+            sums_one[0:2],
+            sums_two[0:2],
+            sums_attend[0:2],
+            sums_two[2:4],
+            bias_up_grad.reshape(FF // feature, feature),
+            jnp.zeros((4, feature), jnp.float32),
+        ],
+        0,
+    )
+    share = vector_partial.size // devices // 128
+    vector_share = jnp.sum(exchange(vector_partial.reshape(devices, share, 128)), 0)
+    wide_grad = jnp.concatenate([first_grad, up_grad], 1)
+    shard_squares = jnp.sum(wide_grad * wide_grad) + jnp.sum(down_grad * down_grad)
+    packet = jnp.concatenate([vector_share, jnp.full((1, 128), shard_squares)], 0)
+    packets = exchange(jnp.broadcast_to(packet[None], (devices, share + 1, 128)))
+    vector_grad = packets[:, :share].reshape(-1, feature)[: vector_weight.shape[0]]
+    total = jnp.sum(packets[:, share, 0]) + jnp.sum(vector_grad * vector_grad)
+    grad_norm = jnp.sqrt(total)
+    factor = clip_norm / jnp.maximum(grad_norm, clip_norm)
+    wide_new, wide_moment_new, wide_average_new = advance(
+        wide_weight, wide_moment, wide_average, wide_grad, factor, decay_rate
+    )
+    down_new, down_moment_new, down_average_new = advance(
+        down_weight, down_moment, down_average, down_grad, factor, decay_rate
+    )
+    vector_new, vector_moment_new, vector_average_new = advance(
+        vector_weight, vector_moment, vector_average, vector_grad, factor, 0.0
+    )
+    return (
+        block_output,
+        input_grad,
+        grad_norm,
+        wide_new,
+        wide_moment_new,
+        wide_average_new,
+        down_new,
+        down_moment_new,
+        down_average_new,
+        vector_new,
+        vector_moment_new,
+        vector_average_new,
+    )
+
+
 def solution(mesh):
     placed = (
         P("dev", None),

time: 649 us -> 407 us (0.63); the launches traced: 641 us -> 406 us
  waiting for transfers between devices: 402 us -> 149 us
  Pallas kernels: 0 us -> 98 us
  matrix products: 76.8 us -> 0 us
  starting transfers between devices: 20.9 us -> 72.5 us
  other arithmetic: 45.4 us -> 23.1 us
  blocking collectives: 39.6 us -> 21.6 us
  between operations: 19 us -> 5.43 us
    reduce_scatter x2 -> x0, waiting for transfers between devices: 236 us -> none  [the longest x1 212 us: body(): lax.psum_scatter(jnp.concatenate([inner_rows(low_one, dqkv_low), jnp.conc...]
    ppermute x0 -> x63, waiting for transfers between devices: none -> 130 us  [the longest x9 40 us: stack_along_z(): lax.ppermute(block, 'dev', shifts(devices, k))]
    pallas_call x0 -> x11, Pallas kernels: none -> 98 us  [the longest x1 23.7 us: feed_back(): pl.pallas_call(kernel, grid=(steps,), out_shape=[shaped((count, feature),...]
    all_gather x2 -> x0, waiting for transfers between devices: 81.7 us -> none  [the longest x1 46.4 us: body(): lax.all_gather(wide_weight.astype(jnp.bfloat16), 'dev', axis=0, tiled=True)]
    dot_general x30 -> x0, matrix products: 76.8 us -> none  [the longest x4 34 us: against(): lax.dot_general(matrix, other, (((1,), (1,)), ((), ())), preferred_elemen...]
    all_to_all x5, waiting for transfers between devices: 84.2 us -> 19.2 us  [exchange(): return lax.all_to_all(rows, 'dev', split_axis=0, concat_axis=0, tiled=True)]
    ppermute x0 -> x63, starting transfers between devices: none -> 56.3 us  [the longest x9 18.1 us: scatter_blocks(): lax.ppermute(total[k].astype(jnp.bfloat16), 'dev', shifts(devices, k))]
    psum x1 -> x0, blocking collectives: 39.6 us -> none  [body(): total = lax.psum(shard_squares, 'dev') + jnp.sum(vector_grad * vector_grad)]
  transfers between devices with their start and end apart: 9 -> 68, of which waited for: 8 -> 23; matrix products, arithmetic and copies ran while one was open for 17% -> 6% of each run, Pallas kernels for 0% -> 24%
where the time goes in v1:
time: 407 us; the launch traced here: 406 us
  waiting for transfers between devices  149 us (37%)
  Pallas kernels  98 us (24%)
  starting transfers between devices  72.5 us (18%)
  local copies, waits for them, and re-layouts  36.4 us (9%)
  other arithmetic  23.1 us (6%)
  blocking collectives  21.6 us (5%)
  between operations  5.43 us (1%)
    ppermute x9, waiting for transfers between devices, stack_along_z(): lax.ppermute(block, 'dev', shifts(devices, k))  40 us
    ppermute x3, waiting for transfers between devices, scatter_blocks(): got_y = lax.ppermute(to_y, 'dev', flips(devices, 4)).astype(jnp.float32)  26.9 us
    unnamed x130, local copies, waits for them, and re-layouts  26 us
    pallas_call x1, Pallas kernels, feed_back(): pl.pallas_call(kernel, grid=(steps,), out_shape=[shaped((count, feature),...  23.7 us
    all_to_all x2, blocking collectives, exchange(): return lax.all_to_all(rows, 'dev', split_axis=0, concat_axis=0, tiled=True)  21.6 us
    all_to_all x5, waiting for transfers between devices, exchange(): return lax.all_to_all(rows, 'dev', split_axis=0, concat_axis=0, tiled=True)  19.2 us
    ppermute x9, starting transfers between devices, scatter_blocks(): lax.ppermute(total[k].astype(jnp.bfloat16), 'dev', shifts(devices, k))  18.1 us
    pallas_call x1, Pallas kernels, attend(): pl.pallas_call(kernel, grid=(pairs,), out_shape=[shaped((count, feature),...  17.3 us
  transfers between devices with their start and end apart: 68, of which 23 were waited for; matrix products, arithmetic and copies ran while one was open for 6% of the time, Pallas kernels for 24%

profile of v1, /device:TPU:0, one launch (start us, length us, event | category | flops | bytes accessed | tf_op | source)
XLA Modules:
  0.0 405.9 jit_solution(15140081574930560454)
XLA Ops:
  4.2 5.0 %collective-permute-start.3 = (bf16[48,1536]{1,0:T(8,128)(2,1)S(1)}, bf16[48,1536]{1,0:T(8,128)(2,1)S(1)}, u32[]{:S(2)}, u32[]{:S(2)}) collective-permute-start(bf16[48,1536]{1,0:T(8,128)(2,1)S(1)} %get-tuple-element.129), channel_id=1, source_target_pairs={{0,24},{1,25},{2,26},{3,27},{4,28},{5,29},{6,30},{7,31},{8,0},{9,1... | collective-permute-start | bytes 442376 | tf_op jit(solution)/shard_map/ppermute | solution.py:338
  10.3 2.5 shard_map.211
  14.0 12.0 %all_to_all.35 = s32[32,1,16]{2,1,0:T(1,128)S(1)} all-to-all(s32[32,1,16]{2,1,0:T(1,128)S(1)} %bitcast.176), channel_id=1, replica_groups=mesh['dev'=32] {'dev'}, dimensions={0} | all-to-all | bytes 4096 | tf_op jit(solution)/shard_map/all_to_all | solution.py:386
  26.0 2.6 all-to-all-start
  28.8 3.7 collective-permute-start.15
  33.5 1.5 collective-permute-start.4
  35.0 10.4 %collective-permute-done.15 = bf16[48,1536]{1,0:T(8,128)(2,1)S(1)} collective-permute-done((bf16[48,1536]{1,0:T(8,128)(2,1)S(1)}, bf16[48,1536]{1,0:T(8,128)(2,1)S(1)}, u32[]{:S(2)}, u32[]{:S(2)}) %collective-permute-start.15) | collective-permute-done | bytes 147488 | tf_op jit(solution)/shard_map/ppermute | solution.py:338
  45.4 16.5 %collective-permute-done.14 = bf16[48,1536]{1,0:T(8,128)(2,1)S(1)} collective-permute-done((bf16[48,1536]{1,0:T(8,128)(2,1)S(1)}, bf16[48,1536]{1,0:T(8,128)(2,1)S(1)}, u32[]{:S(2)}, u32[]{:S(2)}) %collective-permute-start.14) | collective-permute-done | bytes 147488 | tf_op jit(solution)/shard_map/ppermute | solution.py:338
  62.1 1.6 collective-permute-start.5
  64.1 3.4 collective-permute-done.27
  67.5 9.7 %collective-permute-done.26 = bf16[96,768]{1,0:T(8,128)(2,1)S(1)} collective-permute-done((bf16[96,768]{1,0:T(8,128)(2,1)S(1)}, bf16[96,768]{1,0:T(8,128)(2,1)S(1)}, u32[]{:S(2)}, u32[]{:S(2)}) %collective-permute-start.26) | collective-permute-done | bytes 147488 | tf_op jit(solution)/shard_map/ppermute | solution.py:338
  77.2 1.4 collective-permute-start.16
  80.8 1.6 collective-permute-start.6
  82.4 11.1 %collective-permute-done.16.refs_1_ = bf16[4,48,1536]{2,1,0:T(8,128)(2,1)} collective-permute-done((bf16[4,48,1536]{2,1,0:T(8,128)(2,1)S(1)}, bf16[4,48,1536]{2,1,0:T(8,128)(2,1)}, u32[]{:S(2)}, u32[]{:S(2)}) %collective-permute-start.16) | collective-permute-done | bytes 589856 | tf_op jit(solution)/shard_map/ppermute | solution.py:345
  96.3 4.9 %collective-permute-done.6.refs_3_ = bf16[4,48,768]{2,1,0:T(8,128)(2,1)S(1)} collective-permute-done((bf16[4,48,768]{2,1,0:T(8,128)(2,1)S(1)}, bf16[4,48,768]{2,1,0:T(8,128)(2,1)S(1)}, u32[]{:S(2)}, u32[]{:S(2)}) %collective-permute-start.6) | collective-permute-done | bytes 294944 | tf_op jit(solution)/shard_map/ppermute | solution.py:347
  101.9 3.5 all-to-all-start.2
  107.4 9.3 %collective-permute-done.7.refs_4_ = bf16[4,48,768]{2,1,0:T(8,128)(2,1)} collective-permute-done((bf16[4,48,768]{2,1,0:T(8,128)(2,1)}, bf16[4,48,768]{2,1,0:T(8,128)(2,1)}, u32[]{:S(2)}, u32[]{:S(2)}) %collective-permute-start.7) | collective-permute-done | bytes 294944 | tf_op jit(solution)/shard_map/ppermute | solution.py:348
  116.7 1.4 collective-permute-start.19
  119.4 1.7 slice.236
  121.2 5.8 %collective-permute-done.18.refs_3_ = bf16[4,48,768]{2,1,0:T(8,128)(2,1)S(1)} collective-permute-done((bf16[4,48,768]{2,1,0:T(8,128)(2,1)S(1)}, bf16[4,48,768]{2,1,0:T(8,128)(2,1)S(1)}, u32[]{:S(2)}, u32[]{:S(2)}) %collective-permute-start.18) | collective-permute-done | bytes 294944 | tf_op jit(solution)/shard_map/ppermute | solution.py:347
  127.9 1.7 slice.237
  132.4 4.4 %collective-permute-done.30.refs_3_ = bf16[4,96,384]{2,1,0:T(8,128)(2,1)} collective-permute-done((bf16[4,96,384]{2,1,0:T(8,128)(2,1)}, bf16[4,96,384]{2,1,0:T(8,128)(2,1)}, u32[]{:S(2)}, u32[]{:S(2)}) %collective-permute-start.30) | collective-permute-done | bytes 294944 | tf_op jit(solution)/shard_map/ppermute | solution.py:347
  143.0 7.2 %shard_map.212 = (bf16[512,768]{1,0:T(8,128)(2,1)S(1)}, bf16[512,2304]{1,0:T(8,128)(2,1)S(1)}, bf16[768,3072]{1,0:T(8,128)(2,1)S(1)}) custom-call(s32[4]{0:T(128)S(1)} %pad_add_fusion.where_ref, bf16[512,768]{1,0:T(8,128)(2,1)S(1)} %bitcast.157, f32[12,768]{1,0:T(8,128)S(1)} %copy-done.13, bf16[4,48,1536]{2,1,0:T(8,128)(2,1)S(1)} %copy-done.12, ...), custom_call_target="tpu_custom_call" | custom-call | flops 1811939328 | bytes 7077888 | tf_op jit(solution)/shard_map/pallas_call | solution.py:591
  152.2 17.3 %shard_map.213 = (bf16[512,768]{1,0:T(8,128)(2,1)S(1)}, f32[512,768]{1,0:T(8,128)S(1)}, bf16[512,768]{1,0:T(8,128)(2,1)S(1)}, f32[6,8,512]{2,1,0:T(8,128)S(1)}) custom-call(bf16[512,2304]{1,0:T(8,128)(2,1)S(1)} %get-tuple-element.48.q_ref.k_ref.v_ref, bf16[512,2304]{1,0:T(8,128)(2,1)S(1)} %get-tuple-element.48.q_ref.k_ref.v_ref, ...), custom_call_target="tpu_custom_call" | custom-call | flops 1610612736 | bytes 5505024 | tf_op jit(solution)/shard_map/pallas_call | solution.py:682
  172.1 9.4 %shard_map.214 = (bf16[512,3072]{1,0:T(8,128)(2,1)S(1)}, f32[512,3072]{1,0:T(8,128)S(1)}, bf16[768,3072]{1,0:T(8,128)(2,1)S(1)}) custom-call(s32[4]{0:T(128)S(1)} %copy-done.26, bf16[512,768]{1,0:T(8,128)(2,1)S(1)} %get-tuple-element.51.low_ref, f32[1,3072]{1,0:T(1,128)S(1)} %bitcast.163, bf16[4,48,1536]{2,1,0:T(8,128)(2,1)S(1)} %copy-done.10, ...), custom_call_target="tpu_custom_call" | custom-call | flops 2415919104 | bytes 18874368 | tf_op jit(solution)/shard_map/pallas_call | solution.py:749
  182.4 2.6 copy-done.49
  185.0 2.1 copy-done.50
  187.2 1.6 copy-done.51
  189.5 1.9 copy-done.52
  191.3 7.0 %shard_map.221 = (bf16[4,4,96,768]{3,2,1,0:T(8,128)(2,1)S(1)}, bf16[4,4,96,768]{3,2,1,0:T(8,128)(2,1)}) custom-call(s32[4]{0:T(128)S(1)} %copy-done.27, bf16[512,3072]{1,0:T(8,128)(2,1)S(1)} %copy-done.52, bf16[512,768]{1,0:T(8,128)(2,1)} %bitcast.21.grads_ref), custom_call_target="tpu_custom_call" | custom-call | flops 2415919104 | bytes 7864320 | tf_op jit(solution)/shard_map/pallas_call | solution.py:795
  198.4 1.4 copy-done.1
  199.9 23.7 %shard_map.215 = (bf16[512,768]{1,0:T(8,128)(2,1)S(1)}, bf16[4,4,48,1536]{3,2,1,0:T(8,128)(2,1)}, bf16[4,4,48,1536]{3,2,1,0:T(8,128)(2,1)}, f32[512,768]{1,0:T(8...) custom-call(s32[4]{0:T(128)S(1)} %copy-done.27, bf16[512,3072]{1,0:T(8,128)(2,1)} %copy-done.51, ...), custom_call_target="tpu_custom_call" | custom-call | flops 9663676416 | bytes 23592960 | tf_op jit(solution)/shard_map/pallas_call | solution.py:896
  226.1 15.1 %shard_map.217 = (bf16[3,512,768]{2,1,0:T(8,128)(2,1)S(1)}, f32[8,768]{1,0:T(8,128)S(1)}) custom-call(bf16[512,2304]{1,0:T(8,128)(2,1)S(1)} %get-tuple-element.48.q_ref.k_ref.v_ref, bf16[512,2304]{1,0:T(8,128)(2,1)S(1)} %get-tuple-element.48.q_ref.k_ref.v_ref, bf16[512,2304]{1,0:T(8,128)(2,1)S(1)} %get-tuple-element.48.q_ref.k_ref.v_ref, ...), custom_call_target="tpu_custom_call" | custom-call | flops 2818572288 | bytes 6291456 | tf_op jit(solution)/shard_map/pallas_call | solution.py:994
  241.2 5.9 %shard_map.220 = (bf16[4,4,48,1536]{3,2,1,0:T(8,128)(2,1)S(1)}, bf16[4,4,48,1536]{3,2,1,0:T(8,128)(2,1)}) custom-call(s32[4]{0:T(128)S(1)} %copy-done.27, bf16[512,768]{1,0:T(8,128)(2,1)S(1)} %copy-done.48, bf16[3,512,768]{2,1,0:T(8,128)(2,1)S(1)} %get-tuple-element.63.dprojected_ref, bf16[512,768]{1,0:T(8,128)(2,1)S(1)} %copy-done.32, ...), custom_call_target="tpu_custom_call" | custom-call | flops 2415919104 | bytes 4718592 | tf_op jit(solution)/shard_map/pallas_call | solution.py:1042
  247.1 1.4 copy-done.3
  248.6 6.9 %shard_map.218 = (bf16[512,768]{1,0:T(8,128)(2,1)}, f32[8,768]{1,0:T(8,128)S(1)}) custom-call(bf16[512,768]{1,0:T(8,128)(2,1)S(1)} %bitcast.159, bf16[3,512,768]{2,1,0:T(8,128)(2,1)S(1)} %get-tuple-element.63.dprojected_ref, f32[512,768]{1,0:T(8,128)S(1)} %copy-done.5, f32[12,768]{1,0:T(8,128)S(1)} %copy-done.13, bf16[768,3072]{1,0:T(8,128)(2,1)S(1)} %bitcast.156), custom_call_target="tpu_custom_call" | custom-call | flops 1811939328 | bytes 3538944 | tf_op jit(solution)/shard_map/pallas_call | solution.py:1082
  256.9 9.6 %all_to_all.36 = f32[32,3,128]{2,1,0:T(4,128)S(1)} all-to-all(f32[32,3,128]{2,1,0:T(4,128)S(1)} %reshape.129), channel_id=1, replica_groups=mesh['dev'=32] {'dev'}, dimensions={0} | all-to-all | bytes 98304 | tf_op jit(solution)/shard_map/all_to_all | solution.py:386
  266.5 2.6 all-to-all-start.3
  269.2 2.3 add_convert_fusion
  271.7 1.7 collective-permute-start.56
  273.4 1.5 collective-permute-start.58
  274.9 2.4 add_convert_fusion.1
  278.9 2.4 add_convert_fusion.2
  282.5 3.3 collective-permute-done.56
  285.9 1.3 collective-permute-start.40
  288.1 5.4 %collective-permute-done.47 = bf16[4,48,768]{2,1,0:T(8,128)(2,1)S(1)} collective-permute-done((bf16[4,48,768]{2,1,0:T(8,128)(2,1)S(1)}, bf16[4,48,768]{2,1,0:T(8,128)(2,1)S(1)}, u32[]{:S(2)}, u32[]{:S(2)}) %collective-permute-start.47) | collective-permute-done | bytes 294944 | tf_op jit(solution)/shard_map/ppermute | solution.py:362
  295.5 4.4 %collective-permute-done.38 = bf16[4,48,768]{2,1,0:T(8,128)(2,1)S(1)} collective-permute-done((bf16[4,48,768]{2,1,0:T(8,128)(2,1)S(1)}, bf16[4,48,768]{2,1,0:T(8,128)(2,1)S(1)}, u32[]{:S(2)}, u32[]{:S(2)}) %collective-permute-start.38) | collective-permute-done | bytes 294944 | tf_op jit(solution)/shard_map/ppermute | solution.py:362
  301.8 10.7 %collective-permute-done.59 = bf16[4,96,768]{2,1,0:T(8,128)(2,1)S(1)} collective-permute-done((bf16[4,96,768]{2,1,0:T(8,128)(2,1)S(1)}, bf16[4,96,768]{2,1,0:T(8,128)(2,1)S(1)}, u32[]{:S(2)}, u32[]{:S(2)}) %collective-permute-start.59) | collective-permute-done | bytes 589856 | tf_op jit(solution)/shard_map/ppermute | solution.py:367
  313.8 3.3 collective-permute-start.62
  317.1 8.0 %collective-permute-done.50 = bf16[4,48,1536]{2,1,0:T(8,128)(2,1)S(1)} collective-permute-done((bf16[4,48,1536]{2,1,0:T(8,128)(2,1)S(1)}, bf16[4,48,1536]{2,1,0:T(8,128)(2,1)S(1)}, u32[]{:S(2)}, u32[]{:S(2)}) %collective-permute-start.50) | collective-permute-done | bytes 589856 | tf_op jit(solution)/shard_map/ppermute | solution.py:367
  325.1 2.8 collective-permute-start.61
  329.2 8.2 %collective-permute-done.41 = bf16[4,48,1536]{2,1,0:T(8,128)(2,1)S(1)} collective-permute-done((bf16[4,48,1536]{2,1,0:T(8,128)(2,1)S(1)}, bf16[4,48,1536]{2,1,0:T(8,128)(2,1)S(1)}, u32[]{:S(2)}, u32[]{:S(2)}) %collective-permute-start.41) | collective-permute-done | bytes 589856 | tf_op jit(solution)/shard_map/ppermute | solution.py:367
  337.4 3.3 collective-permute-start.53
  342.9 2.7 collective-permute-start.44
  346.7 1.4 multiply_reduce_fusion.1
  348.1 2.7 collective-permute-start.42
  350.8 10.0 %collective-permute-done.52 = bf16[48,1536]{1,0:T(8,128)(2,1)S(1)} collective-permute-done((bf16[48,1536]{1,0:T(8,128)(2,1)S(1)}, bf16[48,1536]{1,0:T(8,128)(2,1)S(1)}, u32[]{:S(2)}, u32[]{:S(2)}) %collective-permute-start.52) | collective-permute-done | bytes 147488 | tf_op jit(solution)/shard_map/ppermute | solution.py:371
  361.6 3.8 all-to-all-start.4
  371.2 14.8 %all-to-all-done.4 = bf16[32,16,768]{2,1,0:T(8,128)(2,1)S(1)} async-done(((bf16[32,16,768]{2,1,0:T(8,128)(2,1)}), bf16[32,16,768]{2,1,0:T(8,128)(2,1)S(1)}, u32[]{:S(2)}, u32[]{:S(2)}) %all-to-all-start.4) | async-done | bytes 786464 | tf_op jit(solution)/shard_map/all_to_all | solution.py:386
  386.6 3.6 all-to-all-start.6
  390.2 1.5 shard_map.216
  391.7 1.5 shard_map.219
  393.2 4.4 %all-to-all-done.6 = f32[32,4,128]{2,1,0:T(4,128)S(1)} async-done(((f32[32,4,128]{2,1,0:T(4,128)}), f32[32,4,128]{2,1,0:T(4,128)S(1)}, u32[]{:S(2)}, u32[]{:S(2)}) %all-to-all-start.6) | async-done | bytes 65568 | tf_op jit(solution)/shard_map/all_to_all | solution.py:386
  400.4 2.6 multiply_add_fusion
  (287 shorter events, 58.8 us)
Async XLA Ops:
  4.2 24.5 %collective-permute-start.3 = (bf16[48,1536]{1,0:T(8,128)(2,1)S(1)}, bf16[48,1536]{1,0:T(8,128)(2,1)S(1)}, u32[]{:S(2)}, u32[]{:S(2)}) collective-permute-start(bf16[48,1536]{1,0:T(8,128)(2,1)S(1)} %get-tuple-element.129), channel_id=1, source_target_pairs={{0,24},{1,25},{2,26},{3,27},{4,28},{5,29},{6,30},{7,31},{8,0},{9,1... | collective-permute-start | bytes 442376 | tf_op jit(solution)/shard_map/ppermute | solution.py:338
  9.2 19.5 %collective-permute-start.2 = (bf16[48,1536]{1,0:T(8,128)(2,1)S(1)}, bf16[48,1536]{1,0:T(8,128)(2,1)S(1)}, u32[]{:S(2)}, u32[]{:S(2)}) collective-permute-start(bf16[48,1536]{1,0:T(8,128)(2,1)S(1)} %get-tuple-element.129), channel_id=1, source_target_pairs={{0,16},{1,17},{2,18},{3,19},{4,20},{5,21},{6,22},{7,23},{8,24},{9,... | collective-permute-start | bytes 442376 | tf_op jit(solution)/shard_map/ppermute | solution.py:338
  9.2 19.5 %collective-permute-start.1 = (bf16[48,1536]{1,0:T(8,128)(2,1)S(1)}, bf16[48,1536]{1,0:T(8,128)(2,1)S(1)}, u32[]{:S(2)}, u32[]{:S(2)}) collective-permute-start(bf16[48,1536]{1,0:T(8,128)(2,1)S(1)} %get-tuple-element.129), channel_id=1, source_target_pairs={{0,8},{1,9},{2,10},{3,11},{4,12},{5,13},{6,14},{7,15},{8,16},{9,17... | collective-permute-start | bytes 442376 | tf_op jit(solution)/shard_map/ppermute | solution.py:338
  26.0 75.9 %all-to-all-start = ((bf16[32,16,768]{2,1,0:T(8,128)(2,1)}), bf16[32,16,768]{2,1,0:T(8,128)(2,1)S(1)}, u32[]{:S(2)}, u32[]{:S(2)}) async-start(bf16[32,16,768]{2,1,0:T(8,128)(2,1)} %bitcast.5), calls=%async_computation | async-start | bytes 1572864 | tf_op jit(solution)/shard_map/all_to_all | solution.py:386
  28.8 16.6 %collective-permute-start.15 = (bf16[48,1536]{1,0:T(8,128)(2,1)S(1)}, bf16[48,1536]{1,0:T(8,128)(2,1)S(1)}, u32[]{:S(2)}, u32[]{:S(2)}) collective-permute-start(bf16[48,1536]{1,0:T(8,128)(2,1)S(1)} %get-tuple-element.52), channel_id=1, source_target_pairs={{0,24},{1,25},{2,26},{3,27},{4,28},{5,29},{6,30},{7,31},{8,0},{9,1... | collective-permute-start | bytes 442376 | tf_op jit(solution)/shard_map/ppermute | solution.py:338
  32.5 29.4 %collective-permute-start.14 = (bf16[48,1536]{1,0:T(8,128)(2,1)S(1)}, bf16[48,1536]{1,0:T(8,128)(2,1)S(1)}, u32[]{:S(2)}, u32[]{:S(2)}) collective-permute-start(bf16[48,1536]{1,0:T(8,128)(2,1)S(1)} %get-tuple-element.52), channel_id=1, source_target_pairs={{0,16},{1,17},{2,18},{3,19},{4,20},{5,21},{6,22},{7,23},{8,24},{9,... | collective-permute-start | bytes 442376 | tf_op jit(solution)/shard_map/ppermute | solution.py:338
  32.5 29.4 %collective-permute-start.13 = (bf16[48,1536]{1,0:T(8,128)(2,1)S(1)}, bf16[48,1536]{1,0:T(8,128)(2,1)S(1)}, u32[]{:S(2)}, u32[]{:S(2)}) collective-permute-start(bf16[48,1536]{1,0:T(8,128)(2,1)S(1)} %get-tuple-element.52), channel_id=1, source_target_pairs={{0,8},{1,9},{2,10},{3,11},{4,12},{5,13},{6,14},{7,15},{8,16},{9,17... | collective-permute-start | bytes 442376 | tf_op jit(solution)/shard_map/ppermute | solution.py:338
  33.5 45.6 %collective-permute-start.4 = (bf16[4,48,1536]{2,1,0:T(8,128)(2,1)S(1)}, bf16[4,48,1536]{2,1,0:T(8,128)(2,1)S(1)}, u32[]{:S(2)}, u32[]{:S(2)}) collective-permute-start(bf16[4,48,1536]{2,1,0:T(8,128)(2,1)S(1)} %pad_maximum_fusion.refs_0_), channel_id=1, source_target_pairs={{0,2},{1,3},{2,0},{3,1},{4,6},{5,7},{6,4},{7,5},{8,10},{9,11},{10,... | collective-permute-start | bytes 1769480 | tf_op jit(solution)/shard_map/ppermute | solution.py:345
  62.1 18.1 %collective-permute-start.5 = (bf16[4,48,1536]{2,1,0:T(8,128)(2,1)S(1)}, bf16[4,48,1536]{2,1,0:T(8,128)(2,1)S(1)}, u32[]{:S(2)}, u32[]{:S(2)}) collective-permute-start(bf16[4,48,1536]{2,1,0:T(8,128)(2,1)S(1)} %pad_maximum_fusion.refs_0_), channel_id=1, source_target_pairs={{0,4},{1,5},{2,6},{3,7},{4,0},{5,1},{6,2},{7,3},{8,12},{9,13},{10,... | collective-permute-start | bytes 1769480 | tf_op jit(solution)/shard_map/ppermute | solution.py:346
  63.7 17.1 %collective-permute-start.8 = (bf16[4,48,1536]{2,1,0:T(8,128)(2,1)S(1)}, bf16[4,48,1536]{2,1,0:T(8,128)(2,1)S(1)}, u32[]{:S(2)}, u32[]{:S(2)}) collective-permute-start(bf16[4,48,1536]{2,1,0:T(8,128)(2,1)S(1)} %pad_maximum_fusion.refs_0_), channel_id=1, source_target_pairs={{0,1},{1,0},{2,3},{3,2},{4,5},{5,4},{6,7},{7,6},{8,9},{9,8},{10,11... | collective-permute-start | bytes 1769480 | tf_op jit(solution)/shard_map/ppermute | solution.py:350
  63.7 13.5 %collective-permute-start.26 = (bf16[96,768]{1,0:T(8,128)(2,1)S(1)}, bf16[96,768]{1,0:T(8,128)(2,1)S(1)}, u32[]{:S(2)}, u32[]{:S(2)}) collective-permute-start(bf16[96,768]{1,0:T(8,128)(2,1)S(1)} %convert_element_type.212), channel_id=1, source_target_pairs={{0,16},{1,17},{2,18},{3,19},{4,20},{5,21},{6,22},{7,23},{8,24},{9,... | collective-permute-start | bytes 442376 | tf_op jit(solution)/shard_map/ppermute | solution.py:338
  67.5 11.2 %collective-permute-start.25 = (bf16[96,768]{1,0:T(8,128)(2,1)S(1)}, bf16[96,768]{1,0:T(8,128)(2,1)S(1)}, u32[]{:S(2)}, u32[]{:S(2)}) collective-permute-start(bf16[96,768]{1,0:T(8,128)(2,1)S(1)} %convert_element_type.212), channel_id=1, source_target_pairs={{0,8},{1,9},{2,10},{3,11},{4,12},{5,13},{6,14},{7,15},{8,16},{9,17... | collective-permute-start | bytes 442376 | tf_op jit(solution)/shard_map/ppermute | solution.py:338
  77.2 16.3 %collective-permute-start.16 = (bf16[4,48,1536]{2,1,0:T(8,128)(2,1)S(1)}, bf16[4,48,1536]{2,1,0:T(8,128)(2,1)}, u32[]{:S(2)}, u32[]{:S(2)}) collective-permute-start(bf16[4,48,1536]{2,1,0:T(8,128)(2,1)S(1)} %pad_maximum_fusion.1.refs_0_), channel_id=1, source_target_pairs={{0,2},{1,3},{2,0},{3,1},{4,6},{5,7},{6,4},{7,5},{8,10},{9,11},{10,... | collective-permute-start | bytes 1769480 | tf_op jit(solution)/shard_map/ppermute | solution.py:345
  78.6 16.4 %collective-permute-start.17 = (bf16[4,48,1536]{2,1,0:T(8,128)(2,1)S(1)}, bf16[4,48,1536]{2,1,0:T(8,128)(2,1)}, u32[]{:S(2)}, u32[]{:S(2)}) collective-permute-start(bf16[4,48,1536]{2,1,0:T(8,128)(2,1)S(1)} %pad_maximum_fusion.1.refs_0_), channel_id=1, source_target_pairs={{0,4},{1,5},{2,6},{3,7},{4,0},{5,1},{6,2},{7,3},{8,12},{9,13},{10,... | collective-permute-start | bytes 1769480 | tf_op jit(solution)/shard_map/ppermute | solution.py:346
  79.2 17.1 %collective-permute-start.20 = (bf16[4,48,1536]{2,1,0:T(8,128)(2,1)S(1)}, bf16[4,48,1536]{2,1,0:T(8,128)(2,1)S(1)}, u32[]{:S(2)}, u32[]{:S(2)}) collective-permute-start(bf16[4,48,1536]{2,1,0:T(8,128)(2,1)S(1)} %pad_maximum_fusion.1.refs_0_), channel_id=1, source_target_pairs={{0,1},{1,0},{2,3},{3,2},{4,5},{5,4},{6,7},{7,6},{8,9},{9,8},{10,11... | collective-permute-start | bytes 1769480 | tf_op jit(solution)/shard_map/ppermute | solution.py:350
  80.2 36.5 %collective-permute-start.28 = (bf16[4,96,768]{2,1,0:T(8,128)(2,1)}, bf16[4,96,768]{2,1,0:T(8,128)(2,1)}, u32[]{:S(2)}, u32[]{:S(2)}) collective-permute-start(bf16[4,96,768]{2,1,0:T(8,128)(2,1)} %pad_maximum_fusion.2.refs_0_), channel_id=1, source_target_pairs={{0,2},{1,3},{2,0},{3,1},{4,6},{5,7},{6,4},{7,5},{8,10},{9,11},{10,... | collective-permute-start | bytes 1769480 | tf_op jit(solution)/shard_map/ppermute | solution.py:345
  80.8 20.4 %collective-permute-start.6 = (bf16[4,48,768]{2,1,0:T(8,128)(2,1)S(1)}, bf16[4,48,768]{2,1,0:T(8,128)(2,1)S(1)}, u32[]{:S(2)}, u32[]{:S(2)}) collective-permute-start(bf16[4,48,768]{2,1,0:T(8,128)(2,1)S(1)} %slice.232), channel_id=1, source_target_pairs={{0,4},{1,5},{2,6},{3,7},{4,0},{5,1},{6,2},{7,3},{8,12},{9,13},{10,... | collective-permute-start | bytes 884744 | tf_op jit(solution)/shard_map/ppermute | solution.py:347
  93.5 25.9 %collective-permute-start.29 = (bf16[4,96,768]{2,1,0:T(8,128)(2,1)}, bf16[4,96,768]{2,1,0:T(8,128)(2,1)}, u32[]{:S(2)}, u32[]{:S(2)}) collective-permute-start(bf16[4,96,768]{2,1,0:T(8,128)(2,1)} %pad_maximum_fusion.2.refs_0_), channel_id=1, source_target_pairs={{0,4},{1,5},{2,6},{3,7},{4,0},{5,1},{6,2},{7,3},{8,12},{9,13},{10,... | collective-permute-start | bytes 1769480 | tf_op jit(solution)/shard_map/ppermute | solution.py:346
  95.0 21.7 %collective-permute-start.7 = (bf16[4,48,768]{2,1,0:T(8,128)(2,1)}, bf16[4,48,768]{2,1,0:T(8,128)(2,1)}, u32[]{:S(2)}, u32[]{:S(2)}) collective-permute-start(bf16[4,48,768]{2,1,0:T(8,128)(2,1)} %slice.233), channel_id=1, source_target_pairs={{0,2},{1,3},{2,0},{3,1},{4,6},{5,7},{6,4},{7,5},{8,10},{9,11},{10,... | collective-permute-start | bytes 884744 | tf_op jit(solution)/shard_map/ppermute | solution.py:348
  96.3 31.2 %collective-permute-start.9 = (bf16[4,48,1536]{2,1,0:T(8,128)(2,1)S(1)}, bf16[4,48,1536]{2,1,0:T(8,128)(2,1)}, u32[]{:S(2)}, u32[]{:S(2)}) collective-permute-start(bf16[4,48,1536]{2,1,0:T(8,128)(2,1)S(1)} %collective-permute-done.4.refs_1_), channel_id=1, source_target_pairs={{0,1},{1,0},{2,3},{3,2},{4,5},{5,4},{6,7},{7,6},{8,9},{9,8},{10,11... | collective-permute-start | bytes 1769480 | tf_op jit(solution)/shard_map/ppermute | solution.py:350
  101.9 25.9 %collective-permute-start.10 = (bf16[4,48,1536]{2,1,0:T(8,128)(2,1)S(1)}, bf16[4,48,1536]{2,1,0:T(8,128)(2,1)}, u32[]{:S(2)}, u32[]{:S(2)}) collective-permute-start(bf16[4,48,1536]{2,1,0:T(8,128)(2,1)S(1)} %collective-permute-done.5.refs_2_), channel_id=1, source_target_pairs={{0,1},{1,0},{2,3},{3,2},{4,5},{5,4},{6,7},{7,6},{8,9},{9,8},{10,11... | collective-permute-start | bytes 1769480 | tf_op jit(solution)/shard_map/ppermute | solution.py:350
  101.9 86.9 %all-to-all-start.2 = ((bf16[32,16,768]{2,1,0:T(8,128)(2,1)}), bf16[32,16,768]{2,1,0:T(8,128)(2,1)}, u32[]{:S(2)}, u32[]{:S(2)}) async-start(bf16[32,16,768]{2,1,0:T(8,128)(2,1)} %bitcast.20), calls=%async_computation.2 | async-start | bytes 1572864 | tf_op jit(solution)/shard_map/all_to_all | solution.py:386
  116.7 10.3 %collective-permute-start.18 = (bf16[4,48,768]{2,1,0:T(8,128)(2,1)S(1)}, bf16[4,48,768]{2,1,0:T(8,128)(2,1)S(1)}, u32[]{:S(2)}, u32[]{:S(2)}) collective-permute-start(bf16[4,48,768]{2,1,0:T(8,128)(2,1)S(1)} %slice.234), channel_id=1, source_target_pairs={{0,4},{1,5},{2,6},{3,7},{4,0},{5,1},{6,2},{7,3},{8,12},{9,13},{10,... | collective-permute-start | bytes 884744 | tf_op jit(solution)/shard_map/ppermute | solution.py:347
  116.7 10.3 %collective-permute-start.19 = (bf16[4,48,768]{2,1,0:T(8,128)(2,1)S(1)}, bf16[4,48,768]{2,1,0:T(8,128)(2,1)S(1)}, u32[]{:S(2)}, u32[]{:S(2)}) collective-permute-start(bf16[4,48,768]{2,1,0:T(8,128)(2,1)S(1)} %slice.235), channel_id=1, source_target_pairs={{0,2},{1,3},{2,0},{3,1},{4,6},{5,7},{6,4},{7,5},{8,10},{9,11},{10,... | collective-permute-start | bytes 884744 | tf_op jit(solution)/shard_map/ppermute | solution.py:348
  119.4 10.2 %collective-permute-start.11 = (bf16[4,48,768]{2,1,0:T(8,128)(2,1)}, bf16[4,48,768]{2,1,0:T(8,128)(2,1)}, u32[]{:S(2)}, u32[]{:S(2)}) collective-permute-start(bf16[4,48,768]{2,1,0:T(8,128)(2,1)} %copy-done.40), channel_id=1, source_target_pairs={{0,1},{1,0},{2,3},{3,2},{4,5},{5,4},{6,7},{7,6},{8,9},{9,8},{10,11... | collective-permute-start | bytes 884744 | tf_op jit(solution)/shard_map/ppermute | solution.py:350
  127.0 24.6 %collective-permute-start.21 = (bf16[4,48,1536]{2,1,0:T(8,128)(2,1)}, bf16[4,48,1536]{2,1,0:T(8,128)(2,1)}, u32[]{:S(2)}, u32[]{:S(2)}) collective-permute-start(bf16[4,48,1536]{2,1,0:T(8,128)(2,1)} %collective-permute-done.16.refs_1_), channel_id=1, source_target_pairs={{0,1},{1,0},{2,3},{3,2},{4,5},{5,4},{6,7},{7,6},{8,9},{9,8},{10,11... | collective-permute-start | bytes 1769480 | tf_op jit(solution)/shard_map/ppermute | solution.py:350
  127.0 24.7 %collective-permute-start.22 = (bf16[4,48,1536]{2,1,0:T(8,128)(2,1)}, bf16[4,48,1536]{2,1,0:T(8,128)(2,1)}, u32[]{:S(2)}, u32[]{:S(2)}) collective-permute-start(bf16[4,48,1536]{2,1,0:T(8,128)(2,1)} %collective-permute-done.17.refs_2_), channel_id=1, source_target_pairs={{0,1},{1,0},{2,3},{3,2},{4,5},{5,4},{6,7},{7,6},{8,9},{9,8},{10,11... | collective-permute-start | bytes 1769480 | tf_op jit(solution)/shard_map/ppermute | solution.py:350
  127.5 9.3 %collective-permute-start.30 = (bf16[4,96,384]{2,1,0:T(8,128)(2,1)}, bf16[4,96,384]{2,1,0:T(8,128)(2,1)}, u32[]{:S(2)}, u32[]{:S(2)}) collective-permute-start(bf16[4,96,384]{2,1,0:T(8,128)(2,1)} %slice.236), channel_id=1, source_target_pairs={{0,4},{1,5},{2,6},{3,7},{4,0},{5,1},{6,2},{7,3},{8,12},{9,13},{10,... | collective-permute-start | bytes 884744 | tf_op jit(solution)/shard_map/ppermute | solution.py:347
  129.6 21.5 %collective-permute-start.31 = (bf16[4,96,384]{2,1,0:T(8,128)(2,1)}, bf16[4,96,384]{2,1,0:T(8,128)(2,1)}, u32[]{:S(2)}, u32[]{:S(2)}) collective-permute-start(bf16[4,96,384]{2,1,0:T(8,128)(2,1)} %slice.237), channel_id=1, source_target_pairs={{0,2},{1,3},{2,0},{3,1},{4,6},{5,7},{6,4},{7,5},{8,10},{9,11},{10,... | collective-permute-start | bytes 884744 | tf_op jit(solution)/shard_map/ppermute | solution.py:348
  132.2 39.3 %collective-permute-start.23 = (bf16[4,48,768]{2,1,0:T(8,128)(2,1)}, bf16[4,48,768]{2,1,0:T(8,128)(2,1)S(1)}, u32[]{:S(2)}, u32[]{:S(2)}) collective-permute-start(bf16[4,48,768]{2,1,0:T(8,128)(2,1)} %copy-done.38), channel_id=1, source_target_pairs={{0,1},{1,0},{2,3},{3,2},{4,5},{5,4},{6,7},{7,6},{8,9},{9,8},{10,11... | collective-permute-start | bytes 884744 | tf_op jit(solution)/shard_map/ppermute | solution.py:350
  136.8 34.8 %collective-permute-start.24 = (bf16[4,48,768]{2,1,0:T(8,128)(2,1)}, bf16[4,48,768]{2,1,0:T(8,128)(2,1)S(1)}, u32[]{:S(2)}, u32[]{:S(2)}) collective-permute-start(bf16[4,48,768]{2,1,0:T(8,128)(2,1)} %copy-done.42), channel_id=1, source_target_pairs={{0,1},{1,0},{2,3},{3,2},{4,5},{5,4},{6,7},{7,6},{8,9},{9,8},{10,11... | collective-permute-start | bytes 884744 | tf_op jit(solution)/shard_map/ppermute | solution.py:350
  151.1 48.7 %collective-permute-start.32 = (bf16[4,96,768]{2,1,0:T(8,128)(2,1)}, bf16[4,96,768]{2,1,0:T(8,128)(2,1)}, u32[]{:S(2)}, u32[]{:S(2)}) collective-permute-start(bf16[4,96,768]{2,1,0:T(8,128)(2,1)} %pad_maximum_fusion.2.refs_0_), channel_id=1, source_target_pairs={{0,1},{1,0},{2,3},{3,2},{4,5},{5,4},{6,7},{7,6},{8,9},{9,8},{10,11... | collective-permute-start | bytes 1769480 | tf_op jit(solution)/shard_map/ppermute | solution.py:350
  151.6 48.2 %collective-permute-start.33 = (bf16[4,96,768]{2,1,0:T(8,128)(2,1)}, bf16[4,96,768]{2,1,0:T(8,128)(2,1)}, u32[]{:S(2)}, u32[]{:S(2)}) collective-permute-start(bf16[4,96,768]{2,1,0:T(8,128)(2,1)} %collective-permute-done.28.refs_1_), channel_id=1, source_target_pairs={{0,1},{1,0},{2,3},{3,2},{4,5},{5,4},{6,7},{7,6},{8,9},{9,8},{10,11... | collective-permute-start | bytes 1769480 | tf_op jit(solution)/shard_map/ppermute | solution.py:350
  151.7 48.2 %collective-permute-start.34 = (bf16[4,96,768]{2,1,0:T(8,128)(2,1)}, bf16[4,96,768]{2,1,0:T(8,128)(2,1)}, u32[]{:S(2)}, u32[]{:S(2)}) collective-permute-start(bf16[4,96,768]{2,1,0:T(8,128)(2,1)} %collective-permute-done.29.refs_2_), channel_id=1, source_target_pairs={{0,1},{1,0},{2,3},{3,2},{4,5},{5,4},{6,7},{7,6},{8,9},{9,8},{10,11... | collective-permute-start | bytes 1769480 | tf_op jit(solution)/shard_map/ppermute | solution.py:350
  171.6 28.3 %collective-permute-start.35 = (bf16[4,96,384]{2,1,0:T(8,128)(2,1)}, bf16[4,96,384]{2,1,0:T(8,128)(2,1)}, u32[]{:S(2)}, u32[]{:S(2)}) collective-permute-start(bf16[4,96,384]{2,1,0:T(8,128)(2,1)} %collective-permute-done.30.refs_3_), channel_id=1, source_target_pairs={{0,1},{1,0},{2,3},{3,2},{4,5},{5,4},{6,7},{7,6},{8,9},{9,8},{10,11... | collective-permute-start | bytes 884744 | tf_op jit(solution)/shard_map/ppermute | solution.py:350
  171.6 28.3 %collective-permute-start.36 = (bf16[4,96,384]{2,1,0:T(8,128)(2,1)}, bf16[4,96,384]{2,1,0:T(8,128)(2,1)}, u32[]{:S(2)}, u32[]{:S(2)}) collective-permute-start(bf16[4,96,384]{2,1,0:T(8,128)(2,1)} %collective-permute-done.31.refs_4_), channel_id=1, source_target_pairs={{0,1},{1,0},{2,3},{3,2},{4,5},{5,4},{6,7},{7,6},{8,9},{9,8},{10,11... | collective-permute-start | bytes 884744 | tf_op jit(solution)/shard_map/ppermute | solution.py:350
  199.8 69.4 %collective-permute-start.55 = (bf16[4,4,96,768]{3,2,1,0:T(8,128)(2,1)}, bf16[4,4,96,768]{3,2,1,0:T(8,128)(2,1)}, u32[]{:S(2)}, u32[]{:S(2)}) collective-permute-start(bf16[4,4,96,768]{3,2,1,0:T(8,128)(2,1)} %get-tuple-element.77), channel_id=1, source_target_pairs={{0,1},{1,0},{2,3},{3,2},{4,5},{5,4},{6,7},{7,6},{8,9},{9,8},{10,11... | collective-permute-start | bytes 7077896 | tf_op jit(solution)/shard_map/ppermute | solution.py:361
  224.5 50.4 %collective-permute-start.46 = (bf16[4,4,48,1536]{3,2,1,0:T(8,128)(2,1)}, bf16[4,4,48,1536]{3,2,1,0:T(8,128)(2,1)}, u32[]{:S(2)}, u32[]{:S(2)}) collective-permute-start(bf16[4,4,48,1536]{3,2,1,0:T(8,128)(2,1)} %get-tuple-element.75), channel_id=1, source_target_pairs={{0,1},{1,0},{2,3},{3,2},{4,5},{5,4},{6,7},{7,6},{8,9},{9,8},{10,11... | collective-permute-start | bytes 7077896 | tf_op jit(solution)/shard_map/ppermute | solution.py:361
  248.5 30.4 %collective-permute-start.37 = (bf16[4,4,48,1536]{3,2,1,0:T(8,128)(2,1)}, bf16[4,4,48,1536]{3,2,1,0:T(8,128)(2,1)}, u32[]{:S(2)}, u32[]{:S(2)}) collective-permute-start(bf16[4,4,48,1536]{3,2,1,0:T(8,128)(2,1)} %get-tuple-element.73), channel_id=1, source_target_pairs={{0,1},{1,0},{2,3},{3,2},{4,5},{5,4},{6,7},{7,6},{8,9},{9,8},{10,11... | collective-permute-start | bytes 7077896 | tf_op jit(solution)/shard_map/ppermute | solution.py:361
  266.5 95.1 %all-to-all-start.3 = ((bf16[32,16,768]{2,1,0:T(8,128)(2,1)}), bf16[32,16,768]{2,1,0:T(8,128)(2,1)S(1)}, u32[]{:S(2)}, u32[]{:S(2)}) async-start(bf16[32,16,768]{2,1,0:T(8,128)(2,1)} %bitcast.162), calls=%async_computation.3 | async-start | bytes 1572864 | tf_op jit(solution)/shard_map/all_to_all | solution.py:386
  271.7 14.2 %collective-permute-start.56 = (bf16[4,96,384]{2,1,0:T(8,128)(2,1)S(1)}, bf16[4,96,384]{2,1,0:T(8,128)(2,1)S(1)}, u32[]{:S(2)}, u32[]{:S(2)}) collective-permute-start(bf16[4,96,384]{2,1,0:T(8,128)(2,1)S(1)} %get-tuple-element.99), channel_id=1, source_target_pairs={{0,4},{1,5},{2,6},{3,7},{4,0},{5,1},{6,2},{7,3},{8,12},{9,13},{10,... | collective-permute-start | bytes 884744 | tf_op jit(solution)/shard_map/ppermute | solution.py:362
  273.4 13.8 %collective-permute-start.58 = (bf16[4,96,384]{2,1,0:T(8,128)(2,1)S(1)}, bf16[4,96,384]{2,1,0:T(8,128)(2,1)S(1)}, u32[]{:S(2)}, u32[]{:S(2)}) collective-permute-start(bf16[4,96,384]{2,1,0:T(8,128)(2,1)S(1)} %get-tuple-element.100), channel_id=1, source_target_pairs={{0,2},{1,3},{2,0},{3,1},{4,6},{5,7},{6,4},{7,5},{8,10},{9,11},{10,... | collective-permute-start | bytes 884744 | tf_op jit(solution)/shard_map/ppermute | solution.py:363
  277.4 16.2 %collective-permute-start.47 = (bf16[4,48,768]{2,1,0:T(8,128)(2,1)S(1)}, bf16[4,48,768]{2,1,0:T(8,128)(2,1)S(1)}, u32[]{:S(2)}, u32[]{:S(2)}) collective-permute-start(bf16[4,48,768]{2,1,0:T(8,128)(2,1)S(1)} %get-tuple-element.111), channel_id=1, source_target_pairs={{0,4},{1,5},{2,6},{3,7},{4,0},{5,1},{6,2},{7,3},{8,12},{9,13},{10,... | collective-permute-start | bytes 884744 | tf_op jit(solution)/shard_map/ppermute | solution.py:362
  278.0 16.6 %collective-permute-start.49 = (bf16[4,48,768]{2,1,0:T(8,128)(2,1)S(1)}, bf16[4,48,768]{2,1,0:T(8,128)(2,1)S(1)}, u32[]{:S(2)}, u32[]{:S(2)}) collective-permute-start(bf16[4,48,768]{2,1,0:T(8,128)(2,1)S(1)} %get-tuple-element.112), channel_id=1, source_target_pairs={{0,2},{1,3},{2,0},{3,1},{4,6},{5,7},{6,4},{7,5},{8,10},{9,11},{10,... | collective-permute-start | bytes 884744 | tf_op jit(solution)/shard_map/ppermute | solution.py:363
  281.4 18.4 %collective-permute-start.38 = (bf16[4,48,768]{2,1,0:T(8,128)(2,1)S(1)}, bf16[4,48,768]{2,1,0:T(8,128)(2,1)S(1)}, u32[]{:S(2)}, u32[]{:S(2)}) collective-permute-start(bf16[4,48,768]{2,1,0:T(8,128)(2,1)S(1)} %get-tuple-element.105), channel_id=1, source_target_pairs={{0,4},{1,5},{2,6},{3,7},{4,0},{5,1},{6,2},{7,3},{8,12},{9,13},{10,... | collective-permute-start | bytes 884744 | tf_op jit(solution)/shard_map/ppermute | solution.py:362
  285.9 15.0 %collective-permute-start.40 = (bf16[4,48,768]{2,1,0:T(8,128)(2,1)S(1)}, bf16[4,48,768]{2,1,0:T(8,128)(2,1)S(1)}, u32[]{:S(2)}, u32[]{:S(2)}) collective-permute-start(bf16[4,48,768]{2,1,0:T(8,128)(2,1)S(1)} %get-tuple-element.106), channel_id=1, source_target_pairs={{0,2},{1,3},{2,0},{3,1},{4,6},{5,7},{6,4},{7,5},{8,10},{9,11},{10,... | collective-permute-start | bytes 884744 | tf_op jit(solution)/shard_map/ppermute | solution.py:363
  287.4 25.0 %collective-permute-start.59 = (bf16[4,96,768]{2,1,0:T(8,128)(2,1)S(1)}, bf16[4,96,768]{2,1,0:T(8,128)(2,1)S(1)}, u32[]{:S(2)}, u32[]{:S(2)}) collective-permute-start(bf16[4,96,768]{2,1,0:T(8,128)(2,1)S(1)} %pad_maximum_fusion.9), channel_id=1, source_target_pairs={{0,4},{1,5},{2,6},{3,7},{4,0},{5,1},{6,2},{7,3},{8,12},{9,13},{10,... | collective-permute-start | bytes 1769480 | tf_op jit(solution)/shard_map/ppermute | solution.py:367
  293.5 20.0 %collective-permute-start.57 = (bf16[4,96,768]{2,1,0:T(8,128)(2,1)S(1)}, bf16[4,96,768]{2,1,0:T(8,128)(2,1)S(1)}, u32[]{:S(2)}, u32[]{:S(2)}) collective-permute-start(bf16[4,96,768]{2,1,0:T(8,128)(2,1)S(1)} %pad_maximum_fusion.8), channel_id=1, source_target_pairs={{0,2},{1,3},{2,0},{3,1},{4,6},{5,7},{6,4},{7,5},{8,10},{9,11},{10,... | collective-permute-start | bytes 1769480 | tf_op jit(solution)/shard_map/ppermute | solution.py:366
  294.8 30.3 %collective-permute-start.50 = (bf16[4,48,1536]{2,1,0:T(8,128)(2,1)S(1)}, bf16[4,48,1536]{2,1,0:T(8,128)(2,1)S(1)}, u32[]{:S(2)}, u32[]{:S(2)}) collective-permute-start(bf16[4,48,1536]{2,1,0:T(8,128)(2,1)S(1)} %pad_maximum_fusion.6), channel_id=1, source_target_pairs={{0,4},{1,5},{2,6},{3,7},{4,0},{5,1},{6,2},{7,3},{8,12},{9,13},{10,... | collective-permute-start | bytes 1769480 | tf_op jit(solution)/shard_map/ppermute | solution.py:367
  299.8 28.1 %collective-permute-start.48 = (bf16[4,48,1536]{2,1,0:T(8,128)(2,1)S(1)}, bf16[4,48,1536]{2,1,0:T(8,128)(2,1)S(1)}, u32[]{:S(2)}, u32[]{:S(2)}) collective-permute-start(bf16[4,48,1536]{2,1,0:T(8,128)(2,1)S(1)} %pad_maximum_fusion.5), channel_id=1, source_target_pairs={{0,2},{1,3},{2,0},{3,1},{4,6},{5,7},{6,4},{7,5},{8,10},{9,11},{10,... | collective-permute-start | bytes 1769480 | tf_op jit(solution)/shard_map/ppermute | solution.py:366
  301.1 36.3 %collective-permute-start.41 = (bf16[4,48,1536]{2,1,0:T(8,128)(2,1)S(1)}, bf16[4,48,1536]{2,1,0:T(8,128)(2,1)S(1)}, u32[]{:S(2)}, u32[]{:S(2)}) collective-permute-start(bf16[4,48,1536]{2,1,0:T(8,128)(2,1)S(1)} %pad_maximum_fusion.4), channel_id=1, source_target_pairs={{0,4},{1,5},{2,6},{3,7},{4,0},{5,1},{6,2},{7,3},{8,12},{9,13},{10,... | collective-permute-start | bytes 1769480 | tf_op jit(solution)/shard_map/ppermute | solution.py:367
  312.5 28.3 %collective-permute-start.39 = (bf16[4,48,1536]{2,1,0:T(8,128)(2,1)S(1)}, bf16[4,48,1536]{2,1,0:T(8,128)(2,1)S(1)}, u32[]{:S(2)}, u32[]{:S(2)}) collective-permute-start(bf16[4,48,1536]{2,1,0:T(8,128)(2,1)S(1)} %pad_maximum_fusion.3), channel_id=1, source_target_pairs={{0,2},{1,3},{2,0},{3,1},{4,6},{5,7},{6,4},{7,5},{8,10},{9,11},{10,... | collective-permute-start | bytes 1769480 | tf_op jit(solution)/shard_map/ppermute | solution.py:366
  313.8 27.9 %collective-permute-start.62 = (bf16[96,768]{1,0:T(8,128)(2,1)S(1)}, bf16[96,768]{1,0:T(8,128)(2,1)S(1)}, u32[]{:S(2)}, u32[]{:S(2)}) collective-permute-start(bf16[96,768]{1,0:T(8,128)(2,1)S(1)} %get-tuple-element.116), channel_id=1, source_target_pairs={{0,24},{1,25},{2,26},{3,27},{4,28},{5,29},{6,30},{7,31},{8,0},{9,1... | collective-permute-start | bytes 442376 | tf_op jit(solution)/shard_map/ppermute | solution.py:371
  325.1 17.8 %collective-permute-start.61 = (bf16[96,768]{1,0:T(8,128)(2,1)S(1)}, bf16[96,768]{1,0:T(8,128)(2,1)S(1)}, u32[]{:S(2)}, u32[]{:S(2)}) collective-permute-start(bf16[96,768]{1,0:T(8,128)(2,1)S(1)} %get-tuple-element.117), channel_id=1, source_target_pairs={{0,16},{1,17},{2,18},{3,19},{4,20},{5,21},{6,22},{7,23},{8,24},{9,... | collective-permute-start | bytes 442376 | tf_op jit(solution)/shard_map/ppermute | solution.py:371
  327.9 17.6 %collective-permute-start.60 = (bf16[96,768]{1,0:T(8,128)(2,1)S(1)}, bf16[96,768]{1,0:T(8,128)(2,1)S(1)}, u32[]{:S(2)}, u32[]{:S(2)}) collective-permute-start(bf16[96,768]{1,0:T(8,128)(2,1)S(1)} %get-tuple-element.115), channel_id=1, source_target_pairs={{0,8},{1,9},{2,10},{3,11},{4,12},{5,13},{6,14},{7,15},{8,16},{9,17... | collective-permute-start | bytes 442376 | tf_op jit(solution)/shard_map/ppermute | solution.py:371
  337.4 10.7 %collective-permute-start.53 = (bf16[48,1536]{1,0:T(8,128)(2,1)S(1)}, bf16[48,1536]{1,0:T(8,128)(2,1)S(1)}, u32[]{:S(2)}, u32[]{:S(2)}) collective-permute-start(bf16[48,1536]{1,0:T(8,128)(2,1)S(1)} %get-tuple-element.122), channel_id=1, source_target_pairs={{0,24},{1,25},{2,26},{3,27},{4,28},{5,29},{6,30},{7,31},{8,0},{9,1... | collective-permute-start | bytes 442376 | tf_op jit(solution)/shard_map/ppermute | solution.py:371
  340.7 20.1 %collective-permute-start.52 = (bf16[48,1536]{1,0:T(8,128)(2,1)S(1)}, bf16[48,1536]{1,0:T(8,128)(2,1)S(1)}, u32[]{:S(2)}, u32[]{:S(2)}) collective-permute-start(bf16[48,1536]{1,0:T(8,128)(2,1)S(1)} %get-tuple-element.123), channel_id=1, source_target_pairs={{0,16},{1,17},{2,18},{3,19},{4,20},{5,21},{6,22},{7,23},{8,24},{9,... | collective-permute-start | bytes 442376 | tf_op jit(solution)/shard_map/ppermute | solution.py:371
  341.7 19.1 %collective-permute-start.51 = (bf16[48,1536]{1,0:T(8,128)(2,1)S(1)}, bf16[48,1536]{1,0:T(8,128)(2,1)S(1)}, u32[]{:S(2)}, u32[]{:S(2)}) collective-permute-start(bf16[48,1536]{1,0:T(8,128)(2,1)S(1)} %get-tuple-element.121), channel_id=1, source_target_pairs={{0,8},{1,9},{2,10},{3,11},{4,12},{5,13},{6,14},{7,15},{8,16},{9,17... | collective-permute-start | bytes 442376 | tf_op jit(solution)/shard_map/ppermute | solution.py:371
  342.9 22.5 %collective-permute-start.44 = (bf16[48,1536]{1,0:T(8,128)(2,1)}, bf16[48,1536]{1,0:T(8,128)(2,1)}, u32[]{:S(2)}, u32[]{:S(2)}) collective-permute-start(bf16[48,1536]{1,0:T(8,128)(2,1)} %get-tuple-element.119), channel_id=1, source_target_pairs={{0,24},{1,25},{2,26},{3,27},{4,28},{5,29},{6,30},{7,31},{8,0},{9,1... | collective-permute-start | bytes 442376 | tf_op jit(solution)/shard_map/ppermute | solution.py:371
  345.6 20.9 %collective-permute-start.43 = (bf16[48,1536]{1,0:T(8,128)(2,1)}, bf16[48,1536]{1,0:T(8,128)(2,1)}, u32[]{:S(2)}, u32[]{:S(2)}) collective-permute-start(bf16[48,1536]{1,0:T(8,128)(2,1)} %get-tuple-element.120), channel_id=1, source_target_pairs={{0,16},{1,17},{2,18},{3,19},{4,20},{5,21},{6,22},{7,23},{8,24},{9,... | collective-permute-start | bytes 442376 | tf_op jit(solution)/shard_map/ppermute | solution.py:371
  348.1 18.4 %collective-permute-start.42 = (bf16[48,1536]{1,0:T(8,128)(2,1)S(1)}, bf16[48,1536]{1,0:T(8,128)(2,1)}, u32[]{:S(2)}, u32[]{:S(2)}) collective-permute-start(bf16[48,1536]{1,0:T(8,128)(2,1)S(1)} %get-tuple-element.118), channel_id=1, source_target_pairs={{0,8},{1,9},{2,10},{3,11},{4,12},{5,13},{6,14},{7,15},{8,16},{9,17... | collective-permute-start | bytes 442376 | tf_op jit(solution)/shard_map/ppermute | solution.py:371
  361.6 6.2 %collective-permute-start.54 = (f32[24,1536]{1,0:T(8,128)}, f32[24,1536]{1,0:T(8,128)}, u32[]{:S(2)}, u32[]{:S(2)}) collective-permute-start(f32[24,1536]{1,0:T(8,128)} %slice_select_fusion), channel_id=1, source_target_pairs={{0,1},{1,0},{2,3},{3,2},{4,5},{5,4},{6,7},{7,6},{8,9},{9,8},{10,11... | collective-permute-start | bytes 442376 | tf_op jit(solution)/shard_map/ppermute | solution.py:381
  361.6 24.4 %all-to-all-start.4 = ((bf16[32,16,768]{2,1,0:T(8,128)(2,1)}), bf16[32,16,768]{2,1,0:T(8,128)(2,1)S(1)}, u32[]{:S(2)}, u32[]{:S(2)}) async-start(bf16[32,16,768]{2,1,0:T(8,128)(2,1)} %bitcast.28), calls=%async_computation.4 | async-start | bytes 1572864 | tf_op jit(solution)/shard_map/all_to_all | solution.py:386
  386.6 11.0 %all-to-all-start.6 = ((f32[32,4,128]{2,1,0:T(4,128)}), f32[32,4,128]{2,1,0:T(4,128)S(1)}, u32[]{:S(2)}, u32[]{:S(2)}) async-start(f32[32,4,128]{2,1,0:T(4,128)} %broadcast_in_dim.5), calls=%async_computation.6 | async-start | bytes 131072 | tf_op jit(solution)/shard_map/all_to_all | solution.py:386
  (68 other events, 872.9 us)

commit v2 on v0

--- a/solution.py
+++ b/solution.py
@@ -3,12 +3,16 @@
 import jax
 import jax.numpy as jnp
 from jax import lax
+from jax.experimental import pallas as pl
+from jax.experimental.pallas import tpu as pltpu
 from jax.sharding import PartitionSpec as P
 
 HEADS = 12
 HEAD = 64
 FF = 3072
 DOCS_DEV = 4
+PLANE = 8
+MIB = 1 << 20
 
 
 epsilon = 1e-05
@@ -70,7 +74,7 @@
     return (is_live, jnp.minimum(slot_of, row_count - 1), anchor)
 
 
-def body(
+def plain_body(
     tokens,
     cotangent,
     segment_ids,
@@ -308,6 +312,1092 @@
     )
 
 
+def flips(devices, mask):
+    return [(i, i ^ mask) for i in range(devices)]
+
+
+def shifts(devices, step):
+    return [(i, (i + PLANE * step) % devices) for i in range(devices)]
+
+
+def place():
+    me = lax.axis_index("dev")
+    return jnp.stack([me // PLANE, (me // 4) % 2, (me // 2) % 2, me % 2]).astype(jnp.int32)
+
+
+def core_order(core, mine, theirs):
+    first = jnp.where(core == 0, mine, theirs)
+    second = jnp.where(core == 0, theirs, mine)
+    return first, second
+
+
+def pin(*values):
+    return lax.optimization_barrier(values)
+
+
+def send(value, mask):
+    return lax.ppermute(value, "dev", flips(lax.axis_size("dev"), mask))
+
+
+def along_z(block):
+    devices = lax.axis_size("dev")
+    depth = devices // PLANE
+    return jnp.stack(
+        [block] + [lax.ppermute(block, "dev", shifts(devices, k)) for k in range(1, depth)], 0
+    )
+
+
+def to_neighbours(own):
+    return send(own, 2), send(own, 4)
+
+
+def to_diagonal(from_x, from_y):
+    half = from_x.shape[0] // 2
+    return send(from_x[:half], 4), send(from_y[half:], 2)
+
+
+def to_partner(*pieces):
+    return tuple(send(piece, 1) for piece in pieces)
+
+
+def total_of(*terms):
+    return sum(term.astype(jnp.float32) for term in terms)
+
+
+def low_sum(*terms):
+    return total_of(*terms).astype(jnp.bfloat16)
+
+
+class Fold:
+    def __init__(self, mine, got):
+        self.mine, self.got = mine, got
+        self.half = mine.shape[1] // 2
+
+    def pair(self, spot, steps):
+        return self.mine[spot, steps], self.got[spot, steps]
+
+    def diagonal(self):
+        first, last = slice(None, self.half), slice(self.half, None)
+        return low_sum(*self.pair(3, first)), low_sum(*self.pair(3, last))
+
+    def neighbours(self, got_a, got_b):
+        first, last = slice(None, self.half), slice(self.half, None)
+        to_x = (low_sum(*self.pair(1, first), got_a), low_sum(*self.pair(1, last)))
+        to_y = (low_sum(*self.pair(2, first)), low_sum(*self.pair(2, last), got_b))
+        return jnp.concatenate(to_x, 0), jnp.concatenate(to_y, 0)
+
+    def column(self, got_x, got_y):
+        total = total_of(*self.pair(0, slice(None)), got_x, got_y)
+        return (total[0],) + tuple(
+            total[k].astype(jnp.bfloat16) for k in range(1, total.shape[0])
+        )
+
+
+def over_diagonal(to_a, to_b):
+    return send(to_a, 4), send(to_b, 2)
+
+
+def over_plane(to_x, to_y):
+    return send(to_x, 2), send(to_y, 4)
+
+
+def over_column(sums):
+    devices = lax.axis_size("dev")
+    return tuple(lax.ppermute(sums[k], "dev", shifts(devices, k)) for k in range(1, len(sums)))
+
+
+def exchange(rows):
+    return lax.all_to_all(rows, "dev", split_axis=0, concat_axis=0, tiled=True)
+
+
+FAR = pl.BlockSpec(memory_space=pltpu.HBM)
+SCALARS = pl.BlockSpec(memory_space=pltpu.SMEM)
+
+
+def whole(*shape):
+    return pl.BlockSpec(shape, lambda *_: (0,) * len(shape))
+
+
+LIMIT = 48
+
+
+def settings(limit):
+    return pltpu.CompilerParams(vmem_limit_bytes=limit * MIB)
+
+
+def cost(flops, moved, exps=0):
+    return pl.CostEstimate(flops=int(flops), bytes_accessed=int(moved), transcendentals=int(exps))
+
+
+def shaped(shape, dtype):
+    return jax.ShapeDtypeStruct(shape, dtype)
+
+
+def by_rows(matrix, other):
+    return lax.dot_general(
+        matrix, other, (((1,), (1,)), ((), ())), preferred_element_type=jnp.float32
+    )
+
+
+def by_columns(matrix, other):
+    return lax.dot_general(
+        matrix, other, (((0,), (0,)), ((), ())), preferred_element_type=jnp.float32
+    )
+
+
+def normed(values):
+    center = values - jnp.mean(values, -1, keepdims=True)
+    scale = lax.rsqrt(jnp.mean(center * center, -1, keepdims=True) + epsilon)
+    return center * scale, scale
+
+
+def norm_back(grad, gain, unit, scale):
+    inner = grad * gain
+    return scale * (
+        inner
+        - jnp.mean(inner, -1, keepdims=True)
+        - unit * jnp.mean(inner * unit, -1, keepdims=True)
+    )
+
+
+def iota(shape, axis):
+    return lax.broadcasted_iota(jnp.int32, shape, axis)
+
+
+def slots_of(ids_row, capacity, groups):
+    count = ids_row.shape[1]
+    square = (count, count)
+    ids = jnp.sum(
+        jnp.where(iota(square, 0) == iota(square, 1), ids_row, 0), axis=1, keepdims=True
+    )
+    group = jnp.right_shift(ids, DOCS_DEV.bit_length() - 1)
+    lanes = max(128, groups)
+    onehot = jnp.where(group == iota((count, lanes), 1), 1.0, 0.0)
+    lower = jnp.where(iota(square, 0) > iota(square, 1), 1.0, 0.0).astype(jnp.bfloat16)
+    earlier = product(lower, onehot.astype(jnp.bfloat16))
+    within = jnp.sum(earlier * onehot, axis=1, keepdims=True).astype(jnp.int32)
+    return ids, jnp.where(ids >= 0, group * capacity + within, -1)
+
+
+def route(ids_row, tokens, cotangent, devices):
+    count, feature = tokens.shape
+
+    def kernel(ids_ref, tokens_ref, cotangent_ref, rows_ref, grads_ref, slot_ref):
+        ids, slot = slots_of(ids_ref[...], count // devices, devices)
+        slot_ref[...] = slot
+        move = jnp.where(slot == iota((count, count), 1), 1.0, 0.0).astype(jnp.bfloat16)
+        code = jnp.where(ids >= 0, jnp.bitwise_and(ids, DOCS_DEV - 1) + 1, 0)
+        code = jnp.broadcast_to(code.astype(jnp.float32), (count, 128)).astype(jnp.bfloat16)
+        rows_ref[:, :feature] = by_columns(move, tokens_ref[...]).astype(jnp.bfloat16)
+        rows_ref[:, feature:] = by_columns(move, code).astype(jnp.bfloat16)
+        grads_ref[...] = by_columns(move, cotangent_ref[...]).astype(jnp.bfloat16)
+
+    return pl.pallas_call(
+        kernel,
+        out_shape=[
+            shaped((count, feature + 128), jnp.bfloat16),
+            shaped((count, feature), jnp.bfloat16),
+            shaped((count, 1), jnp.int32),
+        ],
+        compiler_params=settings(LIMIT),
+        cost_estimate=cost(4 * count * count * feature, 8 * count * feature),
+    )(ids_row, tokens, cotangent)
+
+
+def give_back(slot, rows):
+    count, feature = rows.shape[0], rows.shape[1] // 256 * 256
+
+    def kernel(slot_ref, rows_ref, out_ref):
+        move = jnp.where(slot_ref[...] == iota((count, count), 1), 1.0, 0.0).astype(jnp.bfloat16)
+        out_ref[...] = product(move, rows_ref[...]).astype(jnp.bfloat16)
+
+    return pl.pallas_call(
+        kernel,
+        grid=(1,),
+        out_shape=shaped((count, feature), jnp.bfloat16),
+        in_specs=[whole(count, 1), whole(count, feature)],
+        out_specs=whole(count, feature),
+        compiler_params=settings(LIMIT),
+        cost_estimate=cost(2 * count * count * feature, 4 * count * feature),
+    )(slot, rows)
+
+
+PIECES = 10
+
+
+def pieces_of(where_ref, pieces):
+    z, y, x, core = where_ref[0], where_ref[1], where_ref[2], where_ref[3]
+    for part, group in ((core, pieces[: PIECES // 2]), (1 - core, pieces[PIECES // 2 :])):
+        depth = group[0].shape[0]
+        firsts = (0, 0, 0, 0, depth // 2)
+        columns = ((y, x), (y, 1 - x), (1 - y, x), (1 - y, 1 - x), (1 - y, 1 - x))
+        for piece, first, (yy, xx) in zip(group, firsts, columns, strict=True):
+            for index in range(piece.shape[0]):
+                step = first + index
+                zz = lax.rem(z - step + depth, depth)
+                yield piece.at[index], step, (zz * 2 + yy) * 2 + xx, part
+
+
+def wide_copies(where_ref, pieces, buffer, sems):
+    copies = []
+    for source, _, chip, part in pieces_of(where_ref, pieces):
+        rows, columns = source.shape
+        target = buffer.at[
+            pl.ds(pl.multiple_of(chip * rows, 16), rows),
+            pl.ds(pl.multiple_of(part * columns, 128), columns),
+        ]
+        copies.append(pltpu.make_async_copy(source, target, sems.at[len(copies)]))
+    return copies
+
+
+def down_copies(where_ref, pieces, buffer, sems):
+    copies = []
+    for source, _, chip, part in pieces_of(where_ref, pieces):
+        rows = source.shape[0]
+        row = pl.multiple_of((chip * 2 + part) * rows, 16)
+        copies.append(
+            pltpu.make_async_copy(source, buffer.at[pl.ds(row, rows)], sems.at[len(copies)])
+        )
+    return copies
+
+
+def project(where, work, vector, pieces):
+    count, feature = work.shape[0], vector.shape[1]
+    copies_count = 8 * pieces[0].shape[0]
+    tile = 256
+
+    def kernel(where_ref, work_ref, vector_ref, *refs):
+        (
+            flipped_ref, out_ref, weights_ref, output_ref, low, buffer, sems, store_sems
+        ) = refs[PIECES:]
+        copies = wide_copies(where_ref, refs[:PIECES], buffer, sems)
+        for copy in copies:
+            copy.start()
+
+        def rows_of(index, carry):
+            rows = pl.ds(pl.multiple_of(index * 64, 64), 64)
+            unit, _ = normed(work_ref[rows, :].astype(jnp.float32))
+            low[rows, :] = (unit * vector_ref[0:1, :] + vector_ref[1:2, :]).astype(jnp.bfloat16)
+            return carry
+
+        lax.fori_loop(0, count // 64, rows_of, 0)
+        flipped_ref[...] = low[...].astype(jnp.float32).T.astype(jnp.bfloat16)
+        for copy in copies:
+            copy.wait()
+        stores = [
+            pltpu.make_async_copy(
+                buffer.at[:, pl.ds(0, 3 * feature)], weights_ref, store_sems.at[0]
+            ),
+            pltpu.make_async_copy(
+                buffer.at[:, pl.ds(3 * feature, feature)], output_ref, store_sems.at[1]
+            ),
+        ]
+        for store in stores:
+            store.start()
+        for part, bias in ((0, 4), (1, None), (2, 5)):
+
+            def columns_of(index, carry):
+                inner = pl.ds(pl.multiple_of(index * tile, tile), tile)
+                columns = pl.ds(pl.multiple_of(part * feature + index * tile, tile), tile)
+                value = product(low[...], buffer[:, columns])
+                if bias is not None:
+                    value = value + vector_ref[bias : bias + 1, inner]
+                out_ref[:, columns] = value.astype(jnp.bfloat16)
+                return carry
+
+            lax.fori_loop(0, feature // tile, columns_of, 0)
+        for store in stores:
+            store.wait()
+
+    return pl.pallas_call(
+        kernel,
+        grid=(1,),
+        out_shape=[
+            shaped((feature, count), jnp.bfloat16),
+            shaped((count, 3 * feature), jnp.bfloat16),
+            shaped((feature, 3 * feature), jnp.bfloat16),
+            shaped((feature, feature), jnp.bfloat16),
+        ],
+        in_specs=[SCALARS, whole(count, feature), whole(*vector.shape)] + [FAR] * PIECES,
+        out_specs=[whole(feature, count), whole(count, 3 * feature), FAR, FAR],
+        scratch_shapes=[
+            pltpu.VMEM((count, feature), jnp.bfloat16),
+            pltpu.VMEM((feature, 4 * feature), jnp.bfloat16),
+            pltpu.SemaphoreType.DMA((copies_count,)),
+            pltpu.SemaphoreType.DMA((2,)),
+        ],
+        compiler_params=settings(60),
+        cost_estimate=cost(6 * count * feature * feature, 12 * feature * feature),
+    )(where, work, vector, *pieces)
+
+
+def code_both(code_ref, column, row):
+    code = code_ref[...].astype(jnp.float32)
+    column[...] = code[:, :1]
+    row[...] = code.T[:1]
+
+
+def one_head(values, head):
+    lanes = iota(values.shape, 1)
+    inside = (lanes >= head * HEAD) & (lanes < (head + 1) * HEAD)
+    return jnp.where(inside, values, 0.0).astype(jnp.bfloat16)
+
+
+def attend(projected, work, vector, weights, first, pairs, carried=None):
+    count, feature = work.shape[0], vector.shape[1]
+    all_pairs = feature // 128
+    tile = 256
+    ends = carried is not None
+
+    def kernel(q_ref, k_ref, v_ref, weight_ref, code_ref, work_ref, vector_ref, *refs):
+        if ends:
+            carried_ref, attended_ref, stat_ref, resid_ref, low_ref, total, column, row = refs
+        else:
+            attended_ref, stat_ref, total, column, row = refs
+        pair = pl.program_id(0)
+
+        @pl.when(pair == 0)
+        def _():
+            code_both(code_ref, column, row)
+            total[...] = carried_ref[...] if ends else jnp.zeros_like(total)
+
+        keys = k_ref[...]
+        values = v_ref[...].astype(jnp.float32).T.astype(jnp.bfloat16)
+        scaled = q_ref[...].astype(jnp.float32) * 0.125
+        heads = []
+        for head in range(2):
+            query = one_head(scaled, head)
+            parts = []
+            for start in range(0, count, tile):
+                span = slice(start, start + tile)
+                scores = by_rows(keys, query[span])
+                same = column[...] == row[:, span]
+                scores = jnp.where(same, scores, masked_value)
+                most = jnp.max(scores, 0, keepdims=True)
+                powers = jnp.exp(scores - most)
+                sums = jnp.sum(powers, 0, keepdims=True)
+                low = (powers * (1.0 / sums)).astype(jnp.bfloat16)
+                stat_ref[0, head : head + 1, span] = most + jnp.log(sums)
+                parts.append(product(values[head * HEAD : (head + 1) * HEAD], low))
+            heads.append(jnp.concatenate(parts, 1))
+        both = jnp.concatenate(heads, 0)
+        attended_ref[...] = both.astype(jnp.bfloat16)
+        total[...] += product(both.T.astype(jnp.bfloat16), weight_ref[...])
+
+        if ends:
+
+            @pl.when(pair == pairs - 1)
+            def _():
+                def rows_of(index, carry):
+                    rows = pl.ds(pl.multiple_of(index * 64, 64), 64)
+                    resid = (
+                        work_ref[rows, :].astype(jnp.float32) + total[rows, :] + vector_ref[6:7, :]
+                    )
+                    resid_ref[rows, :] = resid
+                    unit, _ = normed(resid)
+                    low_ref[rows, :] = (unit * vector_ref[2:3, :] + vector_ref[3:4, :]).astype(
+                        jnp.bfloat16
+                    )
+                    return carry
+
+                lax.fori_loop(0, count // 64, rows_of, 0)
+
+    def columns_at(offset):
+        return pl.BlockSpec((count, 128), lambda pair: (0, offset + pair))
+
+    wide = whole(count, feature)
+    return pl.pallas_call(
+        kernel,
+        grid=(pairs,),
+        out_shape=[
+            shaped((pairs * 128, count), jnp.bfloat16),
+            shaped((pairs, 8, count), jnp.float32),
+        ]
+        + (
+            [shaped((count, feature), jnp.float32), shaped((count, feature), jnp.bfloat16)]
+            if ends
+            else [shaped((count, feature), jnp.float32)]
+        ),
+        in_specs=[
+            columns_at(first),
+            columns_at(all_pairs + first),
+            columns_at(2 * all_pairs + first),
+            pl.BlockSpec((128, feature), lambda pair: (first + pair, 0)),
+            pl.BlockSpec((count, 128), lambda pair: (0, all_pairs)),
+            wide,
+            whole(*vector.shape),
+        ]
+        + ([wide] if ends else []),
+        out_specs=[
+            pl.BlockSpec((128, count), lambda pair: (pair, 0)),
+            pl.BlockSpec((1, 8, count), lambda pair: (pair, 0, 0)),
+        ]
+        + ([wide, wide] if ends else [wide]),
+        scratch_shapes=([pltpu.VMEM((count, feature), jnp.float32)] if ends else [])
+        + [pltpu.VMEM((count, 1), jnp.float32), pltpu.VMEM((1, count), jnp.float32)],
+        compiler_params=settings(LIMIT),
+        cost_estimate=cost(
+            8 * count * count * pairs * 128, 14 * count * feature, 2 * pairs * count * count
+        ),
+    )(
+        projected, projected, projected, weights, work, work, vector,
+        *([carried] if ends else []),
+    )
+
+
+def widen(where, low, bias_row, pieces):
+    count, feature = low.shape
+    wide = bias_row.shape[1]
+    tile = feature
+    steps = wide // tile
+
+    def kernel(where_ref, low_ref, bias_ref, *refs):
+        hidden_ref, slope_ref, weights_ref, buffer, sems, store_sem = refs[PIECES:]
+        step = pl.program_id(0)
+        store = pltpu.make_async_copy(buffer, weights_ref, store_sem)
+
+        @pl.when(step == 0)
+        def _():
+            copies = wide_copies(where_ref, refs[:PIECES], buffer, sems)
+            for copy in copies:
+                copy.start()
+            for copy in copies:
+                copy.wait()
+            store.start()
+
+        columns = pl.ds(pl.multiple_of(step * tile, tile), tile)
+        up = product(low_ref[...], buffer[:, columns]) + bias_ref[...]
+        below = 0.5 * (1.0 + lax.erf(up * (0.5**0.5)))
+        hidden_ref[...] = (up * below).astype(jnp.bfloat16)
+        slope_ref[...] = below + up * (jnp.exp(-0.5 * up * up) * ((2.0 * math.pi) ** -0.5))
+
+        @pl.when(step == steps - 1)
+        def _():
+            store.wait()
+
+    block = pl.BlockSpec((count, tile), lambda step: (0, step))
+    return pl.pallas_call(
+        kernel,
+        grid=(steps,),
+        out_shape=[
+            shaped((count, wide), jnp.bfloat16),
+            shaped((count, wide), jnp.float32),
+            shaped((feature, wide), jnp.bfloat16),
+        ],
+        in_specs=[
+            SCALARS,
+            whole(count, feature),
+            pl.BlockSpec((1, tile), lambda step: (0, step)),
+        ]
+        + [FAR] * PIECES,
+        out_specs=[block, block, FAR],
+        scratch_shapes=[
+            pltpu.VMEM((feature, wide), jnp.bfloat16),
+            pltpu.SemaphoreType.DMA((8 * pieces[0].shape[0],)),
+            pltpu.SemaphoreType.DMA,
+        ],
+        compiler_params=settings(60),
+        cost_estimate=cost(
+            2 * count * feature * wide, 2 * feature * wide + 6 * count * wide, count * wide
+        ),
+    )(where, low, bias_row, *pieces)
+
+
+def down_gradient(where, hidden, grads, depth):
+    count, wide = hidden.shape
+    feature = grads.shape[1]
+    rows = wide // (depth * PLANE)
+    part = wide // depth
+
+    def kernel(where_ref, hidden_ref, grads_ref, mine_ref, theirs_ref, result):
+        y, x, core = where_ref[1], where_ref[2], where_ref[3]
+        result[...] = by_columns(hidden_ref[...], grads_ref[...])
+        for yy in range(2):
+            for xx in range(2):
+                spot = jnp.bitwise_xor(y, yy) * 2 + jnp.bitwise_xor(x, xx)
+                first = (yy * 2 + xx) * 2
+                for target, side in ((mine_ref, core), (theirs_ref, 1 - core)):
+                    row = pl.multiple_of((first + side) * rows, 16)
+                    target[spot, 0] = result[pl.ds(row, rows), :].astype(jnp.bfloat16)
+
+    shape = shaped((4, depth, rows, feature), jnp.bfloat16)
+    block = pl.BlockSpec((4, 1, rows, feature), lambda step, where_ref: (0, step, 0, 0))
+    return pl.pallas_call(
+        kernel,
+        out_shape=[shape, shape],
+        grid_spec=pltpu.PrefetchScalarGridSpec(
+            num_scalar_prefetch=1,
+            grid=(depth,),
+            in_specs=[
+                pl.BlockSpec(
+                    (count, part),
+                    lambda step, where_ref: (0, lax.rem(where_ref[0] + step, depth)),
+                ),
+                whole(count, feature),
+            ],
+            out_specs=[block, block],
+            scratch_shapes=[pltpu.VMEM((part, feature), jnp.float32)],
+        ),
+        compiler_params=settings(LIMIT),
+        cost_estimate=cost(2 * count * wide * feature, 2 * wide * (count + feature)),
+    )(where, hidden, grads)
+
+
+def put_wide(where_ref, result, mine_ref, theirs_ref):
+    z, y, x, core = where_ref[0], where_ref[1], where_ref[2], where_ref[3]
+    _, depth, rows, _ = mine_ref.shape
+    for chip in range(4 * depth):
+        zz, yy, xx = chip // 4, (chip // 2) % 2, chip % 2
+        step = lax.rem(zz - z + depth, depth)
+        spot = jnp.bitwise_xor(y, yy) * 2 + jnp.bitwise_xor(x, xx)
+        for target, side in ((mine_ref, core), (theirs_ref, 1 - core)):
+            row = pl.multiple_of((chip * 2 + side) * rows, 8)
+            target[spot, step] = result[pl.ds(row, rows), :].astype(jnp.bfloat16)
+
+
+def narrow(where, hidden, resid, vector, pieces):
+    count, wide = hidden.shape
+    feature = resid.shape[1]
+    tile = 256
+
+    def kernel(where_ref, hidden_ref, resid_ref, vector_ref, *refs):
+        out_ref, weights_ref, buffer, sems, store_sem = refs[PIECES:]
+        copies = down_copies(where_ref, refs[:PIECES], buffer, sems)
+        for copy in copies:
+            copy.start()
+        for copy in copies:
+            copy.wait()
+        store = pltpu.make_async_copy(buffer, weights_ref, store_sem)
+        store.start()
+
+        def columns_of(index, carry):
+            columns = pl.ds(pl.multiple_of(index * tile, tile), tile)
+            value = product(hidden_ref[...], buffer[:, columns])
+            out_ref[:, columns] = (
+                resid_ref[:, columns] + (value + vector_ref[7:8, columns])
+            ).astype(jnp.bfloat16)
+            return carry
+
+        lax.fori_loop(0, feature // tile, columns_of, 0)
+        store.wait()
+
+    return pl.pallas_call(
+        kernel,
+        grid=(1,),
+        out_shape=[
+            shaped((count, feature), jnp.bfloat16),
+            shaped((wide, feature), jnp.bfloat16),
+        ],
+        in_specs=[SCALARS, whole(count, wide), whole(count, feature), whole(*vector.shape)]
+        + [FAR] * PIECES,
+        out_specs=[whole(count, feature), FAR],
+        scratch_shapes=[
+            pltpu.VMEM((wide, feature), jnp.bfloat16),
+            pltpu.SemaphoreType.DMA((8 * pieces[0].shape[0],)),
+            pltpu.SemaphoreType.DMA,
+        ],
+        compiler_params=settings(LIMIT),
+        cost_estimate=cost(2 * count * wide * feature, 6 * wide * feature),
+    )(where, hidden, resid, vector, *pieces)
+
+
+def feed_back(where, slope, low, grads, resid, vector, up_weights, down_weights, attended, depth):
+    count, wide = slope.shape
+    feature = resid.shape[1]
+    tile = feature
+    steps = wide // tile
+    half = feature // 2
+    chip_rows = feature // (PLANE * depth)
+
+    def kernel(
+        where_ref, slope_ref, low_ref, grads_ref, resid_ref, vector_ref, up_ref, down_ref, left_ref, right_ref,
+        dresid_ref, dlow_ref, sums_ref, bias_ref, mine_ref, theirs_ref, back, flipped, result,
+    ):
+        step = pl.program_id(0)
+
+        @pl.when(step == 0)
+        def _():
+            flipped[...] = low_ref[...].astype(jnp.float32).T.astype(jnp.bfloat16)
+            back[...] = jnp.zeros_like(back)
+
+        @pl.when(step < steps)
+        def _():
+            dup = (slope_ref[...] * by_rows(grads_ref[...], down_ref[...])).astype(jnp.bfloat16)
+            bias_ref[...] = jnp.sum(dup.astype(jnp.float32), 0, keepdims=True)
+            back[...] += by_rows(dup, up_ref[...])
+            result[...] = product(flipped[...], dup)
+
+        @pl.when(step == steps)
+        def _():
+            sums_ref[...] = jnp.zeros_like(sums_ref)
+
+            def rows_of(index, carry):
+                rows = pl.ds(pl.multiple_of(index * 64, 64), 64)
+                unit, scale = normed(resid_ref[rows, :])
+                da = back[rows, :]
+                dy = grads_ref[rows, :].astype(jnp.float32)
+                dresid = dy + norm_back(da, vector_ref[2:3, :], unit, scale)
+                dresid_ref[rows, :] = dresid
+                dlow = dresid.astype(jnp.bfloat16)
+                dlow_ref[rows, :] = dlow
+                for row, value in enumerate((da * unit, da, dlow.astype(jnp.float32), dy)):
+                    sums_ref[row : row + 1, :] += jnp.sum(value, 0, keepdims=True)
+                return carry
+
+            lax.fori_loop(0, count // 64, rows_of, 0)
+            result[:half, :] = product(left_ref[...], dlow_ref[...])
+            result[half:, :] = product(right_ref[...], dlow_ref[...])
+
+        put_wide(where_ref, result, mine_ref, theirs_ref)
+
+    def at(step):
+        return jnp.minimum(step, steps - 1)
+
+    def columns_at(rows):
+        return pl.BlockSpec((rows, tile), lambda step: (0, at(step)))
+
+    all_rows = whole(count, feature)
+    split = shaped((4, depth, chip_rows, (steps + 1) * feature), jnp.bfloat16)
+    block = pl.BlockSpec((4, depth, chip_rows, feature), lambda step: (0, 0, 0, step))
+    return pl.pallas_call(
+        kernel,
+        grid=(steps + 1,),
+        out_shape=[
+            shaped((count, feature), jnp.float32),
+            shaped((count, feature), jnp.bfloat16),
+            shaped((8, feature), jnp.float32),
+            shaped((1, wide), jnp.float32),
+            split,
+            split,
+        ],
+        in_specs=[
+            SCALARS,
+            columns_at(count),
+            all_rows,
+            all_rows,
+            all_rows,
+            whole(*vector.shape),
+            columns_at(feature),
+            pl.BlockSpec((tile, feature), lambda step: (at(step), 0)),
+            whole(half, count),
+            whole(half, count),
+        ],
+        out_specs=[all_rows, all_rows, whole(8, feature), columns_at(1), block, block],
+        scratch_shapes=[
+            pltpu.VMEM((count, feature), jnp.float32),
+            pltpu.VMEM((feature, count), jnp.bfloat16),
+            pltpu.VMEM((feature, feature), jnp.float32),
+        ],
+        compiler_params=settings(LIMIT),
+        cost_estimate=cost(6 * count * wide * feature, 8 * wide * feature + 10 * count * wide),
+    )(where, slope, low, grads, resid, vector, up_weights, down_weights, *attended)
+
+
+def attend_back(projected, work, stats, dlow, weights, first, pairs, gradient=None):
+    count, feature = dlow.shape
+    all_pairs = feature // 128
+    tile = 256
+    wide = pairs * 128
+
+    def kernel(q_ref, k_ref, v_ref, code_ref, stat_ref, dlow_ref, weight_ref, *refs):
+        if gradient is None:
+            out_ref, sums_ref, douts, column, row = refs
+        else:
+            (
+                where_ref, flipped_ref, left_ref, out_ref, sums_ref, mine_ref, theirs_ref,
+                douts, column, row, right, result,
+            ) = refs
+        pair = pl.program_id(0)
+
+        @pl.when(pair == 0)
+        def _():
+            code_both(code_ref, column, row)
+            for start in range(0, wide, 128):
+                span = slice(start, start + 128)
+                douts[start // 128] = by_rows(dlow_ref[...], weight_ref[span, :]).astype(
+                    jnp.bfloat16
+                )
+
+        @pl.when(pair < pairs)
+        def _():
+            keys, values = k_ref[...], v_ref[...]
+            flipped = keys.astype(jnp.float32).T.astype(jnp.bfloat16)
+            scaled = q_ref[...].astype(jnp.float32) * 0.125
+            dout = douts[pair].astype(jnp.float32)
+            dkey = jnp.zeros((count, 128), jnp.float32)
+            dvalue = jnp.zeros((count, 128), jnp.float32)
+            heads = []
+            for head in range(2):
+                query = one_head(scaled, head)
+                dhead = one_head(dout, head)
+                parts = []
+                for start in range(0, count, tile):
+                    span = slice(start, start + tile)
+                    scores = by_rows(keys, query[span])
+                    same = column[...] == row[:, span]
+                    probs = jnp.exp(
+                        jnp.where(same, scores, masked_value) - stat_ref[0, head : head + 1, span]
+                    )
+                    dprob = by_rows(values, dhead[span])
+                    inner = jnp.sum(probs * dprob, 0, keepdims=True)
+                    dscore = (probs * (dprob - inner)).astype(jnp.bfloat16)
+                    dvalue = dvalue + product(probs.astype(jnp.bfloat16), dhead[span])
+                    dkey = dkey + product(dscore, query[span])
+                    parts.append(product(flipped[head * HEAD : (head + 1) * HEAD], dscore))
+                heads.append(jnp.concatenate(parts, 1))
+            dquery = (jnp.concatenate(heads, 0).T * 0.125).astype(jnp.bfloat16)
+            dvalue = dvalue.astype(jnp.bfloat16)
+            out_ref[0] = dquery
+            out_ref[1] = dkey.astype(jnp.bfloat16)
+            out_ref[2] = dvalue
+            sums_ref[0:1, :] = jnp.sum(dquery.astype(jnp.float32), 0, keepdims=True)
+            sums_ref[1:2, :] = jnp.sum(dvalue.astype(jnp.float32), 0, keepdims=True)
+            if gradient is not None:
+                right[0, pair] = dquery
+                right[1, pair] = dkey.astype(jnp.bfloat16)
+                right[2, pair] = dvalue
+
+        if gradient is not None:
+
+            @pl.when(pair >= pairs)
+            def _():
+                flipped = flipped_ref[...]
+                result[:, :wide] = product(flipped, left_ref[0])
+                for index in range(pairs):
+                    span = slice(wide + index * 128, wide + (index + 1) * 128)
+                    result[:, span] = product(flipped, right[pair - pairs, index])
+                put_wide(where_ref, result, mine_ref, theirs_ref)
+
+    def at(pair):
+        return jnp.minimum(pair, pairs - 1)
+
+    def part_at(pair):
+        return jnp.maximum(pair - pairs, 0)
+
+    def columns_at(offset):
+        return pl.BlockSpec((count, 128), lambda pair: (0, offset + at(pair)))
+
+    out_shape = [shaped((3, count, wide), jnp.bfloat16), shaped((8, wide), jnp.float32)]
+    in_specs = [
+        columns_at(first),
+        columns_at(all_pairs + first),
+        columns_at(2 * all_pairs + first),
+        pl.BlockSpec((count, 128), lambda pair: (0, all_pairs)),
+        pl.BlockSpec((1, 8, count), lambda pair: (at(pair), 0, 0)),
+        whole(count, feature),
+        pl.BlockSpec((wide, feature), lambda pair: (first // pairs, 0)),
+    ]
+    out_specs = [
+        pl.BlockSpec((3, count, 128), lambda pair: (0, 0, at(pair))),
+        pl.BlockSpec((8, 128), lambda pair: (0, at(pair))),
+    ]
+    scratch = [
+        pltpu.VMEM((pairs, count, 128), jnp.bfloat16),
+        pltpu.VMEM((count, 1), jnp.float32),
+        pltpu.VMEM((1, count), jnp.float32),
+    ]
+    extra = ()
+    if gradient is not None:
+        where, flipped, left, depth = gradient
+        rows = feature // (PLANE * depth)
+        extra = (where, flipped, left)
+        out_shape += [shaped((4, depth, rows, 3 * feature), jnp.bfloat16)] * 2
+        in_specs += [
+            SCALARS,
+            whole(feature, count),
+            pl.BlockSpec((1, count, wide), lambda pair: (part_at(pair), 0, 0)),
+        ]
+        out_specs += [
+            pl.BlockSpec((4, depth, rows, feature), lambda pair: (0, 0, 0, part_at(pair)))
+        ] * 2
+        scratch += [
+            pltpu.VMEM((3, pairs, count, 128), jnp.bfloat16),
+            pltpu.VMEM((feature, feature), jnp.float32),
+        ]
+    return pl.pallas_call(
+        kernel,
+        grid=(pairs if gradient is None else pairs + 3,),
+        out_shape=out_shape,
+        in_specs=in_specs,
+        out_specs=out_specs,
+        scratch_shapes=scratch,
+        compiler_params=settings(LIMIT),
+        cost_estimate=cost(
+            14 * count * count * wide, 16 * count * feature, 2 * pairs * count * count
+        ),
+    )(projected, projected, projected, work, stats, dlow, weights, *extra)
+
+
+def project_back(work, dprojected, dresid, vector, weights, sums_two, sums_attend, bias_up, devices):
+    count, feature = dresid.shape
+    tile = 128
+    half = feature // 2
+    lanes = 16 * feature // devices // 128
+    capacity = count // devices
+
+    def kernel(
+        work_ref, d_ref, e_ref, dresid_ref, vector_ref, weight_ref, two_ref, left_ref, right_ref, bias_ref,
+        out_ref, sums,
+    ):
+        sums[...] = jnp.zeros_like(sums)
+
+        def rows_of(index, carry):
+            rows = pl.ds(pl.multiple_of(index * tile, tile), tile)
+            da = jnp.zeros((tile, feature), jnp.float32)
+            for part in range(3):
+                middle = part * feature + half
+                da += by_rows(d_ref[part, rows, :], weight_ref[:, middle - half : middle])
+                da += by_rows(e_ref[part, rows, :], weight_ref[:, middle : middle + half])
+            unit, scale = normed(work_ref[rows, :].astype(jnp.float32))
+            out_ref[rows, :feature] = (
+                dresid_ref[rows, :] + norm_back(da, vector_ref[0:1, :], unit, scale)
+            ).astype(jnp.bfloat16)
+            sums[0:1, :] += jnp.sum(da * unit, 0, keepdims=True)
+            sums[1:2, :] += jnp.sum(da, 0, keepdims=True)
+            return carry
+
+        lax.fori_loop(0, count // tile, rows_of, 0)
+        sums[2:4, :] = two_ref[0:2, :]
+        sums[4:6, :half] = left_ref[0:2, :]
+        sums[4:6, half:] = right_ref[0:2, :]
+        sums[6:8, :] = two_ref[2:4, :]
+        for row in range(FF // feature):
+            sums[8 + row : 9 + row, :] = bias_ref[0:1, row * feature : (row + 1) * feature]
+        place_in = iota((capacity, 128), 0)
+        for device in range(devices):
+            block = jnp.zeros((capacity, 128), jnp.float32)
+            for lane in range(lanes):
+                first = device * lanes + lane
+                row, column = divmod(first * 128, feature)
+                value = sums[row : row + 1, column : column + 128]
+                high = value.astype(jnp.bfloat16).astype(jnp.float32)
+                block = jnp.where(place_in == lane, high, block)
+                block = jnp.where(place_in == lanes + lane, value - high, block)
+            out_ref[device * capacity : (device + 1) * capacity, feature:] = block.astype(
+                jnp.bfloat16
+            )
+
+    return pl.pallas_call(
+        kernel,
+        grid=(1,),
+        out_shape=shaped((count, feature + 128), jnp.bfloat16),
+        in_specs=[
+            whole(count, feature),
+            whole(3, count, half),
+            whole(3, count, half),
+            whole(count, feature),
+            whole(*vector.shape),
+            whole(feature, 3 * feature),
+            whole(8, feature),
+            whole(8, half),
+            whole(8, half),
+            whole(1, FF),
+        ],
+        out_specs=whole(count, feature + 128),
+        scratch_shapes=[pltpu.VMEM((16, feature), jnp.float32)],
+        compiler_params=settings(LIMIT),
+        cost_estimate=cost(6 * count * feature * feature, 6 * feature * feature),
+    )(work, *dprojected, dresid, vector, weights, sums_two, *sums_attend, bias_up)
+
+
+def structured(devices, feature):
+    rows = feature // devices
+    return devices % PLANE == 0 and feature % devices == 0 and (2 * rows) % 16 == 0
+
+
+def body(
+    tokens,
+    cotangent,
+    segment_ids,
+    wide_weight,
+    wide_moment,
+    wide_average,
+    down_weight,
+    down_moment,
+    down_average,
+    vector_weight,
+    vector_moment,
+    vector_average,
+):
+    devices = lax.axis_size("dev")
+    count, feature = tokens.shape
+    if not structured(devices, feature):
+        return plain_body(
+            tokens,
+            cotangent,
+            segment_ids,
+            wide_weight,
+            wide_moment,
+            wide_average,
+            down_weight,
+            down_moment,
+            down_average,
+            vector_weight,
+            vector_moment,
+            vector_average,
+        )
+    depth = devices // PLANE
+    capacity = count // devices
+    where = place()
+    core = where[3]
+
+    wide_low, down_low = wide_weight.astype(jnp.bfloat16), down_weight.astype(jnp.bfloat16)
+    rows, columns = wide_low.shape
+    parts = wide_low.reshape(rows, 2, 2, columns // 4)
+    keep, give = core_order(core, parts[:, :, 0], parts[:, :, 1])
+    got = lax.ppermute(give, "dev", flips(devices, 1))
+    pair = jnp.concatenate(core_order(core, keep, got), 0)
+
+    send_rows, send_grads, slot = route(segment_ids.reshape(1, count), tokens, cotangent, devices)
+    first_own = along_z(pair[:, 0])
+    send_rows, first_own = pin(send_rows, first_own)
+
+    work = exchange(send_rows.reshape(devices, capacity, -1)).reshape(count, -1)
+    first_near = to_neighbours(first_own)
+    first_near, up_block = pin(first_near, pair[:, 1])
+
+    first_far = to_diagonal(*first_near)
+    first_got = to_partner(first_own, *first_near)
+    first_far, first_got = pin(first_far, first_got)
+    first_got = first_got + to_partner(*first_far)
+    first_got, work, up_block = pin(first_got, work, up_block)
+
+    up_own = along_z(up_block)
+    flipped_one, projected, first_weights, out_weights = project(
+        where, work, vector_weight, (first_own, *first_near, *first_far, *first_got)
+    )
+    projected, up_own, down_block, send_grads = pin(projected, up_own, down_low, send_grads)
+
+    up_near = to_neighbours(up_own)
+    down_own = along_z(down_block)
+    pairs = feature // 256
+    attended_a, stats_a, carried = attend(projected, work, vector_weight, out_weights, 0, pairs)
+    carried, up_near, down_own, send_grads = pin(carried, up_near, down_own, send_grads)
+
+    up_far = to_diagonal(*up_near)
+    up_got = to_partner(up_own, *up_near)
+    grads = exchange(send_grads.reshape(devices, capacity, feature)).reshape(count, feature)
+    attended_b, stats_b, resid, low_two = attend(
+        projected, work, vector_weight, out_weights, pairs, pairs, carried
+    )
+    low_two, up_far, up_got = pin(low_two, up_far, up_got)
+    up_got = up_got + to_partner(*up_far)
+    low_two, up_got, down_own = pin(low_two, up_got, down_own)
+
+    down_near = to_neighbours(down_own)
+    hidden, slope, up_weights = widen(
+        where, low_two, vector_weight[8:].reshape(1, FF), (up_own, *up_near, *up_far, *up_got)
+    )
+    hidden, down_near = pin(hidden, down_near)
+
+    down_far = to_diagonal(*down_near)
+    down_got = to_partner(down_own, *down_near)
+    down_mine, down_theirs = down_gradient(where, hidden, grads, depth)
+    down_far, down_got, down_mine, down_theirs = pin(down_far, down_got, down_mine, down_theirs)
+
+    down_got = pin(*down_got, *to_partner(*down_far))
+    got = send(down_theirs, 1)
+    output, down_weights = narrow(
+        where, hidden, resid, vector_weight, (down_own, *down_near, *down_far, *down_got)
+    )
+    output, down_weights, got = pin(output, down_weights, got)
+
+    down_fold = Fold(down_mine, got)
+    down_to = pin(*down_fold.diagonal())
+    back_out = exchange(output.reshape(devices, capacity, feature)).reshape(count, feature)
+    got = over_diagonal(*down_to)
+    dresid, dlow, sums_two, bias_up_grad, up_mine, up_theirs = feed_back(
+        where, slope, low_two, grads, resid, vector_weight, up_weights, down_weights,
+        (attended_a, attended_b), depth,
+    )
+    dlow, got, up_mine, up_theirs, back_out = pin(dlow, got, up_mine, up_theirs, back_out)
+    down_to, dlow, up_theirs = pin(down_fold.neighbours(*got), dlow, up_theirs)
+
+    down_got = over_plane(*down_to)
+    up_got = send(up_theirs, 1)
+    dleft, sums_left = attend_back(projected, work, stats_a, dlow, out_weights, 0, pairs)
+    up_got, dleft, dlow = pin(up_got, dleft, dlow)
+    up_fold = Fold(up_mine, up_got)
+    up_to, dlow = pin(up_fold.diagonal(), dlow)
+
+    up_got = over_diagonal(*up_to)
+    dright, sums_right, first_mine, first_theirs = attend_back(
+        projected, work, stats_b, dlow, out_weights, pairs, pairs,
+        (where, flipped_one, dleft, depth),
+    )
+    up_got, down_got, dright, first_mine, first_theirs = pin(
+        up_got, down_got, dright, first_mine, first_theirs
+    )
+    up_to, down_sums, dright, first_theirs = pin(
+        up_fold.neighbours(*up_got), down_fold.column(*down_got), dright, first_theirs
+    )
+
+    up_got = over_plane(*up_to)
+    down_got = over_column(down_sums)
+    first_got = send(first_theirs, 1)
+    block_output = give_back(slot, back_out)
+    first_got, dright, block_output = pin(first_got, dright, block_output)
+    first_fold = Fold(first_mine, first_got)
+    first_to, dright = pin(first_fold.diagonal(), dright)
+
+    got = over_diagonal(*first_to)
+    both = project_back(
+        work, (dleft, dright), dresid, vector_weight, first_weights,
+        sums_two, (sums_left, sums_right), bias_up_grad, devices,
+    )
+    both, got, up_got, down_got = pin(both, got, up_got, down_got)
+    first_to, up_sums = pin(first_fold.neighbours(*got), up_fold.column(*up_got))
+
+    back = exchange(both.reshape(devices, capacity, -1))
+    got = over_plane(*first_to)
+    up_got = over_column(up_sums)
+    down_grad = total_of(down_sums[0], *down_got)
+    got, down_grad = pin(got, down_grad)
+    first_sums = pin(*first_fold.column(*got))
+
+    first_got = over_column(first_sums)
+    up_grad = total_of(up_sums[0], *up_got)
+    first_got, up_grad = pin(first_got, up_grad)
+    first_grad = total_of(first_sums[0], *first_got)
+    back, first_grad = pin(back, first_grad)
+    input_grad = give_back(slot, back.reshape(count, -1))
+
+    lanes = 16 * feature // devices // 128
+    vector_share = total_of(back[:, :lanes, feature:], back[:, lanes : 2 * lanes, feature:])
+    vector_share = jnp.sum(vector_share, 0)
+    wide_grad = jnp.concatenate([first_grad, up_grad[:, FF:], up_grad[:, :FF]], 1)
+    shard_squares = sum(jnp.sum(grad * grad) for grad in (down_grad, up_grad, first_grad))
+    packet = jnp.concatenate([vector_share, jnp.full((1, 128), shard_squares)], 0)
+    packets = exchange(jnp.broadcast_to(packet[None], (devices, lanes + 1, 128)))
+    vector_grad = packets[:, :lanes].reshape(-1, feature)[: vector_weight.shape[0]]
+    total = jnp.sum(packets[:, lanes, 0]) + jnp.sum(vector_grad * vector_grad)
+    grad_norm = jnp.sqrt(total)
+    factor = clip_norm / jnp.maximum(grad_norm, clip_norm)
+    wide_new, wide_moment_new, wide_average_new = advance(
+        wide_weight, wide_moment, wide_average, wide_grad, factor, decay_rate
+    )
+    down_new, down_moment_new, down_average_new = advance(
+        down_weight, down_moment, down_average, down_grad, factor, decay_rate
+    )
+    vector_new, vector_moment_new, vector_average_new = advance(
+        vector_weight, vector_moment, vector_average, vector_grad, factor, 0.0
+    )
+    return (
+        block_output,
+        input_grad,
+        grad_norm,
+        wide_new,
+        wide_moment_new,
+        wide_average_new,
+        down_new,
+        down_moment_new,
+        down_average_new,
+        vector_new,
+        vector_moment_new,
+        vector_average_new,
+    )
+
+
 def solution(mesh):
     placed = (
         P("dev", None),

time: 649 us -> 352 us (0.54); the launches traced: 641 us -> 351 us
  waiting for transfers between devices: 402 us -> 98.4 us
  Pallas kernels: 0 us -> 111 us
  matrix products: 76.8 us -> 0 us
  starting transfers between devices: 20.9 us -> 85.8 us
  blocking collectives: 39.6 us -> 0 us
  other arithmetic: 45.4 us -> 27.4 us
  local copies, waits for them, and re-layouts: 37.1 us -> 22.1 us
  between operations: 19 us -> 6.06 us
    reduce_scatter x2 -> x0, waiting for transfers between devices: 236 us -> none  [the longest x1 212 us: body(): lax.psum_scatter(jnp.concatenate([inner_rows(low_one, dqkv_low), jnp.conc...]
    pallas_call x0 -> x13, Pallas kernels: none -> 111 us  [the longest x2 23.2 us: attend_back(): pl.pallas_call(kernel, grid=(pairs if gradient is None else pairs + 3,),...]
    ppermute x0 -> x61, waiting for transfers between devices: none -> 92.5 us  [the longest x42 44.4 us: send(): return lax.ppermute(value, 'dev', flips(lax.axis_size('dev'), mask))]
    all_gather x2 -> x0, waiting for transfers between devices: 81.7 us -> none  [the longest x1 46.4 us: body(): lax.all_gather(wide_weight.astype(jnp.bfloat16), 'dev', axis=0, tiled=True)]
    all_to_all x5, waiting for transfers between devices: 84.2 us -> 5.86 us  [exchange(): return lax.all_to_all(rows, 'dev', split_axis=0, concat_axis=0, tiled=True)]
    dot_general x30 -> x0, matrix products: 76.8 us -> none  [the longest x4 34 us: against(): lax.dot_general(matrix, other, (((1,), (1,)), ((), ())), preferred_elemen...]
    ppermute x0 -> x61, starting transfers between devices: none -> 64.3 us  [the longest x42 31 us: send(): return lax.ppermute(value, 'dev', flips(lax.axis_size('dev'), mask))]
    psum x1 -> x0, blocking collectives: 39.6 us -> none  [body(): total = lax.psum(shard_squares, 'dev') + jnp.sum(vector_grad * vector_grad)]
  transfers between devices with their start and end apart: 9 -> 66, of which waited for: 8 -> 23; matrix products, arithmetic and copies ran while one was open for 17% -> 5% of each run, Pallas kernels for 0% -> 32%
where the time goes in v2:
time: 352 us; the launch traced here: 351 us
  Pallas kernels  111 us (32%)
  waiting for transfers between devices  98.4 us (28%)
  starting transfers between devices  85.8 us (24%)
  other arithmetic  27.4 us (8%)
  local copies, waits for them, and re-layouts  22.1 us (6%)
  between operations  6.06 us (2%)
    ppermute x42, waiting for transfers between devices, send(): return lax.ppermute(value, 'dev', flips(lax.axis_size('dev'), mask))  44.4 us
    ppermute x9, waiting for transfers between devices, over_column(): lax.ppermute(sums[k], 'dev', shifts(devices, k))  36.1 us
    ppermute x42, starting transfers between devices, send(): return lax.ppermute(value, 'dev', flips(lax.axis_size('dev'), mask))  31 us
    pallas_call x2, Pallas kernels, attend_back(): pl.pallas_call(kernel, grid=(pairs if gradient is None else pairs + 3,),...  23.2 us
    all_to_all x5, starting transfers between devices, exchange(): return lax.all_to_all(rows, 'dev', split_axis=0, concat_axis=0, tiled=True)  21.4 us
    pallas_call x2, Pallas kernels, attend(): pl.pallas_call(kernel, grid=(pairs,), out_shape=[shaped((pairs * 128, cou...  19.7 us
    pallas_call x1, Pallas kernels, feed_back(): pl.pallas_call(kernel, grid=(steps + 1,), out_shape=[shaped((count, featu...  17.9 us
    ppermute x9, starting transfers between devices, over_column(): lax.ppermute(sums[k], 'dev', shifts(devices, k))  17.6 us
  transfers between devices with their start and end apart: 66, of which 23 were waited for; matrix products, arithmetic and copies ran while one was open for 5% of the time, Pallas kernels for 32%

profile of v2, /device:TPU:0, one launch (start us, length us, event | category | flops | bytes accessed | tf_op | source)
XLA Modules:
  0.0 351.1 jit_solution(6071829374494773048)
XLA Ops:
  4.2 5.0 %collective-permute-start.3 = (bf16[48,1536]{1,0:T(8,128)(2,1)S(1)}, bf16[48,1536]{1,0:T(8,128)(2,1)S(1)}, u32[]{:S(2)}, u32[]{:S(2)}) collective-permute-start(bf16[48,1536]{1,0:T(8,128)(2,1)S(1)} %get-tuple-element.369), channel_id=1, source_target_pairs={{0,24},{1,25},{2,26},{3,27},{4,28},{5,29},{6,30},{7,31},{8,0},{9,1... | collective-permute-start | bytes 442376 | tf_op jit(solution)/shard_map/ppermute | solution.py:346
  10.3 2.8 shard_map.211
  13.7 8.3 %collective-permute-done.2 = bf16[48,1536]{1,0:T(8,128)(2,1)S(1)} collective-permute-done((bf16[48,1536]{1,0:T(8,128)(2,1)S(1)}, bf16[48,1536]{1,0:T(8,128)(2,1)S(1)}, u32[]{:S(2)}, u32[]{:S(2)}) %collective-permute-start.2) | collective-permute-done | bytes 147488 | tf_op jit(solution)/shard_map/ppermute | solution.py:346
  22.2 5.0 %all-to-all-start = ((bf16[32,16,896]{2,1,0:T(8,128)(2,1)}), bf16[32,16,896]{2,1,0:T(8,128)(2,1)S(1)}, u32[]{:S(2)}, u32[]{:S(2)}) async-start(bf16[32,16,896]{2,1,0:T(8,128)(2,1)} %bitcast.13), calls=%async_computation | async-start | bytes 1835008 | tf_op jit(solution)/shard_map/all_to_all | solution.py:410
  27.2 1.8 collective-permute-start.5
  29.0 1.5 collective-permute-start.4
  30.5 22.0 %collective-permute-done.5.refs_2_ = bf16[4,48,1536]{2,1,0:T(8,128)(2,1)S(1)} collective-permute-done((bf16[4,48,1536]{2,1,0:T(8,128)(2,1)S(1)}, bf16[4,48,1536]{2,1,0:T(8,128)(2,1)S(1)}, u32[]{:S(2)}, u32[]{:S(2)}) %collective-permute-start.5) | collective-permute-done | bytes 589856 | tf_op jit(solution)/shard_map/ppermute | solution.py:339
  53.2 1.5 collective-permute-start.7
  55.2 7.1 %collective-permute-done.7.refs_4_ = bf16[2,48,1536]{2,1,0:T(8,128)(2,1)} collective-permute-done((bf16[2,48,1536]{2,1,0:T(8,128)(2,1)S(1)}, bf16[2,48,1536]{2,1,0:T(8,128)(2,1)}, u32[]{:S(2)}, u32[]{:S(2)}) %collective-permute-start.7) | collective-permute-done | bytes 294944 | tf_op jit(solution)/shard_map/ppermute | solution.py:339
  66.5 3.3 collective-permute-start.15
  71.0 9.1 %shard_map.212 = (bf16[768,512]{1,0:T(8,128)(2,1)}, bf16[512,2304]{1,0:T(8,128)(2,1)}, bf16[768,2304]{1,0:T(8,128)(2,1)}, bf16[768,768]{1,0:T(8,128)(2,1)}) custom-call(s32[4]{0:T(128)} %pad_add_fusion.where_ref.refs_0_, bf16[512,896]{1,0:T(8,128)(2,1)} %bitcast.126, f32[12,768]{1,0:T(8,128)} %vector_ref.11, bf16[4,48,1536]{2,1,0:T(8,128)(2,1)} %copy-done.37, ...), custom_call_target="tpu_custom_call" | custom-call | flops 1811939328 | bytes 7077888 | tf_op jit(solution)/shard_map/pallas_call | solution.py:612
  80.1 2.7 collective-permute-done.14
  86.8 1.5 collective-permute-start.19
  88.3 2.0 collective-permute-start.18
  91.6 8.7 %shard_map.213 = (bf16[384,512]{1,0:T(8,128)(2,1)S(1)}, f32[3,8,512]{2,1,0:T(8,128)S(1)}, f32[512,768]{1,0:T(8,128)S(1)}) custom-call(bf16[512,2304]{1,0:T(8,128)(2,1)} %get-tuple-element.188.q_ref.k_ref.v_ref, bf16[512,2304]{1,0:T(8,128)(2,1)} %get-tuple-element.188.q_ref.k_ref.v_ref, bf16[512,2304]{1,0:T(8,128)(2,1)} %get-tuple-element.188.q_ref.k_ref.v_ref, ...), custom_call_target="tpu_custom_call" | custom-call | flops 805306368 | bytes 5505024 | tf_op jit(solution)/shard_map/pallas_call | solution.py:709
  103.0 1.7 slice.231
  104.7 1.7 slice.232
  108.5 3.5 %all-to-all-start.1 = ((bf16[32,16,768]{2,1,0:T(8,128)(2,1)}), bf16[32,16,768]{2,1,0:T(8,128)(2,1)}, u32[]{:S(2)}, u32[]{:S(2)}) async-start(bf16[32,16,768]{2,1,0:T(8,128)(2,1)} %bitcast.23), calls=%async_computation.1 | async-start | bytes 1572864 | tf_op jit(solution)/shard_map/all_to_all | solution.py:410
  112.1 11.0 %shard_map.214 = (bf16[384,512]{1,0:T(8,128)(2,1)S(1)}, f32[3,8,512]{2,1,0:T(8,128)S(1)}, f32[512,768]{1,0:T(8,128)S(1)}, bf16[512,768]{1,0:T(8,128)(2,1)S(1)}) custom-call(bf16[512,2304]{1,0:T(8,128)(2,1)} %get-tuple-element.188.q_ref.k_ref.v_ref, bf16[512,2304]{1,0:T(8,128)(2,1)} %get-tuple-element.188.q_ref.k_ref.v_ref, ...), custom_call_target="tpu_custom_call" | custom-call | flops 805306368 | bytes 5505024 | tf_op jit(solution)/shard_map/pallas_call | solution.py:709
  129.8 1.5 collective-permute-start.28
  131.9 10.8 %shard_map.215 = (bf16[512,3072]{1,0:T(8,128)(2,1)}, f32[512,3072]{1,0:T(8,128)}, bf16[768,3072]{1,0:T(8,128)(2,1)}) custom-call(s32[4]{0:T(128)} %pad_add_fusion.where_ref.refs_0_, bf16[512,768]{1,0:T(8,128)(2,1)} %copy-done.17, f32[1,3072]{1,0:T(1,128)} %bitcast.148, bf16[4,48,1536]{2,1,0:T(8,128)(2,1)} %pad_maximum_fusion.3.refs_0_, ...), custom_call_target="tpu_custom_call" | custom-call | flops 2415919104 | bytes 14155776 | tf_op jit(solution)/shard_map/pallas_call | solution.py:779
  142.7 1.5 collective-permute-done.29.refs_2_
  145.5 1.7 slice.234
  147.9 1.5 collective-permute-start.31
  150.0 6.2 %shard_map.216 = (bf16[4,4,96,768]{3,2,1,0:T(8,128)(2,1)S(1)}, bf16[4,4,96,768]{3,2,1,0:T(8,128)(2,1)S(1)}) custom-call(s32[4]{0:T(128)S(1)} %copy-done.14, bf16[512,3072]{1,0:T(8,128)(2,1)} %get-tuple-element.217.hidden_ref, bf16[512,768]{1,0:T(8,128)(2,1)} %bitcast.24.grads_ref), custom_call_target="tpu_custom_call" | custom-call | flops 2415919104 | bytes 7864320 | tf_op jit(solution)/shard_map/pallas_call | solution.py:825
  158.9 4.2 %collective-permute-done.35.refs_8_ = bf16[2,96,768]{2,1,0:T(8,128)(2,1)S(1)} collective-permute-done((bf16[2,96,768]{2,1,0:T(8,128)(2,1)}, bf16[2,96,768]{2,1,0:T(8,128)(2,1)S(1)}, u32[]{:S(2)}, u32[]{:S(2)}) %collective-permute-start.35) | collective-permute-done | bytes 294944 | tf_op jit(solution)/shard_map/ppermute | solution.py:339
  163.6 9.2 %shard_map.217 = (bf16[512,768]{1,0:T(8,128)(2,1)S(1)}, bf16[3072,768]{1,0:T(8,128)(2,1)}) custom-call(s32[4]{0:T(128)S(1)} %copy-done.14, bf16[512,3072]{1,0:T(8,128)(2,1)} %get-tuple-element.217.hidden_ref, f32[512,768]{1,0:T(8,128)} %copy-done.7, f32[12,768]{1,0:T(8,128)S(1)} %copy-done.9, bf16[4,96,768]{2,1,0:T(8,128)(2,1)S(1)} %pad_maximum_fusion.4.refs_0_, ...), custom_call_target="tpu_custom_call" | custom-call | flops 2415919104 | bytes 14155776 | tf_op jit(solution)/shard_map/pallas_call | solution.py:884
  175.0 4.4 %all-to-all-start.2 = ((bf16[32,16,768]{2,1,0:T(8,128)(2,1)}), bf16[32,16,768]{2,1,0:T(8,128)(2,1)}, u32[]{:S(2)}, u32[]{:S(2)}) async-start(bf16[32,16,768]{2,1,0:T(8,128)(2,1)} %bitcast.135), calls=%async_computation.2 | async-start | bytes 1572864 | tf_op jit(solution)/shard_map/all_to_all | solution.py:410
  179.5 2.7 fusion.17
  182.1 1.5 collective-permute-start.38
  183.6 1.5 collective-permute-start.39
  185.1 17.9 %shard_map.218 = (f32[512,768]{1,0:T(8,128)S(1)}, bf16[512,768]{1,0:T(8,128)(2,1)S(1)}, f32[8,768]{1,0:T(8,128)S(1)}, f32[1,3072]{1,0:T(1,128)S(1)}, bf16[4,4,24...) custom-call(s32[4]{0:T(128)S(1)} %copy-done.14, f32[512,3072]{1,0:T(8,128)} %get-tuple-element.211.slope_ref, ...), custom_call_target="tpu_custom_call" | custom-call | flops 7247757312 | bytes 34603008 | tf_op jit(solution)/shard_map/pallas_call | solution.py:962
  204.2 1.7 fusion.6
  207.2 9.0 %shard_map.219 = (bf16[3,512,384]{2,1,0:T(8,128)(2,1)S(1)}, f32[8,384]{1,0:T(8,128)S(1)}) custom-call(bf16[512,2304]{1,0:T(8,128)(2,1)} %get-tuple-element.188.q_ref.k_ref.v_ref, bf16[512,2304]{1,0:T(8,128)(2,1)} %get-tuple-element.188.q_ref.k_ref.v_ref, bf16[512,2304]{1,0:T(8,128)(2,1)} %get-tuple-element.188.q_ref.k_ref.v_ref, ...), custom_call_target="tpu_custom_call" | custom-call | flops 1409286144 | bytes 6291456 | tf_op jit(solution)/shard_map/pallas_call | solution.py:1117
  217.3 1.5 collective-permute-start.41
  218.8 1.5 collective-permute-start.42
  220.3 14.2 %shard_map.220 = (bf16[3,512,384]{2,1,0:T(8,128)(2,1)S(1)}, f32[8,384]{1,0:T(8,128)S(1)}, bf16[4,4,24,2304]{3,2,1,0:T(8,128)(2,1)}, bf16[4,4,24,2304]{3,2,1,0:T(8,128)(2,1)}) custom-call(bf16[512,2304]{1,0:T(8,128)(2,1)} %get-tuple-element.188.q_ref.k_ref.v_ref, bf16[512,2304]{1,0:T(8,128)(2,1)} %get-tuple-element.188.q_ref.k_ref.v_ref, ...), custom_call_target="tpu_custom_call" | custom-call | flops 1409286144 | bytes 6291456 | tf_op jit(solution)/shard_map/pallas_call | solution.py:1117
  234.5 1.7 fusion.30
  240.2 2.6 shard_map.221
  242.8 1.5 collective-permute-start.50
  244.3 2.5 collective-permute-start.51
  247.9 1.5 fusion.21
  249.3 1.6 collective-permute-start.46
  252.4 4.8 %collective-permute-done.51 = bf16[96,768]{1,0:T(8,128)(2,1)S(1)} collective-permute-done((bf16[96,768]{1,0:T(8,128)(2,1)S(1)}, bf16[96,768]{1,0:T(8,128)(2,1)S(1)}, u32[]{:S(2)}, u32[]{:S(2)}) %collective-permute-start.51) | collective-permute-done | bytes 147488 | tf_op jit(solution)/shard_map/ppermute | solution.py:406
  257.2 1.5 collective-permute-start.52
  258.7 8.4 %shard_map.222 = bf16[512,896]{1,0:T(8,128)(2,1)} custom-call(bf16[512,896]{1,0:T(8,128)(2,1)S(1)} %bitcast.133, bf16[3,512,384]{2,1,0:T(8,128)(2,1)S(1)} %get-tuple-element.264.refs_2_.d_ref, bf16[3,512,384]{2,1,0:T(8,128)(2,1)S(1)} %get-tuple-element.282.e_ref, f32[512,768]{1,0:T(8,128)S(1)} %copy-done.6, f32[12,768]{1,0:T(8,128)S(1)} %copy-done.9, ...), custom_call_target="tpu_custom_call" | custom-call | flops 1811939328 | bytes 3538944 | tf_op jit(solution)/shard_map/pallas_call | solution.py:1180
  267.2 3.2 collective-permute-done.46
  270.4 1.8 fusion.28
  272.9 2.7 all-to-all-start.3
  275.7 1.6 fusion.8
  277.4 1.8 collective-permute-start.58
  279.3 2.4 collective-permute-start.59
  283.1 1.5 collective-permute-start.53
  284.6 1.5 collective-permute-start.54
  286.1 13.4 %collective-permute-done.58 = bf16[24,3840]{1,0:T(8,128)(2,1)S(1)} collective-permute-done((bf16[24,3840]{1,0:T(8,128)(2,1)S(1)}, bf16[24,3840]{1,0:T(8,128)(2,1)S(1)}, u32[]{:S(2)}, u32[]{:S(2)}) %collective-permute-start.58) | collective-permute-done | bytes 184352 | tf_op jit(solution)/shard_map/ppermute | solution.py:406
  299.5 11.9 %collective-permute-done.59 = bf16[24,3840]{1,0:T(8,128)(2,1)S(1)} collective-permute-done((bf16[24,3840]{1,0:T(8,128)(2,1)S(1)}, bf16[24,3840]{1,0:T(8,128)(2,1)S(1)}, u32[]{:S(2)}, u32[]{:S(2)}) %collective-permute-start.59) | collective-permute-done | bytes 184352 | tf_op jit(solution)/shard_map/ppermute | solution.py:406
  311.5 1.5 fusion.26
  313.0 4.1 %collective-permute-start.55 = (bf16[24,2304]{1,0:T(8,128)(2,1)S(1)}, bf16[24,2304]{1,0:T(8,128)(2,1)S(1)}, u32[]{:S(2)}, u32[]{:S(2)}) collective-permute-start(bf16[24,2304]{1,0:T(8,128)(2,1)S(1)} %get-tuple-element.310), channel_id=1, source_target_pairs={{0,8},{1,9},{2,10},{3,11},{4,12},{5,13},{6,14},{7,15},{8,16},{9,17... | collective-permute-start | bytes 331784 | tf_op jit(solution)/shard_map/ppermute | solution.py:406
  320.3 1.6 collective-permute-done.55
  321.9 4.0 %collective-permute-done.56 = bf16[24,2304]{1,0:T(8,128)(2,1)S(1)} collective-permute-done((bf16[24,2304]{1,0:T(8,128)(2,1)S(1)}, bf16[24,2304]{1,0:T(8,128)(2,1)S(1)}, u32[]{:S(2)}, u32[]{:S(2)}) %collective-permute-start.56) | collective-permute-done | bytes 110624 | tf_op jit(solution)/shard_map/ppermute | solution.py:406
  329.9 5.8 %all-to-all-start.4 = ((f32[32,4,128]{2,1,0:T(4,128)}), f32[32,4,128]{2,1,0:T(4,128)S(1)}, u32[]{:S(2)}, u32[]{:S(2)}) async-start(f32[32,4,128]{2,1,0:T(4,128)} %broadcast_in_dim.2), calls=%async_computation.4 | async-start | bytes 131072 | tf_op jit(solution)/shard_map/all_to_all | solution.py:410
  335.8 1.5 shard_map.223
  337.3 5.9 %all-to-all-done.4 = f32[32,4,128]{2,1,0:T(4,128)S(1)} async-done(((f32[32,4,128]{2,1,0:T(4,128)}), f32[32,4,128]{2,1,0:T(4,128)S(1)}, u32[]{:S(2)}, u32[]{:S(2)}) %all-to-all-start.4) | async-done | bytes 65568 | tf_op jit(solution)/shard_map/all_to_all | solution.py:410
  345.9 2.0 multiply_add_fusion.2
  (255 shorter events, 58.3 us)
Async XLA Ops:
  4.2 9.5 %collective-permute-start.3 = (bf16[48,1536]{1,0:T(8,128)(2,1)S(1)}, bf16[48,1536]{1,0:T(8,128)(2,1)S(1)}, u32[]{:S(2)}, u32[]{:S(2)}) collective-permute-start(bf16[48,1536]{1,0:T(8,128)(2,1)S(1)} %get-tuple-element.369), channel_id=1, source_target_pairs={{0,24},{1,25},{2,26},{3,27},{4,28},{5,29},{6,30},{7,31},{8,0},{9,1... | collective-permute-start | bytes 442376 | tf_op jit(solution)/shard_map/ppermute | solution.py:346
  9.2 12.8 %collective-permute-start.2 = (bf16[48,1536]{1,0:T(8,128)(2,1)S(1)}, bf16[48,1536]{1,0:T(8,128)(2,1)S(1)}, u32[]{:S(2)}, u32[]{:S(2)}) collective-permute-start(bf16[48,1536]{1,0:T(8,128)(2,1)S(1)} %get-tuple-element.369), channel_id=1, source_target_pairs={{0,16},{1,17},{2,18},{3,19},{4,20},{5,21},{6,22},{7,23},{8,24},{9,... | collective-permute-start | bytes 442376 | tf_op jit(solution)/shard_map/ppermute | solution.py:346
  9.2 12.8 %collective-permute-start.1 = (bf16[48,1536]{1,0:T(8,128)(2,1)S(1)}, bf16[48,1536]{1,0:T(8,128)(2,1)S(1)}, u32[]{:S(2)}, u32[]{:S(2)}) collective-permute-start(bf16[48,1536]{1,0:T(8,128)(2,1)S(1)} %get-tuple-element.369), channel_id=1, source_target_pairs={{0,8},{1,9},{2,10},{3,11},{4,12},{5,13},{6,14},{7,15},{8,16},{9,17... | collective-permute-start | bytes 442376 | tf_op jit(solution)/shard_map/ppermute | solution.py:346
  22.2 44.4 %all-to-all-start = ((bf16[32,16,896]{2,1,0:T(8,128)(2,1)}), bf16[32,16,896]{2,1,0:T(8,128)(2,1)S(1)}, u32[]{:S(2)}, u32[]{:S(2)}) async-start(bf16[32,16,896]{2,1,0:T(8,128)(2,1)} %bitcast.13), calls=%async_computation | async-start | bytes 1835008 | tf_op jit(solution)/shard_map/all_to_all | solution.py:410
  27.2 25.3 %collective-permute-start.5 = (bf16[4,48,1536]{2,1,0:T(8,128)(2,1)S(1)}, bf16[4,48,1536]{2,1,0:T(8,128)(2,1)S(1)}, u32[]{:S(2)}, u32[]{:S(2)}) collective-permute-start(bf16[4,48,1536]{2,1,0:T(8,128)(2,1)S(1)} %pad_maximum_fusion.2.refs_0_), channel_id=1, source_target_pairs={{0,4},{1,5},{2,6},{3,7},{4,0},{5,1},{6,2},{7,3},{8,12},{9,13},{10,... | collective-permute-start | bytes 1769480 | tf_op jit(solution)/shard_map/ppermute | solution.py:339
  29.0 23.5 %collective-permute-start.4 = (bf16[4,48,1536]{2,1,0:T(8,128)(2,1)S(1)}, bf16[4,48,1536]{2,1,0:T(8,128)(2,1)S(1)}, u32[]{:S(2)}, u32[]{:S(2)}) collective-permute-start(bf16[4,48,1536]{2,1,0:T(8,128)(2,1)S(1)} %pad_maximum_fusion.2.refs_0_), channel_id=1, source_target_pairs={{0,2},{1,3},{2,0},{3,1},{4,6},{5,7},{6,4},{7,5},{8,10},{9,11},{10,... | collective-permute-start | bytes 1769480 | tf_op jit(solution)/shard_map/ppermute | solution.py:339
  30.5 24.7 %collective-permute-start.8 = (bf16[4,48,1536]{2,1,0:T(8,128)(2,1)S(1)}, bf16[4,48,1536]{2,1,0:T(8,128)(2,1)S(1)}, u32[]{:S(2)}, u32[]{:S(2)}) collective-permute-start(bf16[4,48,1536]{2,1,0:T(8,128)(2,1)S(1)} %pad_maximum_fusion.2.refs_0_), channel_id=1, source_target_pairs={{0,1},{1,0},{2,3},{3,2},{4,5},{5,4},{6,7},{7,6},{8,9},{9,8},{10,11... | collective-permute-start | bytes 1769480 | tf_op jit(solution)/shard_map/ppermute | solution.py:339
  52.5 11.0 %collective-permute-start.9 = (bf16[4,48,1536]{2,1,0:T(8,128)(2,1)S(1)}, bf16[4,48,1536]{2,1,0:T(8,128)(2,1)S(1)}, u32[]{:S(2)}, u32[]{:S(2)}) collective-permute-start(bf16[4,48,1536]{2,1,0:T(8,128)(2,1)S(1)} %collective-permute-done.4.refs_1_), channel_id=1, source_target_pairs={{0,1},{1,0},{2,3},{3,2},{4,5},{5,4},{6,7},{7,6},{8,9},{9,8},{10,11... | collective-permute-start | bytes 1769480 | tf_op jit(solution)/shard_map/ppermute | solution.py:339
  52.6 10.9 %collective-permute-start.10 = (bf16[4,48,1536]{2,1,0:T(8,128)(2,1)S(1)}, bf16[4,48,1536]{2,1,0:T(8,128)(2,1)S(1)}, u32[]{:S(2)}, u32[]{:S(2)}) collective-permute-start(bf16[4,48,1536]{2,1,0:T(8,128)(2,1)S(1)} %collective-permute-done.5.refs_2_), channel_id=1, source_target_pairs={{0,1},{1,0},{2,3},{3,2},{4,5},{5,4},{6,7},{7,6},{8,9},{9,8},{10,11... | collective-permute-start | bytes 1769480 | tf_op jit(solution)/shard_map/ppermute | solution.py:339
  53.2 9.2 %collective-permute-start.7 = (bf16[2,48,1536]{2,1,0:T(8,128)(2,1)S(1)}, bf16[2,48,1536]{2,1,0:T(8,128)(2,1)}, u32[]{:S(2)}, u32[]{:S(2)}) collective-permute-start(bf16[2,48,1536]{2,1,0:T(8,128)(2,1)S(1)} %slice.230), channel_id=1, source_target_pairs={{0,2},{1,3},{2,0},{3,1},{4,6},{5,7},{6,4},{7,5},{8,10},{9,11},{10,... | collective-permute-start | bytes 884744 | tf_op jit(solution)/shard_map/ppermute | solution.py:339
  54.7 8.8 %collective-permute-start.6 = (bf16[2,48,1536]{2,1,0:T(8,128)(2,1)S(1)}, bf16[2,48,1536]{2,1,0:T(8,128)(2,1)}, u32[]{:S(2)}, u32[]{:S(2)}) collective-permute-start(bf16[2,48,1536]{2,1,0:T(8,128)(2,1)S(1)} %slice.229), channel_id=1, source_target_pairs={{0,4},{1,5},{2,6},{3,7},{4,0},{5,1},{6,2},{7,3},{8,12},{9,13},{10,... | collective-permute-start | bytes 884744 | tf_op jit(solution)/shard_map/ppermute | solution.py:339
  63.5 2.0 collective-permute-start.11
  64.6 1.9 collective-permute-start.12
  66.5 13.5 %collective-permute-start.15 = (bf16[48,1536]{1,0:T(8,128)(2,1)S(1)}, bf16[48,1536]{1,0:T(8,128)(2,1)S(1)}, u32[]{:S(2)}, u32[]{:S(2)}) collective-permute-start(bf16[48,1536]{1,0:T(8,128)(2,1)S(1)} %get-tuple-element.186), channel_id=1, source_target_pairs={{0,24},{1,25},{2,26},{3,27},{4,28},{5,29},{6,30},{7,31},{8,0},{9,1... | collective-permute-start | bytes 442376 | tf_op jit(solution)/shard_map/ppermute | solution.py:346
  69.9 12.9 %collective-permute-start.14 = (bf16[48,1536]{1,0:T(8,128)(2,1)S(1)}, bf16[48,1536]{1,0:T(8,128)(2,1)S(1)}, u32[]{:S(2)}, u32[]{:S(2)}) collective-permute-start(bf16[48,1536]{1,0:T(8,128)(2,1)S(1)} %get-tuple-element.186), channel_id=1, source_target_pairs={{0,16},{1,17},{2,18},{3,19},{4,20},{5,21},{6,22},{7,23},{8,24},{9,... | collective-permute-start | bytes 442376 | tf_op jit(solution)/shard_map/ppermute | solution.py:346
  69.9 12.9 %collective-permute-start.13 = (bf16[48,1536]{1,0:T(8,128)(2,1)S(1)}, bf16[48,1536]{1,0:T(8,128)(2,1)S(1)}, u32[]{:S(2)}, u32[]{:S(2)}) collective-permute-start(bf16[48,1536]{1,0:T(8,128)(2,1)S(1)} %get-tuple-element.186), channel_id=1, source_target_pairs={{0,8},{1,9},{2,10},{3,11},{4,12},{5,13},{6,14},{7,15},{8,16},{9,17... | collective-permute-start | bytes 442376 | tf_op jit(solution)/shard_map/ppermute | solution.py:346
  83.7 18.6 %collective-permute-start.17 = (bf16[4,48,1536]{2,1,0:T(8,128)(2,1)}, bf16[4,48,1536]{2,1,0:T(8,128)(2,1)}, u32[]{:S(2)}, u32[]{:S(2)}) collective-permute-start(bf16[4,48,1536]{2,1,0:T(8,128)(2,1)} %pad_maximum_fusion.3.refs_0_), channel_id=1, source_target_pairs={{0,4},{1,5},{2,6},{3,7},{4,0},{5,1},{6,2},{7,3},{8,12},{9,13},{10,... | collective-permute-start | bytes 1769480 | tf_op jit(solution)/shard_map/ppermute | solution.py:339
  84.3 18.1 %collective-permute-start.16 = (bf16[4,48,1536]{2,1,0:T(8,128)(2,1)}, bf16[4,48,1536]{2,1,0:T(8,128)(2,1)}, u32[]{:S(2)}, u32[]{:S(2)}) collective-permute-start(bf16[4,48,1536]{2,1,0:T(8,128)(2,1)} %pad_maximum_fusion.3.refs_0_), channel_id=1, source_target_pairs={{0,2},{1,3},{2,0},{3,1},{4,6},{5,7},{6,4},{7,5},{8,10},{9,11},{10,... | collective-permute-start | bytes 1769480 | tf_op jit(solution)/shard_map/ppermute | solution.py:339
  85.6 16.6 %collective-permute-start.20 = (bf16[96,768]{1,0:T(8,128)(2,1)S(1)}, bf16[96,768]{1,0:T(8,128)(2,1)S(1)}, u32[]{:S(2)}, u32[]{:S(2)}) collective-permute-start(bf16[96,768]{1,0:T(8,128)(2,1)S(1)} %convert_element_type.370), channel_id=1, source_target_pairs={{0,24},{1,25},{2,26},{3,27},{4,28},{5,29},{6,30},{7,31},{8,0},{9,1... | collective-permute-start | bytes 442376 | tf_op jit(solution)/shard_map/ppermute | solution.py:346
  86.8 15.4 %collective-permute-start.19 = (bf16[96,768]{1,0:T(8,128)(2,1)S(1)}, bf16[96,768]{1,0:T(8,128)(2,1)S(1)}, u32[]{:S(2)}, u32[]{:S(2)}) collective-permute-start(bf16[96,768]{1,0:T(8,128)(2,1)S(1)} %convert_element_type.370), channel_id=1, source_target_pairs={{0,16},{1,17},{2,18},{3,19},{4,20},{5,21},{6,22},{7,23},{8,24},{9,... | collective-permute-start | bytes 442376 | tf_op jit(solution)/shard_map/ppermute | solution.py:346
  88.3 13.9 %collective-permute-start.18 = (bf16[96,768]{1,0:T(8,128)(2,1)S(1)}, bf16[96,768]{1,0:T(8,128)(2,1)S(1)}, u32[]{:S(2)}, u32[]{:S(2)}) collective-permute-start(bf16[96,768]{1,0:T(8,128)(2,1)S(1)} %convert_element_type.370), channel_id=1, source_target_pairs={{0,8},{1,9},{2,10},{3,11},{4,12},{5,13},{6,14},{7,15},{8,16},{9,17... | collective-permute-start | bytes 442376 | tf_op jit(solution)/shard_map/ppermute | solution.py:346
  102.2 23.7 %collective-permute-start.23 = (bf16[4,48,1536]{2,1,0:T(8,128)(2,1)}, bf16[4,48,1536]{2,1,0:T(8,128)(2,1)}, u32[]{:S(2)}, u32[]{:S(2)}) collective-permute-start(bf16[4,48,1536]{2,1,0:T(8,128)(2,1)} %pad_maximum_fusion.3.refs_0_), channel_id=1, source_target_pairs={{0,1},{1,0},{2,3},{3,2},{4,5},{5,4},{6,7},{7,6},{8,9},{9,8},{10,11... | collective-permute-start | bytes 1769480 | tf_op jit(solution)/shard_map/ppermute | solution.py:339
  102.4 23.6 %collective-permute-start.24 = (bf16[4,48,1536]{2,1,0:T(8,128)(2,1)}, bf16[4,48,1536]{2,1,0:T(8,128)(2,1)}, u32[]{:S(2)}, u32[]{:S(2)}) collective-permute-start(bf16[4,48,1536]{2,1,0:T(8,128)(2,1)} %collective-permute-done.16.refs_1_), channel_id=1, source_target_pairs={{0,1},{1,0},{2,3},{3,2},{4,5},{5,4},{6,7},{7,6},{8,9},{9,8},{10,11... | collective-permute-start | bytes 1769480 | tf_op jit(solution)/shard_map/ppermute | solution.py:339
  102.9 23.0 %collective-permute-start.25 = (bf16[4,48,1536]{2,1,0:T(8,128)(2,1)}, bf16[4,48,1536]{2,1,0:T(8,128)(2,1)}, u32[]{:S(2)}, u32[]{:S(2)}) collective-permute-start(bf16[4,48,1536]{2,1,0:T(8,128)(2,1)} %collective-permute-done.17.refs_2_), channel_id=1, source_target_pairs={{0,1},{1,0},{2,3},{3,2},{4,5},{5,4},{6,7},{7,6},{8,9},{9,8},{10,11... | collective-permute-start | bytes 1769480 | tf_op jit(solution)/shard_map/ppermute | solution.py:339
  106.4 19.5 %collective-permute-start.22 = (bf16[2,48,1536]{2,1,0:T(8,128)(2,1)}, bf16[2,48,1536]{2,1,0:T(8,128)(2,1)}, u32[]{:S(2)}, u32[]{:S(2)}) collective-permute-start(bf16[2,48,1536]{2,1,0:T(8,128)(2,1)} %slice.232), channel_id=1, source_target_pairs={{0,2},{1,3},{2,0},{3,1},{4,6},{5,7},{6,4},{7,5},{8,10},{9,11},{10,... | collective-permute-start | bytes 884744 | tf_op jit(solution)/shard_map/ppermute | solution.py:339
  107.1 18.9 %collective-permute-start.21 = (bf16[2,48,1536]{2,1,0:T(8,128)(2,1)}, bf16[2,48,1536]{2,1,0:T(8,128)(2,1)}, u32[]{:S(2)}, u32[]{:S(2)}) collective-permute-start(bf16[2,48,1536]{2,1,0:T(8,128)(2,1)} %slice.231), channel_id=1, source_target_pairs={{0,4},{1,5},{2,6},{3,7},{4,0},{5,1},{6,2},{7,3},{8,12},{9,13},{10,... | collective-permute-start | bytes 884744 | tf_op jit(solution)/shard_map/ppermute | solution.py:339
  108.5 41.5 %all-to-all-start.1 = ((bf16[32,16,768]{2,1,0:T(8,128)(2,1)}), bf16[32,16,768]{2,1,0:T(8,128)(2,1)}, u32[]{:S(2)}, u32[]{:S(2)}) async-start(bf16[32,16,768]{2,1,0:T(8,128)(2,1)} %bitcast.23), calls=%async_computation.1 | async-start | bytes 1572864 | tf_op jit(solution)/shard_map/all_to_all | solution.py:410
  126.0 2.3 collective-permute-start.27
  128.3 15.9 %collective-permute-start.29 = (bf16[4,96,768]{2,1,0:T(8,128)(2,1)S(1)}, bf16[4,96,768]{2,1,0:T(8,128)(2,1)S(1)}, u32[]{:S(2)}, u32[]{:S(2)}) collective-permute-start(bf16[4,96,768]{2,1,0:T(8,128)(2,1)S(1)} %pad_maximum_fusion.4.refs_0_), channel_id=1, source_target_pairs={{0,4},{1,5},{2,6},{3,7},{4,0},{5,1},{6,2},{7,3},{8,12},{9,13},{10,... | collective-permute-start | bytes 1769480 | tf_op jit(solution)/shard_map/ppermute | solution.py:339
  129.8 15.2 %collective-permute-start.28 = (bf16[4,96,768]{2,1,0:T(8,128)(2,1)S(1)}, bf16[4,96,768]{2,1,0:T(8,128)(2,1)}, u32[]{:S(2)}, u32[]{:S(2)}) collective-permute-start(bf16[4,96,768]{2,1,0:T(8,128)(2,1)S(1)} %pad_maximum_fusion.4.refs_0_), channel_id=1, source_target_pairs={{0,2},{1,3},{2,0},{3,1},{4,6},{5,7},{6,4},{7,5},{8,10},{9,11},{10,... | collective-permute-start | bytes 1769480 | tf_op jit(solution)/shard_map/ppermute | solution.py:339
  131.9 25.7 %collective-permute-start.32 = (bf16[4,96,768]{2,1,0:T(8,128)(2,1)S(1)}, bf16[4,96,768]{2,1,0:T(8,128)(2,1)}, u32[]{:S(2)}, u32[]{:S(2)}) collective-permute-start(bf16[4,96,768]{2,1,0:T(8,128)(2,1)S(1)} %pad_maximum_fusion.4.refs_0_), channel_id=1, source_target_pairs={{0,1},{1,0},{2,3},{3,2},{4,5},{5,4},{6,7},{7,6},{8,9},{9,8},{10,11... | collective-permute-start | bytes 1769480 | tf_op jit(solution)/shard_map/ppermute | solution.py:339
  145.0 13.4 %collective-permute-start.33 = (bf16[4,96,768]{2,1,0:T(8,128)(2,1)}, bf16[4,96,768]{2,1,0:T(8,128)(2,1)}, u32[]{:S(2)}, u32[]{:S(2)}) collective-permute-start(bf16[4,96,768]{2,1,0:T(8,128)(2,1)} %collective-permute-done.28.refs_1_), channel_id=1, source_target_pairs={{0,1},{1,0},{2,3},{3,2},{4,5},{5,4},{6,7},{7,6},{8,9},{9,8},{10,11... | collective-permute-start | bytes 1769480 | tf_op jit(solution)/shard_map/ppermute | solution.py:339
  145.0 13.4 %collective-permute-start.34 = (bf16[4,96,768]{2,1,0:T(8,128)(2,1)S(1)}, bf16[4,96,768]{2,1,0:T(8,128)(2,1)}, u32[]{:S(2)}, u32[]{:S(2)}) collective-permute-start(bf16[4,96,768]{2,1,0:T(8,128)(2,1)S(1)} %collective-permute-done.29.refs_2_), channel_id=1, source_target_pairs={{0,1},{1,0},{2,3},{3,2},{4,5},{5,4},{6,7},{7,6},{8,9},{9,8},{10,11... | collective-permute-start | bytes 1769480 | tf_op jit(solution)/shard_map/ppermute | solution.py:339
  147.9 9.7 %collective-permute-start.31 = (bf16[2,96,768]{2,1,0:T(8,128)(2,1)}, bf16[2,96,768]{2,1,0:T(8,128)(2,1)}, u32[]{:S(2)}, u32[]{:S(2)}) collective-permute-start(bf16[2,96,768]{2,1,0:T(8,128)(2,1)} %slice.235), channel_id=1, source_target_pairs={{0,2},{1,3},{2,0},{3,1},{4,6},{5,7},{6,4},{7,5},{8,10},{9,11},{10,... | collective-permute-start | bytes 884744 | tf_op jit(solution)/shard_map/ppermute | solution.py:339
  149.4 9.0 %collective-permute-start.30 = (bf16[2,96,768]{2,1,0:T(8,128)(2,1)}, bf16[2,96,768]{2,1,0:T(8,128)(2,1)}, u32[]{:S(2)}, u32[]{:S(2)}) collective-permute-start(bf16[2,96,768]{2,1,0:T(8,128)(2,1)} %slice.234), channel_id=1, source_target_pairs={{0,4},{1,5},{2,6},{3,7},{4,0},{5,1},{6,2},{7,3},{8,12},{9,13},{10,... | collective-permute-start | bytes 884744 | tf_op jit(solution)/shard_map/ppermute | solution.py:339
  158.3 15.3 %collective-permute-start.37 = (bf16[4,4,96,768]{3,2,1,0:T(8,128)(2,1)S(1)}, bf16[4,4,96,768]{3,2,1,0:T(8,128)(2,1)S(1)}, u32[]{:S(2)}, u32[]{:S(2)}) collective-permute-start(bf16[4,4,96,768]{3,2,1,0:T(8,128)(2,1)S(1)} %get-tuple-element.234), channel_id=1, source_target_pairs={{0,1},{1,0},{2,3},{3,2},{4,5},{5,4},{6,7},{7,6},{8,9},{9,8},{10,11... | collective-permute-start | bytes 7077896 | tf_op jit(solution)/shard_map/ppermute | solution.py:339
  158.4 4.8 %collective-permute-start.35 = (bf16[2,96,768]{2,1,0:T(8,128)(2,1)}, bf16[2,96,768]{2,1,0:T(8,128)(2,1)S(1)}, u32[]{:S(2)}, u32[]{:S(2)}) collective-permute-start(bf16[2,96,768]{2,1,0:T(8,128)(2,1)} %collective-permute-done.30.refs_3_), channel_id=1, source_target_pairs={{0,1},{1,0},{2,3},{3,2},{4,5},{5,4},{6,7},{7,6},{8,9},{9,8},{10,11... | collective-permute-start | bytes 884744 | tf_op jit(solution)/shard_map/ppermute | solution.py:339
  158.9 4.7 %collective-permute-start.36 = (bf16[2,96,768]{2,1,0:T(8,128)(2,1)}, bf16[2,96,768]{2,1,0:T(8,128)(2,1)S(1)}, u32[]{:S(2)}, u32[]{:S(2)}) collective-permute-start(bf16[2,96,768]{2,1,0:T(8,128)(2,1)} %collective-permute-done.31.refs_4_), channel_id=1, source_target_pairs={{0,1},{1,0},{2,3},{3,2},{4,5},{5,4},{6,7},{7,6},{8,9},{9,8},{10,11... | collective-permute-start | bytes 884744 | tf_op jit(solution)/shard_map/ppermute | solution.py:339
  175.0 29.1 %all-to-all-start.2 = ((bf16[32,16,768]{2,1,0:T(8,128)(2,1)}), bf16[32,16,768]{2,1,0:T(8,128)(2,1)}, u32[]{:S(2)}, u32[]{:S(2)}) async-start(bf16[32,16,768]{2,1,0:T(8,128)(2,1)} %bitcast.135), calls=%async_computation.2 | async-start | bytes 1572864 | tf_op jit(solution)/shard_map/all_to_all | solution.py:410
  182.1 22.0 %collective-permute-start.38 = (bf16[2,96,768]{2,1,0:T(8,128)(2,1)S(1)}, bf16[2,96,768]{2,1,0:T(8,128)(2,1)}, u32[]{:S(2)}, u32[]{:S(2)}) collective-permute-start(bf16[2,96,768]{2,1,0:T(8,128)(2,1)S(1)} %get-tuple-element.241), channel_id=1, source_target_pairs={{0,4},{1,5},{2,6},{3,7},{4,0},{5,1},{6,2},{7,3},{8,12},{9,13},{10,... | collective-permute-start | bytes 884744 | tf_op jit(solution)/shard_map/ppermute | solution.py:339
  183.6 20.5 %collective-permute-start.39 = (bf16[2,96,768]{2,1,0:T(8,128)(2,1)S(1)}, bf16[2,96,768]{2,1,0:T(8,128)(2,1)}, u32[]{:S(2)}, u32[]{:S(2)}) collective-permute-start(bf16[2,96,768]{2,1,0:T(8,128)(2,1)S(1)} %get-tuple-element.242), channel_id=1, source_target_pairs={{0,2},{1,3},{2,0},{3,1},{4,6},{5,7},{6,4},{7,5},{8,10},{9,11},{10,... | collective-permute-start | bytes 884744 | tf_op jit(solution)/shard_map/ppermute | solution.py:339
  205.9 10.3 %collective-permute-start.40 = (bf16[4,4,24,3840]{3,2,1,0:T(8,128)(2,1)}, bf16[4,4,24,3840]{3,2,1,0:T(8,128)(2,1)S(1)}, u32[]{:S(2)}, u32[]{:S(2)}) collective-permute-start(bf16[4,4,24,3840]{3,2,1,0:T(8,128)(2,1)} %get-tuple-element.251), channel_id=1, source_target_pairs={{0,1},{1,0},{2,3},{3,2},{4,5},{5,4},{6,7},{7,6},{8,9},{9,8},{10,11... | collective-permute-start | bytes 8847368 | tf_op jit(solution)/shard_map/ppermute | solution.py:339
  206.0 28.5 %collective-permute-start.43 = (bf16[4,96,768]{2,1,0:T(8,128)(2,1)S(1)}, bf16[4,96,768]{2,1,0:T(8,128)(2,1)S(1)}, u32[]{:S(2)}, u32[]{:S(2)}) collective-permute-start(bf16[4,96,768]{2,1,0:T(8,128)(2,1)S(1)} %get-tuple-element.259), channel_id=1, source_target_pairs={{0,2},{1,3},{2,0},{3,1},{4,6},{5,7},{6,4},{7,5},{8,10},{9,11},{10,... | collective-permute-start | bytes 1769480 | tf_op jit(solution)/shard_map/ppermute | solution.py:339
  206.7 27.8 %collective-permute-start.44 = (bf16[4,96,768]{2,1,0:T(8,128)(2,1)S(1)}, bf16[4,96,768]{2,1,0:T(8,128)(2,1)S(1)}, u32[]{:S(2)}, u32[]{:S(2)}) collective-permute-start(bf16[4,96,768]{2,1,0:T(8,128)(2,1)S(1)} %get-tuple-element.260), channel_id=1, source_target_pairs={{0,4},{1,5},{2,6},{3,7},{4,0},{5,1},{6,2},{7,3},{8,12},{9,13},{10,... | collective-permute-start | bytes 1769480 | tf_op jit(solution)/shard_map/ppermute | solution.py:339
  217.3 17.2 %collective-permute-start.41 = (bf16[2,24,3840]{2,1,0:T(8,128)(2,1)}, bf16[2,24,3840]{2,1,0:T(8,128)(2,1)S(1)}, u32[]{:S(2)}, u32[]{:S(2)}) collective-permute-start(bf16[2,24,3840]{2,1,0:T(8,128)(2,1)} %get-tuple-element.257), channel_id=1, source_target_pairs={{0,4},{1,5},{2,6},{3,7},{4,0},{5,1},{6,2},{7,3},{8,12},{9,13},{10,... | collective-permute-start | bytes 1105928 | tf_op jit(solution)/shard_map/ppermute | solution.py:339
  218.8 15.7 %collective-permute-start.42 = (bf16[2,24,3840]{2,1,0:T(8,128)(2,1)S(1)}, bf16[2,24,3840]{2,1,0:T(8,128)(2,1)S(1)}, u32[]{:S(2)}, u32[]{:S(2)}) collective-permute-start(bf16[2,24,3840]{2,1,0:T(8,128)(2,1)S(1)} %get-tuple-element.258), channel_id=1, source_target_pairs={{0,2},{1,3},{2,0},{3,1},{4,6},{5,7},{6,4},{7,5},{8,10},{9,11},{10,... | collective-permute-start | bytes 1105928 | tf_op jit(solution)/shard_map/ppermute | solution.py:339
  240.2 7.6 %collective-permute-start.45 = (bf16[4,4,24,2304]{3,2,1,0:T(8,128)(2,1)}, bf16[4,4,24,2304]{3,2,1,0:T(8,128)(2,1)}, u32[]{:S(2)}, u32[]{:S(2)}) collective-permute-start(bf16[4,4,24,2304]{3,2,1,0:T(8,128)(2,1)} %get-tuple-element.274), channel_id=1, source_target_pairs={{0,1},{1,0},{2,3},{3,2},{4,5},{5,4},{6,7},{7,6},{8,9},{9,8},{10,11... | collective-permute-start | bytes 5308424 | tf_op jit(solution)/shard_map/ppermute | solution.py:339
  242.8 8.5 %collective-permute-start.50 = (bf16[96,768]{1,0:T(8,128)(2,1)S(1)}, bf16[96,768]{1,0:T(8,128)(2,1)S(1)}, u32[]{:S(2)}, u32[]{:S(2)}) collective-permute-start(bf16[96,768]{1,0:T(8,128)(2,1)S(1)} %get-tuple-element.293), channel_id=1, source_target_pairs={{0,8},{1,9},{2,10},{3,11},{4,12},{5,13},{6,14},{7,15},{8,16},{9,17... | collective-permute-start | bytes 442376 | tf_op jit(solution)/shard_map/ppermute | solution.py:406
  244.3 12.9 %collective-permute-start.51 = (bf16[96,768]{1,0:T(8,128)(2,1)S(1)}, bf16[96,768]{1,0:T(8,128)(2,1)S(1)}, u32[]{:S(2)}, u32[]{:S(2)}) collective-permute-start(bf16[96,768]{1,0:T(8,128)(2,1)S(1)} %get-tuple-element.294), channel_id=1, source_target_pairs={{0,16},{1,17},{2,18},{3,19},{4,20},{5,21},{6,22},{7,23},{8,24},{9,... | collective-permute-start | bytes 442376 | tf_op jit(solution)/shard_map/ppermute | solution.py:406
  246.8 20.3 %collective-permute-start.48 = (bf16[4,24,3840]{2,1,0:T(8,128)(2,1)}, bf16[4,24,3840]{2,1,0:T(8,128)(2,1)S(1)}, u32[]{:S(2)}, u32[]{:S(2)}) collective-permute-start(bf16[4,24,3840]{2,1,0:T(8,128)(2,1)} %pad_maximum_fusion), channel_id=1, source_target_pairs={{0,2},{1,3},{2,0},{3,1},{4,6},{5,7},{6,4},{7,5},{8,10},{9,11},{10,... | collective-permute-start | bytes 2211848 | tf_op jit(solution)/shard_map/ppermute | solution.py:339
  247.3 19.8 %collective-permute-start.49 = (bf16[4,24,3840]{2,1,0:T(8,128)(2,1)}, bf16[4,24,3840]{2,1,0:T(8,128)(2,1)S(1)}, u32[]{:S(2)}, u32[]{:S(2)}) collective-permute-start(bf16[4,24,3840]{2,1,0:T(8,128)(2,1)} %pad_maximum_fusion.1), channel_id=1, source_target_pairs={{0,4},{1,5},{2,6},{3,7},{4,0},{5,1},{6,2},{7,3},{8,12},{9,13},{10,... | collective-permute-start | bytes 2211848 | tf_op jit(solution)/shard_map/ppermute | solution.py:339
  249.3 21.0 %collective-permute-start.46 = (bf16[2,24,2304]{2,1,0:T(8,128)(2,1)S(1)}, bf16[2,24,2304]{2,1,0:T(8,128)(2,1)S(1)}, u32[]{:S(2)}, u32[]{:S(2)}) collective-permute-start(bf16[2,24,2304]{2,1,0:T(8,128)(2,1)S(1)} %get-tuple-element.289), channel_id=1, source_target_pairs={{0,4},{1,5},{2,6},{3,7},{4,0},{5,1},{6,2},{7,3},{8,12},{9,13},{10,... | collective-permute-start | bytes 663560 | tf_op jit(solution)/shard_map/ppermute | solution.py:339
  251.4 19.0 %collective-permute-start.47 = (bf16[2,24,2304]{2,1,0:T(8,128)(2,1)S(1)}, bf16[2,24,2304]{2,1,0:T(8,128)(2,1)}, u32[]{:S(2)}, u32[]{:S(2)}) collective-permute-start(bf16[2,24,2304]{2,1,0:T(8,128)(2,1)S(1)} %get-tuple-element.290), channel_id=1, source_target_pairs={{0,2},{1,3},{2,0},{3,1},{4,6},{5,7},{6,4},{7,5},{8,10},{9,11},{10,... | collective-permute-start | bytes 663560 | tf_op jit(solution)/shard_map/ppermute | solution.py:339
  257.2 9.9 %collective-permute-start.52 = (bf16[96,768]{1,0:T(8,128)(2,1)S(1)}, bf16[96,768]{1,0:T(8,128)(2,1)S(1)}, u32[]{:S(2)}, u32[]{:S(2)}) collective-permute-start(bf16[96,768]{1,0:T(8,128)(2,1)S(1)} %get-tuple-element.295), channel_id=1, source_target_pairs={{0,24},{1,25},{2,26},{3,27},{4,28},{5,29},{6,30},{7,31},{8,0},{9,1... | collective-permute-start | bytes 442376 | tf_op jit(solution)/shard_map/ppermute | solution.py:406
  272.9 55.0 %all-to-all-start.3 = ((bf16[32,16,896]{2,1,0:T(8,128)(2,1)}), bf16[32,16,896]{2,1,0:T(8,128)(2,1)S(1)}, u32[]{:S(2)}, u32[]{:S(2)}) async-start(bf16[32,16,896]{2,1,0:T(8,128)(2,1)} %bitcast.46), calls=%async_computation.3 | async-start | bytes 1835008 | tf_op jit(solution)/shard_map/all_to_all | solution.py:410
  277.4 22.1 %collective-permute-start.58 = (bf16[24,3840]{1,0:T(8,128)(2,1)S(1)}, bf16[24,3840]{1,0:T(8,128)(2,1)S(1)}, u32[]{:S(2)}, u32[]{:S(2)}) collective-permute-start(bf16[24,3840]{1,0:T(8,128)(2,1)S(1)} %copy-done.42), channel_id=1, source_target_pairs={{0,8},{1,9},{2,10},{3,11},{4,12},{5,13},{6,14},{7,15},{8,16},{9,17... | collective-permute-start | bytes 552968 | tf_op jit(solution)/shard_map/ppermute | solution.py:406
  279.3 32.1 %collective-permute-start.59 = (bf16[24,3840]{1,0:T(8,128)(2,1)S(1)}, bf16[24,3840]{1,0:T(8,128)(2,1)S(1)}, u32[]{:S(2)}, u32[]{:S(2)}) collective-permute-start(bf16[24,3840]{1,0:T(8,128)(2,1)S(1)} %copy-done.41), channel_id=1, source_target_pairs={{0,16},{1,17},{2,18},{3,19},{4,20},{5,21},{6,22},{7,23},{8,24},{9,... | collective-permute-start | bytes 552968 | tf_op jit(solution)/shard_map/ppermute | solution.py:406
  281.7 29.7 %collective-permute-start.60 = (bf16[24,3840]{1,0:T(8,128)(2,1)S(1)}, bf16[24,3840]{1,0:T(8,128)(2,1)S(1)}, u32[]{:S(2)}, u32[]{:S(2)}) collective-permute-start(bf16[24,3840]{1,0:T(8,128)(2,1)S(1)} %copy-done.40), channel_id=1, source_target_pairs={{0,24},{1,25},{2,26},{3,27},{4,28},{5,29},{6,30},{7,31},{8,0},{9,1... | collective-permute-start | bytes 552968 | tf_op jit(solution)/shard_map/ppermute | solution.py:406
  283.1 28.4 %collective-permute-start.53 = (bf16[4,24,2304]{2,1,0:T(8,128)(2,1)S(1)}, bf16[4,24,2304]{2,1,0:T(8,128)(2,1)S(1)}, u32[]{:S(2)}, u32[]{:S(2)}) collective-permute-start(bf16[4,24,2304]{2,1,0:T(8,128)(2,1)S(1)} %pad_maximum_fusion.7), channel_id=1, source_target_pairs={{0,2},{1,3},{2,0},{3,1},{4,6},{5,7},{6,4},{7,5},{8,10},{9,11},{10,... | collective-permute-start | bytes 1327112 | tf_op jit(solution)/shard_map/ppermute | solution.py:339
  284.6 26.9 %collective-permute-start.54 = (bf16[4,24,2304]{2,1,0:T(8,128)(2,1)S(1)}, bf16[4,24,2304]{2,1,0:T(8,128)(2,1)S(1)}, u32[]{:S(2)}, u32[]{:S(2)}) collective-permute-start(bf16[4,24,2304]{2,1,0:T(8,128)(2,1)S(1)} %pad_maximum_fusion.8), channel_id=1, source_target_pairs={{0,4},{1,5},{2,6},{3,7},{4,0},{5,1},{6,2},{7,3},{8,12},{9,13},{10,... | collective-permute-start | bytes 1327112 | tf_op jit(solution)/shard_map/ppermute | solution.py:339
  313.0 8.8 %collective-permute-start.55 = (bf16[24,2304]{1,0:T(8,128)(2,1)S(1)}, bf16[24,2304]{1,0:T(8,128)(2,1)S(1)}, u32[]{:S(2)}, u32[]{:S(2)}) collective-permute-start(bf16[24,2304]{1,0:T(8,128)(2,1)S(1)} %get-tuple-element.310), channel_id=1, source_target_pairs={{0,8},{1,9},{2,10},{3,11},{4,12},{5,13},{6,14},{7,15},{8,16},{9,17... | collective-permute-start | bytes 331784 | tf_op jit(solution)/shard_map/ppermute | solution.py:406
  317.1 8.7 %collective-permute-start.56 = (bf16[24,2304]{1,0:T(8,128)(2,1)S(1)}, bf16[24,2304]{1,0:T(8,128)(2,1)S(1)}, u32[]{:S(2)}, u32[]{:S(2)}) collective-permute-start(bf16[24,2304]{1,0:T(8,128)(2,1)S(1)} %get-tuple-element.311), channel_id=1, source_target_pairs={{0,16},{1,17},{2,18},{3,19},{4,20},{5,21},{6,22},{7,23},{8,24},{9,... | collective-permute-start | bytes 331784 | tf_op jit(solution)/shard_map/ppermute | solution.py:406
  318.4 7.4 %collective-permute-start.57 = (bf16[24,2304]{1,0:T(8,128)(2,1)S(1)}, bf16[24,2304]{1,0:T(8,128)(2,1)S(1)}, u32[]{:S(2)}, u32[]{:S(2)}) collective-permute-start(bf16[24,2304]{1,0:T(8,128)(2,1)S(1)} %get-tuple-element.312), channel_id=1, source_target_pairs={{0,24},{1,25},{2,26},{3,27},{4,28},{5,29},{6,30},{7,31},{8,0},{9,1... | collective-permute-start | bytes 331784 | tf_op jit(solution)/shard_map/ppermute | solution.py:406
  329.9 13.3 %all-to-all-start.4 = ((f32[32,4,128]{2,1,0:T(4,128)}), f32[32,4,128]{2,1,0:T(4,128)S(1)}, u32[]{:S(2)}, u32[]{:S(2)}) async-start(f32[32,4,128]{2,1,0:T(4,128)} %broadcast_in_dim.2), calls=%async_computation.4 | async-start | bytes 131072 | tf_op jit(solution)/shard_map/all_to_all | solution.py:410
  (61 other events, 513.1 us)

commit v3 on v2

--- a/solution.py
+++ b/solution.py
@@ -339,21 +339,23 @@
     return lax.ppermute(value, "dev", flips(lax.axis_size("dev"), mask))
 
 
-def along_z(block):
+def along_z(block, stacks):
     devices = lax.axis_size("dev")
     depth = devices // PLANE
-    return jnp.stack(
-        [block] + [lax.ppermute(block, "dev", shifts(devices, k)) for k in range(1, depth)], 0
-    )
-
-
-def to_neighbours(own):
-    return send(own, 2), send(own, 4)
-
-
-def to_diagonal(from_x, from_y):
-    half = from_x.shape[0] // 2
-    return send(from_x[:half], 4), send(from_y[half:], 2)
+    blocks = [block] + [lax.ppermute(block, "dev", shifts(devices, k)) for k in range(1, depth)]
+    each = depth // stacks
+    return tuple(jnp.stack(blocks[k : k + each], 0) for k in range(0, depth, each))
+
+
+def to_neighbours(*own):
+    return tuple(send(stack, 2) for stack in own) + tuple(send(stack, 4) for stack in own)
+
+
+def to_diagonal(*near):
+    if len(near) == 4:
+        return send(near[0], 4), send(near[3], 2)
+    half = near[0].shape[0] // 2
+    return send(near[0][:half], 4), send(near[1][half:], 2)
 
 
 def to_partner(*pieces):
@@ -522,20 +524,20 @@
     )(slot, rows)
 
 
-PIECES = 10
-
-
 def pieces_of(where_ref, pieces):
     z, y, x, core = where_ref[0], where_ref[1], where_ref[2], where_ref[3]
-    for part, group in ((core, pieces[: PIECES // 2]), (1 - core, pieces[PIECES // 2 :])):
-        depth = group[0].shape[0]
-        firsts = (0, 0, 0, 0, depth // 2)
-        columns = ((y, x), (y, 1 - x), (1 - y, x), (1 - y, 1 - x), (1 - y, 1 - x))
-        for piece, first, (yy, xx) in zip(group, firsts, columns, strict=True):
+    count = len(pieces) // 2
+    depth = 2 * pieces[count - 1].shape[0]
+    columns = ((y, x), (y, 1 - x), (1 - y, x), (1 - y, 1 - x))
+    for part, group in ((core, pieces[:count]), (1 - core, pieces[count:])):
+        reached = 0
+        for piece in group:
             for index in range(piece.shape[0]):
-                step = first + index
+                yy, xx = columns[reached // depth]
+                step = reached % depth
                 zz = lax.rem(z - step + depth, depth)
                 yield piece.at[index], step, (zz * 2 + yy) * 2 + xx, part
+                reached += 1
 
 
 def wide_copies(where_ref, pieces, buffer, sems):
@@ -563,14 +565,14 @@
 
 def project(where, work, vector, pieces):
     count, feature = work.shape[0], vector.shape[1]
-    copies_count = 8 * pieces[0].shape[0]
+    copies_count = sum(piece.shape[0] for piece in pieces)
     tile = 256
 
     def kernel(where_ref, work_ref, vector_ref, *refs):
         (
             flipped_ref, out_ref, weights_ref, output_ref, low, buffer, sems, store_sems
-        ) = refs[PIECES:]
-        copies = wide_copies(where_ref, refs[:PIECES], buffer, sems)
+        ) = refs[len(pieces):]
+        copies = wide_copies(where_ref, refs[:len(pieces)], buffer, sems)
         for copy in copies:
             copy.start()
 
@@ -618,7 +620,7 @@
             shaped((feature, 3 * feature), jnp.bfloat16),
             shaped((feature, feature), jnp.bfloat16),
         ],
-        in_specs=[SCALARS, whole(count, feature), whole(*vector.shape)] + [FAR] * PIECES,
+        in_specs=[SCALARS, whole(count, feature), whole(*vector.shape)] + [FAR] * len(pieces),
         out_specs=[whole(feature, count), whole(count, 3 * feature), FAR, FAR],
         scratch_shapes=[
             pltpu.VMEM((count, feature), jnp.bfloat16),
@@ -631,10 +633,9 @@
     )(where, work, vector, *pieces)
 
 
-def code_both(code_ref, column, row):
+def fill_cap(code_ref, cap):
     code = code_ref[...].astype(jnp.float32)
-    column[...] = code[:, :1]
-    row[...] = code.T[:1]
+    cap[...] = jnp.where(code[:, :1] == code.T[:1], -masked_value, masked_value)
 
 
 def one_head(values, head):
@@ -646,19 +647,19 @@
 def attend(projected, work, vector, weights, first, pairs, carried=None):
     count, feature = work.shape[0], vector.shape[1]
     all_pairs = feature // 128
-    tile = 256
+    tile = 512
     ends = carried is not None
 
     def kernel(q_ref, k_ref, v_ref, weight_ref, code_ref, work_ref, vector_ref, *refs):
         if ends:
-            carried_ref, attended_ref, stat_ref, resid_ref, low_ref, total, column, row = refs
+            carried_ref, attended_ref, stat_ref, resid_ref, low_ref, total, cap = refs
         else:
-            attended_ref, stat_ref, total, column, row = refs
+            attended_ref, stat_ref, total, cap = refs
         pair = pl.program_id(0)
 
         @pl.when(pair == 0)
         def _():
-            code_both(code_ref, column, row)
+            fill_cap(code_ref, cap)
             total[...] = carried_ref[...] if ends else jnp.zeros_like(total)
 
         keys = k_ref[...]
@@ -670,15 +671,15 @@
             parts = []
             for start in range(0, count, tile):
                 span = slice(start, start + tile)
-                scores = by_rows(keys, query[span])
-                same = column[...] == row[:, span]
-                scores = jnp.where(same, scores, masked_value)
+                scores = jnp.minimum(by_rows(keys, query[span]), cap[:, span])
                 most = jnp.max(scores, 0, keepdims=True)
                 powers = jnp.exp(scores - most)
                 sums = jnp.sum(powers, 0, keepdims=True)
-                low = (powers * (1.0 / sums)).astype(jnp.bfloat16)
                 stat_ref[0, head : head + 1, span] = most + jnp.log(sums)
-                parts.append(product(values[head * HEAD : (head + 1) * HEAD], low))
+                mixed = product(
+                    values[head * HEAD : (head + 1) * HEAD], powers.astype(jnp.bfloat16)
+                )
+                parts.append(mixed * (1.0 / sums))
             heads.append(jnp.concatenate(parts, 1))
         both = jnp.concatenate(heads, 0)
         attended_ref[...] = both.astype(jnp.bfloat16)
@@ -734,7 +735,7 @@
         ]
         + ([wide, wide] if ends else [wide]),
         scratch_shapes=([pltpu.VMEM((count, feature), jnp.float32)] if ends else [])
-        + [pltpu.VMEM((count, 1), jnp.float32), pltpu.VMEM((1, count), jnp.float32)],
+        + [pltpu.VMEM((count, count), jnp.float32)],
         compiler_params=settings(LIMIT),
         cost_estimate=cost(
             8 * count * count * pairs * 128, 14 * count * feature, 2 * pairs * count * count
@@ -752,13 +753,13 @@
     steps = wide // tile
 
     def kernel(where_ref, low_ref, bias_ref, *refs):
-        hidden_ref, slope_ref, weights_ref, buffer, sems, store_sem = refs[PIECES:]
+        hidden_ref, slope_ref, weights_ref, buffer, sems, store_sem = refs[len(pieces):]
         step = pl.program_id(0)
         store = pltpu.make_async_copy(buffer, weights_ref, store_sem)
 
         @pl.when(step == 0)
         def _():
-            copies = wide_copies(where_ref, refs[:PIECES], buffer, sems)
+            copies = wide_copies(where_ref, refs[:len(pieces)], buffer, sems)
             for copy in copies:
                 copy.start()
             for copy in copies:
@@ -789,11 +790,11 @@
             whole(count, feature),
             pl.BlockSpec((1, tile), lambda step: (0, step)),
         ]
-        + [FAR] * PIECES,
+        + [FAR] * len(pieces),
         out_specs=[block, block, FAR],
         scratch_shapes=[
             pltpu.VMEM((feature, wide), jnp.bfloat16),
-            pltpu.SemaphoreType.DMA((8 * pieces[0].shape[0],)),
+            pltpu.SemaphoreType.DMA((sum(piece.shape[0] for piece in pieces),)),
             pltpu.SemaphoreType.DMA,
         ],
         compiler_params=settings(60),
@@ -861,8 +862,8 @@
     tile = 256
 
     def kernel(where_ref, hidden_ref, resid_ref, vector_ref, *refs):
-        out_ref, weights_ref, buffer, sems, store_sem = refs[PIECES:]
-        copies = down_copies(where_ref, refs[:PIECES], buffer, sems)
+        out_ref, weights_ref, buffer, sems, store_sem = refs[len(pieces):]
+        copies = down_copies(where_ref, refs[:len(pieces)], buffer, sems)
         for copy in copies:
             copy.start()
         for copy in copies:
@@ -889,11 +890,11 @@
             shaped((wide, feature), jnp.bfloat16),
         ],
         in_specs=[SCALARS, whole(count, wide), whole(count, feature), whole(*vector.shape)]
-        + [FAR] * PIECES,
+        + [FAR] * len(pieces),
         out_specs=[whole(count, feature), FAR],
         scratch_shapes=[
             pltpu.VMEM((wide, feature), jnp.bfloat16),
-            pltpu.SemaphoreType.DMA((8 * pieces[0].shape[0],)),
+            pltpu.SemaphoreType.DMA((sum(piece.shape[0] for piece in pieces),)),
             pltpu.SemaphoreType.DMA,
         ],
         compiler_params=settings(LIMIT),
@@ -988,7 +989,7 @@
             pltpu.VMEM((feature, count), jnp.bfloat16),
             pltpu.VMEM((feature, feature), jnp.float32),
         ],
-        compiler_params=settings(LIMIT),
+        compiler_params=settings(60),
         cost_estimate=cost(6 * count * wide * feature, 8 * wide * feature + 10 * count * wide),
     )(where, slope, low, grads, resid, vector, up_weights, down_weights, *attended)
 
@@ -996,22 +997,22 @@
 def attend_back(projected, work, stats, dlow, weights, first, pairs, gradient=None):
     count, feature = dlow.shape
     all_pairs = feature // 128
-    tile = 256
+    tile = 512
     wide = pairs * 128
 
     def kernel(q_ref, k_ref, v_ref, code_ref, stat_ref, dlow_ref, weight_ref, *refs):
         if gradient is None:
-            out_ref, sums_ref, douts, column, row = refs
+            out_ref, sums_ref, douts, cap = refs
         else:
             (
                 where_ref, flipped_ref, left_ref, out_ref, sums_ref, mine_ref, theirs_ref,
-                douts, column, row, right, result,
+                douts, cap, right, result,
             ) = refs
         pair = pl.program_id(0)
 
         @pl.when(pair == 0)
         def _():
-            code_both(code_ref, column, row)
+            fill_cap(code_ref, cap)
             for start in range(0, wide, 128):
                 span = slice(start, start + 128)
                 douts[start // 128] = by_rows(dlow_ref[...], weight_ref[span, :]).astype(
@@ -1021,31 +1022,26 @@
         @pl.when(pair < pairs)
         def _():
             keys, values = k_ref[...], v_ref[...]
-            flipped = keys.astype(jnp.float32).T.astype(jnp.bfloat16)
+            wide_keys = keys.astype(jnp.float32)
+            dquery = jnp.zeros((count, 128), jnp.float32)
             scaled = q_ref[...].astype(jnp.float32) * 0.125
             dout = douts[pair].astype(jnp.float32)
             dkey = jnp.zeros((count, 128), jnp.float32)
             dvalue = jnp.zeros((count, 128), jnp.float32)
-            heads = []
             for head in range(2):
                 query = one_head(scaled, head)
                 dhead = one_head(dout, head)
-                parts = []
                 for start in range(0, count, tile):
                     span = slice(start, start + tile)
-                    scores = by_rows(keys, query[span])
-                    same = column[...] == row[:, span]
-                    probs = jnp.exp(
-                        jnp.where(same, scores, masked_value) - stat_ref[0, head : head + 1, span]
-                    )
+                    scores = jnp.minimum(by_rows(keys, query[span]), cap[:, span])
+                    probs = jnp.exp(scores - stat_ref[0, head : head + 1, span])
                     dprob = by_rows(values, dhead[span])
                     inner = jnp.sum(probs * dprob, 0, keepdims=True)
                     dscore = (probs * (dprob - inner)).astype(jnp.bfloat16)
                     dvalue = dvalue + product(probs.astype(jnp.bfloat16), dhead[span])
                     dkey = dkey + product(dscore, query[span])
-                    parts.append(product(flipped[head * HEAD : (head + 1) * HEAD], dscore))
-                heads.append(jnp.concatenate(parts, 1))
-            dquery = (jnp.concatenate(heads, 0).T * 0.125).astype(jnp.bfloat16)
+                    dquery = dquery + by_columns(dscore, one_head(wide_keys, head))
+            dquery = (dquery * 0.125).astype(jnp.bfloat16)
             dvalue = dvalue.astype(jnp.bfloat16)
             out_ref[0] = dquery
             out_ref[1] = dkey.astype(jnp.bfloat16)
@@ -1093,8 +1089,7 @@
     ]
     scratch = [
         pltpu.VMEM((pairs, count, 128), jnp.bfloat16),
-        pltpu.VMEM((count, 1), jnp.float32),
-        pltpu.VMEM((1, count), jnp.float32),
+        pltpu.VMEM((count, count), jnp.float32),
     ]
     extra = ()
     if gradient is not None:
@@ -1198,6 +1193,126 @@
         compiler_params=settings(LIMIT),
         cost_estimate=cost(6 * count * feature * feature, 6 * feature * feature),
     )(work, *dprojected, dresid, vector, weights, sums_two, *sums_attend, bias_up)
+
+
+def settle(own, got, back, squares, devices, feature):
+    rows, columns = own.shape
+    lanes = 16 * feature // devices // 128
+    capacity = back.shape[1]
+
+    def kernel(squares_ref, own_ref, *refs):
+        got_refs, (back_ref, grad_ref, packet_ref) = refs[: len(got)], refs[len(got) :]
+        grad = own_ref[...]
+        for ref in got_refs:
+            grad += ref[...].astype(jnp.float32)
+        grad_ref[...] = grad
+        total = squares_ref[0, 0] + jnp.sum(grad * grad)
+        sums = jnp.sum(back_ref[...].astype(jnp.float32), 0)
+        packet_ref[:, :lanes, :] = jnp.broadcast_to(
+            (sums[:lanes] + sums[lanes : 2 * lanes])[None], (devices, lanes, 128)
+        )
+        packet_ref[:, lanes:, :] = jnp.full((devices, 1, 128), total, jnp.float32)
+
+    return pl.pallas_call(
+        kernel,
+        grid=(1,),
+        out_shape=[
+            shaped((rows, columns), jnp.float32),
+            shaped((devices, lanes + 1, 128), jnp.float32),
+        ],
+        in_specs=[SCALARS, whole(rows, columns)]
+        + [whole(rows, columns)] * len(got)
+        + [pl.BlockSpec((devices, capacity, 128), lambda step: (0, 0, feature // 128))],
+        out_specs=[whole(rows, columns), whole(devices, lanes + 1, 128)],
+        compiler_params=settings(60),
+        cost_estimate=cost(8 * rows * columns, 16 * rows * columns),
+    )(squares.reshape(1, 1), own, *got, back)
+
+
+def finish(packets, first_grad, up_grad, down_grad, wide, down, vector):
+    devices, lanes, _ = packets.shape
+    lanes -= 1
+    rows, columns = wide[0].shape
+    down_rows, feature = down[0].shape
+    vector_rows = vector[0].shape[0]
+    steps = 4
+    tile, down_tile = columns // steps, down_rows // steps
+    first_columns = first_grad.shape[1]
+
+    def kernel(packets_ref, first_ref, up_ref, down_grad_ref, *refs):
+        wide_refs, down_refs, vector_refs = refs[:3], refs[3:6], refs[6:9]
+        norm_ref, wide_new, down_new, vector_new = refs[9], refs[10:13], refs[13:16], refs[16:19]
+        sums, factor_ref = refs[19:]
+        step = pl.program_id(0)
+
+        def put(new, old, gradient, decay):
+            for ref, value in zip(
+                new, advance(*(ref[...] for ref in old), gradient, factor_ref[0], decay), strict=True
+            ):
+                ref[...] = value
+
+        @pl.when(step == 0)
+        def _():
+            for place_of in range(vector_rows * feature // 128):
+                device, lane = divmod(place_of, lanes)
+                row, column = divmod(place_of * 128, feature)
+                sums[row : row + 1, column : column + 128] = packets_ref[device, lane : lane + 1]
+            gradient = sums[...]
+            shares = packets_ref[:, lanes, :1]
+            total = jnp.sum(shares) + jnp.sum(gradient * gradient)
+            norm = jnp.sqrt(jnp.full((1, 1), total))
+            norm_ref[...] = norm
+            factor_ref[0] = jnp.sum(clip_norm / jnp.maximum(norm, clip_norm))
+            put(vector_new, vector_refs, gradient, 0.0)
+
+        for index in range(steps):
+
+            @pl.when(step == index)
+            def _():
+                first = index * tile
+                parts = []
+                if first < first_columns:
+                    parts.append(first_ref[:, first : min(first + tile, first_columns)])
+                if first + tile > first_columns:
+                    low = max(first - first_columns, 0)
+                    high = first + tile - first_columns
+                    if low < feature:
+                        parts.append(up_ref[:, FF + low : FF + min(high, feature)])
+                    if high > feature:
+                        parts.append(up_ref[:, max(low - feature, 0) : high - feature])
+                gradient = parts[0] if len(parts) == 1 else jnp.concatenate(parts, 1)
+                put(wide_new, wide_refs, gradient, decay_rate)
+
+        put(down_new, down_refs, down_grad_ref[...], decay_rate)
+
+    def tiles(shape):
+        return pl.BlockSpec(shape, lambda step: (0, step))
+
+    wide_specs = [tiles((rows, tile))] * 3
+    down_specs = [pl.BlockSpec((down_tile, feature), lambda step: (step, 0))] * 3
+    vector_specs = [whole(vector_rows, feature)] * 3
+    return pl.pallas_call(
+        kernel,
+        grid=(steps,),
+        out_shape=[shaped((1, 1), jnp.float32)]
+        + [shaped(part.shape, jnp.float32) for part in (*wide, *down, *vector)],
+        in_specs=[
+            whole(*packets.shape),
+            whole(*first_grad.shape),
+            whole(*up_grad.shape),
+            down_specs[0],
+        ]
+        + wide_specs
+        + down_specs
+        + vector_specs,
+        out_specs=[whole(1, 1)] + wide_specs + down_specs + vector_specs,
+        scratch_shapes=[
+            pltpu.VMEM((vector_rows, feature), jnp.float32),
+            pltpu.SMEM((1,), jnp.float32),
+        ],
+        compiler_params=settings(60),
+        cost_estimate=cost(20 * rows * columns, 40 * rows * columns),
+    )(packets, first_grad, up_grad, down_grad, *wide, *down, *vector)
 
 
 def structured(devices, feature):
@@ -1249,33 +1364,32 @@
     pair = jnp.concatenate(core_order(core, keep, got), 0)
 
     send_rows, send_grads, slot = route(segment_ids.reshape(1, count), tokens, cotangent, devices)
-    first_own = along_z(pair[:, 0])
+    first_own = along_z(pair[:, 0], 2)
     send_rows, first_own = pin(send_rows, first_own)
 
     work = exchange(send_rows.reshape(devices, capacity, -1)).reshape(count, -1)
-    first_near = to_neighbours(first_own)
-    first_near, up_block = pin(first_near, pair[:, 1])
+    first_near = pin(*to_neighbours(*first_own))
 
     first_far = to_diagonal(*first_near)
-    first_got = to_partner(first_own, *first_near)
+    first_got = to_partner(*first_own, *first_near)
     first_far, first_got = pin(first_far, first_got)
     first_got = first_got + to_partner(*first_far)
-    first_got, work, up_block = pin(first_got, work, up_block)
-
-    up_own = along_z(up_block)
+    first_got, work, up_block = pin(first_got, work, pair[:, 1])
+
+    up_own = along_z(up_block, 1)
     flipped_one, projected, first_weights, out_weights = project(
-        where, work, vector_weight, (first_own, *first_near, *first_far, *first_got)
+        where, work, vector_weight, (*first_own, *first_near, *first_far, *first_got)
     )
     projected, up_own, down_block, send_grads = pin(projected, up_own, down_low, send_grads)
 
-    up_near = to_neighbours(up_own)
-    down_own = along_z(down_block)
+    up_near = to_neighbours(*up_own)
+    down_own = along_z(down_block, 2)
     pairs = feature // 256
     attended_a, stats_a, carried = attend(projected, work, vector_weight, out_weights, 0, pairs)
     carried, up_near, down_own, send_grads = pin(carried, up_near, down_own, send_grads)
 
     up_far = to_diagonal(*up_near)
-    up_got = to_partner(up_own, *up_near)
+    up_got = to_partner(*up_own, *up_near)
     grads = exchange(send_grads.reshape(devices, capacity, feature)).reshape(count, feature)
     attended_b, stats_b, resid, low_two = attend(
         projected, work, vector_weight, out_weights, pairs, pairs, carried
@@ -1284,36 +1398,40 @@
     up_got = up_got + to_partner(*up_far)
     low_two, up_got, down_own = pin(low_two, up_got, down_own)
 
-    down_near = to_neighbours(down_own)
+    down_near = to_neighbours(*down_own)
     hidden, slope, up_weights = widen(
-        where, low_two, vector_weight[8:].reshape(1, FF), (up_own, *up_near, *up_far, *up_got)
+        where, low_two, vector_weight[8:].reshape(1, FF), (*up_own, *up_near, *up_far, *up_got)
     )
     hidden, down_near = pin(hidden, down_near)
 
     down_far = to_diagonal(*down_near)
-    down_got = to_partner(down_own, *down_near)
+    down_got = to_partner(*down_own, *down_near)
     down_mine, down_theirs = down_gradient(where, hidden, grads, depth)
     down_far, down_got, down_mine, down_theirs = pin(down_far, down_got, down_mine, down_theirs)
 
-    down_got = pin(*down_got, *to_partner(*down_far))
     got = send(down_theirs, 1)
+    down_got = down_got + to_partner(*down_far)
+    down_got, got = pin(down_got, got)
+    down_fold = Fold(down_mine, got)
+    down_to, down_got = pin(down_fold.diagonal(), down_got)
+
+    got = over_diagonal(*down_to)
     output, down_weights = narrow(
-        where, hidden, resid, vector_weight, (down_own, *down_near, *down_far, *down_got)
+        where, hidden, resid, vector_weight, (*down_own, *down_near, *down_far, *down_got)
     )
     output, down_weights, got = pin(output, down_weights, got)
-
-    down_fold = Fold(down_mine, got)
-    down_to = pin(*down_fold.diagonal())
+    down_to, output = pin(down_fold.neighbours(*got), output)
+
     back_out = exchange(output.reshape(devices, capacity, feature)).reshape(count, feature)
-    got = over_diagonal(*down_to)
+    got = over_plane(*down_to)
     dresid, dlow, sums_two, bias_up_grad, up_mine, up_theirs = feed_back(
         where, slope, low_two, grads, resid, vector_weight, up_weights, down_weights,
         (attended_a, attended_b), depth,
     )
     dlow, got, up_mine, up_theirs, back_out = pin(dlow, got, up_mine, up_theirs, back_out)
-    down_to, dlow, up_theirs = pin(down_fold.neighbours(*got), dlow, up_theirs)
-
-    down_got = over_plane(*down_to)
+    down_sums, dlow, up_theirs = pin(down_fold.column(*got), dlow, up_theirs)
+
+    down_got = over_column(down_sums)
     up_got = send(up_theirs, 1)
     dleft, sums_left = attend_back(projected, work, stats_a, dlow, out_weights, 0, pairs)
     up_got, dleft, dlow = pin(up_got, dleft, dlow)
@@ -1325,77 +1443,50 @@
         projected, work, stats_b, dlow, out_weights, pairs, pairs,
         (where, flipped_one, dleft, depth),
     )
-    up_got, down_got, dright, first_mine, first_theirs = pin(
-        up_got, down_got, dright, first_mine, first_theirs
-    )
-    up_to, down_sums, dright, first_theirs = pin(
-        up_fold.neighbours(*up_got), down_fold.column(*down_got), dright, first_theirs
-    )
-
+    up_got, dright, first_mine, first_theirs, down_got = pin(
+        up_got, dright, first_mine, first_theirs, down_got
+    )
+    up_to, dright, first_theirs = pin(up_fold.neighbours(*up_got), dright, first_theirs)
+
+    first_got = send(first_theirs, 1)
+    first_got, dright, up_to = pin(first_got, dright, up_to)
+    first_fold = Fold(first_mine, first_got)
+    first_to, dright, up_to = pin(first_fold.diagonal(), dright, up_to)
+
+    got = over_diagonal(*first_to)
     up_got = over_plane(*up_to)
-    down_got = over_column(down_sums)
-    first_got = send(first_theirs, 1)
-    block_output = give_back(slot, back_out)
-    first_got, dright, block_output = pin(first_got, dright, block_output)
-    first_fold = Fold(first_mine, first_got)
-    first_to, dright = pin(first_fold.diagonal(), dright)
-
-    got = over_diagonal(*first_to)
     both = project_back(
         work, (dleft, dright), dresid, vector_weight, first_weights,
         sums_two, (sums_left, sums_right), bias_up_grad, devices,
     )
-    both, got, up_got, down_got = pin(both, got, up_got, down_got)
-    first_to, up_sums = pin(first_fold.neighbours(*got), up_fold.column(*up_got))
+    both, got = pin(both, got)
+    first_to = pin(*first_fold.neighbours(*got))
 
     back = exchange(both.reshape(devices, capacity, -1))
     got = over_plane(*first_to)
+    up_sums = pin(*up_fold.column(*up_got))
     up_got = over_column(up_sums)
+    got, up_first, back = pin(got, up_got[0], back)
     down_grad = total_of(down_sums[0], *down_got)
-    got, down_grad = pin(got, down_grad)
-    first_sums = pin(*first_fold.column(*got))
+    first_sums, back_out = pin(first_fold.column(*got), back_out)
 
     first_got = over_column(first_sums)
-    up_grad = total_of(up_sums[0], *up_got)
-    first_got, up_grad = pin(first_got, up_grad)
-    first_grad = total_of(first_sums[0], *first_got)
-    back, first_grad = pin(back, first_grad)
+    up_grad = total_of(up_sums[0], up_first, *up_got[1:])
+    squares = jnp.sum(up_grad * up_grad) + jnp.sum(down_grad * down_grad)
+    block_output = give_back(slot, back_out)
+    first_got, up_grad, block_output, down_grad, squares = pin(
+        first_got, up_grad, block_output, down_grad, squares
+    )
+    first_grad, packet = settle(first_sums[0], first_got, back, squares, devices, feature)
+    packets = exchange(packet)
     input_grad = give_back(slot, back.reshape(count, -1))
-
-    lanes = 16 * feature // devices // 128
-    vector_share = total_of(back[:, :lanes, feature:], back[:, lanes : 2 * lanes, feature:])
-    vector_share = jnp.sum(vector_share, 0)
-    wide_grad = jnp.concatenate([first_grad, up_grad[:, FF:], up_grad[:, :FF]], 1)
-    shard_squares = sum(jnp.sum(grad * grad) for grad in (down_grad, up_grad, first_grad))
-    packet = jnp.concatenate([vector_share, jnp.full((1, 128), shard_squares)], 0)
-    packets = exchange(jnp.broadcast_to(packet[None], (devices, lanes + 1, 128)))
-    vector_grad = packets[:, :lanes].reshape(-1, feature)[: vector_weight.shape[0]]
-    total = jnp.sum(packets[:, lanes, 0]) + jnp.sum(vector_grad * vector_grad)
-    grad_norm = jnp.sqrt(total)
-    factor = clip_norm / jnp.maximum(grad_norm, clip_norm)
-    wide_new, wide_moment_new, wide_average_new = advance(
-        wide_weight, wide_moment, wide_average, wide_grad, factor, decay_rate
-    )
-    down_new, down_moment_new, down_average_new = advance(
-        down_weight, down_moment, down_average, down_grad, factor, decay_rate
-    )
-    vector_new, vector_moment_new, vector_average_new = advance(
-        vector_weight, vector_moment, vector_average, vector_grad, factor, 0.0
-    )
-    return (
-        block_output,
-        input_grad,
-        grad_norm,
-        wide_new,
-        wide_moment_new,
-        wide_average_new,
-        down_new,
-        down_moment_new,
-        down_average_new,
-        vector_new,
-        vector_moment_new,
-        vector_average_new,
-    )
+    grad_norm, *new = finish(
+        packets, first_grad, up_grad, down_grad,
+        (wide_weight, wide_moment, wide_average),
+        (down_weight, down_moment, down_average),
+        (vector_weight, vector_moment, vector_average),
+    )
+    return (block_output, input_grad, grad_norm.reshape(()), *new)
 
 
 def solution(mesh):

time: 352 us -> 330 us (0.938)
  waiting for transfers between devices: 98.4 us -> 81.8 us
  other arithmetic: 27.4 us -> 19.7 us
  starting transfers between devices: 85.8 us -> 92.8 us
    ppermute x9, waiting for transfers between devices: 36.1 us -> 0.07 us  [over_column(): lax.ppermute(sums[k], 'dev', shifts(devices, k))]
    ppermute x42 -> x52, waiting for transfers between devices: 44.4 us -> 58.1 us  [send(): return lax.ppermute(value, 'dev', flips(lax.axis_size('dev'), mask))]
    pallas_call x0 -> x2, Pallas kernels: none -> 6.93 us  [the longest x1 4.9 us: finish(): pl.pallas_call(kernel, grid=(steps,), out_shape=[shaped((1, 1), jnp.float...]
    convert_element_type x6, other arithmetic: 9.77 us -> 3.82 us  [low_sum(): return total_of(*terms).astype(jnp.bfloat16)]
    ppermute x42 -> x52, starting transfers between devices: 31 us -> 36.5 us  [send(): return lax.ppermute(value, 'dev', flips(lax.axis_size('dev'), mask))]
    pallas_call x2, Pallas kernels: 19.7 us -> 14.2 us  [attend(): pl.pallas_call(kernel, grid=(pairs,), out_shape=[shaped((pairs * 128, cou...]
    all_to_all x5, waiting for transfers between devices: 5.86 us -> 10.3 us  [exchange(): return lax.all_to_all(rows, 'dev', split_axis=0, concat_axis=0, tiled=True)]
    add x6 -> x0, other arithmetic: 4.26 us -> none  [the longest x3 4.05 us: advance(): new_average = average_rate * average + (1.0 - average_rate) * new_weight]
  transfers between devices with their start and end apart: 66 -> 76, of which waited for: 23 -> 28; matrix products, arithmetic and copies ran while one was open for 5% -> 5% of each run, Pallas kernels for 32% -> 32%
where the time goes in v3:
time: 330 us; the launch traced here: 329 us
  Pallas kernels  111 us (34%)
  starting transfers between devices  92.8 us (28%)
  waiting for transfers between devices  81.8 us (25%)
  local copies, waits for them, and re-layouts  20.2 us (6%)
  other arithmetic  19.7 us (6%)
    ppermute x52, waiting for transfers between devices, send(): return lax.ppermute(value, 'dev', flips(lax.axis_size('dev'), mask))  58.1 us
    ppermute x52, starting transfers between devices, send(): return lax.ppermute(value, 'dev', flips(lax.axis_size('dev'), mask))  36.5 us
    all_to_all x5, starting transfers between devices, exchange(): return lax.all_to_all(rows, 'dev', split_axis=0, concat_axis=0, tiled=True)  24.1 us
    pallas_call x2, Pallas kernels, attend_back(): pl.pallas_call(kernel, grid=(pairs if gradient is None else pairs + 3,),...  21.5 us
    pallas_call x1, Pallas kernels, feed_back(): pl.pallas_call(kernel, grid=(steps + 1,), out_shape=[shaped((count, featu...  18.9 us
    ppermute x9, starting transfers between devices, over_column(): lax.ppermute(sums[k], 'dev', shifts(devices, k))  16.5 us
    unnamed x150, local copies, waits for them, and re-layouts  15.4 us
    ppermute x9, starting transfers between devices, along_z(): lax.ppermute(block, 'dev', shifts(devices, k))  15.2 us
  transfers between devices with their start and end apart: 76, of which 28 were waited for; matrix products, arithmetic and copies ran while one was open for 5% of the time, Pallas kernels for 32%

profile of v3, /device:TPU:0, one launch (start us, length us, event | category | flops | bytes accessed | tf_op | source)
XLA Modules:
  0.0 329.0 jit_solution(2502925228608809826)
XLA Ops:
  4.2 5.0 %collective-permute-start.3 = (bf16[48,1536]{1,0:T(8,128)(2,1)S(1)}, bf16[48,1536]{1,0:T(8,128)(2,1)S(1)}, u32[]{:S(2)}, u32[]{:S(2)}) collective-permute-start(bf16[48,1536]{1,0:T(8,128)(2,1)S(1)} %get-tuple-element.450), channel_id=1, source_target_pairs={{0,24},{1,25},{2,26},{3,27},{4,28},{5,29},{6,30},{7,31},{8,0},{9,1... | collective-permute-start | bytes 442376 | tf_op jit(solution)/shard_map/ppermute | solution.py:345
  9.3 2.3 shard_map.211
  13.5 8.6 %collective-permute-done.2 = bf16[48,1536]{1,0:T(8,128)(2,1)S(1)} collective-permute-done((bf16[48,1536]{1,0:T(8,128)(2,1)S(1)}, bf16[48,1536]{1,0:T(8,128)(2,1)S(1)}, u32[]{:S(2)}, u32[]{:S(2)}) %collective-permute-start.2) | collective-permute-done | bytes 147488 | tf_op jit(solution)/shard_map/ppermute | solution.py:345
  22.2 4.9 %all-to-all-start = ((bf16[32,16,896]{2,1,0:T(8,128)(2,1)}), bf16[32,16,896]{2,1,0:T(8,128)(2,1)S(1)}, u32[]{:S(2)}, u32[]{:S(2)}) async-start(bf16[32,16,896]{2,1,0:T(8,128)(2,1)} %bitcast.12), calls=%async_computation | async-start | bytes 1835008 | tf_op jit(solution)/shard_map/all_to_all | solution.py:412
  27.1 1.8 collective-permute-start.6
  28.9 1.5 collective-permute-start.4
  31.2 13.8 %collective-permute-done.6.refs_4_ = bf16[2,48,1536]{2,1,0:T(8,128)(2,1)S(1)} collective-permute-done((bf16[2,48,1536]{2,1,0:T(8,128)(2,1)S(1)}, bf16[2,48,1536]{2,1,0:T(8,128)(2,1)S(1)}, u32[]{:S(2)}, u32[]{:S(2)}) %collective-permute-start.6) | collective-permute-done | bytes 294944 | tf_op jit(solution)/shard_map/ppermute | solution.py:339
  45.3 7.1 %collective-permute-done.7.refs_5_ = bf16[2,48,1536]{2,1,0:T(8,128)(2,1)S(1)} collective-permute-done((bf16[2,48,1536]{2,1,0:T(8,128)(2,1)S(1)}, bf16[2,48,1536]{2,1,0:T(8,128)(2,1)S(1)}, u32[]{:S(2)}, u32[]{:S(2)}) %collective-permute-start.7) | collective-permute-done | bytes 294944 | tf_op jit(solution)/shard_map/ppermute | solution.py:339
  53.0 1.4 collective-permute-start.8
  56.0 6.1 %collective-permute-done.8.refs_6_ = bf16[2,48,1536]{2,1,0:T(8,128)(2,1)} collective-permute-done((bf16[2,48,1536]{2,1,0:T(8,128)(2,1)S(1)}, bf16[2,48,1536]{2,1,0:T(8,128)(2,1)}, u32[]{:S(2)}, u32[]{:S(2)}) %collective-permute-start.8) | collective-permute-done | bytes 294944 | tf_op jit(solution)/shard_map/ppermute | solution.py:339
  62.1 1.9 collective-permute-done.9.refs_7_
  66.4 3.4 %collective-permute-start.20 = (bf16[48,1536]{1,0:T(8,128)(2,1)S(1)}, bf16[48,1536]{1,0:T(8,128)(2,1)S(1)}, u32[]{:S(2)}, u32[]{:S(2)}) collective-permute-start(bf16[48,1536]{1,0:T(8,128)(2,1)S(1)} %get-tuple-element.237), channel_id=1, source_target_pairs={{0,24},{1,25},{2,26},{3,27},{4,28},{5,29},{6,30},{7,31},{8,0},{9,1... | collective-permute-start | bytes 442376 | tf_op jit(solution)/shard_map/ppermute | solution.py:345
  70.9 9.2 %shard_map.212 = (bf16[768,512]{1,0:T(8,128)(2,1)}, bf16[512,2304]{1,0:T(8,128)(2,1)}, bf16[768,2304]{1,0:T(8,128)(2,1)}, bf16[768,768]{1,0:T(8,128)(2,1)}) custom-call(s32[4]{0:T(128)} %pad_add_fusion.where_ref.refs_0_, bf16[512,896]{1,0:T(8,128)(2,1)} %bitcast.128, f32[12,768]{1,0:T(8,128)} %refs_6_.1, bf16[2,48,1536]{2,1,0:T(8,128)(2,1)} %copy-done.43, ...), custom_call_target="tpu_custom_call" | custom-call | flops 1811939328 | bytes 7077888 | tf_op jit(solution)/shard_map/pallas_call | solution.py:614
  80.1 2.7 collective-permute-done.19
  84.3 1.5 collective-permute-start.21
  86.9 1.5 collective-permute-start.24
  88.4 2.0 collective-permute-start.23
  91.7 6.0 %shard_map.213 = (bf16[384,512]{1,0:T(8,128)(2,1)S(1)}, f32[3,8,512]{2,1,0:T(8,128)S(1)}, f32[512,768]{1,0:T(8,128)S(1)}) custom-call(bf16[512,2304]{1,0:T(8,128)(2,1)} %get-tuple-element.239.q_ref.k_ref.v_ref, bf16[512,2304]{1,0:T(8,128)(2,1)} %get-tuple-element.239.q_ref.k_ref.v_ref, bf16[512,2304]{1,0:T(8,128)(2,1)} %get-tuple-element.239.q_ref.k_ref.v_ref, ...), custom_call_target="tpu_custom_call" | custom-call | flops 805306368 | bytes 5505024 | tf_op jit(solution)/shard_map/pallas_call | solution.py:710
  101.4 3.5 %all-to-all-start.1 = ((bf16[32,16,768]{2,1,0:T(8,128)(2,1)}), bf16[32,16,768]{2,1,0:T(8,128)(2,1)}, u32[]{:S(2)}, u32[]{:S(2)}) async-start(bf16[32,16,768]{2,1,0:T(8,128)(2,1)} %bitcast.138), calls=%async_computation.1 | async-start | bytes 1572864 | tf_op jit(solution)/shard_map/all_to_all | solution.py:412
  106.9 1.5 collective-permute-start.27
  108.4 1.5 collective-permute-start.26
  109.9 8.2 %shard_map.214 = (bf16[384,512]{1,0:T(8,128)(2,1)S(1)}, f32[3,8,512]{2,1,0:T(8,128)S(1)}, f32[512,768]{1,0:T(8,128)S(1)}, bf16[512,768]{1,0:T(8,128)(2,1)S(1)}) custom-call(bf16[512,2304]{1,0:T(8,128)(2,1)} %get-tuple-element.239.q_ref.k_ref.v_ref, bf16[512,2304]{1,0:T(8,128)(2,1)} %get-tuple-element.239.q_ref.k_ref.v_ref, ...), custom_call_target="tpu_custom_call" | custom-call | flops 805306368 | bytes 5505024 | tf_op jit(solution)/shard_map/pallas_call | solution.py:710
  125.3 1.4 collective-permute-start.36
  128.2 10.9 %shard_map.215 = (bf16[512,3072]{1,0:T(8,128)(2,1)}, f32[512,3072]{1,0:T(8,128)}, bf16[768,3072]{1,0:T(8,128)(2,1)}) custom-call(s32[4]{0:T(128)} %pad_add_fusion.where_ref.refs_0_, bf16[512,768]{1,0:T(8,128)(2,1)} %copy-done.28, f32[1,3072]{1,0:T(1,128)} %bitcast.152, bf16[4,48,1536]{2,1,0:T(8,128)(2,1)} %pad_maximum_fusion.2.refs_0_, ...), custom_call_target="tpu_custom_call" | custom-call | flops 2415919104 | bytes 14155776 | tf_op jit(solution)/shard_map/pallas_call | solution.py:780
  144.9 6.2 %shard_map.216 = (bf16[4,4,96,768]{3,2,1,0:T(8,128)(2,1)S(1)}, bf16[4,4,96,768]{3,2,1,0:T(8,128)(2,1)S(1)}) custom-call(s32[4]{0:T(128)S(1)} %copy-done.24, bf16[512,3072]{1,0:T(8,128)(2,1)} %get-tuple-element.270.hidden_ref, bf16[512,768]{1,0:T(8,128)(2,1)} %bitcast.24.grads_ref), custom_call_target="tpu_custom_call" | custom-call | flops 2415919104 | bytes 7864320 | tf_op jit(solution)/shard_map/pallas_call | solution.py:826
  151.2 2.1 collective-permute-done.38.refs_7_
  153.9 4.2 %collective-permute-done.45.refs_14_ = bf16[2,96,768]{2,1,0:T(8,128)(2,1)S(1)} collective-permute-done((bf16[2,96,768]{2,1,0:T(8,128)(2,1)}, bf16[2,96,768]{2,1,0:T(8,128)(2,1)S(1)}, u32[]{:S(2)}, u32[]{:S(2)}) %collective-permute-start.45) | collective-permute-done | bytes 294944 | tf_op jit(solution)/shard_map/ppermute | solution.py:339
  161.1 9.7 %shard_map.217 = (bf16[512,768]{1,0:T(8,128)(2,1)S(1)}, bf16[3072,768]{1,0:T(8,128)(2,1)}) custom-call(s32[4]{0:T(128)S(1)} %copy-done.24, bf16[512,3072]{1,0:T(8,128)(2,1)} %get-tuple-element.270.hidden_ref, f32[512,768]{1,0:T(8,128)} %copy-done.8, f32[12,768]{1,0:T(8,128)S(1)} %copy-done.11, bf16[2,96,768]{2,1,0:T(8,128)(2,1)S(1)} %pad_maximum_fusion.9.refs_0_, ...), custom_call_target="tpu_custom_call" | custom-call | flops 2415919104 | bytes 14155776 | tf_op jit(solution)/shard_map/pallas_call | solution.py:885
  172.2 5.7 %all-to-all-start.2 = ((bf16[32,16,768]{2,1,0:T(8,128)(2,1)}), bf16[32,16,768]{2,1,0:T(8,128)(2,1)S(1)}, u32[]{:S(2)}, u32[]{:S(2)}) async-start(bf16[32,16,768]{2,1,0:T(8,128)(2,1)} %bitcast.139), calls=%async_computation.2 | async-start | bytes 1572864 | tf_op jit(solution)/shard_map/all_to_all | solution.py:412
  177.9 1.6 collective-permute-start.50
  179.5 1.5 collective-permute-start.51
  181.0 18.9 %shard_map.218 = (f32[512,768]{1,0:T(8,128)}, bf16[512,768]{1,0:T(8,128)(2,1)}, f32[8,768]{1,0:T(8,128)}, f32[1,3072]{1,0:T(1,128)}, bf16[4,4,24,3840]{3,2,1,0:T(8,128)(2,1)}, /*index=5*/bf16[4,4,24,3840]{3,2,1,0:T(8,128)(2,1)}) custom-call(s32[4]{0:T(128)} %pad_add_fusion.where_ref.refs_0_, f32[512,3072]{1,0:T(8,128)} %get-tuple-element.263.slope_ref, ...), custom_call_target="tpu_custom_call" | custom-call | flops 7247757312 | bytes 34603008 | tf_op jit(solution)/shard_map/pallas_call | solution.py:963
  199.9 1.8 collective-permute-done.50
  201.8 1.9 fusion.29
  204.9 8.1 %shard_map.219 = (bf16[3,512,384]{2,1,0:T(8,128)(2,1)S(1)}, f32[8,384]{1,0:T(8,128)S(1)}) custom-call(bf16[512,2304]{1,0:T(8,128)(2,1)} %get-tuple-element.239.q_ref.k_ref.v_ref, bf16[512,2304]{1,0:T(8,128)(2,1)} %get-tuple-element.239.q_ref.k_ref.v_ref, bf16[512,2304]{1,0:T(8,128)(2,1)} %get-tuple-element.239.q_ref.k_ref.v_ref, ...), custom_call_target="tpu_custom_call" | custom-call | flops 1409286144 | bytes 6291456 | tf_op jit(solution)/shard_map/pallas_call | solution.py:1112
  213.4 1.4 collective-permute-start.53
  215.4 1.5 collective-permute-start.55
  216.8 2.4 collective-permute-start.56
  219.2 1.5 collective-permute-start.57
  220.7 13.4 %shard_map.220 = (bf16[3,512,384]{2,1,0:T(8,128)(2,1)S(1)}, f32[8,384]{1,0:T(8,128)S(1)}, bf16[4,4,24,2304]{3,2,1,0:T(8,128)(2,1)}, bf16[4,4,24,2304]{3,2,1,0:T(8,128)(2,1)}) custom-call(bf16[512,2304]{1,0:T(8,128)(2,1)} %get-tuple-element.239.q_ref.k_ref.v_ref, bf16[512,2304]{1,0:T(8,128)(2,1)} %get-tuple-element.239.q_ref.k_ref.v_ref, ...), custom_call_target="tpu_custom_call" | custom-call | flops 1409286144 | bytes 6291456 | tf_op jit(solution)/shard_map/pallas_call | solution.py:1112
  236.4 3.7 %collective-permute-done.58 = bf16[4,4,24,2304]{3,2,1,0:T(8,128)(2,1)S(1)} collective-permute-done((bf16[4,4,24,2304]{3,2,1,0:T(8,128)(2,1)S(1)}, bf16[4,4,24,2304]{3,2,1,0:T(8,128)(2,1)S(1)}, u32[]{:S(2)}, u32[]{:S(2)}) %collective-permute-start.58) | collective-permute-done | bytes 1769504 | tf_op jit(solution)/shard_map/ppermute | solution.py:339
  241.2 1.4 collective-permute-start.59
  245.3 8.4 %shard_map.221 = bf16[512,896]{1,0:T(8,128)(2,1)} custom-call(bf16[512,896]{1,0:T(8,128)(2,1)S(1)} %bitcast.135, bf16[3,512,384]{2,1,0:T(8,128)(2,1)S(1)} %get-tuple-element.336.refs_2_.d_ref, bf16[3,512,384]{2,1,0:T(8,128)(2,1)S(1)} %get-tuple-element.356.e_ref, f32[512,768]{1,0:T(8,128)S(1)} %copy-done.9, f32[12,768]{1,0:T(8,128)S(1)} %copy-done.12, ...), custom_call_target="tpu_custom_call" | custom-call | flops 1811939328 | bytes 3538944 | tf_op jit(solution)/shard_map/pallas_call | solution.py:1175
  255.1 2.8 all-to-all-start.3
  257.9 1.5 fusion.7
  259.6 1.7 collective-permute-start.61
  261.3 1.5 collective-permute-start.62
  262.8 9.4 %collective-permute-done.63 = bf16[4,24,3840]{2,1,0:T(8,128)(2,1)} collective-permute-done((bf16[4,24,3840]{2,1,0:T(8,128)(2,1)}, bf16[4,24,3840]{2,1,0:T(8,128)(2,1)}, u32[]{:S(2)}, u32[]{:S(2)}) %collective-permute-start.63) | collective-permute-done | bytes 737312 | tf_op jit(solution)/shard_map/ppermute | solution.py:339
  272.1 2.1 fusion.27
  275.5 1.4 multiply_reduce_fusion.1
  276.9 3.5 %collective-permute-start.70 = (bf16[24,3840]{1,0:T(8,128)(2,1)}, bf16[24,3840]{1,0:T(8,128)(2,1)}, u32[]{:S(2)}, u32[]{:S(2)}) collective-permute-start(bf16[24,3840]{1,0:T(8,128)(2,1)} %get-tuple-element.382), channel_id=1, source_target_pairs={{0,24},{1,25},{2,26},{3,27},{4,28},{5,29},{6,30},{7,31},{8,0},{9,1... | collective-permute-start | bytes 552968 | tf_op jit(solution)/shard_map/ppermute | solution.py:408
  280.4 3.4 %collective-permute-done.61 = bf16[4,24,2304]{2,1,0:T(8,128)(2,1)S(1)} collective-permute-done((bf16[4,24,2304]{2,1,0:T(8,128)(2,1)S(1)}, bf16[4,24,2304]{2,1,0:T(8,128)(2,1)S(1)}, u32[]{:S(2)}, u32[]{:S(2)}) %collective-permute-start.61) | collective-permute-done | bytes 442400 | tf_op jit(solution)/shard_map/ppermute | solution.py:339
  285.3 4.3 %all-to-all-done.3.refs_3_ = bf16[32,16,896]{2,1,0:T(8,128)(2,1)S(1)} async-done(((bf16[32,16,896]{2,1,0:T(8,128)(2,1)}), bf16[32,16,896]{2,1,0:T(8,128)(2,1)S(1)}, u32[]{:S(2)}, u32[]{:S(2)}) %all-to-all-start.3) | async-done | bytes 917536 | tf_op jit(solution)/shard_map/all_to_all | solution.py:412
  289.7 2.0 fusion.25
  293.0 2.8 collective-permute-start.66
  295.8 1.9 collective-permute-start.67
  297.8 2.9 collective-permute-start.68
  300.7 2.4 multiply_reduce_fusion
  304.4 1.5 shard_map.222
  306.7 2.0 shard_map.224
  308.7 7.2 %all-to-all-start.4 = ((f32[32,4,128]{2,1,0:T(4,128)}), f32[32,4,128]{2,1,0:T(4,128)S(1)}, u32[]{:S(2)}, u32[]{:S(2)}) async-start(f32[32,4,128]{2,1,0:T(4,128)} %get-tuple-element.396), calls=%async_computation.4 | async-start | bytes 131072 | tf_op jit(solution)/shard_map/all_to_all | solution.py:412
  315.9 1.5 shard_map.223
  317.4 5.9 %all-to-all-done.4.packets_ref = f32[32,4,128]{2,1,0:T(4,128)S(1)} async-done(((f32[32,4,128]{2,1,0:T(4,128)}), f32[32,4,128]{2,1,0:T(4,128)S(1)}, u32[]{:S(2)}, u32[]{:S(2)}) %all-to-all-start.4) | async-done | bytes 65568 | tf_op jit(solution)/shard_map/all_to_all | solution.py:412
  323.9 4.9 %shard_map.225 = (f32[1,1]{1,0:T(1,128)}, f32[24,6144]{1,0:T(8,128)}, f32[24,6144]{1,0:T(8,128)}, f32[24,6144]{1,0:T(8,128)}, f32[96,768]{1,0:T(8,128)}, /*index...) custom-call(f32[32,4,128]{2,1,0:T(4,128)} %copy-done.44, ...), custom_call_target="tpu_custom_call" | custom-call | flops 2949120 | bytes 5898240 | tf_op jit(solution)/shard_map/pallas_call | solution.py:1294
  (291 shorter events, 56.2 us)
Async XLA Ops:
  4.2 9.3 %collective-permute-start.3 = (bf16[48,1536]{1,0:T(8,128)(2,1)S(1)}, bf16[48,1536]{1,0:T(8,128)(2,1)S(1)}, u32[]{:S(2)}, u32[]{:S(2)}) collective-permute-start(bf16[48,1536]{1,0:T(8,128)(2,1)S(1)} %get-tuple-element.450), channel_id=1, source_target_pairs={{0,24},{1,25},{2,26},{3,27},{4,28},{5,29},{6,30},{7,31},{8,0},{9,1... | collective-permute-start | bytes 442376 | tf_op jit(solution)/shard_map/ppermute | solution.py:345
  9.2 12.8 %collective-permute-start.2 = (bf16[48,1536]{1,0:T(8,128)(2,1)S(1)}, bf16[48,1536]{1,0:T(8,128)(2,1)S(1)}, u32[]{:S(2)}, u32[]{:S(2)}) collective-permute-start(bf16[48,1536]{1,0:T(8,128)(2,1)S(1)} %get-tuple-element.450), channel_id=1, source_target_pairs={{0,16},{1,17},{2,18},{3,19},{4,20},{5,21},{6,22},{7,23},{8,24},{9,... | collective-permute-start | bytes 442376 | tf_op jit(solution)/shard_map/ppermute | solution.py:345
  12.5 9.6 %collective-permute-start.1 = (bf16[48,1536]{1,0:T(8,128)(2,1)S(1)}, bf16[48,1536]{1,0:T(8,128)(2,1)S(1)}, u32[]{:S(2)}, u32[]{:S(2)}) collective-permute-start(bf16[48,1536]{1,0:T(8,128)(2,1)S(1)} %get-tuple-element.450), channel_id=1, source_target_pairs={{0,8},{1,9},{2,10},{3,11},{4,12},{5,13},{6,14},{7,15},{8,16},{9,17... | collective-permute-start | bytes 442376 | tf_op jit(solution)/shard_map/ppermute | solution.py:345
  22.2 44.2 %all-to-all-start = ((bf16[32,16,896]{2,1,0:T(8,128)(2,1)}), bf16[32,16,896]{2,1,0:T(8,128)(2,1)S(1)}, u32[]{:S(2)}, u32[]{:S(2)}) async-start(bf16[32,16,896]{2,1,0:T(8,128)(2,1)} %bitcast.12), calls=%async_computation | async-start | bytes 1835008 | tf_op jit(solution)/shard_map/all_to_all | solution.py:412
  27.1 17.9 %collective-permute-start.6 = (bf16[2,48,1536]{2,1,0:T(8,128)(2,1)S(1)}, bf16[2,48,1536]{2,1,0:T(8,128)(2,1)S(1)}, u32[]{:S(2)}, u32[]{:S(2)}) collective-permute-start(bf16[2,48,1536]{2,1,0:T(8,128)(2,1)S(1)} %pad_maximum_fusion.7.refs_0_), channel_id=1, source_target_pairs={{0,4},{1,5},{2,6},{3,7},{4,0},{5,1},{6,2},{7,3},{8,12},{9,13},{10,... | collective-permute-start | bytes 884744 | tf_op jit(solution)/shard_map/ppermute | solution.py:339
  28.9 16.4 %collective-permute-start.4 = (bf16[2,48,1536]{2,1,0:T(8,128)(2,1)S(1)}, bf16[2,48,1536]{2,1,0:T(8,128)(2,1)S(1)}, u32[]{:S(2)}, u32[]{:S(2)}) collective-permute-start(bf16[2,48,1536]{2,1,0:T(8,128)(2,1)S(1)} %pad_maximum_fusion.7.refs_0_), channel_id=1, source_target_pairs={{0,2},{1,3},{2,0},{3,1},{4,6},{5,7},{6,4},{7,5},{8,10},{9,11},{10,... | collective-permute-start | bytes 884744 | tf_op jit(solution)/shard_map/ppermute | solution.py:339
  30.4 22.0 %collective-permute-start.7 = (bf16[2,48,1536]{2,1,0:T(8,128)(2,1)S(1)}, bf16[2,48,1536]{2,1,0:T(8,128)(2,1)S(1)}, u32[]{:S(2)}, u32[]{:S(2)}) collective-permute-start(bf16[2,48,1536]{2,1,0:T(8,128)(2,1)S(1)} %pad_maximum_fusion.8.refs_1_), channel_id=1, source_target_pairs={{0,4},{1,5},{2,6},{3,7},{4,0},{5,1},{6,2},{7,3},{8,12},{9,13},{10,... | collective-permute-start | bytes 884744 | tf_op jit(solution)/shard_map/ppermute | solution.py:339
  30.9 21.5 %collective-permute-start.5 = (bf16[2,48,1536]{2,1,0:T(8,128)(2,1)S(1)}, bf16[2,48,1536]{2,1,0:T(8,128)(2,1)S(1)}, u32[]{:S(2)}, u32[]{:S(2)}) collective-permute-start(bf16[2,48,1536]{2,1,0:T(8,128)(2,1)S(1)} %pad_maximum_fusion.8.refs_1_), channel_id=1, source_target_pairs={{0,2},{1,3},{2,0},{3,1},{4,6},{5,7},{6,4},{7,5},{8,10},{9,11},{10,... | collective-permute-start | bytes 884744 | tf_op jit(solution)/shard_map/ppermute | solution.py:339
  31.2 23.2 %collective-permute-start.10 = (bf16[2,48,1536]{2,1,0:T(8,128)(2,1)S(1)}, bf16[2,48,1536]{2,1,0:T(8,128)(2,1)S(1)}, u32[]{:S(2)}, u32[]{:S(2)}) collective-permute-start(bf16[2,48,1536]{2,1,0:T(8,128)(2,1)S(1)} %pad_maximum_fusion.7.refs_0_), channel_id=1, source_target_pairs={{0,1},{1,0},{2,3},{3,2},{4,5},{5,4},{6,7},{7,6},{8,9},{9,8},{10,11... | collective-permute-start | bytes 884744 | tf_op jit(solution)/shard_map/ppermute | solution.py:339
  45.0 9.4 %collective-permute-start.11 = (bf16[2,48,1536]{2,1,0:T(8,128)(2,1)S(1)}, bf16[2,48,1536]{2,1,0:T(8,128)(2,1)S(1)}, u32[]{:S(2)}, u32[]{:S(2)}) collective-permute-start(bf16[2,48,1536]{2,1,0:T(8,128)(2,1)S(1)} %pad_maximum_fusion.8.refs_1_), channel_id=1, source_target_pairs={{0,1},{1,0},{2,3},{3,2},{4,5},{5,4},{6,7},{7,6},{8,9},{9,8},{10,11... | collective-permute-start | bytes 884744 | tf_op jit(solution)/shard_map/ppermute | solution.py:339
  53.0 9.1 %collective-permute-start.8 = (bf16[2,48,1536]{2,1,0:T(8,128)(2,1)S(1)}, bf16[2,48,1536]{2,1,0:T(8,128)(2,1)}, u32[]{:S(2)}, u32[]{:S(2)}) collective-permute-start(bf16[2,48,1536]{2,1,0:T(8,128)(2,1)S(1)} %collective-permute-done.4.refs_2_), channel_id=1, source_target_pairs={{0,4},{1,5},{2,6},{3,7},{4,0},{5,1},{6,2},{7,3},{8,12},{9,13},{10,... | collective-permute-start | bytes 884744 | tf_op jit(solution)/shard_map/ppermute | solution.py:339
  54.4 7.7 %collective-permute-start.15 = (bf16[2,48,1536]{2,1,0:T(8,128)(2,1)S(1)}, bf16[2,48,1536]{2,1,0:T(8,128)(2,1)S(1)}, u32[]{:S(2)}, u32[]{:S(2)}) collective-permute-start(bf16[2,48,1536]{2,1,0:T(8,128)(2,1)S(1)} %collective-permute-done.7.refs_5_), channel_id=1, source_target_pairs={{0,1},{1,0},{2,3},{3,2},{4,5},{5,4},{6,7},{7,6},{8,9},{9,8},{10,11... | collective-permute-start | bytes 884744 | tf_op jit(solution)/shard_map/ppermute | solution.py:339
  54.9 9.1 %collective-permute-start.9 = (bf16[2,48,1536]{2,1,0:T(8,128)(2,1)S(1)}, bf16[2,48,1536]{2,1,0:T(8,128)(2,1)}, u32[]{:S(2)}, u32[]{:S(2)}) collective-permute-start(bf16[2,48,1536]{2,1,0:T(8,128)(2,1)S(1)} %collective-permute-done.7.refs_5_), channel_id=1, source_target_pairs={{0,2},{1,3},{2,0},{3,1},{4,6},{5,7},{6,4},{7,5},{8,10},{9,11},{10,... | collective-permute-start | bytes 884744 | tf_op jit(solution)/shard_map/ppermute | solution.py:339
  66.4 13.7 %collective-permute-start.20 = (bf16[48,1536]{1,0:T(8,128)(2,1)S(1)}, bf16[48,1536]{1,0:T(8,128)(2,1)S(1)}, u32[]{:S(2)}, u32[]{:S(2)}) collective-permute-start(bf16[48,1536]{1,0:T(8,128)(2,1)S(1)} %get-tuple-element.237), channel_id=1, source_target_pairs={{0,24},{1,25},{2,26},{3,27},{4,28},{5,29},{6,30},{7,31},{8,0},{9,1... | collective-permute-start | bytes 442376 | tf_op jit(solution)/shard_map/ppermute | solution.py:345
  69.7 13.0 %collective-permute-start.19 = (bf16[48,1536]{1,0:T(8,128)(2,1)S(1)}, bf16[48,1536]{1,0:T(8,128)(2,1)S(1)}, u32[]{:S(2)}, u32[]{:S(2)}) collective-permute-start(bf16[48,1536]{1,0:T(8,128)(2,1)S(1)} %get-tuple-element.237), channel_id=1, source_target_pairs={{0,16},{1,17},{2,18},{3,19},{4,20},{5,21},{6,22},{7,23},{8,24},{9,... | collective-permute-start | bytes 442376 | tf_op jit(solution)/shard_map/ppermute | solution.py:345
  69.7 13.0 %collective-permute-start.18 = (bf16[48,1536]{1,0:T(8,128)(2,1)S(1)}, bf16[48,1536]{1,0:T(8,128)(2,1)S(1)}, u32[]{:S(2)}, u32[]{:S(2)}) collective-permute-start(bf16[48,1536]{1,0:T(8,128)(2,1)S(1)} %get-tuple-element.237), channel_id=1, source_target_pairs={{0,8},{1,9},{2,10},{3,11},{4,12},{5,13},{6,14},{7,15},{8,16},{9,17... | collective-permute-start | bytes 442376 | tf_op jit(solution)/shard_map/ppermute | solution.py:345
  83.7 17.2 %collective-permute-start.22 = (bf16[4,48,1536]{2,1,0:T(8,128)(2,1)}, bf16[4,48,1536]{2,1,0:T(8,128)(2,1)}, u32[]{:S(2)}, u32[]{:S(2)}) collective-permute-start(bf16[4,48,1536]{2,1,0:T(8,128)(2,1)} %pad_maximum_fusion.2.refs_0_), channel_id=1, source_target_pairs={{0,4},{1,5},{2,6},{3,7},{4,0},{5,1},{6,2},{7,3},{8,12},{9,13},{10,... | collective-permute-start | bytes 1769480 | tf_op jit(solution)/shard_map/ppermute | solution.py:339
  84.3 16.6 %collective-permute-start.21 = (bf16[4,48,1536]{2,1,0:T(8,128)(2,1)}, bf16[4,48,1536]{2,1,0:T(8,128)(2,1)}, u32[]{:S(2)}, u32[]{:S(2)}) collective-permute-start(bf16[4,48,1536]{2,1,0:T(8,128)(2,1)} %pad_maximum_fusion.2.refs_0_), channel_id=1, source_target_pairs={{0,2},{1,3},{2,0},{3,1},{4,6},{5,7},{6,4},{7,5},{8,10},{9,11},{10,... | collective-permute-start | bytes 1769480 | tf_op jit(solution)/shard_map/ppermute | solution.py:339
  85.7 13.9 %collective-permute-start.25 = (bf16[96,768]{1,0:T(8,128)(2,1)S(1)}, bf16[96,768]{1,0:T(8,128)(2,1)S(1)}, u32[]{:S(2)}, u32[]{:S(2)}) collective-permute-start(bf16[96,768]{1,0:T(8,128)(2,1)S(1)} %convert_element_type.355), channel_id=1, source_target_pairs={{0,24},{1,25},{2,26},{3,27},{4,28},{5,29},{6,30},{7,31},{8,0},{9,1... | collective-permute-start | bytes 442376 | tf_op jit(solution)/shard_map/ppermute | solution.py:345
  86.9 13.8 %collective-permute-start.24 = (bf16[96,768]{1,0:T(8,128)(2,1)S(1)}, bf16[96,768]{1,0:T(8,128)(2,1)S(1)}, u32[]{:S(2)}, u32[]{:S(2)}) collective-permute-start(bf16[96,768]{1,0:T(8,128)(2,1)S(1)} %convert_element_type.355), channel_id=1, source_target_pairs={{0,16},{1,17},{2,18},{3,19},{4,20},{5,21},{6,22},{7,23},{8,24},{9,... | collective-permute-start | bytes 442376 | tf_op jit(solution)/shard_map/ppermute | solution.py:345
  88.4 12.3 %collective-permute-start.23 = (bf16[96,768]{1,0:T(8,128)(2,1)S(1)}, bf16[96,768]{1,0:T(8,128)(2,1)S(1)}, u32[]{:S(2)}, u32[]{:S(2)}) collective-permute-start(bf16[96,768]{1,0:T(8,128)(2,1)S(1)} %convert_element_type.355), channel_id=1, source_target_pairs={{0,8},{1,9},{2,10},{3,11},{4,12},{5,13},{6,14},{7,15},{8,16},{9,17... | collective-permute-start | bytes 442376 | tf_op jit(solution)/shard_map/ppermute | solution.py:345
  99.7 21.2 %collective-permute-start.28 = (bf16[4,48,1536]{2,1,0:T(8,128)(2,1)}, bf16[4,48,1536]{2,1,0:T(8,128)(2,1)}, u32[]{:S(2)}, u32[]{:S(2)}) collective-permute-start(bf16[4,48,1536]{2,1,0:T(8,128)(2,1)} %pad_maximum_fusion.2.refs_0_), channel_id=1, source_target_pairs={{0,1},{1,0},{2,3},{3,2},{4,5},{5,4},{6,7},{7,6},{8,9},{9,8},{10,11... | collective-permute-start | bytes 1769480 | tf_op jit(solution)/shard_map/ppermute | solution.py:339
  100.8 20.6 %collective-permute-start.29 = (bf16[4,48,1536]{2,1,0:T(8,128)(2,1)}, bf16[4,48,1536]{2,1,0:T(8,128)(2,1)}, u32[]{:S(2)}, u32[]{:S(2)}) collective-permute-start(bf16[4,48,1536]{2,1,0:T(8,128)(2,1)} %collective-permute-done.21.refs_1_), channel_id=1, source_target_pairs={{0,1},{1,0},{2,3},{3,2},{4,5},{5,4},{6,7},{7,6},{8,9},{9,8},{10,11... | collective-permute-start | bytes 1769480 | tf_op jit(solution)/shard_map/ppermute | solution.py:339
  100.9 20.5 %collective-permute-start.30 = (bf16[4,48,1536]{2,1,0:T(8,128)(2,1)}, bf16[4,48,1536]{2,1,0:T(8,128)(2,1)}, u32[]{:S(2)}, u32[]{:S(2)}) collective-permute-start(bf16[4,48,1536]{2,1,0:T(8,128)(2,1)} %collective-permute-done.22.refs_2_), channel_id=1, source_target_pairs={{0,1},{1,0},{2,3},{3,2},{4,5},{5,4},{6,7},{7,6},{8,9},{9,8},{10,11... | collective-permute-start | bytes 1769480 | tf_op jit(solution)/shard_map/ppermute | solution.py:339
  101.4 43.5 %all-to-all-start.1 = ((bf16[32,16,768]{2,1,0:T(8,128)(2,1)}), bf16[32,16,768]{2,1,0:T(8,128)(2,1)}, u32[]{:S(2)}, u32[]{:S(2)}) async-start(bf16[32,16,768]{2,1,0:T(8,128)(2,1)} %bitcast.138), calls=%async_computation.1 | async-start | bytes 1572864 | tf_op jit(solution)/shard_map/all_to_all | solution.py:412
  106.9 14.2 %collective-permute-start.27 = (bf16[2,48,1536]{2,1,0:T(8,128)(2,1)S(1)}, bf16[2,48,1536]{2,1,0:T(8,128)(2,1)S(1)}, u32[]{:S(2)}, u32[]{:S(2)}) collective-permute-start(bf16[2,48,1536]{2,1,0:T(8,128)(2,1)S(1)} %slice.197), channel_id=1, source_target_pairs={{0,2},{1,3},{2,0},{3,1},{4,6},{5,7},{6,4},{7,5},{8,10},{9,11},{10,... | collective-permute-start | bytes 884744 | tf_op jit(solution)/shard_map/ppermute | solution.py:339
  108.4 13.0 %collective-permute-start.26 = (bf16[2,48,1536]{2,1,0:T(8,128)(2,1)S(1)}, bf16[2,48,1536]{2,1,0:T(8,128)(2,1)S(1)}, u32[]{:S(2)}, u32[]{:S(2)}) collective-permute-start(bf16[2,48,1536]{2,1,0:T(8,128)(2,1)S(1)} %slice.196), channel_id=1, source_target_pairs={{0,4},{1,5},{2,6},{3,7},{4,0},{5,1},{6,2},{7,3},{8,12},{9,13},{10,... | collective-permute-start | bytes 884744 | tf_op jit(solution)/shard_map/ppermute | solution.py:339
  123.5 15.6 %collective-permute-start.35 = (bf16[2,96,768]{2,1,0:T(8,128)(2,1)S(1)}, bf16[2,96,768]{2,1,0:T(8,128)(2,1)S(1)}, u32[]{:S(2)}, u32[]{:S(2)}) collective-permute-start(bf16[2,96,768]{2,1,0:T(8,128)(2,1)S(1)} %pad_maximum_fusion.9.refs_0_), channel_id=1, source_target_pairs={{0,4},{1,5},{2,6},{3,7},{4,0},{5,1},{6,2},{7,3},{8,12},{9,13},{10,... | collective-permute-start | bytes 884744 | tf_op jit(solution)/shard_map/ppermute | solution.py:339
  124.7 15.0 %collective-permute-start.33 = (bf16[2,96,768]{2,1,0:T(8,128)(2,1)S(1)}, bf16[2,96,768]{2,1,0:T(8,128)(2,1)}, u32[]{:S(2)}, u32[]{:S(2)}) collective-permute-start(bf16[2,96,768]{2,1,0:T(8,128)(2,1)S(1)} %pad_maximum_fusion.9.refs_0_), channel_id=1, source_target_pairs={{0,2},{1,3},{2,0},{3,1},{4,6},{5,7},{6,4},{7,5},{8,10},{9,11},{10,... | collective-permute-start | bytes 884744 | tf_op jit(solution)/shard_map/ppermute | solution.py:339
  125.3 14.4 %collective-permute-start.36 = (bf16[2,96,768]{2,1,0:T(8,128)(2,1)S(1)}, bf16[2,96,768]{2,1,0:T(8,128)(2,1)}, u32[]{:S(2)}, u32[]{:S(2)}) collective-permute-start(bf16[2,96,768]{2,1,0:T(8,128)(2,1)S(1)} %pad_maximum_fusion.10.refs_1_), channel_id=1, source_target_pairs={{0,4},{1,5},{2,6},{3,7},{4,0},{5,1},{6,2},{7,3},{8,12},{9,13},{10,... | collective-permute-start | bytes 884744 | tf_op jit(solution)/shard_map/ppermute | solution.py:339
  126.7 13.1 %collective-permute-start.34 = (bf16[2,96,768]{2,1,0:T(8,128)(2,1)S(1)}, bf16[2,96,768]{2,1,0:T(8,128)(2,1)S(1)}, u32[]{:S(2)}, u32[]{:S(2)}) collective-permute-start(bf16[2,96,768]{2,1,0:T(8,128)(2,1)S(1)} %pad_maximum_fusion.10.refs_1_), channel_id=1, source_target_pairs={{0,2},{1,3},{2,0},{3,1},{4,6},{5,7},{6,4},{7,5},{8,10},{9,11},{10,... | collective-permute-start | bytes 884744 | tf_op jit(solution)/shard_map/ppermute | solution.py:339
  128.1 14.0 %collective-permute-start.39 = (bf16[2,96,768]{2,1,0:T(8,128)(2,1)S(1)}, bf16[2,96,768]{2,1,0:T(8,128)(2,1)}, u32[]{:S(2)}, u32[]{:S(2)}) collective-permute-start(bf16[2,96,768]{2,1,0:T(8,128)(2,1)S(1)} %pad_maximum_fusion.9.refs_0_), channel_id=1, source_target_pairs={{0,1},{1,0},{2,3},{3,2},{4,5},{5,4},{6,7},{7,6},{8,9},{9,8},{10,11... | collective-permute-start | bytes 884744 | tf_op jit(solution)/shard_map/ppermute | solution.py:339
  140.5 10.7 %collective-permute-start.41 = (bf16[2,96,768]{2,1,0:T(8,128)(2,1)}, bf16[2,96,768]{2,1,0:T(8,128)(2,1)}, u32[]{:S(2)}, u32[]{:S(2)}) collective-permute-start(bf16[2,96,768]{2,1,0:T(8,128)(2,1)} %collective-permute-done.33.refs_2_), channel_id=1, source_target_pairs={{0,1},{1,0},{2,3},{3,2},{4,5},{5,4},{6,7},{7,6},{8,9},{9,8},{10,11... | collective-permute-start | bytes 884744 | tf_op jit(solution)/shard_map/ppermute | solution.py:339
  141.0 10.2 %collective-permute-start.37 = (bf16[2,96,768]{2,1,0:T(8,128)(2,1)}, bf16[2,96,768]{2,1,0:T(8,128)(2,1)}, u32[]{:S(2)}, u32[]{:S(2)}) collective-permute-start(bf16[2,96,768]{2,1,0:T(8,128)(2,1)} %collective-permute-done.33.refs_2_), channel_id=1, source_target_pairs={{0,4},{1,5},{2,6},{3,7},{4,0},{5,1},{6,2},{7,3},{8,12},{9,13},{10,... | collective-permute-start | bytes 884744 | tf_op jit(solution)/shard_map/ppermute | solution.py:339
  142.2 9.0 %collective-permute-start.43 = (bf16[2,96,768]{2,1,0:T(8,128)(2,1)S(1)}, bf16[2,96,768]{2,1,0:T(8,128)(2,1)}, u32[]{:S(2)}, u32[]{:S(2)}) collective-permute-start(bf16[2,96,768]{2,1,0:T(8,128)(2,1)S(1)} %collective-permute-done.35.refs_4_), channel_id=1, source_target_pairs={{0,1},{1,0},{2,3},{3,2},{4,5},{5,4},{6,7},{7,6},{8,9},{9,8},{10,11... | collective-permute-start | bytes 884744 | tf_op jit(solution)/shard_map/ppermute | solution.py:339
  142.9 8.3 %collective-permute-start.44 = (bf16[2,96,768]{2,1,0:T(8,128)(2,1)}, bf16[2,96,768]{2,1,0:T(8,128)(2,1)}, u32[]{:S(2)}, u32[]{:S(2)}) collective-permute-start(bf16[2,96,768]{2,1,0:T(8,128)(2,1)} %collective-permute-done.36.refs_5_), channel_id=1, source_target_pairs={{0,1},{1,0},{2,3},{3,2},{4,5},{5,4},{6,7},{7,6},{8,9},{9,8},{10,11... | collective-permute-start | bytes 884744 | tf_op jit(solution)/shard_map/ppermute | solution.py:339
  144.1 9.2 %collective-permute-start.38 = (bf16[2,96,768]{2,1,0:T(8,128)(2,1)}, bf16[2,96,768]{2,1,0:T(8,128)(2,1)}, u32[]{:S(2)}, u32[]{:S(2)}) collective-permute-start(bf16[2,96,768]{2,1,0:T(8,128)(2,1)} %collective-permute-done.36.refs_5_), channel_id=1, source_target_pairs={{0,2},{1,3},{2,0},{3,1},{4,6},{5,7},{6,4},{7,5},{8,10},{9,11},{10,... | collective-permute-start | bytes 884744 | tf_op jit(solution)/shard_map/ppermute | solution.py:339
  153.4 5.4 %collective-permute-start.47 = (bf16[4,4,96,768]{3,2,1,0:T(8,128)(2,1)S(1)}, bf16[4,4,96,768]{3,2,1,0:T(8,128)(2,1)S(1)}, u32[]{:S(2)}, u32[]{:S(2)}) collective-permute-start(bf16[4,4,96,768]{3,2,1,0:T(8,128)(2,1)S(1)} %get-tuple-element.286), channel_id=1, source_target_pairs={{0,1},{1,0},{2,3},{3,2},{4,5},{5,4},{6,7},{7,6},{8,9},{9,8},{10,11... | collective-permute-start | bytes 7077896 | tf_op jit(solution)/shard_map/ppermute | solution.py:339
  153.4 4.8 %collective-permute-start.45 = (bf16[2,96,768]{2,1,0:T(8,128)(2,1)}, bf16[2,96,768]{2,1,0:T(8,128)(2,1)S(1)}, u32[]{:S(2)}, u32[]{:S(2)}) collective-permute-start(bf16[2,96,768]{2,1,0:T(8,128)(2,1)} %collective-permute-done.37.refs_6_), channel_id=1, source_target_pairs={{0,1},{1,0},{2,3},{3,2},{4,5},{5,4},{6,7},{7,6},{8,9},{9,8},{10,11... | collective-permute-start | bytes 884744 | tf_op jit(solution)/shard_map/ppermute | solution.py:339
  159.0 11.7 %collective-permute-start.48 = (bf16[2,96,768]{2,1,0:T(8,128)(2,1)S(1)}, bf16[2,96,768]{2,1,0:T(8,128)(2,1)S(1)}, u32[]{:S(2)}, u32[]{:S(2)}) collective-permute-start(bf16[2,96,768]{2,1,0:T(8,128)(2,1)S(1)} %get-tuple-element.306), channel_id=1, source_target_pairs={{0,4},{1,5},{2,6},{3,7},{4,0},{5,1},{6,2},{7,3},{8,12},{9,13},{10,... | collective-permute-start | bytes 884744 | tf_op jit(solution)/shard_map/ppermute | solution.py:339
  160.0 10.8 %collective-permute-start.49 = (bf16[2,96,768]{2,1,0:T(8,128)(2,1)S(1)}, bf16[2,96,768]{2,1,0:T(8,128)(2,1)S(1)}, u32[]{:S(2)}, u32[]{:S(2)}) collective-permute-start(bf16[2,96,768]{2,1,0:T(8,128)(2,1)S(1)} %get-tuple-element.307), channel_id=1, source_target_pairs={{0,2},{1,3},{2,0},{3,1},{4,6},{5,7},{6,4},{7,5},{8,10},{9,11},{10,... | collective-permute-start | bytes 884744 | tf_op jit(solution)/shard_map/ppermute | solution.py:339
  172.2 29.6 %all-to-all-start.2 = ((bf16[32,16,768]{2,1,0:T(8,128)(2,1)}), bf16[32,16,768]{2,1,0:T(8,128)(2,1)S(1)}, u32[]{:S(2)}, u32[]{:S(2)}) async-start(bf16[32,16,768]{2,1,0:T(8,128)(2,1)} %bitcast.139), calls=%async_computation.2 | async-start | bytes 1572864 | tf_op jit(solution)/shard_map/all_to_all | solution.py:412
  177.9 23.8 %collective-permute-start.50 = (bf16[4,96,768]{2,1,0:T(8,128)(2,1)}, bf16[4,96,768]{2,1,0:T(8,128)(2,1)}, u32[]{:S(2)}, u32[]{:S(2)}) collective-permute-start(bf16[4,96,768]{2,1,0:T(8,128)(2,1)} %get-tuple-element.315), channel_id=1, source_target_pairs={{0,2},{1,3},{2,0},{3,1},{4,6},{5,7},{6,4},{7,5},{8,10},{9,11},{10,... | collective-permute-start | bytes 1769480 | tf_op jit(solution)/shard_map/ppermute | solution.py:339
  179.5 22.3 %collective-permute-start.51 = (bf16[4,96,768]{2,1,0:T(8,128)(2,1)}, bf16[4,96,768]{2,1,0:T(8,128)(2,1)}, u32[]{:S(2)}, u32[]{:S(2)}) collective-permute-start(bf16[4,96,768]{2,1,0:T(8,128)(2,1)} %get-tuple-element.316), channel_id=1, source_target_pairs={{0,4},{1,5},{2,6},{3,7},{4,0},{5,1},{6,2},{7,3},{8,12},{9,13},{10,... | collective-permute-start | bytes 1769480 | tf_op jit(solution)/shard_map/ppermute | solution.py:339
  203.8 9.2 %collective-permute-start.52 = (bf16[4,4,24,3840]{3,2,1,0:T(8,128)(2,1)}, bf16[4,4,24,3840]{3,2,1,0:T(8,128)(2,1)S(1)}, u32[]{:S(2)}, u32[]{:S(2)}) collective-permute-start(bf16[4,4,24,3840]{3,2,1,0:T(8,128)(2,1)} %get-tuple-element.325), channel_id=1, source_target_pairs={{0,1},{1,0},{2,3},{3,2},{4,5},{5,4},{6,7},{7,6},{8,9},{9,8},{10,11... | collective-permute-start | bytes 8847368 | tf_op jit(solution)/shard_map/ppermute | solution.py:339
  213.4 20.8 %collective-permute-start.53 = (bf16[2,24,3840]{2,1,0:T(8,128)(2,1)S(1)}, bf16[2,24,3840]{2,1,0:T(8,128)(2,1)S(1)}, u32[]{:S(2)}, u32[]{:S(2)}) collective-permute-start(bf16[2,24,3840]{2,1,0:T(8,128)(2,1)S(1)} %get-tuple-element.331), channel_id=1, source_target_pairs={{0,4},{1,5},{2,6},{3,7},{4,0},{5,1},{6,2},{7,3},{8,12},{9,13},{10,... | collective-permute-start | bytes 1105928 | tf_op jit(solution)/shard_map/ppermute | solution.py:339
  214.8 19.3 %collective-permute-start.54 = (bf16[2,24,3840]{2,1,0:T(8,128)(2,1)S(1)}, bf16[2,24,3840]{2,1,0:T(8,128)(2,1)S(1)}, u32[]{:S(2)}, u32[]{:S(2)}) collective-permute-start(bf16[2,24,3840]{2,1,0:T(8,128)(2,1)S(1)} %get-tuple-element.332), channel_id=1, source_target_pairs={{0,2},{1,3},{2,0},{3,1},{4,6},{5,7},{6,4},{7,5},{8,10},{9,11},{10,... | collective-permute-start | bytes 1105928 | tf_op jit(solution)/shard_map/ppermute | solution.py:339
  215.4 18.7 %collective-permute-start.55 = (bf16[96,768]{1,0:T(8,128)(2,1)S(1)}, bf16[96,768]{1,0:T(8,128)(2,1)S(1)}, u32[]{:S(2)}, u32[]{:S(2)}) collective-permute-start(bf16[96,768]{1,0:T(8,128)(2,1)S(1)} %get-tuple-element.340), channel_id=1, source_target_pairs={{0,8},{1,9},{2,10},{3,11},{4,12},{5,13},{6,14},{7,15},{8,16},{9,17... | collective-permute-start | bytes 442376 | tf_op jit(solution)/shard_map/ppermute | solution.py:408
  216.8 17.3 %collective-permute-start.56 = (bf16[96,768]{1,0:T(8,128)(2,1)S(1)}, bf16[96,768]{1,0:T(8,128)(2,1)S(1)}, u32[]{:S(2)}, u32[]{:S(2)}) collective-permute-start(bf16[96,768]{1,0:T(8,128)(2,1)S(1)} %get-tuple-element.341), channel_id=1, source_target_pairs={{0,16},{1,17},{2,18},{3,19},{4,20},{5,21},{6,22},{7,23},{8,24},{9,... | collective-permute-start | bytes 442376 | tf_op jit(solution)/shard_map/ppermute | solution.py:408
  219.2 14.9 %collective-permute-start.57 = (bf16[96,768]{1,0:T(8,128)(2,1)S(1)}, bf16[96,768]{1,0:T(8,128)(2,1)S(1)}, u32[]{:S(2)}, u32[]{:S(2)}) collective-permute-start(bf16[96,768]{1,0:T(8,128)(2,1)S(1)} %get-tuple-element.342), channel_id=1, source_target_pairs={{0,24},{1,25},{2,26},{3,27},{4,28},{5,29},{6,30},{7,31},{8,0},{9,1... | collective-permute-start | bytes 442376 | tf_op jit(solution)/shard_map/ppermute | solution.py:408
  241.2 12.5 %collective-permute-start.59 = (bf16[2,24,2304]{2,1,0:T(8,128)(2,1)S(1)}, bf16[2,24,2304]{2,1,0:T(8,128)(2,1)S(1)}, u32[]{:S(2)}, u32[]{:S(2)}) collective-permute-start(bf16[2,24,2304]{2,1,0:T(8,128)(2,1)S(1)} %get-tuple-element.363), channel_id=1, source_target_pairs={{0,4},{1,5},{2,6},{3,7},{4,0},{5,1},{6,2},{7,3},{8,12},{9,13},{10,... | collective-permute-start | bytes 663560 | tf_op jit(solution)/shard_map/ppermute | solution.py:339
  242.7 11.1 %collective-permute-start.60 = (bf16[2,24,2304]{2,1,0:T(8,128)(2,1)S(1)}, bf16[2,24,2304]{2,1,0:T(8,128)(2,1)S(1)}, u32[]{:S(2)}, u32[]{:S(2)}) collective-permute-start(bf16[2,24,2304]{2,1,0:T(8,128)(2,1)S(1)} %get-tuple-element.364), channel_id=1, source_target_pairs={{0,2},{1,3},{2,0},{3,1},{4,6},{5,7},{6,4},{7,5},{8,10},{9,11},{10,... | collective-permute-start | bytes 663560 | tf_op jit(solution)/shard_map/ppermute | solution.py:339
  243.4 28.7 %collective-permute-start.63 = (bf16[4,24,3840]{2,1,0:T(8,128)(2,1)}, bf16[4,24,3840]{2,1,0:T(8,128)(2,1)}, u32[]{:S(2)}, u32[]{:S(2)}) collective-permute-start(bf16[4,24,3840]{2,1,0:T(8,128)(2,1)} %pad_maximum_fusion), channel_id=1, source_target_pairs={{0,2},{1,3},{2,0},{3,1},{4,6},{5,7},{6,4},{7,5},{8,10},{9,11},{10,... | collective-permute-start | bytes 2211848 | tf_op jit(solution)/shard_map/ppermute | solution.py:339
  244.7 27.4 %collective-permute-start.64 = (bf16[4,24,3840]{2,1,0:T(8,128)(2,1)}, bf16[4,24,3840]{2,1,0:T(8,128)(2,1)}, u32[]{:S(2)}, u32[]{:S(2)}) collective-permute-start(bf16[4,24,3840]{2,1,0:T(8,128)(2,1)} %pad_maximum_fusion.1), channel_id=1, source_target_pairs={{0,4},{1,5},{2,6},{3,7},{4,0},{5,1},{6,2},{7,3},{8,12},{9,13},{10,... | collective-permute-start | bytes 2211848 | tf_op jit(solution)/shard_map/ppermute | solution.py:339
  255.1 34.6 %all-to-all-start.3 = ((bf16[32,16,896]{2,1,0:T(8,128)(2,1)}), bf16[32,16,896]{2,1,0:T(8,128)(2,1)S(1)}, u32[]{:S(2)}, u32[]{:S(2)}) async-start(bf16[32,16,896]{2,1,0:T(8,128)(2,1)} %bitcast.56), calls=%async_computation.3 | async-start | bytes 1835008 | tf_op jit(solution)/shard_map/all_to_all | solution.py:412
  259.6 24.2 %collective-permute-start.61 = (bf16[4,24,2304]{2,1,0:T(8,128)(2,1)S(1)}, bf16[4,24,2304]{2,1,0:T(8,128)(2,1)S(1)}, u32[]{:S(2)}, u32[]{:S(2)}) collective-permute-start(bf16[4,24,2304]{2,1,0:T(8,128)(2,1)S(1)} %pad_maximum_fusion.5), channel_id=1, source_target_pairs={{0,2},{1,3},{2,0},{3,1},{4,6},{5,7},{6,4},{7,5},{8,10},{9,11},{10,... | collective-permute-start | bytes 1327112 | tf_op jit(solution)/shard_map/ppermute | solution.py:339
  261.3 22.5 %collective-permute-start.62 = (bf16[4,24,2304]{2,1,0:T(8,128)(2,1)S(1)}, bf16[4,24,2304]{2,1,0:T(8,128)(2,1)S(1)}, u32[]{:S(2)}, u32[]{:S(2)}) collective-permute-start(bf16[4,24,2304]{2,1,0:T(8,128)(2,1)S(1)} %pad_maximum_fusion.6), channel_id=1, source_target_pairs={{0,4},{1,5},{2,6},{3,7},{4,0},{5,1},{6,2},{7,3},{8,12},{9,13},{10,... | collective-permute-start | bytes 1327112 | tf_op jit(solution)/shard_map/ppermute | solution.py:339
  275.1 9.5 %collective-permute-start.65 = (bf16[24,3840]{1,0:T(8,128)(2,1)S(1)}, bf16[24,3840]{1,0:T(8,128)(2,1)S(1)}, u32[]{:S(2)}, u32[]{:S(2)}) collective-permute-start(bf16[24,3840]{1,0:T(8,128)(2,1)S(1)} %get-tuple-element.371), channel_id=1, source_target_pairs={{0,8},{1,9},{2,10},{3,11},{4,12},{5,13},{6,14},{7,15},{8,16},{9,17... | collective-permute-start | bytes 552968 | tf_op jit(solution)/shard_map/ppermute | solution.py:408
  276.9 23.8 %collective-permute-start.69 = (bf16[24,3840]{1,0:T(8,128)(2,1)}, bf16[24,3840]{1,0:T(8,128)(2,1)S(1)}, u32[]{:S(2)}, u32[]{:S(2)}) collective-permute-start(bf16[24,3840]{1,0:T(8,128)(2,1)} %get-tuple-element.381), channel_id=1, source_target_pairs={{0,16},{1,17},{2,18},{3,19},{4,20},{5,21},{6,22},{7,23},{8,24},{9,... | collective-permute-start | bytes 552968 | tf_op jit(solution)/shard_map/ppermute | solution.py:408
  276.9 23.8 %collective-permute-start.70 = (bf16[24,3840]{1,0:T(8,128)(2,1)}, bf16[24,3840]{1,0:T(8,128)(2,1)}, u32[]{:S(2)}, u32[]{:S(2)}) collective-permute-start(bf16[24,3840]{1,0:T(8,128)(2,1)} %get-tuple-element.382), channel_id=1, source_target_pairs={{0,24},{1,25},{2,26},{3,27},{4,28},{5,29},{6,30},{7,31},{8,0},{9,1... | collective-permute-start | bytes 552968 | tf_op jit(solution)/shard_map/ppermute | solution.py:408
  293.0 12.9 %collective-permute-start.66 = (bf16[24,2304]{1,0:T(8,128)(2,1)}, bf16[24,2304]{1,0:T(8,128)(2,1)S(1)}, u32[]{:S(2)}, u32[]{:S(2)}) collective-permute-start(bf16[24,2304]{1,0:T(8,128)(2,1)} %get-tuple-element.376), channel_id=1, source_target_pairs={{0,8},{1,9},{2,10},{3,11},{4,12},{5,13},{6,14},{7,15},{8,16},{9,17... | collective-permute-start | bytes 331784 | tf_op jit(solution)/shard_map/ppermute | solution.py:408
  295.8 10.1 %collective-permute-start.67 = (bf16[24,2304]{1,0:T(8,128)(2,1)S(1)}, bf16[24,2304]{1,0:T(8,128)(2,1)S(1)}, u32[]{:S(2)}, u32[]{:S(2)}) collective-permute-start(bf16[24,2304]{1,0:T(8,128)(2,1)S(1)} %get-tuple-element.377), channel_id=1, source_target_pairs={{0,16},{1,17},{2,18},{3,19},{4,20},{5,21},{6,22},{7,23},{8,24},{9,... | collective-permute-start | bytes 331784 | tf_op jit(solution)/shard_map/ppermute | solution.py:408
  297.8 8.2 %collective-permute-start.68 = (bf16[24,2304]{1,0:T(8,128)(2,1)S(1)}, bf16[24,2304]{1,0:T(8,128)(2,1)S(1)}, u32[]{:S(2)}, u32[]{:S(2)}) collective-permute-start(bf16[24,2304]{1,0:T(8,128)(2,1)S(1)} %get-tuple-element.378), channel_id=1, source_target_pairs={{0,24},{1,25},{2,26},{3,27},{4,28},{5,29},{6,30},{7,31},{8,0},{9,1... | collective-permute-start | bytes 331784 | tf_op jit(solution)/shard_map/ppermute | solution.py:408
  308.7 14.6 %all-to-all-start.4 = ((f32[32,4,128]{2,1,0:T(4,128)}), f32[32,4,128]{2,1,0:T(4,128)S(1)}, u32[]{:S(2)}, u32[]{:S(2)}) async-start(f32[32,4,128]{2,1,0:T(4,128)} %get-tuple-element.396), calls=%async_computation.4 | async-start | bytes 131072 | tf_op jit(solution)/shard_map/all_to_all | solution.py:412
  (86 other events, 639.4 us)

commit v4 on v3

--- a/solution.py
+++ b/solution.py
@@ -644,23 +644,25 @@
     return jnp.where(inside, values, 0.0).astype(jnp.bfloat16)
 
 
-def attend(projected, work, vector, weights, first, pairs, carried=None):
+def attend(projected, work, vector, weights, first, pairs, left=None):
     count, feature = work.shape[0], vector.shape[1]
     all_pairs = feature // 128
     tile = 512
-    ends = carried is not None
-
-    def kernel(q_ref, k_ref, v_ref, weight_ref, code_ref, work_ref, vector_ref, *refs):
+    ends = left is not None
+
+    def kernel(q_ref, k_ref, v_ref, code_ref, *refs):
         if ends:
-            carried_ref, attended_ref, stat_ref, resid_ref, low_ref, total, cap = refs
+            (
+                weight_ref, work_ref, vector_ref, left_ref, flipped_ref, stat_ref, resid_ref, low_ref,
+                cap, right, total,
+            ) = refs
         else:
-            attended_ref, stat_ref, total, cap = refs
+            flipped_ref, stat_ref, attended_ref, cap = refs
         pair = pl.program_id(0)
 
         @pl.when(pair == 0)
         def _():
             fill_cap(code_ref, cap)
-            total[...] = carried_ref[...] if ends else jnp.zeros_like(total)
 
         keys = k_ref[...]
         values = v_ref[...].astype(jnp.float32).T.astype(jnp.bfloat16)
@@ -682,13 +684,26 @@
                 parts.append(mixed * (1.0 / sums))
             heads.append(jnp.concatenate(parts, 1))
         both = jnp.concatenate(heads, 0)
-        attended_ref[...] = both.astype(jnp.bfloat16)
-        total[...] += product(both.T.astype(jnp.bfloat16), weight_ref[...])
+        flipped_ref[...] = both.astype(jnp.bfloat16)
+        attended = both.T.astype(jnp.bfloat16)
+        if ends:
+            right[pair] = attended
+        else:
+            attended_ref[...] = attended
 
         if ends:
 
             @pl.when(pair == pairs - 1)
             def _():
+                middle = feature - pairs * 128
+                for start in range(0, feature, 256):
+                    span = slice(start, start + 256)
+                    value = product(left_ref[...], weight_ref[:middle, span])
+                    for index in range(pairs):
+                        rows = slice(middle + index * 128, middle + (index + 1) * 128)
+                        value = value + product(right[index], weight_ref[rows, span])
+                    total[:, span] = value
+
                 def rows_of(index, carry):
                     rows = pl.ds(pl.multiple_of(index * 64, 64), 64)
                     resid = (
@@ -717,32 +732,40 @@
         + (
             [shaped((count, feature), jnp.float32), shaped((count, feature), jnp.bfloat16)]
             if ends
-            else [shaped((count, feature), jnp.float32)]
+            else [shaped((count, pairs * 128), jnp.bfloat16)]
         ),
         in_specs=[
             columns_at(first),
             columns_at(all_pairs + first),
             columns_at(2 * all_pairs + first),
-            pl.BlockSpec((128, feature), lambda pair: (first + pair, 0)),
             pl.BlockSpec((count, 128), lambda pair: (0, all_pairs)),
-            wide,
-            whole(*vector.shape),
         ]
-        + ([wide] if ends else []),
+        + (
+            [whole(feature, feature), wide, whole(*vector.shape), whole(*left.shape)]
+            if ends
+            else []
+        ),
         out_specs=[
             pl.BlockSpec((128, count), lambda pair: (pair, 0)),
             pl.BlockSpec((1, 8, count), lambda pair: (pair, 0, 0)),
         ]
-        + ([wide, wide] if ends else [wide]),
-        scratch_shapes=([pltpu.VMEM((count, feature), jnp.float32)] if ends else [])
-        + [pltpu.VMEM((count, count), jnp.float32)],
-        compiler_params=settings(LIMIT),
+        + ([wide, wide] if ends else [columns_at(0)]),
+        scratch_shapes=[pltpu.VMEM((count, count), jnp.float32)]
+        + (
+            [
+                pltpu.VMEM((pairs, count, 128), jnp.bfloat16),
+                pltpu.VMEM((count, feature), jnp.float32),
+            ]
+            if ends
+            else []
+        ),
+        compiler_params=settings(60),
         cost_estimate=cost(
             8 * count * count * pairs * 128, 14 * count * feature, 2 * pairs * count * count
         ),
     )(
-        projected, projected, projected, weights, work, work, vector,
-        *([carried] if ends else []),
+        projected, projected, projected, work,
+        *([weights, work, vector, left] if ends else []),
     )
 
 
@@ -994,20 +1017,15 @@
     )(where, slope, low, grads, resid, vector, up_weights, down_weights, *attended)
 
 
-def attend_back(projected, work, stats, dlow, weights, first, pairs, gradient=None):
+def attend_back(projected, work, stats, dlow, weights, first, pairs):
     count, feature = dlow.shape
     all_pairs = feature // 128
     tile = 512
     wide = pairs * 128
 
-    def kernel(q_ref, k_ref, v_ref, code_ref, stat_ref, dlow_ref, weight_ref, *refs):
-        if gradient is None:
-            out_ref, sums_ref, douts, cap = refs
-        else:
-            (
-                where_ref, flipped_ref, left_ref, out_ref, sums_ref, mine_ref, theirs_ref,
-                douts, cap, right, result,
-            ) = refs
+    def kernel(
+        q_ref, k_ref, v_ref, code_ref, stat_ref, dlow_ref, weight_ref, out_ref, sums_ref, douts, cap
+    ):
         pair = pl.program_id(0)
 
         @pl.when(pair == 0)
@@ -1019,108 +1037,91 @@
                     jnp.bfloat16
                 )
 
-        @pl.when(pair < pairs)
-        def _():
-            keys, values = k_ref[...], v_ref[...]
-            wide_keys = keys.astype(jnp.float32)
-            dquery = jnp.zeros((count, 128), jnp.float32)
-            scaled = q_ref[...].astype(jnp.float32) * 0.125
-            dout = douts[pair].astype(jnp.float32)
-            dkey = jnp.zeros((count, 128), jnp.float32)
-            dvalue = jnp.zeros((count, 128), jnp.float32)
-            for head in range(2):
-                query = one_head(scaled, head)
-                dhead = one_head(dout, head)
-                for start in range(0, count, tile):
-                    span = slice(start, start + tile)
-                    scores = jnp.minimum(by_rows(keys, query[span]), cap[:, span])
-                    probs = jnp.exp(scores - stat_ref[0, head : head + 1, span])
-                    dprob = by_rows(values, dhead[span])
-                    inner = jnp.sum(probs * dprob, 0, keepdims=True)
-                    dscore = (probs * (dprob - inner)).astype(jnp.bfloat16)
-                    dvalue = dvalue + product(probs.astype(jnp.bfloat16), dhead[span])
-                    dkey = dkey + product(dscore, query[span])
-                    dquery = dquery + by_columns(dscore, one_head(wide_keys, head))
-            dquery = (dquery * 0.125).astype(jnp.bfloat16)
-            dvalue = dvalue.astype(jnp.bfloat16)
-            out_ref[0] = dquery
-            out_ref[1] = dkey.astype(jnp.bfloat16)
-            out_ref[2] = dvalue
-            sums_ref[0:1, :] = jnp.sum(dquery.astype(jnp.float32), 0, keepdims=True)
-            sums_ref[1:2, :] = jnp.sum(dvalue.astype(jnp.float32), 0, keepdims=True)
-            if gradient is not None:
-                right[0, pair] = dquery
-                right[1, pair] = dkey.astype(jnp.bfloat16)
-                right[2, pair] = dvalue
-
-        if gradient is not None:
-
-            @pl.when(pair >= pairs)
-            def _():
-                flipped = flipped_ref[...]
-                result[:, :wide] = product(flipped, left_ref[0])
-                for index in range(pairs):
-                    span = slice(wide + index * 128, wide + (index + 1) * 128)
-                    result[:, span] = product(flipped, right[pair - pairs, index])
-                put_wide(where_ref, result, mine_ref, theirs_ref)
-
-    def at(pair):
-        return jnp.minimum(pair, pairs - 1)
-
-    def part_at(pair):
-        return jnp.maximum(pair - pairs, 0)
+        keys, values = k_ref[...], v_ref[...]
+        wide_keys = keys.astype(jnp.float32)
+        dquery = jnp.zeros((count, 128), jnp.float32)
+        scaled = q_ref[...].astype(jnp.float32) * 0.125
+        dout = douts[pair].astype(jnp.float32)
+        dkey = jnp.zeros((count, 128), jnp.float32)
+        dvalue = jnp.zeros((count, 128), jnp.float32)
+        for head in range(2):
+            query = one_head(scaled, head)
+            dhead = one_head(dout, head)
+            for start in range(0, count, tile):
+                span = slice(start, start + tile)
+                scores = jnp.minimum(by_rows(keys, query[span]), cap[:, span])
+                probs = jnp.exp(scores - stat_ref[0, head : head + 1, span])
+                dprob = by_rows(values, dhead[span])
+                inner = jnp.sum(probs * dprob, 0, keepdims=True)
+                dscore = (probs * (dprob - inner)).astype(jnp.bfloat16)
+                dvalue = dvalue + product(probs.astype(jnp.bfloat16), dhead[span])
+                dkey = dkey + product(dscore, query[span])
+                dquery = dquery + by_columns(dscore, one_head(wide_keys, head))
+        dquery = (dquery * 0.125).astype(jnp.bfloat16)
+        dvalue = dvalue.astype(jnp.bfloat16)
+        out_ref[0] = dquery
+        out_ref[1] = dkey.astype(jnp.bfloat16)
+        out_ref[2] = dvalue
+        sums_ref[0:1, :] = jnp.sum(dquery.astype(jnp.float32), 0, keepdims=True)
+        sums_ref[1:2, :] = jnp.sum(dvalue.astype(jnp.float32), 0, keepdims=True)
 
     def columns_at(offset):
-        return pl.BlockSpec((count, 128), lambda pair: (0, offset + at(pair)))
-
-    out_shape = [shaped((3, count, wide), jnp.bfloat16), shaped((8, wide), jnp.float32)]
-    in_specs = [
-        columns_at(first),
-        columns_at(all_pairs + first),
-        columns_at(2 * all_pairs + first),
-        pl.BlockSpec((count, 128), lambda pair: (0, all_pairs)),
-        pl.BlockSpec((1, 8, count), lambda pair: (at(pair), 0, 0)),
-        whole(count, feature),
-        pl.BlockSpec((wide, feature), lambda pair: (first // pairs, 0)),
-    ]
-    out_specs = [
-        pl.BlockSpec((3, count, 128), lambda pair: (0, 0, at(pair))),
-        pl.BlockSpec((8, 128), lambda pair: (0, at(pair))),
-    ]
-    scratch = [
-        pltpu.VMEM((pairs, count, 128), jnp.bfloat16),
-        pltpu.VMEM((count, count), jnp.float32),
-    ]
-    extra = ()
-    if gradient is not None:
-        where, flipped, left, depth = gradient
-        rows = feature // (PLANE * depth)
-        extra = (where, flipped, left)
-        out_shape += [shaped((4, depth, rows, 3 * feature), jnp.bfloat16)] * 2
-        in_specs += [
-            SCALARS,
-            whole(feature, count),
-            pl.BlockSpec((1, count, wide), lambda pair: (part_at(pair), 0, 0)),
-        ]
-        out_specs += [
-            pl.BlockSpec((4, depth, rows, feature), lambda pair: (0, 0, 0, part_at(pair)))
-        ] * 2
-        scratch += [
-            pltpu.VMEM((3, pairs, count, 128), jnp.bfloat16),
-            pltpu.VMEM((feature, feature), jnp.float32),
-        ]
+        return pl.BlockSpec((count, 128), lambda pair: (0, offset + pair))
+
     return pl.pallas_call(
         kernel,
-        grid=(pairs if gradient is None else pairs + 3,),
-        out_shape=out_shape,
-        in_specs=in_specs,
-        out_specs=out_specs,
-        scratch_shapes=scratch,
+        grid=(pairs,),
+        out_shape=[
+            shaped((3, count, wide), jnp.bfloat16),
+            shaped((8, wide), jnp.float32),
+        ],
+        in_specs=[
+            columns_at(first),
+            columns_at(all_pairs + first),
+            columns_at(2 * all_pairs + first),
+            pl.BlockSpec((count, 128), lambda pair: (0, all_pairs)),
+            pl.BlockSpec((1, 8, count), lambda pair: (pair, 0, 0)),
+            whole(count, feature),
+            pl.BlockSpec((wide, feature), lambda pair: (first // pairs, 0)),
+        ],
+        out_specs=[
+            pl.BlockSpec((3, count, 128), lambda pair: (0, 0, pair)),
+            pl.BlockSpec((8, 128), lambda pair: (0, pair)),
+        ],
+        scratch_shapes=[
+            pltpu.VMEM((pairs, count, 128), jnp.bfloat16),
+            pltpu.VMEM((count, count), jnp.float32),
+        ],
         compiler_params=settings(LIMIT),
         cost_estimate=cost(
             14 * count * count * wide, 16 * count * feature, 2 * pairs * count * count
         ),
-    )(projected, projected, projected, work, stats, dlow, weights, *extra)
+    )(projected, projected, projected, work, stats, dlow, weights)
+
+
+def first_gradient(where, flipped, dprojected, depth):
+    feature, count = flipped.shape
+    half = feature // 2
+    rows = feature // (PLANE * depth)
+
+    def kernel(where_ref, flipped_ref, d_ref, e_ref, mine_ref, theirs_ref, result):
+        result[:, :half] = product(flipped_ref[...], d_ref[0])
+        result[:, half:] = product(flipped_ref[...], e_ref[0])
+        put_wide(where_ref, result, mine_ref, theirs_ref)
+
+    shape = shaped((4, depth, rows, 3 * feature), jnp.bfloat16)
+    block = pl.BlockSpec((4, depth, rows, feature), lambda step: (0, 0, 0, step))
+    part = pl.BlockSpec((1, count, half), lambda step: (step, 0, 0))
+    return pl.pallas_call(
+        kernel,
+        grid=(3,),
+        out_shape=[shape, shape],
+        in_specs=[SCALARS, whole(feature, count), part, part],
+        out_specs=[block, block],
+        scratch_shapes=[pltpu.VMEM((feature, feature), jnp.float32)],
+        compiler_params=settings(60),
+        cost_estimate=cost(6 * count * feature * feature, 16 * feature * feature),
+    )(where, flipped, *dprojected)
 
 
 def project_back(work, dprojected, dresid, vector, weights, sums_two, sums_attend, bias_up, devices):
@@ -1439,34 +1440,33 @@
     up_to, dlow = pin(up_fold.diagonal(), dlow)
 
     up_got = over_diagonal(*up_to)
-    dright, sums_right, first_mine, first_theirs = attend_back(
-        projected, work, stats_b, dlow, out_weights, pairs, pairs,
-        (where, flipped_one, dleft, depth),
-    )
-    up_got, dright, first_mine, first_theirs, down_got = pin(
-        up_got, dright, first_mine, first_theirs, down_got
-    )
-    up_to, dright, first_theirs = pin(up_fold.neighbours(*up_got), dright, first_theirs)
-
-    first_got = send(first_theirs, 1)
-    first_got, dright, up_to = pin(first_got, dright, up_to)
-    first_fold = Fold(first_mine, first_got)
-    first_to, dright, up_to = pin(first_fold.diagonal(), dright, up_to)
-
-    got = over_diagonal(*first_to)
+    dright, sums_right = attend_back(projected, work, stats_b, dlow, out_weights, pairs, pairs)
+    up_got, dright, down_got = pin(up_got, dright, down_got)
+    up_to, dright = pin(up_fold.neighbours(*up_got), dright)
+
     up_got = over_plane(*up_to)
     both = project_back(
         work, (dleft, dright), dresid, vector_weight, first_weights,
         sums_two, (sums_left, sums_right), bias_up_grad, devices,
     )
-    both, got = pin(both, got)
+    both, dright = pin(both, dright)
+
+    back = exchange(both.reshape(devices, capacity, -1))
+    first_mine, first_theirs = first_gradient(where, flipped_one, (dleft, dright), depth)
+    first_mine, first_theirs, up_got = pin(first_mine, first_theirs, up_got)
+
+    first_got = send(first_theirs, 1)
+    up_sums = up_fold.column(*up_got)
+    first_got, up_sums = pin(first_got, up_sums)
+    first_fold = Fold(first_mine, first_got)
+    first_to, up_sums = pin(first_fold.diagonal(), up_sums)
+
+    up_got = over_column(up_sums)
+    got, back = pin(over_diagonal(*first_to), back)
     first_to = pin(*first_fold.neighbours(*got))
 
-    back = exchange(both.reshape(devices, capacity, -1))
     got = over_plane(*first_to)
-    up_sums = pin(*up_fold.column(*up_got))
-    up_got = over_column(up_sums)
-    got, up_first, back = pin(got, up_got[0], back)
+    got, up_first = pin(got, up_got[0])
     down_grad = total_of(down_sums[0], *down_got)
     first_sums, back_out = pin(first_fold.column(*got), back_out)
 

time: 330 us -> 323 us (0.979)
  local copies, waits for them, and re-layouts: 20.2 us -> 11.3 us
    ppermute x52, waiting for transfers between devices: 58.1 us -> 43.3 us  [send(): return lax.ppermute(value, 'dev', flips(lax.axis_size('dev'), mask))]
    ppermute x9, waiting for transfers between devices: 0.07 us -> 9.72 us  [over_column(): lax.ppermute(sums[k], 'dev', shifts(devices, k))]
    unnamed x150 -> x134, local copies, waits for them, and re-layouts: 15.4 us -> 8.07 us
    all_to_all x5, waiting for transfers between devices: 10.3 us -> 14.7 us  [exchange(): return lax.all_to_all(rows, 'dev', split_axis=0, concat_axis=0, tiled=True)]
    ppermute x9, waiting for transfers between devices: 12.3 us -> 16 us  [along_z(): lax.ppermute(block, 'dev', shifts(devices, k))]
    ppermute x9, starting transfers between devices: 16.5 us -> 13.2 us  [over_column(): lax.ppermute(sums[k], 'dev', shifts(devices, k))]
    pallas_call x2 -> x3, Pallas kernels: 21.5 us -> 22.2 us  [the longest x2 16 us: attend_back(): pl.pallas_call(kernel, grid=(pairs,), out_shape=[shaped((3, count, wide),...]
  transfers between devices with their start and end apart: 76 -> 76, of which waited for: 28 -> 29; matrix products, arithmetic and copies ran while one was open for 5% -> 4% of each run, Pallas kernels for 32% -> 33%
where the time goes in v4:
time: 323 us; the launch traced here: 322 us
  Pallas kernels  114 us (35%)
  starting transfers between devices  90.9 us (28%)
  waiting for transfers between devices  84.8 us (26%)
  other arithmetic  17.5 us (5%)
  local copies, waits for them, and re-layouts  11.3 us (3%)
  between operations  3.25 us (1%)
    ppermute x52, waiting for transfers between devices, send(): return lax.ppermute(value, 'dev', flips(lax.axis_size('dev'), mask))  43.3 us
    ppermute x52, starting transfers between devices, send(): return lax.ppermute(value, 'dev', flips(lax.axis_size('dev'), mask))  38.2 us
    all_to_all x5, starting transfers between devices, exchange(): return lax.all_to_all(rows, 'dev', split_axis=0, concat_axis=0, tiled=True)  23.9 us
    pallas_call x1, Pallas kernels, feed_back(): pl.pallas_call(kernel, grid=(steps + 1,), out_shape=[shaped((count, featu...  18.9 us
    pallas_call x2, Pallas kernels, attend(): pl.pallas_call(kernel, grid=(pairs,), out_shape=[shaped((pairs * 128, cou...  16.2 us
    pallas_call x2, Pallas kernels, attend_back(): pl.pallas_call(kernel, grid=(pairs,), out_shape=[shaped((3, count, wide),...  16 us
    ppermute x9, waiting for transfers between devices, along_z(): lax.ppermute(block, 'dev', shifts(devices, k))  16 us
    ppermute x9, starting transfers between devices, along_z(): lax.ppermute(block, 'dev', shifts(devices, k))  15.1 us
  transfers between devices with their start and end apart: 76, of which 29 were waited for; matrix products, arithmetic and copies ran while one was open for 4% of the time, Pallas kernels for 33%

profile of v4, /device:TPU:0, one launch (start us, length us, event | category | flops | bytes accessed | tf_op | source)
XLA Modules:
  0.0 321.9 jit_solution(12862844737477039273)
XLA Ops:
  4.2 5.0 %collective-permute-start.3 = (bf16[48,1536]{1,0:T(8,128)(2,1)S(1)}, bf16[48,1536]{1,0:T(8,128)(2,1)S(1)}, u32[]{:S(2)}, u32[]{:S(2)}) collective-permute-start(bf16[48,1536]{1,0:T(8,128)(2,1)S(1)} %get-tuple-element.450), channel_id=1, source_target_pairs={{0,24},{1,25},{2,26},{3,27},{4,28},{5,29},{6,30},{7,31},{8,0},{9,1... | collective-permute-start | bytes 442376 | tf_op jit(solution)/shard_map/ppermute | solution.py:345
  9.3 2.8 shard_map.211
  13.5 8.6 %collective-permute-done.2 = bf16[48,1536]{1,0:T(8,128)(2,1)S(1)} collective-permute-done((bf16[48,1536]{1,0:T(8,128)(2,1)S(1)}, bf16[48,1536]{1,0:T(8,128)(2,1)S(1)}, u32[]{:S(2)}, u32[]{:S(2)}) %collective-permute-start.2) | collective-permute-done | bytes 147488 | tf_op jit(solution)/shard_map/ppermute | solution.py:345
  22.2 4.9 %all-to-all-start = ((bf16[32,16,896]{2,1,0:T(8,128)(2,1)}), bf16[32,16,896]{2,1,0:T(8,128)(2,1)S(1)}, u32[]{:S(2)}, u32[]{:S(2)}) async-start(bf16[32,16,896]{2,1,0:T(8,128)(2,1)} %bitcast.12), calls=%async_computation | async-start | bytes 1835008 | tf_op jit(solution)/shard_map/all_to_all | solution.py:412
  27.1 1.8 collective-permute-start.6
  28.9 1.5 collective-permute-start.4
  31.2 13.8 %collective-permute-done.6.refs_4_ = bf16[2,48,1536]{2,1,0:T(8,128)(2,1)S(1)} collective-permute-done((bf16[2,48,1536]{2,1,0:T(8,128)(2,1)S(1)}, bf16[2,48,1536]{2,1,0:T(8,128)(2,1)S(1)}, u32[]{:S(2)}, u32[]{:S(2)}) %collective-permute-start.6) | collective-permute-done | bytes 294944 | tf_op jit(solution)/shard_map/ppermute | solution.py:339
  45.3 7.1 %collective-permute-done.7.refs_5_ = bf16[2,48,1536]{2,1,0:T(8,128)(2,1)S(1)} collective-permute-done((bf16[2,48,1536]{2,1,0:T(8,128)(2,1)S(1)}, bf16[2,48,1536]{2,1,0:T(8,128)(2,1)S(1)}, u32[]{:S(2)}, u32[]{:S(2)}) %collective-permute-start.7) | collective-permute-done | bytes 294944 | tf_op jit(solution)/shard_map/ppermute | solution.py:339
  56.0 6.1 %collective-permute-done.8.refs_6_ = bf16[2,48,1536]{2,1,0:T(8,128)(2,1)} collective-permute-done((bf16[2,48,1536]{2,1,0:T(8,128)(2,1)S(1)}, bf16[2,48,1536]{2,1,0:T(8,128)(2,1)}, u32[]{:S(2)}, u32[]{:S(2)}) %collective-permute-start.8) | collective-permute-done | bytes 294944 | tf_op jit(solution)/shard_map/ppermute | solution.py:339
  62.1 1.9 collective-permute-done.9.refs_7_
  66.4 3.3 %collective-permute-start.20 = (bf16[48,1536]{1,0:T(8,128)(2,1)S(1)}, bf16[48,1536]{1,0:T(8,128)(2,1)S(1)}, u32[]{:S(2)}, u32[]{:S(2)}) collective-permute-start(bf16[48,1536]{1,0:T(8,128)(2,1)S(1)} %get-tuple-element.238), channel_id=1, source_target_pairs={{0,24},{1,25},{2,26},{3,27},{4,28},{5,29},{6,30},{7,31},{8,0},{9,1... | collective-permute-start | bytes 442376 | tf_op jit(solution)/shard_map/ppermute | solution.py:345
  70.9 9.2 %shard_map.212 = (bf16[768,512]{1,0:T(8,128)(2,1)}, bf16[512,2304]{1,0:T(8,128)(2,1)}, bf16[768,2304]{1,0:T(8,128)(2,1)}, bf16[768,768]{1,0:T(8,128)(2,1)}) custom-call(s32[4]{0:T(128)} %pad_add_fusion.where_ref, bf16[512,896]{1,0:T(8,128)(2,1)} %bitcast.128, f32[12,768]{1,0:T(8,128)} %refs_6_.1, bf16[2,48,1536]{2,1,0:T(8,128)(2,1)} %copy-done.38, ...), custom_call_target="tpu_custom_call" | custom-call | flops 1811939328 | bytes 7077888 | tf_op jit(solution)/shard_map/pallas_call | solution.py:614
  80.0 2.7 collective-permute-done.19
  83.5 1.5 collective-permute-start.21
  86.1 1.5 collective-permute-start.24
  87.6 2.0 collective-permute-start.23
  89.7 5.9 %shard_map.213 = (bf16[384,512]{1,0:T(8,128)(2,1)}, f32[3,8,512]{2,1,0:T(8,128)}, bf16[512,384]{1,0:T(8,128)(2,1)}) custom-call(bf16[512,2304]{1,0:T(8,128)(2,1)} %get-tuple-element.240.q_ref.k_ref.v_ref, bf16[512,2304]{1,0:T(8,128)(2,1)} %get-tuple-element.240.q_ref.k_ref.v_ref, bf16[512,2304]{1,0:T(8,128)(2,1)} %get-tuple-element.240.q_ref.k_ref.v_ref, ...), custom_call_target="tpu_custom_call" | custom-call | flops 805306368 | bytes 5505024 | tf_op jit(solution)/shard_map/pallas_call | solution.py:725
  95.6 4.3 %collective-permute-done.24 = bf16[96,768]{1,0:T(8,128)(2,1)S(1)} collective-permute-done((bf16[96,768]{1,0:T(8,128)(2,1)S(1)}, bf16[96,768]{1,0:T(8,128)(2,1)S(1)}, u32[]{:S(2)}, u32[]{:S(2)}) %collective-permute-start.24) | collective-permute-done | bytes 147488 | tf_op jit(solution)/shard_map/ppermute | solution.py:345
  100.6 2.8 all-to-all-start.1
  104.5 1.5 collective-permute-start.27
  106.0 1.5 collective-permute-start.26
  107.5 10.3 %shard_map.214 = (bf16[384,512]{1,0:T(8,128)(2,1)}, f32[3,8,512]{2,1,0:T(8,128)}, f32[512,768]{1,0:T(8,128)}, bf16[512,768]{1,0:T(8,128)(2,1)}) custom-call(bf16[512,2304]{1,0:T(8,128)(2,1)} %get-tuple-element.240.q_ref.k_ref.v_ref, bf16[512,2304]{1,0:T(8,128)(2,1)} %get-tuple-element.240.q_ref.k_ref.v_ref, ...), custom_call_target="tpu_custom_call" | custom-call | flops 805306368 | bytes 5505024 | tf_op jit(solution)/shard_map/pallas_call | solution.py:725
  117.8 1.9 collective-permute-done.27.refs_4_
  123.8 1.5 collective-permute-start.36
  126.5 11.0 %shard_map.215 = (bf16[512,3072]{1,0:T(8,128)(2,1)}, f32[512,3072]{1,0:T(8,128)}, bf16[768,3072]{1,0:T(8,128)(2,1)}) custom-call(s32[4]{0:T(128)} %pad_add_fusion.where_ref, bf16[512,768]{1,0:T(8,128)(2,1)} %get-tuple-element.258.low_ref, f32[1,3072]{1,0:T(1,128)} %bitcast.152, bf16[4,48,1536]{2,1,0:T(8,128)(2,1)} %copy-done.36, ...), custom_call_target="tpu_custom_call" | custom-call | flops 2415919104 | bytes 14155776 | tf_op jit(solution)/shard_map/pallas_call | solution.py:803
  146.3 6.0 %shard_map.216 = (bf16[4,4,96,768]{3,2,1,0:T(8,128)(2,1)S(1)}, bf16[4,4,96,768]{3,2,1,0:T(8,128)(2,1)S(1)}) custom-call(s32[4]{0:T(128)S(1)} %copy-done.26, bf16[512,3072]{1,0:T(8,128)(2,1)} %get-tuple-element.271.hidden_ref, bf16[512,768]{1,0:T(8,128)(2,1)S(1)} %bitcast.138), custom_call_target="tpu_custom_call" | custom-call | flops 2415919104 | bytes 7864320 | tf_op jit(solution)/shard_map/pallas_call | solution.py:849
  153.2 4.2 %collective-permute-done.45.refs_14_ = bf16[2,96,768]{2,1,0:T(8,128)(2,1)S(1)} collective-permute-done((bf16[2,96,768]{2,1,0:T(8,128)(2,1)}, bf16[2,96,768]{2,1,0:T(8,128)(2,1)S(1)}, u32[]{:S(2)}, u32[]{:S(2)}) %collective-permute-start.45) | collective-permute-done | bytes 294944 | tf_op jit(solution)/shard_map/ppermute | solution.py:339
  160.6 9.6 %shard_map.217 = (bf16[512,768]{1,0:T(8,128)(2,1)S(1)}, bf16[3072,768]{1,0:T(8,128)(2,1)}) custom-call(s32[4]{0:T(128)S(1)} %copy-done.26, bf16[512,3072]{1,0:T(8,128)(2,1)} %get-tuple-element.271.hidden_ref, f32[512,768]{1,0:T(8,128)} %get-tuple-element.287.resid_ref, f32[12,768]{1,0:T(8,128)S(1)} %copy-done.9, ...), custom_call_target="tpu_custom_call" | custom-call | flops 2415919104 | bytes 14155776 | tf_op jit(solution)/shard_map/pallas_call | solution.py:908
  171.6 5.7 %all-to-all-start.2 = ((bf16[32,16,768]{2,1,0:T(8,128)(2,1)}), bf16[32,16,768]{2,1,0:T(8,128)(2,1)S(1)}, u32[]{:S(2)}, u32[]{:S(2)}) async-start(bf16[32,16,768]{2,1,0:T(8,128)(2,1)} %bitcast.139), calls=%async_computation.2 | async-start | bytes 1572864 | tf_op jit(solution)/shard_map/all_to_all | solution.py:412
  177.3 1.6 collective-permute-start.50
  178.9 1.5 collective-permute-start.51
  180.4 18.9 %shard_map.218 = (f32[512,768]{1,0:T(8,128)}, bf16[512,768]{1,0:T(8,128)(2,1)}, f32[8,768]{1,0:T(8,128)}, f32[1,3072]{1,0:T(1,128)}, bf16[4,4,24,3840]{3,2,1,0:T(8,128)(2,1)}, /*index=5*/bf16[4,4,24,3840]{3,2,1,0:T(8,128)(2,1)}) custom-call(s32[4]{0:T(128)} %pad_add_fusion.where_ref, f32[512,3072]{1,0:T(8,128)} %get-tuple-element.286.slope_ref, ...), custom_call_target="tpu_custom_call" | custom-call | flops 7247757312 | bytes 34603008 | tf_op jit(solution)/shard_map/pallas_call | solution.py:986
  199.3 1.8 collective-permute-done.50
  201.2 1.9 fusion.29
  204.3 8.1 %shard_map.219 = (bf16[3,512,384]{2,1,0:T(8,128)(2,1)S(1)}, f32[8,384]{1,0:T(8,128)S(1)}) custom-call(bf16[512,2304]{1,0:T(8,128)(2,1)} %get-tuple-element.240.q_ref.k_ref.v_ref, bf16[512,2304]{1,0:T(8,128)(2,1)} %get-tuple-element.240.q_ref.k_ref.v_ref, bf16[512,2304]{1,0:T(8,128)(2,1)} %get-tuple-element.240.q_ref.k_ref.v_ref, ...), custom_call_target="tpu_custom_call" | custom-call | flops 1409286144 | bytes 6291456 | tf_op jit(solution)/shard_map/pallas_call | solution.py:1071
  212.8 1.4 collective-permute-start.53
  214.8 1.5 collective-permute-start.55
  216.3 2.4 collective-permute-start.56
  218.6 1.5 collective-permute-start.57
  220.1 7.9 %shard_map.220 = (bf16[3,512,384]{2,1,0:T(8,128)(2,1)S(1)}, f32[8,384]{1,0:T(8,128)S(1)}) custom-call(bf16[512,2304]{1,0:T(8,128)(2,1)} %get-tuple-element.240.q_ref.k_ref.v_ref, bf16[512,2304]{1,0:T(8,128)(2,1)} %get-tuple-element.240.q_ref.k_ref.v_ref, bf16[512,2304]{1,0:T(8,128)(2,1)} %get-tuple-element.240.q_ref.k_ref.v_ref, ...), custom_call_target="tpu_custom_call" | custom-call | flops 1409286144 | bytes 6291456 | tf_op jit(solution)/shard_map/pallas_call | solution.py:1071
  230.4 1.5 collective-permute-start.58
  232.5 8.5 %shard_map.221 = bf16[512,896]{1,0:T(8,128)(2,1)} custom-call(bf16[512,896]{1,0:T(8,128)(2,1)S(1)} %bitcast.134, bf16[3,512,384]{2,1,0:T(8,128)(2,1)S(1)} %get-tuple-element.329.d_ref, bf16[3,512,384]{2,1,0:T(8,128)(2,1)S(1)} %get-tuple-element.351.e_ref, f32[512,768]{1,0:T(8,128)S(1)} %copy-done.6, f32[12,768]{1,0:T(8,128)S(1)} %copy-done.10, ...), custom_call_target="tpu_custom_call" | custom-call | flops 1811939328 | bytes 3538944 | tf_op jit(solution)/shard_map/pallas_call | solution.py:1176
  241.0 6.1 %all-to-all-start.3 = ((bf16[32,16,896]{2,1,0:T(8,128)(2,1)}), bf16[32,16,896]{2,1,0:T(8,128)(2,1)S(1)}, u32[]{:S(2)}, u32[]{:S(2)}) async-start(bf16[32,16,896]{2,1,0:T(8,128)(2,1)} %bitcast.53), calls=%async_computation.3 | async-start | bytes 1835008 | tf_op jit(solution)/shard_map/all_to_all | solution.py:412
  247.1 6.2 %shard_map.222 = (bf16[4,4,24,2304]{3,2,1,0:T(8,128)(2,1)}, bf16[4,4,24,2304]{3,2,1,0:T(8,128)(2,1)}) custom-call(s32[4]{0:T(128)} %pad_add_fusion.where_ref, bf16[768,512]{1,0:T(8,128)(2,1)} %get-tuple-element.236.flipped_ref, bf16[3,512,384]{2,1,0:T(8,128)(2,1)} %copy-done.7, bf16[3,512,384]{2,1,0:T(8,128)(2,1)} %copy-done.8), custom_call_target="tpu_custom_call" | custom-call | flops 1811939328 | bytes 9437184 | tf_op jit(solution)/shard_map/pallas_call | solution.py:1115
  253.3 1.9 fusion.27
  258.5 1.5 collective-permute-start.61
  260.0 1.5 collective-permute-start.62
  261.5 8.8 %all-to-all-done.3.refs_3_ = bf16[32,16,896]{2,1,0:T(8,128)(2,1)S(1)} async-done(((bf16[32,16,896]{2,1,0:T(8,128)(2,1)}), bf16[32,16,896]{2,1,0:T(8,128)(2,1)S(1)}, u32[]{:S(2)}, u32[]{:S(2)}) %all-to-all-start.3) | async-done | bytes 917536 | tf_op jit(solution)/shard_map/all_to_all | solution.py:412
  270.3 1.8 fusion.7
  272.3 1.5 collective-permute-start.63
  273.8 1.5 collective-permute-start.64
  275.3 1.6 collective-permute-start.65
  278.7 2.0 collective-permute-start.70
  280.7 4.1 %collective-permute-done.65 = bf16[24,3840]{1,0:T(8,128)(2,1)S(1)} collective-permute-done((bf16[24,3840]{1,0:T(8,128)(2,1)S(1)}, bf16[24,3840]{1,0:T(8,128)(2,1)S(1)}, u32[]{:S(2)}, u32[]{:S(2)}) %collective-permute-start.65) | collective-permute-done | bytes 184352 | tf_op jit(solution)/shard_map/ppermute | solution.py:408
  287.7 1.6 collective-permute-start.66
  289.5 2.1 collective-permute-start.68
  291.6 1.5 multiply_reduce_fusion
  294.5 1.5 shard_map.223
  296.0 5.6 %collective-permute-done.67.refs_1_ = bf16[24,2304]{1,0:T(8,128)(2,1)S(1)} collective-permute-done((bf16[24,2304]{1,0:T(8,128)(2,1)S(1)}, bf16[24,2304]{1,0:T(8,128)(2,1)S(1)}, u32[]{:S(2)}, u32[]{:S(2)}) %collective-permute-start.67) | collective-permute-done | bytes 110624 | tf_op jit(solution)/shard_map/ppermute | solution.py:408
  302.3 2.0 shard_map.225
  304.3 4.4 %all-to-all-start.4 = ((f32[32,4,128]{2,1,0:T(4,128)}), f32[32,4,128]{2,1,0:T(4,128)S(1)}, u32[]{:S(2)}, u32[]{:S(2)}) async-start(f32[32,4,128]{2,1,0:T(4,128)} %get-tuple-element.396), calls=%async_computation.4 | async-start | bytes 131072 | tf_op jit(solution)/shard_map/all_to_all | solution.py:412
  308.7 1.5 shard_map.224
  310.2 5.9 %all-to-all-done.4.packets_ref = f32[32,4,128]{2,1,0:T(4,128)S(1)} async-done(((f32[32,4,128]{2,1,0:T(4,128)}), f32[32,4,128]{2,1,0:T(4,128)S(1)}, u32[]{:S(2)}, u32[]{:S(2)}) %all-to-all-start.4) | async-done | bytes 65568 | tf_op jit(solution)/shard_map/all_to_all | solution.py:412
  316.8 4.9 %shard_map.226 = (f32[1,1]{1,0:T(1,128)}, f32[24,6144]{1,0:T(8,128)}, f32[24,6144]{1,0:T(8,128)}, f32[24,6144]{1,0:T(8,128)}, f32[96,768]{1,0:T(8,128)}, /*index...) custom-call(f32[32,4,128]{2,1,0:T(4,128)} %copy-done.39, ...), custom_call_target="tpu_custom_call" | custom-call | flops 2949120 | bytes 5898240 | tf_op jit(solution)/shard_map/pallas_call | solution.py:1295
  (276 shorter events, 51.1 us)
Async XLA Ops:
  4.2 9.3 %collective-permute-start.3 = (bf16[48,1536]{1,0:T(8,128)(2,1)S(1)}, bf16[48,1536]{1,0:T(8,128)(2,1)S(1)}, u32[]{:S(2)}, u32[]{:S(2)}) collective-permute-start(bf16[48,1536]{1,0:T(8,128)(2,1)S(1)} %get-tuple-element.450), channel_id=1, source_target_pairs={{0,24},{1,25},{2,26},{3,27},{4,28},{5,29},{6,30},{7,31},{8,0},{9,1... | collective-permute-start | bytes 442376 | tf_op jit(solution)/shard_map/ppermute | solution.py:345
  9.2 12.8 %collective-permute-start.2 = (bf16[48,1536]{1,0:T(8,128)(2,1)S(1)}, bf16[48,1536]{1,0:T(8,128)(2,1)S(1)}, u32[]{:S(2)}, u32[]{:S(2)}) collective-permute-start(bf16[48,1536]{1,0:T(8,128)(2,1)S(1)} %get-tuple-element.450), channel_id=1, source_target_pairs={{0,16},{1,17},{2,18},{3,19},{4,20},{5,21},{6,22},{7,23},{8,24},{9,... | collective-permute-start | bytes 442376 | tf_op jit(solution)/shard_map/ppermute | solution.py:345
  12.0 10.1 %collective-permute-start.1 = (bf16[48,1536]{1,0:T(8,128)(2,1)S(1)}, bf16[48,1536]{1,0:T(8,128)(2,1)S(1)}, u32[]{:S(2)}, u32[]{:S(2)}) collective-permute-start(bf16[48,1536]{1,0:T(8,128)(2,1)S(1)} %get-tuple-element.450), channel_id=1, source_target_pairs={{0,8},{1,9},{2,10},{3,11},{4,12},{5,13},{6,14},{7,15},{8,16},{9,17... | collective-permute-start | bytes 442376 | tf_op jit(solution)/shard_map/ppermute | solution.py:345
  22.2 44.2 %all-to-all-start = ((bf16[32,16,896]{2,1,0:T(8,128)(2,1)}), bf16[32,16,896]{2,1,0:T(8,128)(2,1)S(1)}, u32[]{:S(2)}, u32[]{:S(2)}) async-start(bf16[32,16,896]{2,1,0:T(8,128)(2,1)} %bitcast.12), calls=%async_computation | async-start | bytes 1835008 | tf_op jit(solution)/shard_map/all_to_all | solution.py:412
  27.1 17.9 %collective-permute-start.6 = (bf16[2,48,1536]{2,1,0:T(8,128)(2,1)S(1)}, bf16[2,48,1536]{2,1,0:T(8,128)(2,1)S(1)}, u32[]{:S(2)}, u32[]{:S(2)}) collective-permute-start(bf16[2,48,1536]{2,1,0:T(8,128)(2,1)S(1)} %pad_maximum_fusion.7.refs_0_), channel_id=1, source_target_pairs={{0,4},{1,5},{2,6},{3,7},{4,0},{5,1},{6,2},{7,3},{8,12},{9,13},{10,... | collective-permute-start | bytes 884744 | tf_op jit(solution)/shard_map/ppermute | solution.py:339
  28.9 16.4 %collective-permute-start.4 = (bf16[2,48,1536]{2,1,0:T(8,128)(2,1)S(1)}, bf16[2,48,1536]{2,1,0:T(8,128)(2,1)S(1)}, u32[]{:S(2)}, u32[]{:S(2)}) collective-permute-start(bf16[2,48,1536]{2,1,0:T(8,128)(2,1)S(1)} %pad_maximum_fusion.7.refs_0_), channel_id=1, source_target_pairs={{0,2},{1,3},{2,0},{3,1},{4,6},{5,7},{6,4},{7,5},{8,10},{9,11},{10,... | collective-permute-start | bytes 884744 | tf_op jit(solution)/shard_map/ppermute | solution.py:339
  30.4 22.0 %collective-permute-start.7 = (bf16[2,48,1536]{2,1,0:T(8,128)(2,1)S(1)}, bf16[2,48,1536]{2,1,0:T(8,128)(2,1)S(1)}, u32[]{:S(2)}, u32[]{:S(2)}) collective-permute-start(bf16[2,48,1536]{2,1,0:T(8,128)(2,1)S(1)} %pad_maximum_fusion.8.refs_1_), channel_id=1, source_target_pairs={{0,4},{1,5},{2,6},{3,7},{4,0},{5,1},{6,2},{7,3},{8,12},{9,13},{10,... | collective-permute-start | bytes 884744 | tf_op jit(solution)/shard_map/ppermute | solution.py:339
  30.9 21.5 %collective-permute-start.5 = (bf16[2,48,1536]{2,1,0:T(8,128)(2,1)S(1)}, bf16[2,48,1536]{2,1,0:T(8,128)(2,1)S(1)}, u32[]{:S(2)}, u32[]{:S(2)}) collective-permute-start(bf16[2,48,1536]{2,1,0:T(8,128)(2,1)S(1)} %pad_maximum_fusion.8.refs_1_), channel_id=1, source_target_pairs={{0,2},{1,3},{2,0},{3,1},{4,6},{5,7},{6,4},{7,5},{8,10},{9,11},{10,... | collective-permute-start | bytes 884744 | tf_op jit(solution)/shard_map/ppermute | solution.py:339
  31.2 23.2 %collective-permute-start.10 = (bf16[2,48,1536]{2,1,0:T(8,128)(2,1)S(1)}, bf16[2,48,1536]{2,1,0:T(8,128)(2,1)S(1)}, u32[]{:S(2)}, u32[]{:S(2)}) collective-permute-start(bf16[2,48,1536]{2,1,0:T(8,128)(2,1)S(1)} %pad_maximum_fusion.7.refs_0_), channel_id=1, source_target_pairs={{0,1},{1,0},{2,3},{3,2},{4,5},{5,4},{6,7},{7,6},{8,9},{9,8},{10,11... | collective-permute-start | bytes 884744 | tf_op jit(solution)/shard_map/ppermute | solution.py:339
  45.0 9.4 %collective-permute-start.11 = (bf16[2,48,1536]{2,1,0:T(8,128)(2,1)S(1)}, bf16[2,48,1536]{2,1,0:T(8,128)(2,1)S(1)}, u32[]{:S(2)}, u32[]{:S(2)}) collective-permute-start(bf16[2,48,1536]{2,1,0:T(8,128)(2,1)S(1)} %pad_maximum_fusion.8.refs_1_), channel_id=1, source_target_pairs={{0,1},{1,0},{2,3},{3,2},{4,5},{5,4},{6,7},{7,6},{8,9},{9,8},{10,11... | collective-permute-start | bytes 884744 | tf_op jit(solution)/shard_map/ppermute | solution.py:339
  53.0 9.1 %collective-permute-start.8 = (bf16[2,48,1536]{2,1,0:T(8,128)(2,1)S(1)}, bf16[2,48,1536]{2,1,0:T(8,128)(2,1)}, u32[]{:S(2)}, u32[]{:S(2)}) collective-permute-start(bf16[2,48,1536]{2,1,0:T(8,128)(2,1)S(1)} %collective-permute-done.4.refs_2_), channel_id=1, source_target_pairs={{0,4},{1,5},{2,6},{3,7},{4,0},{5,1},{6,2},{7,3},{8,12},{9,13},{10,... | collective-permute-start | bytes 884744 | tf_op jit(solution)/shard_map/ppermute | solution.py:339
  54.4 7.7 %collective-permute-start.15 = (bf16[2,48,1536]{2,1,0:T(8,128)(2,1)S(1)}, bf16[2,48,1536]{2,1,0:T(8,128)(2,1)S(1)}, u32[]{:S(2)}, u32[]{:S(2)}) collective-permute-start(bf16[2,48,1536]{2,1,0:T(8,128)(2,1)S(1)} %collective-permute-done.7.refs_5_), channel_id=1, source_target_pairs={{0,1},{1,0},{2,3},{3,2},{4,5},{5,4},{6,7},{7,6},{8,9},{9,8},{10,11... | collective-permute-start | bytes 884744 | tf_op jit(solution)/shard_map/ppermute | solution.py:339
  54.9 9.1 %collective-permute-start.9 = (bf16[2,48,1536]{2,1,0:T(8,128)(2,1)S(1)}, bf16[2,48,1536]{2,1,0:T(8,128)(2,1)}, u32[]{:S(2)}, u32[]{:S(2)}) collective-permute-start(bf16[2,48,1536]{2,1,0:T(8,128)(2,1)S(1)} %collective-permute-done.7.refs_5_), channel_id=1, source_target_pairs={{0,2},{1,3},{2,0},{3,1},{4,6},{5,7},{6,4},{7,5},{8,10},{9,11},{10,... | collective-permute-start | bytes 884744 | tf_op jit(solution)/shard_map/ppermute | solution.py:339
  66.4 13.6 %collective-permute-start.20 = (bf16[48,1536]{1,0:T(8,128)(2,1)S(1)}, bf16[48,1536]{1,0:T(8,128)(2,1)S(1)}, u32[]{:S(2)}, u32[]{:S(2)}) collective-permute-start(bf16[48,1536]{1,0:T(8,128)(2,1)S(1)} %get-tuple-element.238), channel_id=1, source_target_pairs={{0,24},{1,25},{2,26},{3,27},{4,28},{5,29},{6,30},{7,31},{8,0},{9,1... | collective-permute-start | bytes 442376 | tf_op jit(solution)/shard_map/ppermute | solution.py:345
  69.7 13.0 %collective-permute-start.19 = (bf16[48,1536]{1,0:T(8,128)(2,1)S(1)}, bf16[48,1536]{1,0:T(8,128)(2,1)S(1)}, u32[]{:S(2)}, u32[]{:S(2)}) collective-permute-start(bf16[48,1536]{1,0:T(8,128)(2,1)S(1)} %get-tuple-element.238), channel_id=1, source_target_pairs={{0,16},{1,17},{2,18},{3,19},{4,20},{5,21},{6,22},{7,23},{8,24},{9,... | collective-permute-start | bytes 442376 | tf_op jit(solution)/shard_map/ppermute | solution.py:345
  69.7 13.0 %collective-permute-start.18 = (bf16[48,1536]{1,0:T(8,128)(2,1)S(1)}, bf16[48,1536]{1,0:T(8,128)(2,1)S(1)}, u32[]{:S(2)}, u32[]{:S(2)}) collective-permute-start(bf16[48,1536]{1,0:T(8,128)(2,1)S(1)} %get-tuple-element.238), channel_id=1, source_target_pairs={{0,8},{1,9},{2,10},{3,11},{4,12},{5,13},{6,14},{7,15},{8,16},{9,17... | collective-permute-start | bytes 442376 | tf_op jit(solution)/shard_map/ppermute | solution.py:345
  82.8 17.2 %collective-permute-start.22 = (bf16[4,48,1536]{2,1,0:T(8,128)(2,1)S(1)}, bf16[4,48,1536]{2,1,0:T(8,128)(2,1)S(1)}, u32[]{:S(2)}, u32[]{:S(2)}) collective-permute-start(bf16[4,48,1536]{2,1,0:T(8,128)(2,1)S(1)} %pad_maximum_fusion.2.refs_0_), channel_id=1, source_target_pairs={{0,4},{1,5},{2,6},{3,7},{4,0},{5,1},{6,2},{7,3},{8,12},{9,13},{10,... | collective-permute-start | bytes 1769480 | tf_op jit(solution)/shard_map/ppermute | solution.py:339
  83.5 16.6 %collective-permute-start.21 = (bf16[4,48,1536]{2,1,0:T(8,128)(2,1)S(1)}, bf16[4,48,1536]{2,1,0:T(8,128)(2,1)}, u32[]{:S(2)}, u32[]{:S(2)}) collective-permute-start(bf16[4,48,1536]{2,1,0:T(8,128)(2,1)S(1)} %pad_maximum_fusion.2.refs_0_), channel_id=1, source_target_pairs={{0,2},{1,3},{2,0},{3,1},{4,6},{5,7},{6,4},{7,5},{8,10},{9,11},{10,... | collective-permute-start | bytes 1769480 | tf_op jit(solution)/shard_map/ppermute | solution.py:339
  85.0 10.6 %collective-permute-start.25 = (bf16[96,768]{1,0:T(8,128)(2,1)S(1)}, bf16[96,768]{1,0:T(8,128)(2,1)S(1)}, u32[]{:S(2)}, u32[]{:S(2)}) collective-permute-start(bf16[96,768]{1,0:T(8,128)(2,1)S(1)} %convert_element_type.355), channel_id=1, source_target_pairs={{0,24},{1,25},{2,26},{3,27},{4,28},{5,29},{6,30},{7,31},{8,0},{9,1... | collective-permute-start | bytes 442376 | tf_op jit(solution)/shard_map/ppermute | solution.py:345
  86.1 13.8 %collective-permute-start.24 = (bf16[96,768]{1,0:T(8,128)(2,1)S(1)}, bf16[96,768]{1,0:T(8,128)(2,1)S(1)}, u32[]{:S(2)}, u32[]{:S(2)}) collective-permute-start(bf16[96,768]{1,0:T(8,128)(2,1)S(1)} %convert_element_type.355), channel_id=1, source_target_pairs={{0,16},{1,17},{2,18},{3,19},{4,20},{5,21},{6,22},{7,23},{8,24},{9,... | collective-permute-start | bytes 442376 | tf_op jit(solution)/shard_map/ppermute | solution.py:345
  87.6 12.3 %collective-permute-start.23 = (bf16[96,768]{1,0:T(8,128)(2,1)S(1)}, bf16[96,768]{1,0:T(8,128)(2,1)S(1)}, u32[]{:S(2)}, u32[]{:S(2)}) collective-permute-start(bf16[96,768]{1,0:T(8,128)(2,1)S(1)} %convert_element_type.355), channel_id=1, source_target_pairs={{0,8},{1,9},{2,10},{3,11},{4,12},{5,13},{6,14},{7,15},{8,16},{9,17... | collective-permute-start | bytes 442376 | tf_op jit(solution)/shard_map/ppermute | solution.py:345
  95.6 22.2 %collective-permute-start.28 = (bf16[4,48,1536]{2,1,0:T(8,128)(2,1)S(1)}, bf16[4,48,1536]{2,1,0:T(8,128)(2,1)}, u32[]{:S(2)}, u32[]{:S(2)}) collective-permute-start(bf16[4,48,1536]{2,1,0:T(8,128)(2,1)S(1)} %pad_maximum_fusion.2.refs_0_), channel_id=1, source_target_pairs={{0,1},{1,0},{2,3},{3,2},{4,5},{5,4},{6,7},{7,6},{8,9},{9,8},{10,11... | collective-permute-start | bytes 1769480 | tf_op jit(solution)/shard_map/ppermute | solution.py:339
  100.1 19.7 %collective-permute-start.29 = (bf16[4,48,1536]{2,1,0:T(8,128)(2,1)}, bf16[4,48,1536]{2,1,0:T(8,128)(2,1)}, u32[]{:S(2)}, u32[]{:S(2)}) collective-permute-start(bf16[4,48,1536]{2,1,0:T(8,128)(2,1)} %collective-permute-done.21.refs_1_), channel_id=1, source_target_pairs={{0,1},{1,0},{2,3},{3,2},{4,5},{5,4},{6,7},{7,6},{8,9},{9,8},{10,11... | collective-permute-start | bytes 1769480 | tf_op jit(solution)/shard_map/ppermute | solution.py:339
  100.1 19.6 %collective-permute-start.30 = (bf16[4,48,1536]{2,1,0:T(8,128)(2,1)S(1)}, bf16[4,48,1536]{2,1,0:T(8,128)(2,1)}, u32[]{:S(2)}, u32[]{:S(2)}) collective-permute-start(bf16[4,48,1536]{2,1,0:T(8,128)(2,1)S(1)} %collective-permute-done.22.refs_2_), channel_id=1, source_target_pairs={{0,1},{1,0},{2,3},{3,2},{4,5},{5,4},{6,7},{7,6},{8,9},{9,8},{10,11... | collective-permute-start | bytes 1769480 | tf_op jit(solution)/shard_map/ppermute | solution.py:339
  100.6 43.7 %all-to-all-start.1 = ((bf16[32,16,768]{2,1,0:T(8,128)(2,1)}), bf16[32,16,768]{2,1,0:T(8,128)(2,1)S(1)}, u32[]{:S(2)}, u32[]{:S(2)}) async-start(bf16[32,16,768]{2,1,0:T(8,128)(2,1)} %bitcast.23), calls=%async_computation.1 | async-start | bytes 1572864 | tf_op jit(solution)/shard_map/all_to_all | solution.py:412
  104.5 15.2 %collective-permute-start.27 = (bf16[2,48,1536]{2,1,0:T(8,128)(2,1)S(1)}, bf16[2,48,1536]{2,1,0:T(8,128)(2,1)S(1)}, u32[]{:S(2)}, u32[]{:S(2)}) collective-permute-start(bf16[2,48,1536]{2,1,0:T(8,128)(2,1)S(1)} %slice.197), channel_id=1, source_target_pairs={{0,2},{1,3},{2,0},{3,1},{4,6},{5,7},{6,4},{7,5},{8,10},{9,11},{10,... | collective-permute-start | bytes 884744 | tf_op jit(solution)/shard_map/ppermute | solution.py:339
  106.0 13.7 %collective-permute-start.26 = (bf16[2,48,1536]{2,1,0:T(8,128)(2,1)S(1)}, bf16[2,48,1536]{2,1,0:T(8,128)(2,1)}, u32[]{:S(2)}, u32[]{:S(2)}) collective-permute-start(bf16[2,48,1536]{2,1,0:T(8,128)(2,1)S(1)} %slice.196), channel_id=1, source_target_pairs={{0,4},{1,5},{2,6},{3,7},{4,0},{5,1},{6,2},{7,3},{8,12},{9,13},{10,... | collective-permute-start | bytes 884744 | tf_op jit(solution)/shard_map/ppermute | solution.py:339
  121.8 15.7 %collective-permute-start.35 = (bf16[2,96,768]{2,1,0:T(8,128)(2,1)S(1)}, bf16[2,96,768]{2,1,0:T(8,128)(2,1)}, u32[]{:S(2)}, u32[]{:S(2)}) collective-permute-start(bf16[2,96,768]{2,1,0:T(8,128)(2,1)S(1)} %pad_maximum_fusion.9.refs_0_), channel_id=1, source_target_pairs={{0,4},{1,5},{2,6},{3,7},{4,0},{5,1},{6,2},{7,3},{8,12},{9,13},{10,... | collective-permute-start | bytes 884744 | tf_op jit(solution)/shard_map/ppermute | solution.py:339
  123.1 14.9 %collective-permute-start.33 = (bf16[2,96,768]{2,1,0:T(8,128)(2,1)S(1)}, bf16[2,96,768]{2,1,0:T(8,128)(2,1)}, u32[]{:S(2)}, u32[]{:S(2)}) collective-permute-start(bf16[2,96,768]{2,1,0:T(8,128)(2,1)S(1)} %pad_maximum_fusion.9.refs_0_), channel_id=1, source_target_pairs={{0,2},{1,3},{2,0},{3,1},{4,6},{5,7},{6,4},{7,5},{8,10},{9,11},{10,... | collective-permute-start | bytes 884744 | tf_op jit(solution)/shard_map/ppermute | solution.py:339
  123.8 14.2 %collective-permute-start.36 = (bf16[2,96,768]{2,1,0:T(8,128)(2,1)S(1)}, bf16[2,96,768]{2,1,0:T(8,128)(2,1)}, u32[]{:S(2)}, u32[]{:S(2)}) collective-permute-start(bf16[2,96,768]{2,1,0:T(8,128)(2,1)S(1)} %pad_maximum_fusion.10.refs_1_), channel_id=1, source_target_pairs={{0,4},{1,5},{2,6},{3,7},{4,0},{5,1},{6,2},{7,3},{8,12},{9,13},{10,... | collective-permute-start | bytes 884744 | tf_op jit(solution)/shard_map/ppermute | solution.py:339
  125.3 12.9 %collective-permute-start.34 = (bf16[2,96,768]{2,1,0:T(8,128)(2,1)S(1)}, bf16[2,96,768]{2,1,0:T(8,128)(2,1)S(1)}, u32[]{:S(2)}, u32[]{:S(2)}) collective-permute-start(bf16[2,96,768]{2,1,0:T(8,128)(2,1)S(1)} %pad_maximum_fusion.10.refs_1_), channel_id=1, source_target_pairs={{0,2},{1,3},{2,0},{3,1},{4,6},{5,7},{6,4},{7,5},{8,10},{9,11},{10,... | collective-permute-start | bytes 884744 | tf_op jit(solution)/shard_map/ppermute | solution.py:339
  126.5 14.2 %collective-permute-start.39 = (bf16[2,96,768]{2,1,0:T(8,128)(2,1)S(1)}, bf16[2,96,768]{2,1,0:T(8,128)(2,1)S(1)}, u32[]{:S(2)}, u32[]{:S(2)}) collective-permute-start(bf16[2,96,768]{2,1,0:T(8,128)(2,1)S(1)} %pad_maximum_fusion.9.refs_0_), channel_id=1, source_target_pairs={{0,1},{1,0},{2,3},{3,2},{4,5},{5,4},{6,7},{7,6},{8,9},{9,8},{10,11... | collective-permute-start | bytes 884744 | tf_op jit(solution)/shard_map/ppermute | solution.py:339
  138.9 13.4 %collective-permute-start.41 = (bf16[2,96,768]{2,1,0:T(8,128)(2,1)}, bf16[2,96,768]{2,1,0:T(8,128)(2,1)}, u32[]{:S(2)}, u32[]{:S(2)}) collective-permute-start(bf16[2,96,768]{2,1,0:T(8,128)(2,1)} %collective-permute-done.33.refs_2_), channel_id=1, source_target_pairs={{0,1},{1,0},{2,3},{3,2},{4,5},{5,4},{6,7},{7,6},{8,9},{9,8},{10,11... | collective-permute-start | bytes 884744 | tf_op jit(solution)/shard_map/ppermute | solution.py:339
  139.4 12.9 %collective-permute-start.37 = (bf16[2,96,768]{2,1,0:T(8,128)(2,1)}, bf16[2,96,768]{2,1,0:T(8,128)(2,1)}, u32[]{:S(2)}, u32[]{:S(2)}) collective-permute-start(bf16[2,96,768]{2,1,0:T(8,128)(2,1)} %collective-permute-done.33.refs_2_), channel_id=1, source_target_pairs={{0,4},{1,5},{2,6},{3,7},{4,0},{5,1},{6,2},{7,3},{8,12},{9,13},{10,... | collective-permute-start | bytes 884744 | tf_op jit(solution)/shard_map/ppermute | solution.py:339
  141.4 10.9 %collective-permute-start.43 = (bf16[2,96,768]{2,1,0:T(8,128)(2,1)}, bf16[2,96,768]{2,1,0:T(8,128)(2,1)}, u32[]{:S(2)}, u32[]{:S(2)}) collective-permute-start(bf16[2,96,768]{2,1,0:T(8,128)(2,1)} %collective-permute-done.35.refs_4_), channel_id=1, source_target_pairs={{0,1},{1,0},{2,3},{3,2},{4,5},{5,4},{6,7},{7,6},{8,9},{9,8},{10,11... | collective-permute-start | bytes 884744 | tf_op jit(solution)/shard_map/ppermute | solution.py:339
  142.1 10.2 %collective-permute-start.44 = (bf16[2,96,768]{2,1,0:T(8,128)(2,1)}, bf16[2,96,768]{2,1,0:T(8,128)(2,1)}, u32[]{:S(2)}, u32[]{:S(2)}) collective-permute-start(bf16[2,96,768]{2,1,0:T(8,128)(2,1)} %collective-permute-done.36.refs_5_), channel_id=1, source_target_pairs={{0,1},{1,0},{2,3},{3,2},{4,5},{5,4},{6,7},{7,6},{8,9},{9,8},{10,11... | collective-permute-start | bytes 884744 | tf_op jit(solution)/shard_map/ppermute | solution.py:339
  143.3 9.2 %collective-permute-start.38 = (bf16[2,96,768]{2,1,0:T(8,128)(2,1)}, bf16[2,96,768]{2,1,0:T(8,128)(2,1)}, u32[]{:S(2)}, u32[]{:S(2)}) collective-permute-start(bf16[2,96,768]{2,1,0:T(8,128)(2,1)} %collective-permute-done.36.refs_5_), channel_id=1, source_target_pairs={{0,2},{1,3},{2,0},{3,1},{4,6},{5,7},{6,4},{7,5},{8,10},{9,11},{10,... | collective-permute-start | bytes 884744 | tf_op jit(solution)/shard_map/ppermute | solution.py:339
  152.6 5.4 %collective-permute-start.47 = (bf16[4,4,96,768]{3,2,1,0:T(8,128)(2,1)S(1)}, bf16[4,4,96,768]{3,2,1,0:T(8,128)(2,1)S(1)}, u32[]{:S(2)}, u32[]{:S(2)}) collective-permute-start(bf16[4,4,96,768]{3,2,1,0:T(8,128)(2,1)S(1)} %get-tuple-element.284), channel_id=1, source_target_pairs={{0,1},{1,0},{2,3},{3,2},{4,5},{5,4},{6,7},{7,6},{8,9},{9,8},{10,11... | collective-permute-start | bytes 7077896 | tf_op jit(solution)/shard_map/ppermute | solution.py:339
  152.6 4.8 %collective-permute-start.45 = (bf16[2,96,768]{2,1,0:T(8,128)(2,1)}, bf16[2,96,768]{2,1,0:T(8,128)(2,1)S(1)}, u32[]{:S(2)}, u32[]{:S(2)}) collective-permute-start(bf16[2,96,768]{2,1,0:T(8,128)(2,1)} %collective-permute-done.37.refs_6_), channel_id=1, source_target_pairs={{0,1},{1,0},{2,3},{3,2},{4,5},{5,4},{6,7},{7,6},{8,9},{9,8},{10,11... | collective-permute-start | bytes 884744 | tf_op jit(solution)/shard_map/ppermute | solution.py:339
  158.3 11.9 %collective-permute-start.48 = (bf16[2,96,768]{2,1,0:T(8,128)(2,1)S(1)}, bf16[2,96,768]{2,1,0:T(8,128)(2,1)S(1)}, u32[]{:S(2)}, u32[]{:S(2)}) collective-permute-start(bf16[2,96,768]{2,1,0:T(8,128)(2,1)S(1)} %get-tuple-element.307), channel_id=1, source_target_pairs={{0,4},{1,5},{2,6},{3,7},{4,0},{5,1},{6,2},{7,3},{8,12},{9,13},{10,... | collective-permute-start | bytes 884744 | tf_op jit(solution)/shard_map/ppermute | solution.py:339
  159.4 10.8 %collective-permute-start.49 = (bf16[2,96,768]{2,1,0:T(8,128)(2,1)S(1)}, bf16[2,96,768]{2,1,0:T(8,128)(2,1)S(1)}, u32[]{:S(2)}, u32[]{:S(2)}) collective-permute-start(bf16[2,96,768]{2,1,0:T(8,128)(2,1)S(1)} %get-tuple-element.308), channel_id=1, source_target_pairs={{0,2},{1,3},{2,0},{3,1},{4,6},{5,7},{6,4},{7,5},{8,10},{9,11},{10,... | collective-permute-start | bytes 884744 | tf_op jit(solution)/shard_map/ppermute | solution.py:339
  171.6 29.6 %all-to-all-start.2 = ((bf16[32,16,768]{2,1,0:T(8,128)(2,1)}), bf16[32,16,768]{2,1,0:T(8,128)(2,1)S(1)}, u32[]{:S(2)}, u32[]{:S(2)}) async-start(bf16[32,16,768]{2,1,0:T(8,128)(2,1)} %bitcast.139), calls=%async_computation.2 | async-start | bytes 1572864 | tf_op jit(solution)/shard_map/all_to_all | solution.py:412
  177.3 23.8 %collective-permute-start.50 = (bf16[4,96,768]{2,1,0:T(8,128)(2,1)}, bf16[4,96,768]{2,1,0:T(8,128)(2,1)}, u32[]{:S(2)}, u32[]{:S(2)}) collective-permute-start(bf16[4,96,768]{2,1,0:T(8,128)(2,1)} %get-tuple-element.316), channel_id=1, source_target_pairs={{0,2},{1,3},{2,0},{3,1},{4,6},{5,7},{6,4},{7,5},{8,10},{9,11},{10,... | collective-permute-start | bytes 1769480 | tf_op jit(solution)/shard_map/ppermute | solution.py:339
  178.9 22.3 %collective-permute-start.51 = (bf16[4,96,768]{2,1,0:T(8,128)(2,1)}, bf16[4,96,768]{2,1,0:T(8,128)(2,1)}, u32[]{:S(2)}, u32[]{:S(2)}) collective-permute-start(bf16[4,96,768]{2,1,0:T(8,128)(2,1)} %get-tuple-element.317), channel_id=1, source_target_pairs={{0,4},{1,5},{2,6},{3,7},{4,0},{5,1},{6,2},{7,3},{8,12},{9,13},{10,... | collective-permute-start | bytes 1769480 | tf_op jit(solution)/shard_map/ppermute | solution.py:339
  203.1 9.3 %collective-permute-start.52 = (bf16[4,4,24,3840]{3,2,1,0:T(8,128)(2,1)}, bf16[4,4,24,3840]{3,2,1,0:T(8,128)(2,1)S(1)}, u32[]{:S(2)}, u32[]{:S(2)}) collective-permute-start(bf16[4,4,24,3840]{3,2,1,0:T(8,128)(2,1)} %get-tuple-element.325), channel_id=1, source_target_pairs={{0,1},{1,0},{2,3},{3,2},{4,5},{5,4},{6,7},{7,6},{8,9},{9,8},{10,11... | collective-permute-start | bytes 8847368 | tf_op jit(solution)/shard_map/ppermute | solution.py:339
  212.8 15.3 %collective-permute-start.53 = (bf16[2,24,3840]{2,1,0:T(8,128)(2,1)S(1)}, bf16[2,24,3840]{2,1,0:T(8,128)(2,1)S(1)}, u32[]{:S(2)}, u32[]{:S(2)}) collective-permute-start(bf16[2,24,3840]{2,1,0:T(8,128)(2,1)S(1)} %get-tuple-element.333), channel_id=1, source_target_pairs={{0,4},{1,5},{2,6},{3,7},{4,0},{5,1},{6,2},{7,3},{8,12},{9,13},{10,... | collective-permute-start | bytes 1105928 | tf_op jit(solution)/shard_map/ppermute | solution.py:339
  214.2 13.9 %collective-permute-start.54 = (bf16[2,24,3840]{2,1,0:T(8,128)(2,1)S(1)}, bf16[2,24,3840]{2,1,0:T(8,128)(2,1)S(1)}, u32[]{:S(2)}, u32[]{:S(2)}) collective-permute-start(bf16[2,24,3840]{2,1,0:T(8,128)(2,1)S(1)} %get-tuple-element.334), channel_id=1, source_target_pairs={{0,2},{1,3},{2,0},{3,1},{4,6},{5,7},{6,4},{7,5},{8,10},{9,11},{10,... | collective-permute-start | bytes 1105928 | tf_op jit(solution)/shard_map/ppermute | solution.py:339
  214.8 13.3 %collective-permute-start.55 = (bf16[96,768]{1,0:T(8,128)(2,1)S(1)}, bf16[96,768]{1,0:T(8,128)(2,1)S(1)}, u32[]{:S(2)}, u32[]{:S(2)}) collective-permute-start(bf16[96,768]{1,0:T(8,128)(2,1)S(1)} %get-tuple-element.338), channel_id=1, source_target_pairs={{0,8},{1,9},{2,10},{3,11},{4,12},{5,13},{6,14},{7,15},{8,16},{9,17... | collective-permute-start | bytes 442376 | tf_op jit(solution)/shard_map/ppermute | solution.py:408
  216.3 11.8 %collective-permute-start.56 = (bf16[96,768]{1,0:T(8,128)(2,1)S(1)}, bf16[96,768]{1,0:T(8,128)(2,1)S(1)}, u32[]{:S(2)}, u32[]{:S(2)}) collective-permute-start(bf16[96,768]{1,0:T(8,128)(2,1)S(1)} %get-tuple-element.339), channel_id=1, source_target_pairs={{0,16},{1,17},{2,18},{3,19},{4,20},{5,21},{6,22},{7,23},{8,24},{9,... | collective-permute-start | bytes 442376 | tf_op jit(solution)/shard_map/ppermute | solution.py:408
  218.6 9.5 %collective-permute-start.57 = (bf16[96,768]{1,0:T(8,128)(2,1)S(1)}, bf16[96,768]{1,0:T(8,128)(2,1)S(1)}, u32[]{:S(2)}, u32[]{:S(2)}) collective-permute-start(bf16[96,768]{1,0:T(8,128)(2,1)S(1)} %get-tuple-element.340), channel_id=1, source_target_pairs={{0,24},{1,25},{2,26},{3,27},{4,28},{5,29},{6,30},{7,31},{8,0},{9,1... | collective-permute-start | bytes 442376 | tf_op jit(solution)/shard_map/ppermute | solution.py:408
  230.4 22.9 %collective-permute-start.58 = (bf16[4,24,3840]{2,1,0:T(8,128)(2,1)}, bf16[4,24,3840]{2,1,0:T(8,128)(2,1)S(1)}, u32[]{:S(2)}, u32[]{:S(2)}) collective-permute-start(bf16[4,24,3840]{2,1,0:T(8,128)(2,1)} %pad_maximum_fusion), channel_id=1, source_target_pairs={{0,2},{1,3},{2,0},{3,1},{4,6},{5,7},{6,4},{7,5},{8,10},{9,11},{10,... | collective-permute-start | bytes 2211848 | tf_op jit(solution)/shard_map/ppermute | solution.py:339
  231.8 21.4 %collective-permute-start.59 = (bf16[4,24,3840]{2,1,0:T(8,128)(2,1)}, bf16[4,24,3840]{2,1,0:T(8,128)(2,1)}, u32[]{:S(2)}, u32[]{:S(2)}) collective-permute-start(bf16[4,24,3840]{2,1,0:T(8,128)(2,1)} %pad_maximum_fusion.1), channel_id=1, source_target_pairs={{0,4},{1,5},{2,6},{3,7},{4,0},{5,1},{6,2},{7,3},{8,12},{9,13},{10,... | collective-permute-start | bytes 2211848 | tf_op jit(solution)/shard_map/ppermute | solution.py:339
  241.0 29.3 %all-to-all-start.3 = ((bf16[32,16,896]{2,1,0:T(8,128)(2,1)}), bf16[32,16,896]{2,1,0:T(8,128)(2,1)S(1)}, u32[]{:S(2)}, u32[]{:S(2)}) async-start(bf16[32,16,896]{2,1,0:T(8,128)(2,1)} %bitcast.53), calls=%async_computation.3 | async-start | bytes 1835008 | tf_op jit(solution)/shard_map/all_to_all | solution.py:412
  258.5 11.8 %collective-permute-start.61 = (bf16[2,24,2304]{2,1,0:T(8,128)(2,1)}, bf16[2,24,2304]{2,1,0:T(8,128)(2,1)S(1)}, u32[]{:S(2)}, u32[]{:S(2)}) collective-permute-start(bf16[2,24,2304]{2,1,0:T(8,128)(2,1)} %get-tuple-element.365), channel_id=1, source_target_pairs={{0,4},{1,5},{2,6},{3,7},{4,0},{5,1},{6,2},{7,3},{8,12},{9,13},{10,... | collective-permute-start | bytes 663560 | tf_op jit(solution)/shard_map/ppermute | solution.py:339
  260.0 10.3 %collective-permute-start.62 = (bf16[2,24,2304]{2,1,0:T(8,128)(2,1)}, bf16[2,24,2304]{2,1,0:T(8,128)(2,1)S(1)}, u32[]{:S(2)}, u32[]{:S(2)}) collective-permute-start(bf16[2,24,2304]{2,1,0:T(8,128)(2,1)} %get-tuple-element.366), channel_id=1, source_target_pairs={{0,2},{1,3},{2,0},{3,1},{4,6},{5,7},{6,4},{7,5},{8,10},{9,11},{10,... | collective-permute-start | bytes 663560 | tf_op jit(solution)/shard_map/ppermute | solution.py:339
  272.3 12.5 %collective-permute-start.63 = (bf16[4,24,2304]{2,1,0:T(8,128)(2,1)S(1)}, bf16[4,24,2304]{2,1,0:T(8,128)(2,1)S(1)}, u32[]{:S(2)}, u32[]{:S(2)}) collective-permute-start(bf16[4,24,2304]{2,1,0:T(8,128)(2,1)S(1)} %pad_maximum_fusion.5), channel_id=1, source_target_pairs={{0,2},{1,3},{2,0},{3,1},{4,6},{5,7},{6,4},{7,5},{8,10},{9,11},{10,... | collective-permute-start | bytes 1327112 | tf_op jit(solution)/shard_map/ppermute | solution.py:339
  273.8 11.8 %collective-permute-start.64 = (bf16[4,24,2304]{2,1,0:T(8,128)(2,1)S(1)}, bf16[4,24,2304]{2,1,0:T(8,128)(2,1)S(1)}, u32[]{:S(2)}, u32[]{:S(2)}) collective-permute-start(bf16[4,24,2304]{2,1,0:T(8,128)(2,1)S(1)} %pad_maximum_fusion.6), channel_id=1, source_target_pairs={{0,4},{1,5},{2,6},{3,7},{4,0},{5,1},{6,2},{7,3},{8,12},{9,13},{10,... | collective-permute-start | bytes 1327112 | tf_op jit(solution)/shard_map/ppermute | solution.py:339
  275.3 9.4 %collective-permute-start.65 = (bf16[24,3840]{1,0:T(8,128)(2,1)S(1)}, bf16[24,3840]{1,0:T(8,128)(2,1)S(1)}, u32[]{:S(2)}, u32[]{:S(2)}) collective-permute-start(bf16[24,3840]{1,0:T(8,128)(2,1)S(1)} %copy-done.42), channel_id=1, source_target_pairs={{0,8},{1,9},{2,10},{3,11},{4,12},{5,13},{6,14},{7,15},{8,16},{9,17... | collective-permute-start | bytes 552968 | tf_op jit(solution)/shard_map/ppermute | solution.py:408
  278.3 13.3 %collective-permute-start.69 = (bf16[24,3840]{1,0:T(8,128)(2,1)S(1)}, bf16[24,3840]{1,0:T(8,128)(2,1)S(1)}, u32[]{:S(2)}, u32[]{:S(2)}) collective-permute-start(bf16[24,3840]{1,0:T(8,128)(2,1)S(1)} %copy-done.41), channel_id=1, source_target_pairs={{0,16},{1,17},{2,18},{3,19},{4,20},{5,21},{6,22},{7,23},{8,24},{9,... | collective-permute-start | bytes 552968 | tf_op jit(solution)/shard_map/ppermute | solution.py:408
  278.7 12.9 %collective-permute-start.70 = (bf16[24,3840]{1,0:T(8,128)(2,1)S(1)}, bf16[24,3840]{1,0:T(8,128)(2,1)S(1)}, u32[]{:S(2)}, u32[]{:S(2)}) collective-permute-start(bf16[24,3840]{1,0:T(8,128)(2,1)S(1)} %copy-done.40), channel_id=1, source_target_pairs={{0,24},{1,25},{2,26},{3,27},{4,28},{5,29},{6,30},{7,31},{8,0},{9,1... | collective-permute-start | bytes 552968 | tf_op jit(solution)/shard_map/ppermute | solution.py:408
  287.7 8.3 %collective-permute-start.66 = (bf16[24,2304]{1,0:T(8,128)(2,1)S(1)}, bf16[24,2304]{1,0:T(8,128)(2,1)S(1)}, u32[]{:S(2)}, u32[]{:S(2)}) collective-permute-start(bf16[24,2304]{1,0:T(8,128)(2,1)S(1)} %get-tuple-element.376), channel_id=1, source_target_pairs={{0,8},{1,9},{2,10},{3,11},{4,12},{5,13},{6,14},{7,15},{8,16},{9,17... | collective-permute-start | bytes 331784 | tf_op jit(solution)/shard_map/ppermute | solution.py:408
  289.3 12.3 %collective-permute-start.67 = (bf16[24,2304]{1,0:T(8,128)(2,1)S(1)}, bf16[24,2304]{1,0:T(8,128)(2,1)S(1)}, u32[]{:S(2)}, u32[]{:S(2)}) collective-permute-start(bf16[24,2304]{1,0:T(8,128)(2,1)S(1)} %get-tuple-element.377), channel_id=1, source_target_pairs={{0,16},{1,17},{2,18},{3,19},{4,20},{5,21},{6,22},{7,23},{8,24},{9,... | collective-permute-start | bytes 331784 | tf_op jit(solution)/shard_map/ppermute | solution.py:408
  289.5 12.1 %collective-permute-start.68 = (bf16[24,2304]{1,0:T(8,128)(2,1)S(1)}, bf16[24,2304]{1,0:T(8,128)(2,1)S(1)}, u32[]{:S(2)}, u32[]{:S(2)}) collective-permute-start(bf16[24,2304]{1,0:T(8,128)(2,1)S(1)} %get-tuple-element.378), channel_id=1, source_target_pairs={{0,24},{1,25},{2,26},{3,27},{4,28},{5,29},{6,30},{7,31},{8,0},{9,1... | collective-permute-start | bytes 331784 | tf_op jit(solution)/shard_map/ppermute | solution.py:408
  304.3 11.8 %all-to-all-start.4 = ((f32[32,4,128]{2,1,0:T(4,128)}), f32[32,4,128]{2,1,0:T(4,128)S(1)}, u32[]{:S(2)}, u32[]{:S(2)}) async-start(f32[32,4,128]{2,1,0:T(4,128)} %get-tuple-element.396), calls=%async_computation.4 | async-start | bytes 131072 | tf_op jit(solution)/shard_map/all_to_all | solution.py:412
  (78 other events, 629.5 us)

commit v5 on v4

--- a/solution.py
+++ b/solution.py
@@ -339,10 +339,15 @@
     return lax.ppermute(value, "dev", flips(lax.axis_size("dev"), mask))
 
 
-def along_z(block, stacks):
+def along_z(block):
     devices = lax.axis_size("dev")
-    depth = devices // PLANE
-    blocks = [block] + [lax.ppermute(block, "dev", shifts(devices, k)) for k in range(1, depth)]
+    return [block] + [
+        lax.ppermute(block, "dev", shifts(devices, k)) for k in range(1, devices // PLANE)
+    ]
+
+
+def stacked(blocks, stacks):
+    depth = len(blocks)
     each = depth // stacks
     return tuple(jnp.stack(blocks[k : k + each], 0) for k in range(0, depth, each))
 
@@ -1365,8 +1370,9 @@
     pair = jnp.concatenate(core_order(core, keep, got), 0)
 
     send_rows, send_grads, slot = route(segment_ids.reshape(1, count), tokens, cotangent, devices)
-    first_own = along_z(pair[:, 0], 2)
-    send_rows, first_own = pin(send_rows, first_own)
+    first_own = along_z(pair[:, 0])
+    send_rows, first_own[1] = pin(send_rows, first_own[1])
+    first_own = stacked(first_own, 2)
 
     work = exchange(send_rows.reshape(devices, capacity, -1)).reshape(count, -1)
     first_near = pin(*to_neighbours(*first_own))
@@ -1377,14 +1383,14 @@
     first_got = first_got + to_partner(*first_far)
     first_got, work, up_block = pin(first_got, work, pair[:, 1])
 
-    up_own = along_z(up_block, 1)
+    up_own = stacked(along_z(up_block), 1)
     flipped_one, projected, first_weights, out_weights = project(
         where, work, vector_weight, (*first_own, *first_near, *first_far, *first_got)
     )
     projected, up_own, down_block, send_grads = pin(projected, up_own, down_low, send_grads)
 
     up_near = to_neighbours(*up_own)
-    down_own = along_z(down_block, 2)
+    down_own = stacked(along_z(down_block), 2)
     pairs = feature // 256
     attended_a, stats_a, carried = attend(projected, work, vector_weight, out_weights, 0, pairs)
     carried, up_near, down_own, send_grads = pin(carried, up_near, down_own, send_grads)
@@ -1461,9 +1467,9 @@
     first_fold = Fold(first_mine, first_got)
     first_to, up_sums = pin(first_fold.diagonal(), up_sums)
 
+    got = pin(*over_diagonal(*first_to))
+    first_to, back, up_sums = pin(first_fold.neighbours(*got), back, up_sums)
     up_got = over_column(up_sums)
-    got, back = pin(over_diagonal(*first_to), back)
-    first_to = pin(*first_fold.neighbours(*got))
 
     got = over_plane(*first_to)
     got, up_first = pin(got, up_got[0])

time: 323 us -> 318 us (0.985)
  waiting for transfers between devices: 84.8 us -> 76.6 us
  starting transfers between devices: 90.9 us -> 95.3 us
    ppermute x9, waiting for transfers between devices: 16 us -> 7.88 us  [along_z(): lax.ppermute(block, 'dev', shifts(devices, k))]
    ppermute x52, waiting for transfers between devices: 43.3 us -> 50 us  [send(): return lax.ppermute(value, 'dev', flips(lax.axis_size('dev'), mask))]
    all_to_all x5, waiting for transfers between devices: 14.7 us -> 8.85 us  [exchange(): return lax.all_to_all(rows, 'dev', split_axis=0, concat_axis=0, tiled=True)]
    all_to_all x5, starting transfers between devices: 23.9 us -> 28.4 us  [exchange(): return lax.all_to_all(rows, 'dev', split_axis=0, concat_axis=0, tiled=True)]
    unnamed x134 -> x122, local copies, waits for them, and re-layouts: 8.07 us -> 8.03 us
  transfers between devices with their start and end apart: 76 -> 76, of which waited for: 29 -> 30; matrix products, arithmetic and copies ran while one was open for 4% -> 4% of each run, Pallas kernels for 33% -> 34%
where the time goes in v5:
time: 318 us; the launch traced here: 316 us
  Pallas kernels  114 us (36%)
  starting transfers between devices  95.3 us (30%)
  waiting for transfers between devices  76.6 us (24%)
  other arithmetic  15.9 us (5%)
  local copies, waits for them, and re-layouts  11.3 us (4%)
  between operations  3.22 us (1%)
    ppermute x52, waiting for transfers between devices, send(): return lax.ppermute(value, 'dev', flips(lax.axis_size('dev'), mask))  50 us
    ppermute x52, starting transfers between devices, send(): return lax.ppermute(value, 'dev', flips(lax.axis_size('dev'), mask))  38.3 us
    all_to_all x5, starting transfers between devices, exchange(): return lax.all_to_all(rows, 'dev', split_axis=0, concat_axis=0, tiled=True)  28.4 us
    pallas_call x1, Pallas kernels, feed_back(): pl.pallas_call(kernel, grid=(steps + 1,), out_shape=[shaped((count, featu...  18.9 us
    pallas_call x2, Pallas kernels, attend(): pl.pallas_call(kernel, grid=(pairs,), out_shape=[shaped((pairs * 128, cou...  16.2 us
    pallas_call x2, Pallas kernels, attend_back(): pl.pallas_call(kernel, grid=(pairs,), out_shape=[shaped((3, count, wide),...  16 us
    ppermute x9, starting transfers between devices, along_z(): lax.ppermute(block, 'dev', shifts(devices, k))  15.2 us
    ppermute x9, starting transfers between devices, over_column(): lax.ppermute(sums[k], 'dev', shifts(devices, k))  13 us
  transfers between devices with their start and end apart: 76, of which 30 were waited for; matrix products, arithmetic and copies ran while one was open for 4% of the time, Pallas kernels for 34%

profile of v5, /device:TPU:0, one launch (start us, length us, event | category | flops | bytes accessed | tf_op | source)
XLA Modules:
  0.0 316.4 jit_solution(3184995585661227504)
XLA Ops:
  4.2 3.0 collective-permute-start.1
  7.2 2.1 collective-permute-start.4
  10.3 2.8 shard_map.211
  13.9 9.5 %all-to-all-start = ((bf16[32,16,896]{2,1,0:T(8,128)(2,1)}), bf16[32,16,896]{2,1,0:T(8,128)(2,1)S(1)}, u32[]{:S(2)}, u32[]{:S(2)}) async-start(bf16[32,16,896]{2,1,0:T(8,128)(2,1)} %bitcast.12), calls=%async_computation | async-start | bytes 1835008 | tf_op jit(solution)/shard_map/all_to_all | solution.py:417
  23.5 1.8 collective-permute-start.7
  25.3 1.5 collective-permute-start.5
  27.7 13.6 %collective-permute-done.7.refs_5_ = bf16[2,48,1536]{2,1,0:T(8,128)(2,1)S(1)} collective-permute-done((bf16[2,48,1536]{2,1,0:T(8,128)(2,1)S(1)}, bf16[2,48,1536]{2,1,0:T(8,128)(2,1)S(1)}, u32[]{:S(2)}, u32[]{:S(2)}) %collective-permute-start.7) | collective-permute-done | bytes 294944 | tf_op jit(solution)/shard_map/ppermute | solution.py:339
  41.7 7.1 %collective-permute-done.6.refs_4_ = bf16[2,48,1536]{2,1,0:T(8,128)(2,1)S(1)} collective-permute-done((bf16[2,48,1536]{2,1,0:T(8,128)(2,1)S(1)}, bf16[2,48,1536]{2,1,0:T(8,128)(2,1)S(1)}, u32[]{:S(2)}, u32[]{:S(2)}) %collective-permute-start.6) | collective-permute-done | bytes 294944 | tf_op jit(solution)/shard_map/ppermute | solution.py:339
  49.3 1.4 collective-permute-start.8
  52.3 6.1 %collective-permute-done.8.refs_6_ = bf16[2,48,1536]{2,1,0:T(8,128)(2,1)} collective-permute-done((bf16[2,48,1536]{2,1,0:T(8,128)(2,1)S(1)}, bf16[2,48,1536]{2,1,0:T(8,128)(2,1)}, u32[]{:S(2)}, u32[]{:S(2)}) %collective-permute-start.8) | collective-permute-done | bytes 294944 | tf_op jit(solution)/shard_map/ppermute | solution.py:339
  58.4 1.9 collective-permute-done.9.refs_7_
  62.7 3.3 %collective-permute-start.20 = (bf16[48,1536]{1,0:T(8,128)(2,1)S(1)}, bf16[48,1536]{1,0:T(8,128)(2,1)S(1)}, u32[]{:S(2)}, u32[]{:S(2)}) collective-permute-start(bf16[48,1536]{1,0:T(8,128)(2,1)S(1)} %get-tuple-element.240), channel_id=1, source_target_pairs={{0,24},{1,25},{2,26},{3,27},{4,28},{5,29},{6,30},{7,31},{8,0},{9,1... | collective-permute-start | bytes 442376 | tf_op jit(solution)/shard_map/ppermute | solution.py:345
  67.2 9.2 %shard_map.212 = (bf16[768,512]{1,0:T(8,128)(2,1)}, bf16[512,2304]{1,0:T(8,128)(2,1)}, bf16[768,2304]{1,0:T(8,128)(2,1)}, bf16[768,768]{1,0:T(8,128)(2,1)}) custom-call(s32[4]{0:T(128)} %pad_add_fusion.where_ref, bf16[512,896]{1,0:T(8,128)(2,1)} %bitcast.128, f32[12,768]{1,0:T(8,128)} %refs_6_.1, bf16[2,48,1536]{2,1,0:T(8,128)(2,1)} %copy-done.38, ...), custom_call_target="tpu_custom_call" | custom-call | flops 1811939328 | bytes 7077888 | tf_op jit(solution)/shard_map/pallas_call | solution.py:619
  76.4 2.7 collective-permute-done.19
  79.8 1.5 collective-permute-start.21
  82.5 1.5 collective-permute-start.24
  84.0 2.0 collective-permute-start.23
  86.0 5.9 %shard_map.213 = (bf16[384,512]{1,0:T(8,128)(2,1)}, f32[3,8,512]{2,1,0:T(8,128)}, bf16[512,384]{1,0:T(8,128)(2,1)}) custom-call(bf16[512,2304]{1,0:T(8,128)(2,1)} %get-tuple-element.242.q_ref.k_ref.v_ref, bf16[512,2304]{1,0:T(8,128)(2,1)} %get-tuple-element.242.q_ref.k_ref.v_ref, bf16[512,2304]{1,0:T(8,128)(2,1)} %get-tuple-element.242.q_ref.k_ref.v_ref, ...), custom_call_target="tpu_custom_call" | custom-call | flops 805306368 | bytes 5505024 | tf_op jit(solution)/shard_map/pallas_call | solution.py:730
  92.0 4.3 %collective-permute-done.24 = bf16[96,768]{1,0:T(8,128)(2,1)S(1)} collective-permute-done((bf16[96,768]{1,0:T(8,128)(2,1)S(1)}, bf16[96,768]{1,0:T(8,128)(2,1)S(1)}, u32[]{:S(2)}, u32[]{:S(2)}) %collective-permute-start.24) | collective-permute-done | bytes 147488 | tf_op jit(solution)/shard_map/ppermute | solution.py:345
  97.0 2.8 all-to-all-start.1
  100.8 1.5 collective-permute-start.27
  102.3 1.5 collective-permute-start.26
  103.8 10.3 %shard_map.214 = (bf16[384,512]{1,0:T(8,128)(2,1)}, f32[3,8,512]{2,1,0:T(8,128)}, f32[512,768]{1,0:T(8,128)}, bf16[512,768]{1,0:T(8,128)(2,1)}) custom-call(bf16[512,2304]{1,0:T(8,128)(2,1)} %get-tuple-element.242.q_ref.k_ref.v_ref, bf16[512,2304]{1,0:T(8,128)(2,1)} %get-tuple-element.242.q_ref.k_ref.v_ref, ...), custom_call_target="tpu_custom_call" | custom-call | flops 805306368 | bytes 5505024 | tf_op jit(solution)/shard_map/pallas_call | solution.py:730
  114.2 1.9 collective-permute-done.27.refs_4_
  120.2 1.5 collective-permute-start.36
  122.8 10.9 %shard_map.215 = (bf16[512,3072]{1,0:T(8,128)(2,1)}, f32[512,3072]{1,0:T(8,128)}, bf16[768,3072]{1,0:T(8,128)(2,1)}) custom-call(s32[4]{0:T(128)} %pad_add_fusion.where_ref, bf16[512,768]{1,0:T(8,128)(2,1)} %get-tuple-element.260.low_ref, f32[1,3072]{1,0:T(1,128)} %bitcast.152, bf16[4,48,1536]{2,1,0:T(8,128)(2,1)} %copy-done.36, ...), custom_call_target="tpu_custom_call" | custom-call | flops 2415919104 | bytes 14155776 | tf_op jit(solution)/shard_map/pallas_call | solution.py:808
  142.7 6.0 %shard_map.216 = (bf16[4,4,96,768]{3,2,1,0:T(8,128)(2,1)S(1)}, bf16[4,4,96,768]{3,2,1,0:T(8,128)(2,1)S(1)}) custom-call(s32[4]{0:T(128)S(1)} %copy-done.26, bf16[512,3072]{1,0:T(8,128)(2,1)} %get-tuple-element.273.hidden_ref, bf16[512,768]{1,0:T(8,128)(2,1)S(1)} %bitcast.138), custom_call_target="tpu_custom_call" | custom-call | flops 2415919104 | bytes 7864320 | tf_op jit(solution)/shard_map/pallas_call | solution.py:854
  149.5 4.2 %collective-permute-done.45.refs_14_ = bf16[2,96,768]{2,1,0:T(8,128)(2,1)S(1)} collective-permute-done((bf16[2,96,768]{2,1,0:T(8,128)(2,1)}, bf16[2,96,768]{2,1,0:T(8,128)(2,1)S(1)}, u32[]{:S(2)}, u32[]{:S(2)}) %collective-permute-start.45) | collective-permute-done | bytes 294944 | tf_op jit(solution)/shard_map/ppermute | solution.py:339
  156.9 9.6 %shard_map.217 = (bf16[512,768]{1,0:T(8,128)(2,1)S(1)}, bf16[3072,768]{1,0:T(8,128)(2,1)}) custom-call(s32[4]{0:T(128)S(1)} %copy-done.26, bf16[512,3072]{1,0:T(8,128)(2,1)} %get-tuple-element.273.hidden_ref, f32[512,768]{1,0:T(8,128)} %get-tuple-element.289.resid_ref, f32[12,768]{1,0:T(8,128)S(1)} %copy-done.9, ...), custom_call_target="tpu_custom_call" | custom-call | flops 2415919104 | bytes 14155776 | tf_op jit(solution)/shard_map/pallas_call | solution.py:913
  167.9 5.7 %all-to-all-start.2 = ((bf16[32,16,768]{2,1,0:T(8,128)(2,1)}), bf16[32,16,768]{2,1,0:T(8,128)(2,1)S(1)}, u32[]{:S(2)}, u32[]{:S(2)}) async-start(bf16[32,16,768]{2,1,0:T(8,128)(2,1)} %bitcast.139), calls=%async_computation.2 | async-start | bytes 1572864 | tf_op jit(solution)/shard_map/all_to_all | solution.py:417
  173.6 1.6 collective-permute-start.50
  175.2 1.5 collective-permute-start.51
  176.7 18.9 %shard_map.218 = (f32[512,768]{1,0:T(8,128)}, bf16[512,768]{1,0:T(8,128)(2,1)}, f32[8,768]{1,0:T(8,128)}, f32[1,3072]{1,0:T(1,128)}, bf16[4,4,24,3840]{3,2,1,0:T(8,128)(2,1)}, /*index=5*/bf16[4,4,24,3840]{3,2,1,0:T(8,128)(2,1)}) custom-call(s32[4]{0:T(128)} %pad_add_fusion.where_ref, f32[512,3072]{1,0:T(8,128)} %get-tuple-element.288.slope_ref, ...), custom_call_target="tpu_custom_call" | custom-call | flops 7247757312 | bytes 34603008 | tf_op jit(solution)/shard_map/pallas_call | solution.py:991
  195.6 1.8 collective-permute-done.50
  197.5 1.9 fusion.29
  200.6 8.1 %shard_map.219 = (bf16[3,512,384]{2,1,0:T(8,128)(2,1)S(1)}, f32[8,384]{1,0:T(8,128)S(1)}) custom-call(bf16[512,2304]{1,0:T(8,128)(2,1)} %get-tuple-element.242.q_ref.k_ref.v_ref, bf16[512,2304]{1,0:T(8,128)(2,1)} %get-tuple-element.242.q_ref.k_ref.v_ref, bf16[512,2304]{1,0:T(8,128)(2,1)} %get-tuple-element.242.q_ref.k_ref.v_ref, ...), custom_call_target="tpu_custom_call" | custom-call | flops 1409286144 | bytes 6291456 | tf_op jit(solution)/shard_map/pallas_call | solution.py:1076
  209.1 1.4 collective-permute-start.53
  211.1 1.5 collective-permute-start.55
  212.6 2.4 collective-permute-start.56
  215.0 1.5 collective-permute-start.57
  216.4 7.9 %shard_map.220 = (bf16[3,512,384]{2,1,0:T(8,128)(2,1)S(1)}, f32[8,384]{1,0:T(8,128)S(1)}) custom-call(bf16[512,2304]{1,0:T(8,128)(2,1)} %get-tuple-element.242.q_ref.k_ref.v_ref, bf16[512,2304]{1,0:T(8,128)(2,1)} %get-tuple-element.242.q_ref.k_ref.v_ref, bf16[512,2304]{1,0:T(8,128)(2,1)} %get-tuple-element.242.q_ref.k_ref.v_ref, ...), custom_call_target="tpu_custom_call" | custom-call | flops 1409286144 | bytes 6291456 | tf_op jit(solution)/shard_map/pallas_call | solution.py:1076
  226.7 1.5 collective-permute-start.58
  228.9 8.5 %shard_map.221 = bf16[512,896]{1,0:T(8,128)(2,1)} custom-call(bf16[512,896]{1,0:T(8,128)(2,1)S(1)} %bitcast.134, bf16[3,512,384]{2,1,0:T(8,128)(2,1)S(1)} %get-tuple-element.331.d_ref, bf16[3,512,384]{2,1,0:T(8,128)(2,1)S(1)} %get-tuple-element.353.e_ref, f32[512,768]{1,0:T(8,128)S(1)} %copy-done.6, f32[12,768]{1,0:T(8,128)S(1)} %copy-done.10, ...), custom_call_target="tpu_custom_call" | custom-call | flops 1811939328 | bytes 3538944 | tf_op jit(solution)/shard_map/pallas_call | solution.py:1181
  237.4 6.1 %all-to-all-start.3 = ((bf16[32,16,896]{2,1,0:T(8,128)(2,1)}), bf16[32,16,896]{2,1,0:T(8,128)(2,1)S(1)}, u32[]{:S(2)}, u32[]{:S(2)}) async-start(bf16[32,16,896]{2,1,0:T(8,128)(2,1)} %bitcast.56), calls=%async_computation.3 | async-start | bytes 1835008 | tf_op jit(solution)/shard_map/all_to_all | solution.py:417
  243.5 6.1 %shard_map.222 = (bf16[4,4,24,2304]{3,2,1,0:T(8,128)(2,1)}, bf16[4,4,24,2304]{3,2,1,0:T(8,128)(2,1)}) custom-call(s32[4]{0:T(128)} %pad_add_fusion.where_ref, bf16[768,512]{1,0:T(8,128)(2,1)} %get-tuple-element.238.flipped_ref, bf16[3,512,384]{2,1,0:T(8,128)(2,1)} %copy-done.7, bf16[3,512,384]{2,1,0:T(8,128)(2,1)} %copy-done.8), custom_call_target="tpu_custom_call" | custom-call | flops 1811939328 | bytes 9437184 | tf_op jit(solution)/shard_map/pallas_call | solution.py:1120
  249.7 1.9 fusion.27
  253.8 1.6 collective-permute-start.61
  255.4 1.5 collective-permute-start.62
  256.9 6.1 %collective-permute-done.61 = bf16[2,24,2304]{2,1,0:T(8,128)(2,1)S(1)} collective-permute-done((bf16[2,24,2304]{2,1,0:T(8,128)(2,1)S(1)}, bf16[2,24,2304]{2,1,0:T(8,128)(2,1)S(1)}, u32[]{:S(2)}, u32[]{:S(2)}) %collective-permute-start.61) | collective-permute-done | bytes 221216 | tf_op jit(solution)/shard_map/ppermute | solution.py:339
  263.7 2.9 all-to-all-done.3.refs_3_
  266.6 1.5 collective-permute-start.63
  268.1 1.5 collective-permute-start.64
  270.9 2.4 multiply_reduce_fusion.1
  274.0 1.8 collective-permute-start.70
  275.9 2.8 collective-permute-done.65
  283.8 2.0 collective-permute-start.68
  285.8 1.5 multiply_reduce_fusion
  288.7 1.5 shard_map.223
  290.2 6.0 %collective-permute-done.67.refs_1_ = bf16[24,2304]{1,0:T(8,128)(2,1)S(1)} collective-permute-done((bf16[24,2304]{1,0:T(8,128)(2,1)S(1)}, bf16[24,2304]{1,0:T(8,128)(2,1)S(1)}, u32[]{:S(2)}, u32[]{:S(2)}) %collective-permute-start.67) | collective-permute-done | bytes 110624 | tf_op jit(solution)/shard_map/ppermute | solution.py:413
  296.9 2.0 shard_map.225
  298.9 4.3 %all-to-all-start.4 = ((f32[32,4,128]{2,1,0:T(4,128)}), f32[32,4,128]{2,1,0:T(4,128)S(1)}, u32[]{:S(2)}, u32[]{:S(2)}) async-start(f32[32,4,128]{2,1,0:T(4,128)} %get-tuple-element.402), calls=%async_computation.4 | async-start | bytes 131072 | tf_op jit(solution)/shard_map/all_to_all | solution.py:417
  303.3 1.5 shard_map.224
  304.8 5.9 %all-to-all-done.4.packets_ref = f32[32,4,128]{2,1,0:T(4,128)S(1)} async-done(((f32[32,4,128]{2,1,0:T(4,128)}), f32[32,4,128]{2,1,0:T(4,128)S(1)}, u32[]{:S(2)}, u32[]{:S(2)}) %all-to-all-start.4) | async-done | bytes 65568 | tf_op jit(solution)/shard_map/all_to_all | solution.py:417
  311.3 4.9 %shard_map.226 = (f32[1,1]{1,0:T(1,128)}, f32[24,6144]{1,0:T(8,128)}, f32[24,6144]{1,0:T(8,128)}, f32[24,6144]{1,0:T(8,128)}, f32[96,768]{1,0:T(8,128)}, /*index...) custom-call(f32[32,4,128]{2,1,0:T(4,128)} %copy-done.39, ...), custom_call_target="tpu_custom_call" | custom-call | flops 2949120 | bytes 5898240 | tf_op jit(solution)/shard_map/pallas_call | solution.py:1300
  (264 shorter events, 51.8 us)
Async XLA Ops:
  4.2 9.7 %collective-permute-start.1 = (bf16[48,1536]{1,0:T(8,128)(2,1)S(1)}, bf16[48,1536]{1,0:T(8,128)(2,1)S(1)}, u32[]{:S(2)}, u32[]{:S(2)}) collective-permute-start(bf16[48,1536]{1,0:T(8,128)(2,1)S(1)} %get-tuple-element.456), channel_id=1, source_target_pairs={{0,8},{1,9},{2,10},{3,11},{4,12},{5,13},{6,14},{7,15},{8,16},{9,17... | collective-permute-start | bytes 442376 | tf_op jit(solution)/shard_map/ppermute | solution.py:345
  7.2 16.2 %collective-permute-start.4 = (bf16[48,1536]{1,0:T(8,128)(2,1)S(1)}, bf16[48,1536]{1,0:T(8,128)(2,1)S(1)}, u32[]{:S(2)}, u32[]{:S(2)}) collective-permute-start(bf16[48,1536]{1,0:T(8,128)(2,1)S(1)} %get-tuple-element.456), channel_id=1, source_target_pairs={{0,24},{1,25},{2,26},{3,27},{4,28},{5,29},{6,30},{7,31},{8,0},{9,1... | collective-permute-start | bytes 442376 | tf_op jit(solution)/shard_map/ppermute | solution.py:345
  9.3 14.1 %collective-permute-start.3 = (bf16[48,1536]{1,0:T(8,128)(2,1)S(1)}, bf16[48,1536]{1,0:T(8,128)(2,1)S(1)}, u32[]{:S(2)}, u32[]{:S(2)}) collective-permute-start(bf16[48,1536]{1,0:T(8,128)(2,1)S(1)} %get-tuple-element.456), channel_id=1, source_target_pairs={{0,16},{1,17},{2,18},{3,19},{4,20},{5,21},{6,22},{7,23},{8,24},{9,... | collective-permute-start | bytes 442376 | tf_op jit(solution)/shard_map/ppermute | solution.py:345
  13.9 48.8 %all-to-all-start = ((bf16[32,16,896]{2,1,0:T(8,128)(2,1)}), bf16[32,16,896]{2,1,0:T(8,128)(2,1)S(1)}, u32[]{:S(2)}, u32[]{:S(2)}) async-start(bf16[32,16,896]{2,1,0:T(8,128)(2,1)} %bitcast.12), calls=%async_computation | async-start | bytes 1835008 | tf_op jit(solution)/shard_map/all_to_all | solution.py:417
  23.5 17.9 %collective-permute-start.7 = (bf16[2,48,1536]{2,1,0:T(8,128)(2,1)S(1)}, bf16[2,48,1536]{2,1,0:T(8,128)(2,1)S(1)}, u32[]{:S(2)}, u32[]{:S(2)}) collective-permute-start(bf16[2,48,1536]{2,1,0:T(8,128)(2,1)S(1)} %pad_maximum_fusion.8.refs_1_), channel_id=1, source_target_pairs={{0,4},{1,5},{2,6},{3,7},{4,0},{5,1},{6,2},{7,3},{8,12},{9,13},{10,... | collective-permute-start | bytes 884744 | tf_op jit(solution)/shard_map/ppermute | solution.py:339
  25.3 16.4 %collective-permute-start.5 = (bf16[2,48,1536]{2,1,0:T(8,128)(2,1)S(1)}, bf16[2,48,1536]{2,1,0:T(8,128)(2,1)S(1)}, u32[]{:S(2)}, u32[]{:S(2)}) collective-permute-start(bf16[2,48,1536]{2,1,0:T(8,128)(2,1)S(1)} %pad_maximum_fusion.8.refs_1_), channel_id=1, source_target_pairs={{0,2},{1,3},{2,0},{3,1},{4,6},{5,7},{6,4},{7,5},{8,10},{9,11},{10,... | collective-permute-start | bytes 884744 | tf_op jit(solution)/shard_map/ppermute | solution.py:339
  26.8 21.9 %collective-permute-start.6 = (bf16[2,48,1536]{2,1,0:T(8,128)(2,1)S(1)}, bf16[2,48,1536]{2,1,0:T(8,128)(2,1)S(1)}, u32[]{:S(2)}, u32[]{:S(2)}) collective-permute-start(bf16[2,48,1536]{2,1,0:T(8,128)(2,1)S(1)} %pad_maximum_fusion.7.refs_0_), channel_id=1, source_target_pairs={{0,4},{1,5},{2,6},{3,7},{4,0},{5,1},{6,2},{7,3},{8,12},{9,13},{10,... | collective-permute-start | bytes 884744 | tf_op jit(solution)/shard_map/ppermute | solution.py:339
  27.5 21.3 %collective-permute-start.2 = (bf16[2,48,1536]{2,1,0:T(8,128)(2,1)S(1)}, bf16[2,48,1536]{2,1,0:T(8,128)(2,1)S(1)}, u32[]{:S(2)}, u32[]{:S(2)}) collective-permute-start(bf16[2,48,1536]{2,1,0:T(8,128)(2,1)S(1)} %pad_maximum_fusion.7.refs_0_), channel_id=1, source_target_pairs={{0,2},{1,3},{2,0},{3,1},{4,6},{5,7},{6,4},{7,5},{8,10},{9,11},{10,... | collective-permute-start | bytes 884744 | tf_op jit(solution)/shard_map/ppermute | solution.py:339
  27.7 23.0 %collective-permute-start.11 = (bf16[2,48,1536]{2,1,0:T(8,128)(2,1)S(1)}, bf16[2,48,1536]{2,1,0:T(8,128)(2,1)S(1)}, u32[]{:S(2)}, u32[]{:S(2)}) collective-permute-start(bf16[2,48,1536]{2,1,0:T(8,128)(2,1)S(1)} %pad_maximum_fusion.8.refs_1_), channel_id=1, source_target_pairs={{0,1},{1,0},{2,3},{3,2},{4,5},{5,4},{6,7},{7,6},{8,9},{9,8},{10,11... | collective-permute-start | bytes 884744 | tf_op jit(solution)/shard_map/ppermute | solution.py:339
  41.4 9.4 %collective-permute-start.10 = (bf16[2,48,1536]{2,1,0:T(8,128)(2,1)S(1)}, bf16[2,48,1536]{2,1,0:T(8,128)(2,1)S(1)}, u32[]{:S(2)}, u32[]{:S(2)}) collective-permute-start(bf16[2,48,1536]{2,1,0:T(8,128)(2,1)S(1)} %pad_maximum_fusion.7.refs_0_), channel_id=1, source_target_pairs={{0,1},{1,0},{2,3},{3,2},{4,5},{5,4},{6,7},{7,6},{8,9},{9,8},{10,11... | collective-permute-start | bytes 884744 | tf_op jit(solution)/shard_map/ppermute | solution.py:339
  49.3 9.1 %collective-permute-start.8 = (bf16[2,48,1536]{2,1,0:T(8,128)(2,1)S(1)}, bf16[2,48,1536]{2,1,0:T(8,128)(2,1)}, u32[]{:S(2)}, u32[]{:S(2)}) collective-permute-start(bf16[2,48,1536]{2,1,0:T(8,128)(2,1)S(1)} %collective-permute-done.2.refs_2_), channel_id=1, source_target_pairs={{0,4},{1,5},{2,6},{3,7},{4,0},{5,1},{6,2},{7,3},{8,12},{9,13},{10,... | collective-permute-start | bytes 884744 | tf_op jit(solution)/shard_map/ppermute | solution.py:339
  50.8 7.7 %collective-permute-start.15 = (bf16[2,48,1536]{2,1,0:T(8,128)(2,1)S(1)}, bf16[2,48,1536]{2,1,0:T(8,128)(2,1)S(1)}, u32[]{:S(2)}, u32[]{:S(2)}) collective-permute-start(bf16[2,48,1536]{2,1,0:T(8,128)(2,1)S(1)} %collective-permute-done.7.refs_5_), channel_id=1, source_target_pairs={{0,1},{1,0},{2,3},{3,2},{4,5},{5,4},{6,7},{7,6},{8,9},{9,8},{10,11... | collective-permute-start | bytes 884744 | tf_op jit(solution)/shard_map/ppermute | solution.py:339
  51.3 9.1 %collective-permute-start.9 = (bf16[2,48,1536]{2,1,0:T(8,128)(2,1)S(1)}, bf16[2,48,1536]{2,1,0:T(8,128)(2,1)}, u32[]{:S(2)}, u32[]{:S(2)}) collective-permute-start(bf16[2,48,1536]{2,1,0:T(8,128)(2,1)S(1)} %collective-permute-done.7.refs_5_), channel_id=1, source_target_pairs={{0,2},{1,3},{2,0},{3,1},{4,6},{5,7},{6,4},{7,5},{8,10},{9,11},{10,... | collective-permute-start | bytes 884744 | tf_op jit(solution)/shard_map/ppermute | solution.py:339
  62.7 13.6 %collective-permute-start.20 = (bf16[48,1536]{1,0:T(8,128)(2,1)S(1)}, bf16[48,1536]{1,0:T(8,128)(2,1)S(1)}, u32[]{:S(2)}, u32[]{:S(2)}) collective-permute-start(bf16[48,1536]{1,0:T(8,128)(2,1)S(1)} %get-tuple-element.240), channel_id=1, source_target_pairs={{0,24},{1,25},{2,26},{3,27},{4,28},{5,29},{6,30},{7,31},{8,0},{9,1... | collective-permute-start | bytes 442376 | tf_op jit(solution)/shard_map/ppermute | solution.py:345
  66.0 13.0 %collective-permute-start.19 = (bf16[48,1536]{1,0:T(8,128)(2,1)S(1)}, bf16[48,1536]{1,0:T(8,128)(2,1)S(1)}, u32[]{:S(2)}, u32[]{:S(2)}) collective-permute-start(bf16[48,1536]{1,0:T(8,128)(2,1)S(1)} %get-tuple-element.240), channel_id=1, source_target_pairs={{0,16},{1,17},{2,18},{3,19},{4,20},{5,21},{6,22},{7,23},{8,24},{9,... | collective-permute-start | bytes 442376 | tf_op jit(solution)/shard_map/ppermute | solution.py:345
  66.0 13.0 %collective-permute-start.18 = (bf16[48,1536]{1,0:T(8,128)(2,1)S(1)}, bf16[48,1536]{1,0:T(8,128)(2,1)S(1)}, u32[]{:S(2)}, u32[]{:S(2)}) collective-permute-start(bf16[48,1536]{1,0:T(8,128)(2,1)S(1)} %get-tuple-element.240), channel_id=1, source_target_pairs={{0,8},{1,9},{2,10},{3,11},{4,12},{5,13},{6,14},{7,15},{8,16},{9,17... | collective-permute-start | bytes 442376 | tf_op jit(solution)/shard_map/ppermute | solution.py:345
  79.1 17.2 %collective-permute-start.22 = (bf16[4,48,1536]{2,1,0:T(8,128)(2,1)S(1)}, bf16[4,48,1536]{2,1,0:T(8,128)(2,1)S(1)}, u32[]{:S(2)}, u32[]{:S(2)}) collective-permute-start(bf16[4,48,1536]{2,1,0:T(8,128)(2,1)S(1)} %pad_maximum_fusion.2.refs_0_), channel_id=1, source_target_pairs={{0,4},{1,5},{2,6},{3,7},{4,0},{5,1},{6,2},{7,3},{8,12},{9,13},{10,... | collective-permute-start | bytes 1769480 | tf_op jit(solution)/shard_map/ppermute | solution.py:339
  79.8 16.6 %collective-permute-start.21 = (bf16[4,48,1536]{2,1,0:T(8,128)(2,1)S(1)}, bf16[4,48,1536]{2,1,0:T(8,128)(2,1)}, u32[]{:S(2)}, u32[]{:S(2)}) collective-permute-start(bf16[4,48,1536]{2,1,0:T(8,128)(2,1)S(1)} %pad_maximum_fusion.2.refs_0_), channel_id=1, source_target_pairs={{0,2},{1,3},{2,0},{3,1},{4,6},{5,7},{6,4},{7,5},{8,10},{9,11},{10,... | collective-permute-start | bytes 1769480 | tf_op jit(solution)/shard_map/ppermute | solution.py:339
  81.3 10.6 %collective-permute-start.25 = (bf16[96,768]{1,0:T(8,128)(2,1)S(1)}, bf16[96,768]{1,0:T(8,128)(2,1)S(1)}, u32[]{:S(2)}, u32[]{:S(2)}) collective-permute-start(bf16[96,768]{1,0:T(8,128)(2,1)S(1)} %convert_element_type.355), channel_id=1, source_target_pairs={{0,24},{1,25},{2,26},{3,27},{4,28},{5,29},{6,30},{7,31},{8,0},{9,1... | collective-permute-start | bytes 442376 | tf_op jit(solution)/shard_map/ppermute | solution.py:345
  82.5 13.8 %collective-permute-start.24 = (bf16[96,768]{1,0:T(8,128)(2,1)S(1)}, bf16[96,768]{1,0:T(8,128)(2,1)S(1)}, u32[]{:S(2)}, u32[]{:S(2)}) collective-permute-start(bf16[96,768]{1,0:T(8,128)(2,1)S(1)} %convert_element_type.355), channel_id=1, source_target_pairs={{0,16},{1,17},{2,18},{3,19},{4,20},{5,21},{6,22},{7,23},{8,24},{9,... | collective-permute-start | bytes 442376 | tf_op jit(solution)/shard_map/ppermute | solution.py:345
  84.0 12.3 %collective-permute-start.23 = (bf16[96,768]{1,0:T(8,128)(2,1)S(1)}, bf16[96,768]{1,0:T(8,128)(2,1)S(1)}, u32[]{:S(2)}, u32[]{:S(2)}) collective-permute-start(bf16[96,768]{1,0:T(8,128)(2,1)S(1)} %convert_element_type.355), channel_id=1, source_target_pairs={{0,8},{1,9},{2,10},{3,11},{4,12},{5,13},{6,14},{7,15},{8,16},{9,17... | collective-permute-start | bytes 442376 | tf_op jit(solution)/shard_map/ppermute | solution.py:345
  91.9 22.2 %collective-permute-start.28 = (bf16[4,48,1536]{2,1,0:T(8,128)(2,1)S(1)}, bf16[4,48,1536]{2,1,0:T(8,128)(2,1)}, u32[]{:S(2)}, u32[]{:S(2)}) collective-permute-start(bf16[4,48,1536]{2,1,0:T(8,128)(2,1)S(1)} %pad_maximum_fusion.2.refs_0_), channel_id=1, source_target_pairs={{0,1},{1,0},{2,3},{3,2},{4,5},{5,4},{6,7},{7,6},{8,9},{9,8},{10,11... | collective-permute-start | bytes 1769480 | tf_op jit(solution)/shard_map/ppermute | solution.py:339
  96.4 19.7 %collective-permute-start.29 = (bf16[4,48,1536]{2,1,0:T(8,128)(2,1)}, bf16[4,48,1536]{2,1,0:T(8,128)(2,1)}, u32[]{:S(2)}, u32[]{:S(2)}) collective-permute-start(bf16[4,48,1536]{2,1,0:T(8,128)(2,1)} %collective-permute-done.21.refs_1_), channel_id=1, source_target_pairs={{0,1},{1,0},{2,3},{3,2},{4,5},{5,4},{6,7},{7,6},{8,9},{9,8},{10,11... | collective-permute-start | bytes 1769480 | tf_op jit(solution)/shard_map/ppermute | solution.py:339
  96.5 19.6 %collective-permute-start.30 = (bf16[4,48,1536]{2,1,0:T(8,128)(2,1)S(1)}, bf16[4,48,1536]{2,1,0:T(8,128)(2,1)}, u32[]{:S(2)}, u32[]{:S(2)}) collective-permute-start(bf16[4,48,1536]{2,1,0:T(8,128)(2,1)S(1)} %collective-permute-done.22.refs_2_), channel_id=1, source_target_pairs={{0,1},{1,0},{2,3},{3,2},{4,5},{5,4},{6,7},{7,6},{8,9},{9,8},{10,11... | collective-permute-start | bytes 1769480 | tf_op jit(solution)/shard_map/ppermute | solution.py:339
  97.0 43.7 %all-to-all-start.1 = ((bf16[32,16,768]{2,1,0:T(8,128)(2,1)}), bf16[32,16,768]{2,1,0:T(8,128)(2,1)S(1)}, u32[]{:S(2)}, u32[]{:S(2)}) async-start(bf16[32,16,768]{2,1,0:T(8,128)(2,1)} %bitcast.23), calls=%async_computation.1 | async-start | bytes 1572864 | tf_op jit(solution)/shard_map/all_to_all | solution.py:417
  100.8 15.2 %collective-permute-start.27 = (bf16[2,48,1536]{2,1,0:T(8,128)(2,1)S(1)}, bf16[2,48,1536]{2,1,0:T(8,128)(2,1)S(1)}, u32[]{:S(2)}, u32[]{:S(2)}) collective-permute-start(bf16[2,48,1536]{2,1,0:T(8,128)(2,1)S(1)} %slice.197), channel_id=1, source_target_pairs={{0,2},{1,3},{2,0},{3,1},{4,6},{5,7},{6,4},{7,5},{8,10},{9,11},{10,... | collective-permute-start | bytes 884744 | tf_op jit(solution)/shard_map/ppermute | solution.py:339
  102.3 13.7 %collective-permute-start.26 = (bf16[2,48,1536]{2,1,0:T(8,128)(2,1)S(1)}, bf16[2,48,1536]{2,1,0:T(8,128)(2,1)}, u32[]{:S(2)}, u32[]{:S(2)}) collective-permute-start(bf16[2,48,1536]{2,1,0:T(8,128)(2,1)S(1)} %slice.196), channel_id=1, source_target_pairs={{0,4},{1,5},{2,6},{3,7},{4,0},{5,1},{6,2},{7,3},{8,12},{9,13},{10,... | collective-permute-start | bytes 884744 | tf_op jit(solution)/shard_map/ppermute | solution.py:339
  118.1 15.6 %collective-permute-start.35 = (bf16[2,96,768]{2,1,0:T(8,128)(2,1)S(1)}, bf16[2,96,768]{2,1,0:T(8,128)(2,1)}, u32[]{:S(2)}, u32[]{:S(2)}) collective-permute-start(bf16[2,96,768]{2,1,0:T(8,128)(2,1)S(1)} %pad_maximum_fusion.9.refs_0_), channel_id=1, source_target_pairs={{0,4},{1,5},{2,6},{3,7},{4,0},{5,1},{6,2},{7,3},{8,12},{9,13},{10,... | collective-permute-start | bytes 884744 | tf_op jit(solution)/shard_map/ppermute | solution.py:339
  119.5 14.9 %collective-permute-start.33 = (bf16[2,96,768]{2,1,0:T(8,128)(2,1)S(1)}, bf16[2,96,768]{2,1,0:T(8,128)(2,1)}, u32[]{:S(2)}, u32[]{:S(2)}) collective-permute-start(bf16[2,96,768]{2,1,0:T(8,128)(2,1)S(1)} %pad_maximum_fusion.9.refs_0_), channel_id=1, source_target_pairs={{0,2},{1,3},{2,0},{3,1},{4,6},{5,7},{6,4},{7,5},{8,10},{9,11},{10,... | collective-permute-start | bytes 884744 | tf_op jit(solution)/shard_map/ppermute | solution.py:339
  120.2 14.2 %collective-permute-start.36 = (bf16[2,96,768]{2,1,0:T(8,128)(2,1)S(1)}, bf16[2,96,768]{2,1,0:T(8,128)(2,1)}, u32[]{:S(2)}, u32[]{:S(2)}) collective-permute-start(bf16[2,96,768]{2,1,0:T(8,128)(2,1)S(1)} %pad_maximum_fusion.10.refs_1_), channel_id=1, source_target_pairs={{0,4},{1,5},{2,6},{3,7},{4,0},{5,1},{6,2},{7,3},{8,12},{9,13},{10,... | collective-permute-start | bytes 884744 | tf_op jit(solution)/shard_map/ppermute | solution.py:339
  121.7 12.9 %collective-permute-start.34 = (bf16[2,96,768]{2,1,0:T(8,128)(2,1)S(1)}, bf16[2,96,768]{2,1,0:T(8,128)(2,1)S(1)}, u32[]{:S(2)}, u32[]{:S(2)}) collective-permute-start(bf16[2,96,768]{2,1,0:T(8,128)(2,1)S(1)} %pad_maximum_fusion.10.refs_1_), channel_id=1, source_target_pairs={{0,2},{1,3},{2,0},{3,1},{4,6},{5,7},{6,4},{7,5},{8,10},{9,11},{10,... | collective-permute-start | bytes 884744 | tf_op jit(solution)/shard_map/ppermute | solution.py:339
  122.8 14.2 %collective-permute-start.39 = (bf16[2,96,768]{2,1,0:T(8,128)(2,1)S(1)}, bf16[2,96,768]{2,1,0:T(8,128)(2,1)S(1)}, u32[]{:S(2)}, u32[]{:S(2)}) collective-permute-start(bf16[2,96,768]{2,1,0:T(8,128)(2,1)S(1)} %pad_maximum_fusion.9.refs_0_), channel_id=1, source_target_pairs={{0,1},{1,0},{2,3},{3,2},{4,5},{5,4},{6,7},{7,6},{8,9},{9,8},{10,11... | collective-permute-start | bytes 884744 | tf_op jit(solution)/shard_map/ppermute | solution.py:339
  135.3 13.4 %collective-permute-start.41 = (bf16[2,96,768]{2,1,0:T(8,128)(2,1)}, bf16[2,96,768]{2,1,0:T(8,128)(2,1)}, u32[]{:S(2)}, u32[]{:S(2)}) collective-permute-start(bf16[2,96,768]{2,1,0:T(8,128)(2,1)} %collective-permute-done.33.refs_2_), channel_id=1, source_target_pairs={{0,1},{1,0},{2,3},{3,2},{4,5},{5,4},{6,7},{7,6},{8,9},{9,8},{10,11... | collective-permute-start | bytes 884744 | tf_op jit(solution)/shard_map/ppermute | solution.py:339
  135.8 12.9 %collective-permute-start.37 = (bf16[2,96,768]{2,1,0:T(8,128)(2,1)}, bf16[2,96,768]{2,1,0:T(8,128)(2,1)}, u32[]{:S(2)}, u32[]{:S(2)}) collective-permute-start(bf16[2,96,768]{2,1,0:T(8,128)(2,1)} %collective-permute-done.33.refs_2_), channel_id=1, source_target_pairs={{0,4},{1,5},{2,6},{3,7},{4,0},{5,1},{6,2},{7,3},{8,12},{9,13},{10,... | collective-permute-start | bytes 884744 | tf_op jit(solution)/shard_map/ppermute | solution.py:339
  137.7 10.9 %collective-permute-start.43 = (bf16[2,96,768]{2,1,0:T(8,128)(2,1)}, bf16[2,96,768]{2,1,0:T(8,128)(2,1)}, u32[]{:S(2)}, u32[]{:S(2)}) collective-permute-start(bf16[2,96,768]{2,1,0:T(8,128)(2,1)} %collective-permute-done.35.refs_4_), channel_id=1, source_target_pairs={{0,1},{1,0},{2,3},{3,2},{4,5},{5,4},{6,7},{7,6},{8,9},{9,8},{10,11... | collective-permute-start | bytes 884744 | tf_op jit(solution)/shard_map/ppermute | solution.py:339
  138.4 10.2 %collective-permute-start.44 = (bf16[2,96,768]{2,1,0:T(8,128)(2,1)}, bf16[2,96,768]{2,1,0:T(8,128)(2,1)}, u32[]{:S(2)}, u32[]{:S(2)}) collective-permute-start(bf16[2,96,768]{2,1,0:T(8,128)(2,1)} %collective-permute-done.36.refs_5_), channel_id=1, source_target_pairs={{0,1},{1,0},{2,3},{3,2},{4,5},{5,4},{6,7},{7,6},{8,9},{9,8},{10,11... | collective-permute-start | bytes 884744 | tf_op jit(solution)/shard_map/ppermute | solution.py:339
  139.7 9.2 %collective-permute-start.38 = (bf16[2,96,768]{2,1,0:T(8,128)(2,1)}, bf16[2,96,768]{2,1,0:T(8,128)(2,1)}, u32[]{:S(2)}, u32[]{:S(2)}) collective-permute-start(bf16[2,96,768]{2,1,0:T(8,128)(2,1)} %collective-permute-done.36.refs_5_), channel_id=1, source_target_pairs={{0,2},{1,3},{2,0},{3,1},{4,6},{5,7},{6,4},{7,5},{8,10},{9,11},{10,... | collective-permute-start | bytes 884744 | tf_op jit(solution)/shard_map/ppermute | solution.py:339
  148.9 5.4 %collective-permute-start.47 = (bf16[4,4,96,768]{3,2,1,0:T(8,128)(2,1)S(1)}, bf16[4,4,96,768]{3,2,1,0:T(8,128)(2,1)S(1)}, u32[]{:S(2)}, u32[]{:S(2)}) collective-permute-start(bf16[4,4,96,768]{3,2,1,0:T(8,128)(2,1)S(1)} %get-tuple-element.286), channel_id=1, source_target_pairs={{0,1},{1,0},{2,3},{3,2},{4,5},{5,4},{6,7},{7,6},{8,9},{9,8},{10,11... | collective-permute-start | bytes 7077896 | tf_op jit(solution)/shard_map/ppermute | solution.py:339
  149.0 4.8 %collective-permute-start.45 = (bf16[2,96,768]{2,1,0:T(8,128)(2,1)}, bf16[2,96,768]{2,1,0:T(8,128)(2,1)S(1)}, u32[]{:S(2)}, u32[]{:S(2)}) collective-permute-start(bf16[2,96,768]{2,1,0:T(8,128)(2,1)} %collective-permute-done.37.refs_6_), channel_id=1, source_target_pairs={{0,1},{1,0},{2,3},{3,2},{4,5},{5,4},{6,7},{7,6},{8,9},{9,8},{10,11... | collective-permute-start | bytes 884744 | tf_op jit(solution)/shard_map/ppermute | solution.py:339
  154.6 11.9 %collective-permute-start.48 = (bf16[2,96,768]{2,1,0:T(8,128)(2,1)S(1)}, bf16[2,96,768]{2,1,0:T(8,128)(2,1)S(1)}, u32[]{:S(2)}, u32[]{:S(2)}) collective-permute-start(bf16[2,96,768]{2,1,0:T(8,128)(2,1)S(1)} %get-tuple-element.309), channel_id=1, source_target_pairs={{0,4},{1,5},{2,6},{3,7},{4,0},{5,1},{6,2},{7,3},{8,12},{9,13},{10,... | collective-permute-start | bytes 884744 | tf_op jit(solution)/shard_map/ppermute | solution.py:339
  155.7 10.8 %collective-permute-start.49 = (bf16[2,96,768]{2,1,0:T(8,128)(2,1)S(1)}, bf16[2,96,768]{2,1,0:T(8,128)(2,1)S(1)}, u32[]{:S(2)}, u32[]{:S(2)}) collective-permute-start(bf16[2,96,768]{2,1,0:T(8,128)(2,1)S(1)} %get-tuple-element.310), channel_id=1, source_target_pairs={{0,2},{1,3},{2,0},{3,1},{4,6},{5,7},{6,4},{7,5},{8,10},{9,11},{10,... | collective-permute-start | bytes 884744 | tf_op jit(solution)/shard_map/ppermute | solution.py:339
  167.9 29.6 %all-to-all-start.2 = ((bf16[32,16,768]{2,1,0:T(8,128)(2,1)}), bf16[32,16,768]{2,1,0:T(8,128)(2,1)S(1)}, u32[]{:S(2)}, u32[]{:S(2)}) async-start(bf16[32,16,768]{2,1,0:T(8,128)(2,1)} %bitcast.139), calls=%async_computation.2 | async-start | bytes 1572864 | tf_op jit(solution)/shard_map/all_to_all | solution.py:417
  173.6 23.8 %collective-permute-start.50 = (bf16[4,96,768]{2,1,0:T(8,128)(2,1)}, bf16[4,96,768]{2,1,0:T(8,128)(2,1)}, u32[]{:S(2)}, u32[]{:S(2)}) collective-permute-start(bf16[4,96,768]{2,1,0:T(8,128)(2,1)} %get-tuple-element.318), channel_id=1, source_target_pairs={{0,2},{1,3},{2,0},{3,1},{4,6},{5,7},{6,4},{7,5},{8,10},{9,11},{10,... | collective-permute-start | bytes 1769480 | tf_op jit(solution)/shard_map/ppermute | solution.py:339
  175.2 22.3 %collective-permute-start.51 = (bf16[4,96,768]{2,1,0:T(8,128)(2,1)}, bf16[4,96,768]{2,1,0:T(8,128)(2,1)}, u32[]{:S(2)}, u32[]{:S(2)}) collective-permute-start(bf16[4,96,768]{2,1,0:T(8,128)(2,1)} %get-tuple-element.319), channel_id=1, source_target_pairs={{0,4},{1,5},{2,6},{3,7},{4,0},{5,1},{6,2},{7,3},{8,12},{9,13},{10,... | collective-permute-start | bytes 1769480 | tf_op jit(solution)/shard_map/ppermute | solution.py:339
  199.5 9.3 %collective-permute-start.52 = (bf16[4,4,24,3840]{3,2,1,0:T(8,128)(2,1)}, bf16[4,4,24,3840]{3,2,1,0:T(8,128)(2,1)S(1)}, u32[]{:S(2)}, u32[]{:S(2)}) collective-permute-start(bf16[4,4,24,3840]{3,2,1,0:T(8,128)(2,1)} %get-tuple-element.327), channel_id=1, source_target_pairs={{0,1},{1,0},{2,3},{3,2},{4,5},{5,4},{6,7},{7,6},{8,9},{9,8},{10,11... | collective-permute-start | bytes 8847368 | tf_op jit(solution)/shard_map/ppermute | solution.py:339
  209.1 15.3 %collective-permute-start.53 = (bf16[2,24,3840]{2,1,0:T(8,128)(2,1)S(1)}, bf16[2,24,3840]{2,1,0:T(8,128)(2,1)S(1)}, u32[]{:S(2)}, u32[]{:S(2)}) collective-permute-start(bf16[2,24,3840]{2,1,0:T(8,128)(2,1)S(1)} %get-tuple-element.335), channel_id=1, source_target_pairs={{0,4},{1,5},{2,6},{3,7},{4,0},{5,1},{6,2},{7,3},{8,12},{9,13},{10,... | collective-permute-start | bytes 1105928 | tf_op jit(solution)/shard_map/ppermute | solution.py:339
  210.6 13.9 %collective-permute-start.54 = (bf16[2,24,3840]{2,1,0:T(8,128)(2,1)S(1)}, bf16[2,24,3840]{2,1,0:T(8,128)(2,1)S(1)}, u32[]{:S(2)}, u32[]{:S(2)}) collective-permute-start(bf16[2,24,3840]{2,1,0:T(8,128)(2,1)S(1)} %get-tuple-element.336), channel_id=1, source_target_pairs={{0,2},{1,3},{2,0},{3,1},{4,6},{5,7},{6,4},{7,5},{8,10},{9,11},{10,... | collective-permute-start | bytes 1105928 | tf_op jit(solution)/shard_map/ppermute | solution.py:339
  211.1 13.3 %collective-permute-start.55 = (bf16[96,768]{1,0:T(8,128)(2,1)S(1)}, bf16[96,768]{1,0:T(8,128)(2,1)S(1)}, u32[]{:S(2)}, u32[]{:S(2)}) collective-permute-start(bf16[96,768]{1,0:T(8,128)(2,1)S(1)} %get-tuple-element.340), channel_id=1, source_target_pairs={{0,8},{1,9},{2,10},{3,11},{4,12},{5,13},{6,14},{7,15},{8,16},{9,17... | collective-permute-start | bytes 442376 | tf_op jit(solution)/shard_map/ppermute | solution.py:413
  212.6 11.8 %collective-permute-start.56 = (bf16[96,768]{1,0:T(8,128)(2,1)S(1)}, bf16[96,768]{1,0:T(8,128)(2,1)S(1)}, u32[]{:S(2)}, u32[]{:S(2)}) collective-permute-start(bf16[96,768]{1,0:T(8,128)(2,1)S(1)} %get-tuple-element.341), channel_id=1, source_target_pairs={{0,16},{1,17},{2,18},{3,19},{4,20},{5,21},{6,22},{7,23},{8,24},{9,... | collective-permute-start | bytes 442376 | tf_op jit(solution)/shard_map/ppermute | solution.py:413
  215.0 9.5 %collective-permute-start.57 = (bf16[96,768]{1,0:T(8,128)(2,1)S(1)}, bf16[96,768]{1,0:T(8,128)(2,1)S(1)}, u32[]{:S(2)}, u32[]{:S(2)}) collective-permute-start(bf16[96,768]{1,0:T(8,128)(2,1)S(1)} %get-tuple-element.342), channel_id=1, source_target_pairs={{0,24},{1,25},{2,26},{3,27},{4,28},{5,29},{6,30},{7,31},{8,0},{9,1... | collective-permute-start | bytes 442376 | tf_op jit(solution)/shard_map/ppermute | solution.py:413
  226.7 22.9 %collective-permute-start.58 = (bf16[4,24,3840]{2,1,0:T(8,128)(2,1)}, bf16[4,24,3840]{2,1,0:T(8,128)(2,1)S(1)}, u32[]{:S(2)}, u32[]{:S(2)}) collective-permute-start(bf16[4,24,3840]{2,1,0:T(8,128)(2,1)} %pad_maximum_fusion), channel_id=1, source_target_pairs={{0,2},{1,3},{2,0},{3,1},{4,6},{5,7},{6,4},{7,5},{8,10},{9,11},{10,... | collective-permute-start | bytes 2211848 | tf_op jit(solution)/shard_map/ppermute | solution.py:339
  228.2 21.4 %collective-permute-start.59 = (bf16[4,24,3840]{2,1,0:T(8,128)(2,1)}, bf16[4,24,3840]{2,1,0:T(8,128)(2,1)}, u32[]{:S(2)}, u32[]{:S(2)}) collective-permute-start(bf16[4,24,3840]{2,1,0:T(8,128)(2,1)} %pad_maximum_fusion.1), channel_id=1, source_target_pairs={{0,4},{1,5},{2,6},{3,7},{4,0},{5,1},{6,2},{7,3},{8,12},{9,13},{10,... | collective-permute-start | bytes 2211848 | tf_op jit(solution)/shard_map/ppermute | solution.py:339
  237.4 29.3 %all-to-all-start.3 = ((bf16[32,16,896]{2,1,0:T(8,128)(2,1)}), bf16[32,16,896]{2,1,0:T(8,128)(2,1)S(1)}, u32[]{:S(2)}, u32[]{:S(2)}) async-start(bf16[32,16,896]{2,1,0:T(8,128)(2,1)} %bitcast.56), calls=%async_computation.3 | async-start | bytes 1835008 | tf_op jit(solution)/shard_map/all_to_all | solution.py:417
  253.8 9.2 %collective-permute-start.61 = (bf16[2,24,2304]{2,1,0:T(8,128)(2,1)S(1)}, bf16[2,24,2304]{2,1,0:T(8,128)(2,1)S(1)}, u32[]{:S(2)}, u32[]{:S(2)}) collective-permute-start(bf16[2,24,2304]{2,1,0:T(8,128)(2,1)S(1)} %get-tuple-element.367), channel_id=1, source_target_pairs={{0,4},{1,5},{2,6},{3,7},{4,0},{5,1},{6,2},{7,3},{8,12},{9,13},{10,... | collective-permute-start | bytes 663560 | tf_op jit(solution)/shard_map/ppermute | solution.py:339
  255.4 8.0 %collective-permute-start.62 = (bf16[2,24,2304]{2,1,0:T(8,128)(2,1)S(1)}, bf16[2,24,2304]{2,1,0:T(8,128)(2,1)S(1)}, u32[]{:S(2)}, u32[]{:S(2)}) collective-permute-start(bf16[2,24,2304]{2,1,0:T(8,128)(2,1)S(1)} %get-tuple-element.368), channel_id=1, source_target_pairs={{0,2},{1,3},{2,0},{3,1},{4,6},{5,7},{6,4},{7,5},{8,10},{9,11},{10,... | collective-permute-start | bytes 663560 | tf_op jit(solution)/shard_map/ppermute | solution.py:339
  266.6 12.1 %collective-permute-start.63 = (bf16[4,24,2304]{2,1,0:T(8,128)(2,1)S(1)}, bf16[4,24,2304]{2,1,0:T(8,128)(2,1)S(1)}, u32[]{:S(2)}, u32[]{:S(2)}) collective-permute-start(bf16[4,24,2304]{2,1,0:T(8,128)(2,1)S(1)} %pad_maximum_fusion.5), channel_id=1, source_target_pairs={{0,2},{1,3},{2,0},{3,1},{4,6},{5,7},{6,4},{7,5},{8,10},{9,11},{10,... | collective-permute-start | bytes 1327112 | tf_op jit(solution)/shard_map/ppermute | solution.py:339
  268.1 11.8 %collective-permute-start.64 = (bf16[4,24,2304]{2,1,0:T(8,128)(2,1)S(1)}, bf16[4,24,2304]{2,1,0:T(8,128)(2,1)S(1)}, u32[]{:S(2)}, u32[]{:S(2)}) collective-permute-start(bf16[4,24,2304]{2,1,0:T(8,128)(2,1)S(1)} %pad_maximum_fusion.6), channel_id=1, source_target_pairs={{0,4},{1,5},{2,6},{3,7},{4,0},{5,1},{6,2},{7,3},{8,12},{9,13},{10,... | collective-permute-start | bytes 1327112 | tf_op jit(solution)/shard_map/ppermute | solution.py:339
  269.6 9.1 %collective-permute-start.65 = (bf16[24,3840]{1,0:T(8,128)(2,1)}, bf16[24,3840]{1,0:T(8,128)(2,1)S(1)}, u32[]{:S(2)}, u32[]{:S(2)}) collective-permute-start(bf16[24,3840]{1,0:T(8,128)(2,1)} %get-tuple-element.378), channel_id=1, source_target_pairs={{0,8},{1,9},{2,10},{3,11},{4,12},{5,13},{6,14},{7,15},{8,16},{9,17... | collective-permute-start | bytes 552968 | tf_op jit(solution)/shard_map/ppermute | solution.py:413
  273.4 12.5 %collective-permute-start.69 = (bf16[24,3840]{1,0:T(8,128)(2,1)}, bf16[24,3840]{1,0:T(8,128)(2,1)S(1)}, u32[]{:S(2)}, u32[]{:S(2)}) collective-permute-start(bf16[24,3840]{1,0:T(8,128)(2,1)} %get-tuple-element.387), channel_id=1, source_target_pairs={{0,16},{1,17},{2,18},{3,19},{4,20},{5,21},{6,22},{7,23},{8,24},{9,... | collective-permute-start | bytes 552968 | tf_op jit(solution)/shard_map/ppermute | solution.py:413
  274.0 11.8 %collective-permute-start.70 = (bf16[24,3840]{1,0:T(8,128)(2,1)}, bf16[24,3840]{1,0:T(8,128)(2,1)S(1)}, u32[]{:S(2)}, u32[]{:S(2)}) collective-permute-start(bf16[24,3840]{1,0:T(8,128)(2,1)} %get-tuple-element.388), channel_id=1, source_target_pairs={{0,24},{1,25},{2,26},{3,27},{4,28},{5,29},{6,30},{7,31},{8,0},{9,1... | collective-permute-start | bytes 552968 | tf_op jit(solution)/shard_map/ppermute | solution.py:413
  282.0 8.2 %collective-permute-start.66 = (bf16[24,2304]{1,0:T(8,128)(2,1)S(1)}, bf16[24,2304]{1,0:T(8,128)(2,1)S(1)}, u32[]{:S(2)}, u32[]{:S(2)}) collective-permute-start(bf16[24,2304]{1,0:T(8,128)(2,1)S(1)} %get-tuple-element.382), channel_id=1, source_target_pairs={{0,8},{1,9},{2,10},{3,11},{4,12},{5,13},{6,14},{7,15},{8,16},{9,17... | collective-permute-start | bytes 331784 | tf_op jit(solution)/shard_map/ppermute | solution.py:413
  283.2 13.1 %collective-permute-start.67 = (bf16[24,2304]{1,0:T(8,128)(2,1)S(1)}, bf16[24,2304]{1,0:T(8,128)(2,1)S(1)}, u32[]{:S(2)}, u32[]{:S(2)}) collective-permute-start(bf16[24,2304]{1,0:T(8,128)(2,1)S(1)} %get-tuple-element.383), channel_id=1, source_target_pairs={{0,16},{1,17},{2,18},{3,19},{4,20},{5,21},{6,22},{7,23},{8,24},{9,... | collective-permute-start | bytes 331784 | tf_op jit(solution)/shard_map/ppermute | solution.py:413
  283.8 12.4 %collective-permute-start.68 = (bf16[24,2304]{1,0:T(8,128)(2,1)S(1)}, bf16[24,2304]{1,0:T(8,128)(2,1)S(1)}, u32[]{:S(2)}, u32[]{:S(2)}) collective-permute-start(bf16[24,2304]{1,0:T(8,128)(2,1)S(1)} %get-tuple-element.384), channel_id=1, source_target_pairs={{0,24},{1,25},{2,26},{3,27},{4,28},{5,29},{6,30},{7,31},{8,0},{9,1... | collective-permute-start | bytes 331784 | tf_op jit(solution)/shard_map/ppermute | solution.py:413
  298.9 11.7 %all-to-all-start.4 = ((f32[32,4,128]{2,1,0:T(4,128)}), f32[32,4,128]{2,1,0:T(4,128)S(1)}, u32[]{:S(2)}, u32[]{:S(2)}) async-start(f32[32,4,128]{2,1,0:T(4,128)} %get-tuple-element.402), calls=%async_computation.4 | async-start | bytes 131072 | tf_op jit(solution)/shard_map/all_to_all | solution.py:417
  (72 other events, 590.8 us)

commit v6 on v5

--- a/solution.py
+++ b/solution.py
@@ -1241,7 +1241,7 @@
     rows, columns = wide[0].shape
     down_rows, feature = down[0].shape
     vector_rows = vector[0].shape[0]
-    steps = 4
+    steps = 2
     tile, down_tile = columns // steps, down_rows // steps
     first_columns = first_grad.shape[1]
 

time: 318 us -> 316 us (level)
  no operation moved by 1% of the time
where the time goes in v6:
time: 316 us; the launch traced here: 315 us
  Pallas kernels  113 us (36%)
  starting transfers between devices  95.3 us (30%)
  waiting for transfers between devices  76.6 us (24%)
  other arithmetic  15.9 us (5%)
  local copies, waits for them, and re-layouts  11.3 us (4%)
  between operations  3.22 us (1%)
    ppermute x52, waiting for transfers between devices, send(): return lax.ppermute(value, 'dev', flips(lax.axis_size('dev'), mask))  50 us
    ppermute x52, starting transfers between devices, send(): return lax.ppermute(value, 'dev', flips(lax.axis_size('dev'), mask))  38.3 us
    all_to_all x5, starting transfers between devices, exchange(): return lax.all_to_all(rows, 'dev', split_axis=0, concat_axis=0, tiled=True)  28.4 us
    pallas_call x1, Pallas kernels, feed_back(): pl.pallas_call(kernel, grid=(steps + 1,), out_shape=[shaped((count, featu...  18.9 us
    pallas_call x2, Pallas kernels, attend(): pl.pallas_call(kernel, grid=(pairs,), out_shape=[shaped((pairs * 128, cou...  16.2 us
    pallas_call x2, Pallas kernels, attend_back(): pl.pallas_call(kernel, grid=(pairs,), out_shape=[shaped((3, count, wide),...  16 us
    ppermute x9, starting transfers between devices, along_z(): lax.ppermute(block, 'dev', shifts(devices, k))  15.2 us
    ppermute x9, starting transfers between devices, over_column(): lax.ppermute(sums[k], 'dev', shifts(devices, k))  13 us
  transfers between devices with their start and end apart: 76, of which 30 were waited for; matrix products, arithmetic and copies ran while one was open for 4% of the time, Pallas kernels for 34%

profile of v6, /device:TPU:0, one launch (start us, length us, event | category | flops | bytes accessed | tf_op | source)
XLA Modules:
  0.0 315.3 jit_solution(12973667903145832645)
XLA Ops:
  4.2 3.0 collective-permute-start.1
  7.2 2.1 collective-permute-start.4
  10.3 2.8 shard_map.211
  13.9 9.5 %all-to-all-start = ((bf16[32,16,896]{2,1,0:T(8,128)(2,1)}), bf16[32,16,896]{2,1,0:T(8,128)(2,1)S(1)}, u32[]{:S(2)}, u32[]{:S(2)}) async-start(bf16[32,16,896]{2,1,0:T(8,128)(2,1)} %bitcast.12), calls=%async_computation | async-start | bytes 1835008 | tf_op jit(solution)/shard_map/all_to_all | solution.py:417
  23.5 1.8 collective-permute-start.7
  25.3 1.5 collective-permute-start.5
  27.7 13.6 %collective-permute-done.7.refs_5_ = bf16[2,48,1536]{2,1,0:T(8,128)(2,1)S(1)} collective-permute-done((bf16[2,48,1536]{2,1,0:T(8,128)(2,1)S(1)}, bf16[2,48,1536]{2,1,0:T(8,128)(2,1)S(1)}, u32[]{:S(2)}, u32[]{:S(2)}) %collective-permute-start.7) | collective-permute-done | bytes 294944 | tf_op jit(solution)/shard_map/ppermute | solution.py:339
  41.7 7.1 %collective-permute-done.6.refs_4_ = bf16[2,48,1536]{2,1,0:T(8,128)(2,1)S(1)} collective-permute-done((bf16[2,48,1536]{2,1,0:T(8,128)(2,1)S(1)}, bf16[2,48,1536]{2,1,0:T(8,128)(2,1)S(1)}, u32[]{:S(2)}, u32[]{:S(2)}) %collective-permute-start.6) | collective-permute-done | bytes 294944 | tf_op jit(solution)/shard_map/ppermute | solution.py:339
  49.3 1.4 collective-permute-start.8
  52.3 6.1 %collective-permute-done.8.refs_6_ = bf16[2,48,1536]{2,1,0:T(8,128)(2,1)} collective-permute-done((bf16[2,48,1536]{2,1,0:T(8,128)(2,1)S(1)}, bf16[2,48,1536]{2,1,0:T(8,128)(2,1)}, u32[]{:S(2)}, u32[]{:S(2)}) %collective-permute-start.8) | collective-permute-done | bytes 294944 | tf_op jit(solution)/shard_map/ppermute | solution.py:339
  58.4 1.9 collective-permute-done.9.refs_7_
  62.7 3.3 %collective-permute-start.20 = (bf16[48,1536]{1,0:T(8,128)(2,1)S(1)}, bf16[48,1536]{1,0:T(8,128)(2,1)S(1)}, u32[]{:S(2)}, u32[]{:S(2)}) collective-permute-start(bf16[48,1536]{1,0:T(8,128)(2,1)S(1)} %get-tuple-element.240), channel_id=1, source_target_pairs={{0,24},{1,25},{2,26},{3,27},{4,28},{5,29},{6,30},{7,31},{8,0},{9,1... | collective-permute-start | bytes 442376 | tf_op jit(solution)/shard_map/ppermute | solution.py:345
  67.2 9.2 %shard_map.212 = (bf16[768,512]{1,0:T(8,128)(2,1)}, bf16[512,2304]{1,0:T(8,128)(2,1)}, bf16[768,2304]{1,0:T(8,128)(2,1)}, bf16[768,768]{1,0:T(8,128)(2,1)}) custom-call(s32[4]{0:T(128)} %pad_add_fusion.where_ref, bf16[512,896]{1,0:T(8,128)(2,1)} %bitcast.128, f32[12,768]{1,0:T(8,128)} %refs_6_.1, bf16[2,48,1536]{2,1,0:T(8,128)(2,1)} %copy-done.38, ...), custom_call_target="tpu_custom_call" | custom-call | flops 1811939328 | bytes 7077888 | tf_op jit(solution)/shard_map/pallas_call | solution.py:619
  76.4 2.7 collective-permute-done.19
  79.8 1.5 collective-permute-start.21
  82.5 1.5 collective-permute-start.24
  84.0 2.0 collective-permute-start.23
  86.0 5.9 %shard_map.213 = (bf16[384,512]{1,0:T(8,128)(2,1)}, f32[3,8,512]{2,1,0:T(8,128)}, bf16[512,384]{1,0:T(8,128)(2,1)}) custom-call(bf16[512,2304]{1,0:T(8,128)(2,1)} %get-tuple-element.242.q_ref.k_ref.v_ref, bf16[512,2304]{1,0:T(8,128)(2,1)} %get-tuple-element.242.q_ref.k_ref.v_ref, bf16[512,2304]{1,0:T(8,128)(2,1)} %get-tuple-element.242.q_ref.k_ref.v_ref, ...), custom_call_target="tpu_custom_call" | custom-call | flops 805306368 | bytes 5505024 | tf_op jit(solution)/shard_map/pallas_call | solution.py:730
  92.0 4.3 %collective-permute-done.24 = bf16[96,768]{1,0:T(8,128)(2,1)S(1)} collective-permute-done((bf16[96,768]{1,0:T(8,128)(2,1)S(1)}, bf16[96,768]{1,0:T(8,128)(2,1)S(1)}, u32[]{:S(2)}, u32[]{:S(2)}) %collective-permute-start.24) | collective-permute-done | bytes 147488 | tf_op jit(solution)/shard_map/ppermute | solution.py:345
  97.0 2.8 all-to-all-start.1
  100.8 1.5 collective-permute-start.27
  102.3 1.5 collective-permute-start.26
  103.8 10.3 %shard_map.214 = (bf16[384,512]{1,0:T(8,128)(2,1)}, f32[3,8,512]{2,1,0:T(8,128)}, f32[512,768]{1,0:T(8,128)}, bf16[512,768]{1,0:T(8,128)(2,1)}) custom-call(bf16[512,2304]{1,0:T(8,128)(2,1)} %get-tuple-element.242.q_ref.k_ref.v_ref, bf16[512,2304]{1,0:T(8,128)(2,1)} %get-tuple-element.242.q_ref.k_ref.v_ref, ...), custom_call_target="tpu_custom_call" | custom-call | flops 805306368 | bytes 5505024 | tf_op jit(solution)/shard_map/pallas_call | solution.py:730
  114.2 1.9 collective-permute-done.27.refs_4_
  120.2 1.5 collective-permute-start.36
  122.8 10.9 %shard_map.215 = (bf16[512,3072]{1,0:T(8,128)(2,1)}, f32[512,3072]{1,0:T(8,128)}, bf16[768,3072]{1,0:T(8,128)(2,1)}) custom-call(s32[4]{0:T(128)} %pad_add_fusion.where_ref, bf16[512,768]{1,0:T(8,128)(2,1)} %get-tuple-element.260.low_ref, f32[1,3072]{1,0:T(1,128)} %bitcast.152, bf16[4,48,1536]{2,1,0:T(8,128)(2,1)} %copy-done.36, ...), custom_call_target="tpu_custom_call" | custom-call | flops 2415919104 | bytes 14155776 | tf_op jit(solution)/shard_map/pallas_call | solution.py:808
  142.7 6.0 %shard_map.216 = (bf16[4,4,96,768]{3,2,1,0:T(8,128)(2,1)S(1)}, bf16[4,4,96,768]{3,2,1,0:T(8,128)(2,1)S(1)}) custom-call(s32[4]{0:T(128)S(1)} %copy-done.26, bf16[512,3072]{1,0:T(8,128)(2,1)} %get-tuple-element.273.hidden_ref, bf16[512,768]{1,0:T(8,128)(2,1)S(1)} %bitcast.138), custom_call_target="tpu_custom_call" | custom-call | flops 2415919104 | bytes 7864320 | tf_op jit(solution)/shard_map/pallas_call | solution.py:854
  149.5 4.2 %collective-permute-done.45.refs_14_ = bf16[2,96,768]{2,1,0:T(8,128)(2,1)S(1)} collective-permute-done((bf16[2,96,768]{2,1,0:T(8,128)(2,1)}, bf16[2,96,768]{2,1,0:T(8,128)(2,1)S(1)}, u32[]{:S(2)}, u32[]{:S(2)}) %collective-permute-start.45) | collective-permute-done | bytes 294944 | tf_op jit(solution)/shard_map/ppermute | solution.py:339
  156.9 9.6 %shard_map.217 = (bf16[512,768]{1,0:T(8,128)(2,1)S(1)}, bf16[3072,768]{1,0:T(8,128)(2,1)}) custom-call(s32[4]{0:T(128)S(1)} %copy-done.26, bf16[512,3072]{1,0:T(8,128)(2,1)} %get-tuple-element.273.hidden_ref, f32[512,768]{1,0:T(8,128)} %get-tuple-element.289.resid_ref, f32[12,768]{1,0:T(8,128)S(1)} %copy-done.9, ...), custom_call_target="tpu_custom_call" | custom-call | flops 2415919104 | bytes 14155776 | tf_op jit(solution)/shard_map/pallas_call | solution.py:913
  167.9 5.7 %all-to-all-start.2 = ((bf16[32,16,768]{2,1,0:T(8,128)(2,1)}), bf16[32,16,768]{2,1,0:T(8,128)(2,1)S(1)}, u32[]{:S(2)}, u32[]{:S(2)}) async-start(bf16[32,16,768]{2,1,0:T(8,128)(2,1)} %bitcast.139), calls=%async_computation.2 | async-start | bytes 1572864 | tf_op jit(solution)/shard_map/all_to_all | solution.py:417
  173.6 1.6 collective-permute-start.50
  175.2 1.5 collective-permute-start.51
  176.7 18.9 %shard_map.218 = (f32[512,768]{1,0:T(8,128)}, bf16[512,768]{1,0:T(8,128)(2,1)}, f32[8,768]{1,0:T(8,128)}, f32[1,3072]{1,0:T(1,128)}, bf16[4,4,24,3840]{3,2,1,0:T(8,128)(2,1)}, /*index=5*/bf16[4,4,24,3840]{3,2,1,0:T(8,128)(2,1)}) custom-call(s32[4]{0:T(128)} %pad_add_fusion.where_ref, f32[512,3072]{1,0:T(8,128)} %get-tuple-element.288.slope_ref, ...), custom_call_target="tpu_custom_call" | custom-call | flops 7247757312 | bytes 34603008 | tf_op jit(solution)/shard_map/pallas_call | solution.py:991
  195.6 1.8 collective-permute-done.50
  197.5 1.9 fusion.29
  200.6 8.1 %shard_map.219 = (bf16[3,512,384]{2,1,0:T(8,128)(2,1)S(1)}, f32[8,384]{1,0:T(8,128)S(1)}) custom-call(bf16[512,2304]{1,0:T(8,128)(2,1)} %get-tuple-element.242.q_ref.k_ref.v_ref, bf16[512,2304]{1,0:T(8,128)(2,1)} %get-tuple-element.242.q_ref.k_ref.v_ref, bf16[512,2304]{1,0:T(8,128)(2,1)} %get-tuple-element.242.q_ref.k_ref.v_ref, ...), custom_call_target="tpu_custom_call" | custom-call | flops 1409286144 | bytes 6291456 | tf_op jit(solution)/shard_map/pallas_call | solution.py:1076
  209.1 1.4 collective-permute-start.53
  211.1 1.5 collective-permute-start.55
  212.6 2.4 collective-permute-start.56
  215.0 1.5 collective-permute-start.57
  216.4 7.9 %shard_map.220 = (bf16[3,512,384]{2,1,0:T(8,128)(2,1)S(1)}, f32[8,384]{1,0:T(8,128)S(1)}) custom-call(bf16[512,2304]{1,0:T(8,128)(2,1)} %get-tuple-element.242.q_ref.k_ref.v_ref, bf16[512,2304]{1,0:T(8,128)(2,1)} %get-tuple-element.242.q_ref.k_ref.v_ref, bf16[512,2304]{1,0:T(8,128)(2,1)} %get-tuple-element.242.q_ref.k_ref.v_ref, ...), custom_call_target="tpu_custom_call" | custom-call | flops 1409286144 | bytes 6291456 | tf_op jit(solution)/shard_map/pallas_call | solution.py:1076
  226.7 1.5 collective-permute-start.58
  228.9 8.5 %shard_map.221 = bf16[512,896]{1,0:T(8,128)(2,1)} custom-call(bf16[512,896]{1,0:T(8,128)(2,1)S(1)} %bitcast.134, bf16[3,512,384]{2,1,0:T(8,128)(2,1)S(1)} %get-tuple-element.331.d_ref, bf16[3,512,384]{2,1,0:T(8,128)(2,1)S(1)} %get-tuple-element.353.e_ref, f32[512,768]{1,0:T(8,128)S(1)} %copy-done.6, f32[12,768]{1,0:T(8,128)S(1)} %copy-done.10, ...), custom_call_target="tpu_custom_call" | custom-call | flops 1811939328 | bytes 3538944 | tf_op jit(solution)/shard_map/pallas_call | solution.py:1181
  237.4 6.1 %all-to-all-start.3 = ((bf16[32,16,896]{2,1,0:T(8,128)(2,1)}), bf16[32,16,896]{2,1,0:T(8,128)(2,1)S(1)}, u32[]{:S(2)}, u32[]{:S(2)}) async-start(bf16[32,16,896]{2,1,0:T(8,128)(2,1)} %bitcast.56), calls=%async_computation.3 | async-start | bytes 1835008 | tf_op jit(solution)/shard_map/all_to_all | solution.py:417
  243.5 6.1 %shard_map.222 = (bf16[4,4,24,2304]{3,2,1,0:T(8,128)(2,1)}, bf16[4,4,24,2304]{3,2,1,0:T(8,128)(2,1)}) custom-call(s32[4]{0:T(128)} %pad_add_fusion.where_ref, bf16[768,512]{1,0:T(8,128)(2,1)} %get-tuple-element.238.flipped_ref, bf16[3,512,384]{2,1,0:T(8,128)(2,1)} %copy-done.7, bf16[3,512,384]{2,1,0:T(8,128)(2,1)} %copy-done.8), custom_call_target="tpu_custom_call" | custom-call | flops 1811939328 | bytes 9437184 | tf_op jit(solution)/shard_map/pallas_call | solution.py:1120
  249.7 1.9 fusion.27
  253.8 1.6 collective-permute-start.61
  255.4 1.5 collective-permute-start.62
  256.9 6.1 %collective-permute-done.61 = bf16[2,24,2304]{2,1,0:T(8,128)(2,1)S(1)} collective-permute-done((bf16[2,24,2304]{2,1,0:T(8,128)(2,1)S(1)}, bf16[2,24,2304]{2,1,0:T(8,128)(2,1)S(1)}, u32[]{:S(2)}, u32[]{:S(2)}) %collective-permute-start.61) | collective-permute-done | bytes 221216 | tf_op jit(solution)/shard_map/ppermute | solution.py:339
  263.7 2.9 all-to-all-done.3.refs_3_
  266.6 1.5 collective-permute-start.63
  268.1 1.5 collective-permute-start.64
  270.9 2.4 multiply_reduce_fusion.1
  274.0 1.8 collective-permute-start.70
  275.9 2.8 collective-permute-done.65
  283.8 2.0 collective-permute-start.68
  285.8 1.5 multiply_reduce_fusion
  288.7 1.5 shard_map.223
  290.2 6.0 %collective-permute-done.67.refs_1_ = bf16[24,2304]{1,0:T(8,128)(2,1)S(1)} collective-permute-done((bf16[24,2304]{1,0:T(8,128)(2,1)S(1)}, bf16[24,2304]{1,0:T(8,128)(2,1)S(1)}, u32[]{:S(2)}, u32[]{:S(2)}) %collective-permute-start.67) | collective-permute-done | bytes 110624 | tf_op jit(solution)/shard_map/ppermute | solution.py:413
  296.9 2.0 shard_map.225
  298.9 4.3 %all-to-all-start.4 = ((f32[32,4,128]{2,1,0:T(4,128)}), f32[32,4,128]{2,1,0:T(4,128)S(1)}, u32[]{:S(2)}, u32[]{:S(2)}) async-start(f32[32,4,128]{2,1,0:T(4,128)} %get-tuple-element.402), calls=%async_computation.4 | async-start | bytes 131072 | tf_op jit(solution)/shard_map/all_to_all | solution.py:417
  303.3 1.5 shard_map.224
  304.8 5.9 %all-to-all-done.4.packets_ref = f32[32,4,128]{2,1,0:T(4,128)S(1)} async-done(((f32[32,4,128]{2,1,0:T(4,128)}), f32[32,4,128]{2,1,0:T(4,128)S(1)}, u32[]{:S(2)}, u32[]{:S(2)}) %all-to-all-start.4) | async-done | bytes 65568 | tf_op jit(solution)/shard_map/all_to_all | solution.py:417
  311.3 3.8 %shard_map.226 = (f32[1,1]{1,0:T(1,128)}, f32[24,6144]{1,0:T(8,128)}, f32[24,6144]{1,0:T(8,128)}, f32[24,6144]{1,0:T(8,128)}, f32[96,768]{1,0:T(8,128)}, /*index...) custom-call(f32[32,4,128]{2,1,0:T(4,128)} %copy-done.39, ...), custom_call_target="tpu_custom_call" | custom-call | flops 2949120 | bytes 5898240 | tf_op jit(solution)/shard_map/pallas_call | solution.py:1300
  (264 shorter events, 51.8 us)
Async XLA Ops:
  4.2 9.7 %collective-permute-start.1 = (bf16[48,1536]{1,0:T(8,128)(2,1)S(1)}, bf16[48,1536]{1,0:T(8,128)(2,1)S(1)}, u32[]{:S(2)}, u32[]{:S(2)}) collective-permute-start(bf16[48,1536]{1,0:T(8,128)(2,1)S(1)} %get-tuple-element.456), channel_id=1, source_target_pairs={{0,8},{1,9},{2,10},{3,11},{4,12},{5,13},{6,14},{7,15},{8,16},{9,17... | collective-permute-start | bytes 442376 | tf_op jit(solution)/shard_map/ppermute | solution.py:345
  7.2 16.2 %collective-permute-start.4 = (bf16[48,1536]{1,0:T(8,128)(2,1)S(1)}, bf16[48,1536]{1,0:T(8,128)(2,1)S(1)}, u32[]{:S(2)}, u32[]{:S(2)}) collective-permute-start(bf16[48,1536]{1,0:T(8,128)(2,1)S(1)} %get-tuple-element.456), channel_id=1, source_target_pairs={{0,24},{1,25},{2,26},{3,27},{4,28},{5,29},{6,30},{7,31},{8,0},{9,1... | collective-permute-start | bytes 442376 | tf_op jit(solution)/shard_map/ppermute | solution.py:345
  9.3 14.1 %collective-permute-start.3 = (bf16[48,1536]{1,0:T(8,128)(2,1)S(1)}, bf16[48,1536]{1,0:T(8,128)(2,1)S(1)}, u32[]{:S(2)}, u32[]{:S(2)}) collective-permute-start(bf16[48,1536]{1,0:T(8,128)(2,1)S(1)} %get-tuple-element.456), channel_id=1, source_target_pairs={{0,16},{1,17},{2,18},{3,19},{4,20},{5,21},{6,22},{7,23},{8,24},{9,... | collective-permute-start | bytes 442376 | tf_op jit(solution)/shard_map/ppermute | solution.py:345
  13.9 48.8 %all-to-all-start = ((bf16[32,16,896]{2,1,0:T(8,128)(2,1)}), bf16[32,16,896]{2,1,0:T(8,128)(2,1)S(1)}, u32[]{:S(2)}, u32[]{:S(2)}) async-start(bf16[32,16,896]{2,1,0:T(8,128)(2,1)} %bitcast.12), calls=%async_computation | async-start | bytes 1835008 | tf_op jit(solution)/shard_map/all_to_all | solution.py:417
  23.5 17.9 %collective-permute-start.7 = (bf16[2,48,1536]{2,1,0:T(8,128)(2,1)S(1)}, bf16[2,48,1536]{2,1,0:T(8,128)(2,1)S(1)}, u32[]{:S(2)}, u32[]{:S(2)}) collective-permute-start(bf16[2,48,1536]{2,1,0:T(8,128)(2,1)S(1)} %pad_maximum_fusion.8.refs_1_), channel_id=1, source_target_pairs={{0,4},{1,5},{2,6},{3,7},{4,0},{5,1},{6,2},{7,3},{8,12},{9,13},{10,... | collective-permute-start | bytes 884744 | tf_op jit(solution)/shard_map/ppermute | solution.py:339
  25.3 16.4 %collective-permute-start.5 = (bf16[2,48,1536]{2,1,0:T(8,128)(2,1)S(1)}, bf16[2,48,1536]{2,1,0:T(8,128)(2,1)S(1)}, u32[]{:S(2)}, u32[]{:S(2)}) collective-permute-start(bf16[2,48,1536]{2,1,0:T(8,128)(2,1)S(1)} %pad_maximum_fusion.8.refs_1_), channel_id=1, source_target_pairs={{0,2},{1,3},{2,0},{3,1},{4,6},{5,7},{6,4},{7,5},{8,10},{9,11},{10,... | collective-permute-start | bytes 884744 | tf_op jit(solution)/shard_map/ppermute | solution.py:339
  26.8 21.9 %collective-permute-start.6 = (bf16[2,48,1536]{2,1,0:T(8,128)(2,1)S(1)}, bf16[2,48,1536]{2,1,0:T(8,128)(2,1)S(1)}, u32[]{:S(2)}, u32[]{:S(2)}) collective-permute-start(bf16[2,48,1536]{2,1,0:T(8,128)(2,1)S(1)} %pad_maximum_fusion.7.refs_0_), channel_id=1, source_target_pairs={{0,4},{1,5},{2,6},{3,7},{4,0},{5,1},{6,2},{7,3},{8,12},{9,13},{10,... | collective-permute-start | bytes 884744 | tf_op jit(solution)/shard_map/ppermute | solution.py:339
  27.5 21.3 %collective-permute-start.2 = (bf16[2,48,1536]{2,1,0:T(8,128)(2,1)S(1)}, bf16[2,48,1536]{2,1,0:T(8,128)(2,1)S(1)}, u32[]{:S(2)}, u32[]{:S(2)}) collective-permute-start(bf16[2,48,1536]{2,1,0:T(8,128)(2,1)S(1)} %pad_maximum_fusion.7.refs_0_), channel_id=1, source_target_pairs={{0,2},{1,3},{2,0},{3,1},{4,6},{5,7},{6,4},{7,5},{8,10},{9,11},{10,... | collective-permute-start | bytes 884744 | tf_op jit(solution)/shard_map/ppermute | solution.py:339
  27.7 23.0 %collective-permute-start.11 = (bf16[2,48,1536]{2,1,0:T(8,128)(2,1)S(1)}, bf16[2,48,1536]{2,1,0:T(8,128)(2,1)S(1)}, u32[]{:S(2)}, u32[]{:S(2)}) collective-permute-start(bf16[2,48,1536]{2,1,0:T(8,128)(2,1)S(1)} %pad_maximum_fusion.8.refs_1_), channel_id=1, source_target_pairs={{0,1},{1,0},{2,3},{3,2},{4,5},{5,4},{6,7},{7,6},{8,9},{9,8},{10,11... | collective-permute-start | bytes 884744 | tf_op jit(solution)/shard_map/ppermute | solution.py:339
  41.4 9.4 %collective-permute-start.10 = (bf16[2,48,1536]{2,1,0:T(8,128)(2,1)S(1)}, bf16[2,48,1536]{2,1,0:T(8,128)(2,1)S(1)}, u32[]{:S(2)}, u32[]{:S(2)}) collective-permute-start(bf16[2,48,1536]{2,1,0:T(8,128)(2,1)S(1)} %pad_maximum_fusion.7.refs_0_), channel_id=1, source_target_pairs={{0,1},{1,0},{2,3},{3,2},{4,5},{5,4},{6,7},{7,6},{8,9},{9,8},{10,11... | collective-permute-start | bytes 884744 | tf_op jit(solution)/shard_map/ppermute | solution.py:339
  49.3 9.1 %collective-permute-start.8 = (bf16[2,48,1536]{2,1,0:T(8,128)(2,1)S(1)}, bf16[2,48,1536]{2,1,0:T(8,128)(2,1)}, u32[]{:S(2)}, u32[]{:S(2)}) collective-permute-start(bf16[2,48,1536]{2,1,0:T(8,128)(2,1)S(1)} %collective-permute-done.2.refs_2_), channel_id=1, source_target_pairs={{0,4},{1,5},{2,6},{3,7},{4,0},{5,1},{6,2},{7,3},{8,12},{9,13},{10,... | collective-permute-start | bytes 884744 | tf_op jit(solution)/shard_map/ppermute | solution.py:339
  50.8 7.7 %collective-permute-start.15 = (bf16[2,48,1536]{2,1,0:T(8,128)(2,1)S(1)}, bf16[2,48,1536]{2,1,0:T(8,128)(2,1)S(1)}, u32[]{:S(2)}, u32[]{:S(2)}) collective-permute-start(bf16[2,48,1536]{2,1,0:T(8,128)(2,1)S(1)} %collective-permute-done.7.refs_5_), channel_id=1, source_target_pairs={{0,1},{1,0},{2,3},{3,2},{4,5},{5,4},{6,7},{7,6},{8,9},{9,8},{10,11... | collective-permute-start | bytes 884744 | tf_op jit(solution)/shard_map/ppermute | solution.py:339
  51.3 9.1 %collective-permute-start.9 = (bf16[2,48,1536]{2,1,0:T(8,128)(2,1)S(1)}, bf16[2,48,1536]{2,1,0:T(8,128)(2,1)}, u32[]{:S(2)}, u32[]{:S(2)}) collective-permute-start(bf16[2,48,1536]{2,1,0:T(8,128)(2,1)S(1)} %collective-permute-done.7.refs_5_), channel_id=1, source_target_pairs={{0,2},{1,3},{2,0},{3,1},{4,6},{5,7},{6,4},{7,5},{8,10},{9,11},{10,... | collective-permute-start | bytes 884744 | tf_op jit(solution)/shard_map/ppermute | solution.py:339
  62.7 13.6 %collective-permute-start.20 = (bf16[48,1536]{1,0:T(8,128)(2,1)S(1)}, bf16[48,1536]{1,0:T(8,128)(2,1)S(1)}, u32[]{:S(2)}, u32[]{:S(2)}) collective-permute-start(bf16[48,1536]{1,0:T(8,128)(2,1)S(1)} %get-tuple-element.240), channel_id=1, source_target_pairs={{0,24},{1,25},{2,26},{3,27},{4,28},{5,29},{6,30},{7,31},{8,0},{9,1... | collective-permute-start | bytes 442376 | tf_op jit(solution)/shard_map/ppermute | solution.py:345
  66.0 13.0 %collective-permute-start.19 = (bf16[48,1536]{1,0:T(8,128)(2,1)S(1)}, bf16[48,1536]{1,0:T(8,128)(2,1)S(1)}, u32[]{:S(2)}, u32[]{:S(2)}) collective-permute-start(bf16[48,1536]{1,0:T(8,128)(2,1)S(1)} %get-tuple-element.240), channel_id=1, source_target_pairs={{0,16},{1,17},{2,18},{3,19},{4,20},{5,21},{6,22},{7,23},{8,24},{9,... | collective-permute-start | bytes 442376 | tf_op jit(solution)/shard_map/ppermute | solution.py:345
  66.0 13.0 %collective-permute-start.18 = (bf16[48,1536]{1,0:T(8,128)(2,1)S(1)}, bf16[48,1536]{1,0:T(8,128)(2,1)S(1)}, u32[]{:S(2)}, u32[]{:S(2)}) collective-permute-start(bf16[48,1536]{1,0:T(8,128)(2,1)S(1)} %get-tuple-element.240), channel_id=1, source_target_pairs={{0,8},{1,9},{2,10},{3,11},{4,12},{5,13},{6,14},{7,15},{8,16},{9,17... | collective-permute-start | bytes 442376 | tf_op jit(solution)/shard_map/ppermute | solution.py:345
  79.1 17.2 %collective-permute-start.22 = (bf16[4,48,1536]{2,1,0:T(8,128)(2,1)S(1)}, bf16[4,48,1536]{2,1,0:T(8,128)(2,1)S(1)}, u32[]{:S(2)}, u32[]{:S(2)}) collective-permute-start(bf16[4,48,1536]{2,1,0:T(8,128)(2,1)S(1)} %pad_maximum_fusion.2.refs_0_), channel_id=1, source_target_pairs={{0,4},{1,5},{2,6},{3,7},{4,0},{5,1},{6,2},{7,3},{8,12},{9,13},{10,... | collective-permute-start | bytes 1769480 | tf_op jit(solution)/shard_map/ppermute | solution.py:339
  79.8 16.6 %collective-permute-start.21 = (bf16[4,48,1536]{2,1,0:T(8,128)(2,1)S(1)}, bf16[4,48,1536]{2,1,0:T(8,128)(2,1)}, u32[]{:S(2)}, u32[]{:S(2)}) collective-permute-start(bf16[4,48,1536]{2,1,0:T(8,128)(2,1)S(1)} %pad_maximum_fusion.2.refs_0_), channel_id=1, source_target_pairs={{0,2},{1,3},{2,0},{3,1},{4,6},{5,7},{6,4},{7,5},{8,10},{9,11},{10,... | collective-permute-start | bytes 1769480 | tf_op jit(solution)/shard_map/ppermute | solution.py:339
  81.3 10.6 %collective-permute-start.25 = (bf16[96,768]{1,0:T(8,128)(2,1)S(1)}, bf16[96,768]{1,0:T(8,128)(2,1)S(1)}, u32[]{:S(2)}, u32[]{:S(2)}) collective-permute-start(bf16[96,768]{1,0:T(8,128)(2,1)S(1)} %convert_element_type.355), channel_id=1, source_target_pairs={{0,24},{1,25},{2,26},{3,27},{4,28},{5,29},{6,30},{7,31},{8,0},{9,1... | collective-permute-start | bytes 442376 | tf_op jit(solution)/shard_map/ppermute | solution.py:345
  82.5 13.8 %collective-permute-start.24 = (bf16[96,768]{1,0:T(8,128)(2,1)S(1)}, bf16[96,768]{1,0:T(8,128)(2,1)S(1)}, u32[]{:S(2)}, u32[]{:S(2)}) collective-permute-start(bf16[96,768]{1,0:T(8,128)(2,1)S(1)} %convert_element_type.355), channel_id=1, source_target_pairs={{0,16},{1,17},{2,18},{3,19},{4,20},{5,21},{6,22},{7,23},{8,24},{9,... | collective-permute-start | bytes 442376 | tf_op jit(solution)/shard_map/ppermute | solution.py:345
  84.0 12.3 %collective-permute-start.23 = (bf16[96,768]{1,0:T(8,128)(2,1)S(1)}, bf16[96,768]{1,0:T(8,128)(2,1)S(1)}, u32[]{:S(2)}, u32[]{:S(2)}) collective-permute-start(bf16[96,768]{1,0:T(8,128)(2,1)S(1)} %convert_element_type.355), channel_id=1, source_target_pairs={{0,8},{1,9},{2,10},{3,11},{4,12},{5,13},{6,14},{7,15},{8,16},{9,17... | collective-permute-start | bytes 442376 | tf_op jit(solution)/shard_map/ppermute | solution.py:345
  91.9 22.2 %collective-permute-start.28 = (bf16[4,48,1536]{2,1,0:T(8,128)(2,1)S(1)}, bf16[4,48,1536]{2,1,0:T(8,128)(2,1)}, u32[]{:S(2)}, u32[]{:S(2)}) collective-permute-start(bf16[4,48,1536]{2,1,0:T(8,128)(2,1)S(1)} %pad_maximum_fusion.2.refs_0_), channel_id=1, source_target_pairs={{0,1},{1,0},{2,3},{3,2},{4,5},{5,4},{6,7},{7,6},{8,9},{9,8},{10,11... | collective-permute-start | bytes 1769480 | tf_op jit(solution)/shard_map/ppermute | solution.py:339
  96.4 19.7 %collective-permute-start.29 = (bf16[4,48,1536]{2,1,0:T(8,128)(2,1)}, bf16[4,48,1536]{2,1,0:T(8,128)(2,1)}, u32[]{:S(2)}, u32[]{:S(2)}) collective-permute-start(bf16[4,48,1536]{2,1,0:T(8,128)(2,1)} %collective-permute-done.21.refs_1_), channel_id=1, source_target_pairs={{0,1},{1,0},{2,3},{3,2},{4,5},{5,4},{6,7},{7,6},{8,9},{9,8},{10,11... | collective-permute-start | bytes 1769480 | tf_op jit(solution)/shard_map/ppermute | solution.py:339
  96.5 19.6 %collective-permute-start.30 = (bf16[4,48,1536]{2,1,0:T(8,128)(2,1)S(1)}, bf16[4,48,1536]{2,1,0:T(8,128)(2,1)}, u32[]{:S(2)}, u32[]{:S(2)}) collective-permute-start(bf16[4,48,1536]{2,1,0:T(8,128)(2,1)S(1)} %collective-permute-done.22.refs_2_), channel_id=1, source_target_pairs={{0,1},{1,0},{2,3},{3,2},{4,5},{5,4},{6,7},{7,6},{8,9},{9,8},{10,11... | collective-permute-start | bytes 1769480 | tf_op jit(solution)/shard_map/ppermute | solution.py:339
  97.0 43.7 %all-to-all-start.1 = ((bf16[32,16,768]{2,1,0:T(8,128)(2,1)}), bf16[32,16,768]{2,1,0:T(8,128)(2,1)S(1)}, u32[]{:S(2)}, u32[]{:S(2)}) async-start(bf16[32,16,768]{2,1,0:T(8,128)(2,1)} %bitcast.23), calls=%async_computation.1 | async-start | bytes 1572864 | tf_op jit(solution)/shard_map/all_to_all | solution.py:417
  100.8 15.2 %collective-permute-start.27 = (bf16[2,48,1536]{2,1,0:T(8,128)(2,1)S(1)}, bf16[2,48,1536]{2,1,0:T(8,128)(2,1)S(1)}, u32[]{:S(2)}, u32[]{:S(2)}) collective-permute-start(bf16[2,48,1536]{2,1,0:T(8,128)(2,1)S(1)} %slice.197), channel_id=1, source_target_pairs={{0,2},{1,3},{2,0},{3,1},{4,6},{5,7},{6,4},{7,5},{8,10},{9,11},{10,... | collective-permute-start | bytes 884744 | tf_op jit(solution)/shard_map/ppermute | solution.py:339
  102.3 13.7 %collective-permute-start.26 = (bf16[2,48,1536]{2,1,0:T(8,128)(2,1)S(1)}, bf16[2,48,1536]{2,1,0:T(8,128)(2,1)}, u32[]{:S(2)}, u32[]{:S(2)}) collective-permute-start(bf16[2,48,1536]{2,1,0:T(8,128)(2,1)S(1)} %slice.196), channel_id=1, source_target_pairs={{0,4},{1,5},{2,6},{3,7},{4,0},{5,1},{6,2},{7,3},{8,12},{9,13},{10,... | collective-permute-start | bytes 884744 | tf_op jit(solution)/shard_map/ppermute | solution.py:339
  118.1 15.6 %collective-permute-start.35 = (bf16[2,96,768]{2,1,0:T(8,128)(2,1)S(1)}, bf16[2,96,768]{2,1,0:T(8,128)(2,1)}, u32[]{:S(2)}, u32[]{:S(2)}) collective-permute-start(bf16[2,96,768]{2,1,0:T(8,128)(2,1)S(1)} %pad_maximum_fusion.9.refs_0_), channel_id=1, source_target_pairs={{0,4},{1,5},{2,6},{3,7},{4,0},{5,1},{6,2},{7,3},{8,12},{9,13},{10,... | collective-permute-start | bytes 884744 | tf_op jit(solution)/shard_map/ppermute | solution.py:339
  119.5 14.9 %collective-permute-start.33 = (bf16[2,96,768]{2,1,0:T(8,128)(2,1)S(1)}, bf16[2,96,768]{2,1,0:T(8,128)(2,1)}, u32[]{:S(2)}, u32[]{:S(2)}) collective-permute-start(bf16[2,96,768]{2,1,0:T(8,128)(2,1)S(1)} %pad_maximum_fusion.9.refs_0_), channel_id=1, source_target_pairs={{0,2},{1,3},{2,0},{3,1},{4,6},{5,7},{6,4},{7,5},{8,10},{9,11},{10,... | collective-permute-start | bytes 884744 | tf_op jit(solution)/shard_map/ppermute | solution.py:339
  120.2 14.2 %collective-permute-start.36 = (bf16[2,96,768]{2,1,0:T(8,128)(2,1)S(1)}, bf16[2,96,768]{2,1,0:T(8,128)(2,1)}, u32[]{:S(2)}, u32[]{:S(2)}) collective-permute-start(bf16[2,96,768]{2,1,0:T(8,128)(2,1)S(1)} %pad_maximum_fusion.10.refs_1_), channel_id=1, source_target_pairs={{0,4},{1,5},{2,6},{3,7},{4,0},{5,1},{6,2},{7,3},{8,12},{9,13},{10,... | collective-permute-start | bytes 884744 | tf_op jit(solution)/shard_map/ppermute | solution.py:339
  121.7 12.9 %collective-permute-start.34 = (bf16[2,96,768]{2,1,0:T(8,128)(2,1)S(1)}, bf16[2,96,768]{2,1,0:T(8,128)(2,1)S(1)}, u32[]{:S(2)}, u32[]{:S(2)}) collective-permute-start(bf16[2,96,768]{2,1,0:T(8,128)(2,1)S(1)} %pad_maximum_fusion.10.refs_1_), channel_id=1, source_target_pairs={{0,2},{1,3},{2,0},{3,1},{4,6},{5,7},{6,4},{7,5},{8,10},{9,11},{10,... | collective-permute-start | bytes 884744 | tf_op jit(solution)/shard_map/ppermute | solution.py:339
  122.8 14.2 %collective-permute-start.39 = (bf16[2,96,768]{2,1,0:T(8,128)(2,1)S(1)}, bf16[2,96,768]{2,1,0:T(8,128)(2,1)S(1)}, u32[]{:S(2)}, u32[]{:S(2)}) collective-permute-start(bf16[2,96,768]{2,1,0:T(8,128)(2,1)S(1)} %pad_maximum_fusion.9.refs_0_), channel_id=1, source_target_pairs={{0,1},{1,0},{2,3},{3,2},{4,5},{5,4},{6,7},{7,6},{8,9},{9,8},{10,11... | collective-permute-start | bytes 884744 | tf_op jit(solution)/shard_map/ppermute | solution.py:339
  135.3 13.4 %collective-permute-start.41 = (bf16[2,96,768]{2,1,0:T(8,128)(2,1)}, bf16[2,96,768]{2,1,0:T(8,128)(2,1)}, u32[]{:S(2)}, u32[]{:S(2)}) collective-permute-start(bf16[2,96,768]{2,1,0:T(8,128)(2,1)} %collective-permute-done.33.refs_2_), channel_id=1, source_target_pairs={{0,1},{1,0},{2,3},{3,2},{4,5},{5,4},{6,7},{7,6},{8,9},{9,8},{10,11... | collective-permute-start | bytes 884744 | tf_op jit(solution)/shard_map/ppermute | solution.py:339
  135.8 12.9 %collective-permute-start.37 = (bf16[2,96,768]{2,1,0:T(8,128)(2,1)}, bf16[2,96,768]{2,1,0:T(8,128)(2,1)}, u32[]{:S(2)}, u32[]{:S(2)}) collective-permute-start(bf16[2,96,768]{2,1,0:T(8,128)(2,1)} %collective-permute-done.33.refs_2_), channel_id=1, source_target_pairs={{0,4},{1,5},{2,6},{3,7},{4,0},{5,1},{6,2},{7,3},{8,12},{9,13},{10,... | collective-permute-start | bytes 884744 | tf_op jit(solution)/shard_map/ppermute | solution.py:339
  137.7 10.9 %collective-permute-start.43 = (bf16[2,96,768]{2,1,0:T(8,128)(2,1)}, bf16[2,96,768]{2,1,0:T(8,128)(2,1)}, u32[]{:S(2)}, u32[]{:S(2)}) collective-permute-start(bf16[2,96,768]{2,1,0:T(8,128)(2,1)} %collective-permute-done.35.refs_4_), channel_id=1, source_target_pairs={{0,1},{1,0},{2,3},{3,2},{4,5},{5,4},{6,7},{7,6},{8,9},{9,8},{10,11... | collective-permute-start | bytes 884744 | tf_op jit(solution)/shard_map/ppermute | solution.py:339
  138.4 10.2 %collective-permute-start.44 = (bf16[2,96,768]{2,1,0:T(8,128)(2,1)}, bf16[2,96,768]{2,1,0:T(8,128)(2,1)}, u32[]{:S(2)}, u32[]{:S(2)}) collective-permute-start(bf16[2,96,768]{2,1,0:T(8,128)(2,1)} %collective-permute-done.36.refs_5_), channel_id=1, source_target_pairs={{0,1},{1,0},{2,3},{3,2},{4,5},{5,4},{6,7},{7,6},{8,9},{9,8},{10,11... | collective-permute-start | bytes 884744 | tf_op jit(solution)/shard_map/ppermute | solution.py:339
  139.7 9.2 %collective-permute-start.38 = (bf16[2,96,768]{2,1,0:T(8,128)(2,1)}, bf16[2,96,768]{2,1,0:T(8,128)(2,1)}, u32[]{:S(2)}, u32[]{:S(2)}) collective-permute-start(bf16[2,96,768]{2,1,0:T(8,128)(2,1)} %collective-permute-done.36.refs_5_), channel_id=1, source_target_pairs={{0,2},{1,3},{2,0},{3,1},{4,6},{5,7},{6,4},{7,5},{8,10},{9,11},{10,... | collective-permute-start | bytes 884744 | tf_op jit(solution)/shard_map/ppermute | solution.py:339
  148.9 5.4 %collective-permute-start.47 = (bf16[4,4,96,768]{3,2,1,0:T(8,128)(2,1)S(1)}, bf16[4,4,96,768]{3,2,1,0:T(8,128)(2,1)S(1)}, u32[]{:S(2)}, u32[]{:S(2)}) collective-permute-start(bf16[4,4,96,768]{3,2,1,0:T(8,128)(2,1)S(1)} %get-tuple-element.286), channel_id=1, source_target_pairs={{0,1},{1,0},{2,3},{3,2},{4,5},{5,4},{6,7},{7,6},{8,9},{9,8},{10,11... | collective-permute-start | bytes 7077896 | tf_op jit(solution)/shard_map/ppermute | solution.py:339
  149.0 4.8 %collective-permute-start.45 = (bf16[2,96,768]{2,1,0:T(8,128)(2,1)}, bf16[2,96,768]{2,1,0:T(8,128)(2,1)S(1)}, u32[]{:S(2)}, u32[]{:S(2)}) collective-permute-start(bf16[2,96,768]{2,1,0:T(8,128)(2,1)} %collective-permute-done.37.refs_6_), channel_id=1, source_target_pairs={{0,1},{1,0},{2,3},{3,2},{4,5},{5,4},{6,7},{7,6},{8,9},{9,8},{10,11... | collective-permute-start | bytes 884744 | tf_op jit(solution)/shard_map/ppermute | solution.py:339
  154.6 11.9 %collective-permute-start.48 = (bf16[2,96,768]{2,1,0:T(8,128)(2,1)S(1)}, bf16[2,96,768]{2,1,0:T(8,128)(2,1)S(1)}, u32[]{:S(2)}, u32[]{:S(2)}) collective-permute-start(bf16[2,96,768]{2,1,0:T(8,128)(2,1)S(1)} %get-tuple-element.309), channel_id=1, source_target_pairs={{0,4},{1,5},{2,6},{3,7},{4,0},{5,1},{6,2},{7,3},{8,12},{9,13},{10,... | collective-permute-start | bytes 884744 | tf_op jit(solution)/shard_map/ppermute | solution.py:339
  155.7 10.8 %collective-permute-start.49 = (bf16[2,96,768]{2,1,0:T(8,128)(2,1)S(1)}, bf16[2,96,768]{2,1,0:T(8,128)(2,1)S(1)}, u32[]{:S(2)}, u32[]{:S(2)}) collective-permute-start(bf16[2,96,768]{2,1,0:T(8,128)(2,1)S(1)} %get-tuple-element.310), channel_id=1, source_target_pairs={{0,2},{1,3},{2,0},{3,1},{4,6},{5,7},{6,4},{7,5},{8,10},{9,11},{10,... | collective-permute-start | bytes 884744 | tf_op jit(solution)/shard_map/ppermute | solution.py:339
  167.9 29.6 %all-to-all-start.2 = ((bf16[32,16,768]{2,1,0:T(8,128)(2,1)}), bf16[32,16,768]{2,1,0:T(8,128)(2,1)S(1)}, u32[]{:S(2)}, u32[]{:S(2)}) async-start(bf16[32,16,768]{2,1,0:T(8,128)(2,1)} %bitcast.139), calls=%async_computation.2 | async-start | bytes 1572864 | tf_op jit(solution)/shard_map/all_to_all | solution.py:417
  173.6 23.8 %collective-permute-start.50 = (bf16[4,96,768]{2,1,0:T(8,128)(2,1)}, bf16[4,96,768]{2,1,0:T(8,128)(2,1)}, u32[]{:S(2)}, u32[]{:S(2)}) collective-permute-start(bf16[4,96,768]{2,1,0:T(8,128)(2,1)} %get-tuple-element.318), channel_id=1, source_target_pairs={{0,2},{1,3},{2,0},{3,1},{4,6},{5,7},{6,4},{7,5},{8,10},{9,11},{10,... | collective-permute-start | bytes 1769480 | tf_op jit(solution)/shard_map/ppermute | solution.py:339
  175.2 22.3 %collective-permute-start.51 = (bf16[4,96,768]{2,1,0:T(8,128)(2,1)}, bf16[4,96,768]{2,1,0:T(8,128)(2,1)}, u32[]{:S(2)}, u32[]{:S(2)}) collective-permute-start(bf16[4,96,768]{2,1,0:T(8,128)(2,1)} %get-tuple-element.319), channel_id=1, source_target_pairs={{0,4},{1,5},{2,6},{3,7},{4,0},{5,1},{6,2},{7,3},{8,12},{9,13},{10,... | collective-permute-start | bytes 1769480 | tf_op jit(solution)/shard_map/ppermute | solution.py:339
  199.5 9.3 %collective-permute-start.52 = (bf16[4,4,24,3840]{3,2,1,0:T(8,128)(2,1)}, bf16[4,4,24,3840]{3,2,1,0:T(8,128)(2,1)S(1)}, u32[]{:S(2)}, u32[]{:S(2)}) collective-permute-start(bf16[4,4,24,3840]{3,2,1,0:T(8,128)(2,1)} %get-tuple-element.327), channel_id=1, source_target_pairs={{0,1},{1,0},{2,3},{3,2},{4,5},{5,4},{6,7},{7,6},{8,9},{9,8},{10,11... | collective-permute-start | bytes 8847368 | tf_op jit(solution)/shard_map/ppermute | solution.py:339
  209.1 15.3 %collective-permute-start.53 = (bf16[2,24,3840]{2,1,0:T(8,128)(2,1)S(1)}, bf16[2,24,3840]{2,1,0:T(8,128)(2,1)S(1)}, u32[]{:S(2)}, u32[]{:S(2)}) collective-permute-start(bf16[2,24,3840]{2,1,0:T(8,128)(2,1)S(1)} %get-tuple-element.335), channel_id=1, source_target_pairs={{0,4},{1,5},{2,6},{3,7},{4,0},{5,1},{6,2},{7,3},{8,12},{9,13},{10,... | collective-permute-start | bytes 1105928 | tf_op jit(solution)/shard_map/ppermute | solution.py:339
  210.6 13.9 %collective-permute-start.54 = (bf16[2,24,3840]{2,1,0:T(8,128)(2,1)S(1)}, bf16[2,24,3840]{2,1,0:T(8,128)(2,1)S(1)}, u32[]{:S(2)}, u32[]{:S(2)}) collective-permute-start(bf16[2,24,3840]{2,1,0:T(8,128)(2,1)S(1)} %get-tuple-element.336), channel_id=1, source_target_pairs={{0,2},{1,3},{2,0},{3,1},{4,6},{5,7},{6,4},{7,5},{8,10},{9,11},{10,... | collective-permute-start | bytes 1105928 | tf_op jit(solution)/shard_map/ppermute | solution.py:339
  211.1 13.3 %collective-permute-start.55 = (bf16[96,768]{1,0:T(8,128)(2,1)S(1)}, bf16[96,768]{1,0:T(8,128)(2,1)S(1)}, u32[]{:S(2)}, u32[]{:S(2)}) collective-permute-start(bf16[96,768]{1,0:T(8,128)(2,1)S(1)} %get-tuple-element.340), channel_id=1, source_target_pairs={{0,8},{1,9},{2,10},{3,11},{4,12},{5,13},{6,14},{7,15},{8,16},{9,17... | collective-permute-start | bytes 442376 | tf_op jit(solution)/shard_map/ppermute | solution.py:413
  212.6 11.8 %collective-permute-start.56 = (bf16[96,768]{1,0:T(8,128)(2,1)S(1)}, bf16[96,768]{1,0:T(8,128)(2,1)S(1)}, u32[]{:S(2)}, u32[]{:S(2)}) collective-permute-start(bf16[96,768]{1,0:T(8,128)(2,1)S(1)} %get-tuple-element.341), channel_id=1, source_target_pairs={{0,16},{1,17},{2,18},{3,19},{4,20},{5,21},{6,22},{7,23},{8,24},{9,... | collective-permute-start | bytes 442376 | tf_op jit(solution)/shard_map/ppermute | solution.py:413
  215.0 9.5 %collective-permute-start.57 = (bf16[96,768]{1,0:T(8,128)(2,1)S(1)}, bf16[96,768]{1,0:T(8,128)(2,1)S(1)}, u32[]{:S(2)}, u32[]{:S(2)}) collective-permute-start(bf16[96,768]{1,0:T(8,128)(2,1)S(1)} %get-tuple-element.342), channel_id=1, source_target_pairs={{0,24},{1,25},{2,26},{3,27},{4,28},{5,29},{6,30},{7,31},{8,0},{9,1... | collective-permute-start | bytes 442376 | tf_op jit(solution)/shard_map/ppermute | solution.py:413
  226.7 22.9 %collective-permute-start.58 = (bf16[4,24,3840]{2,1,0:T(8,128)(2,1)}, bf16[4,24,3840]{2,1,0:T(8,128)(2,1)S(1)}, u32[]{:S(2)}, u32[]{:S(2)}) collective-permute-start(bf16[4,24,3840]{2,1,0:T(8,128)(2,1)} %pad_maximum_fusion), channel_id=1, source_target_pairs={{0,2},{1,3},{2,0},{3,1},{4,6},{5,7},{6,4},{7,5},{8,10},{9,11},{10,... | collective-permute-start | bytes 2211848 | tf_op jit(solution)/shard_map/ppermute | solution.py:339
  228.2 21.4 %collective-permute-start.59 = (bf16[4,24,3840]{2,1,0:T(8,128)(2,1)}, bf16[4,24,3840]{2,1,0:T(8,128)(2,1)}, u32[]{:S(2)}, u32[]{:S(2)}) collective-permute-start(bf16[4,24,3840]{2,1,0:T(8,128)(2,1)} %pad_maximum_fusion.1), channel_id=1, source_target_pairs={{0,4},{1,5},{2,6},{3,7},{4,0},{5,1},{6,2},{7,3},{8,12},{9,13},{10,... | collective-permute-start | bytes 2211848 | tf_op jit(solution)/shard_map/ppermute | solution.py:339
  237.4 29.3 %all-to-all-start.3 = ((bf16[32,16,896]{2,1,0:T(8,128)(2,1)}), bf16[32,16,896]{2,1,0:T(8,128)(2,1)S(1)}, u32[]{:S(2)}, u32[]{:S(2)}) async-start(bf16[32,16,896]{2,1,0:T(8,128)(2,1)} %bitcast.56), calls=%async_computation.3 | async-start | bytes 1835008 | tf_op jit(solution)/shard_map/all_to_all | solution.py:417
  253.8 9.2 %collective-permute-start.61 = (bf16[2,24,2304]{2,1,0:T(8,128)(2,1)S(1)}, bf16[2,24,2304]{2,1,0:T(8,128)(2,1)S(1)}, u32[]{:S(2)}, u32[]{:S(2)}) collective-permute-start(bf16[2,24,2304]{2,1,0:T(8,128)(2,1)S(1)} %get-tuple-element.367), channel_id=1, source_target_pairs={{0,4},{1,5},{2,6},{3,7},{4,0},{5,1},{6,2},{7,3},{8,12},{9,13},{10,... | collective-permute-start | bytes 663560 | tf_op jit(solution)/shard_map/ppermute | solution.py:339
  255.4 8.0 %collective-permute-start.62 = (bf16[2,24,2304]{2,1,0:T(8,128)(2,1)S(1)}, bf16[2,24,2304]{2,1,0:T(8,128)(2,1)S(1)}, u32[]{:S(2)}, u32[]{:S(2)}) collective-permute-start(bf16[2,24,2304]{2,1,0:T(8,128)(2,1)S(1)} %get-tuple-element.368), channel_id=1, source_target_pairs={{0,2},{1,3},{2,0},{3,1},{4,6},{5,7},{6,4},{7,5},{8,10},{9,11},{10,... | collective-permute-start | bytes 663560 | tf_op jit(solution)/shard_map/ppermute | solution.py:339
  266.6 12.1 %collective-permute-start.63 = (bf16[4,24,2304]{2,1,0:T(8,128)(2,1)S(1)}, bf16[4,24,2304]{2,1,0:T(8,128)(2,1)S(1)}, u32[]{:S(2)}, u32[]{:S(2)}) collective-permute-start(bf16[4,24,2304]{2,1,0:T(8,128)(2,1)S(1)} %pad_maximum_fusion.5), channel_id=1, source_target_pairs={{0,2},{1,3},{2,0},{3,1},{4,6},{5,7},{6,4},{7,5},{8,10},{9,11},{10,... | collective-permute-start | bytes 1327112 | tf_op jit(solution)/shard_map/ppermute | solution.py:339
  268.1 11.8 %collective-permute-start.64 = (bf16[4,24,2304]{2,1,0:T(8,128)(2,1)S(1)}, bf16[4,24,2304]{2,1,0:T(8,128)(2,1)S(1)}, u32[]{:S(2)}, u32[]{:S(2)}) collective-permute-start(bf16[4,24,2304]{2,1,0:T(8,128)(2,1)S(1)} %pad_maximum_fusion.6), channel_id=1, source_target_pairs={{0,4},{1,5},{2,6},{3,7},{4,0},{5,1},{6,2},{7,3},{8,12},{9,13},{10,... | collective-permute-start | bytes 1327112 | tf_op jit(solution)/shard_map/ppermute | solution.py:339
  269.6 9.1 %collective-permute-start.65 = (bf16[24,3840]{1,0:T(8,128)(2,1)}, bf16[24,3840]{1,0:T(8,128)(2,1)S(1)}, u32[]{:S(2)}, u32[]{:S(2)}) collective-permute-start(bf16[24,3840]{1,0:T(8,128)(2,1)} %get-tuple-element.378), channel_id=1, source_target_pairs={{0,8},{1,9},{2,10},{3,11},{4,12},{5,13},{6,14},{7,15},{8,16},{9,17... | collective-permute-start | bytes 552968 | tf_op jit(solution)/shard_map/ppermute | solution.py:413
  273.4 12.5 %collective-permute-start.69 = (bf16[24,3840]{1,0:T(8,128)(2,1)}, bf16[24,3840]{1,0:T(8,128)(2,1)S(1)}, u32[]{:S(2)}, u32[]{:S(2)}) collective-permute-start(bf16[24,3840]{1,0:T(8,128)(2,1)} %get-tuple-element.387), channel_id=1, source_target_pairs={{0,16},{1,17},{2,18},{3,19},{4,20},{5,21},{6,22},{7,23},{8,24},{9,... | collective-permute-start | bytes 552968 | tf_op jit(solution)/shard_map/ppermute | solution.py:413
  274.0 11.8 %collective-permute-start.70 = (bf16[24,3840]{1,0:T(8,128)(2,1)}, bf16[24,3840]{1,0:T(8,128)(2,1)S(1)}, u32[]{:S(2)}, u32[]{:S(2)}) collective-permute-start(bf16[24,3840]{1,0:T(8,128)(2,1)} %get-tuple-element.388), channel_id=1, source_target_pairs={{0,24},{1,25},{2,26},{3,27},{4,28},{5,29},{6,30},{7,31},{8,0},{9,1... | collective-permute-start | bytes 552968 | tf_op jit(solution)/shard_map/ppermute | solution.py:413
  282.0 8.2 %collective-permute-start.66 = (bf16[24,2304]{1,0:T(8,128)(2,1)S(1)}, bf16[24,2304]{1,0:T(8,128)(2,1)S(1)}, u32[]{:S(2)}, u32[]{:S(2)}) collective-permute-start(bf16[24,2304]{1,0:T(8,128)(2,1)S(1)} %get-tuple-element.382), channel_id=1, source_target_pairs={{0,8},{1,9},{2,10},{3,11},{4,12},{5,13},{6,14},{7,15},{8,16},{9,17... | collective-permute-start | bytes 331784 | tf_op jit(solution)/shard_map/ppermute | solution.py:413
  283.2 13.1 %collective-permute-start.67 = (bf16[24,2304]{1,0:T(8,128)(2,1)S(1)}, bf16[24,2304]{1,0:T(8,128)(2,1)S(1)}, u32[]{:S(2)}, u32[]{:S(2)}) collective-permute-start(bf16[24,2304]{1,0:T(8,128)(2,1)S(1)} %get-tuple-element.383), channel_id=1, source_target_pairs={{0,16},{1,17},{2,18},{3,19},{4,20},{5,21},{6,22},{7,23},{8,24},{9,... | collective-permute-start | bytes 331784 | tf_op jit(solution)/shard_map/ppermute | solution.py:413
  283.8 12.4 %collective-permute-start.68 = (bf16[24,2304]{1,0:T(8,128)(2,1)S(1)}, bf16[24,2304]{1,0:T(8,128)(2,1)S(1)}, u32[]{:S(2)}, u32[]{:S(2)}) collective-permute-start(bf16[24,2304]{1,0:T(8,128)(2,1)S(1)} %get-tuple-element.384), channel_id=1, source_target_pairs={{0,24},{1,25},{2,26},{3,27},{4,28},{5,29},{6,30},{7,31},{8,0},{9,1... | collective-permute-start | bytes 331784 | tf_op jit(solution)/shard_map/ppermute | solution.py:413
  298.9 11.7 %all-to-all-start.4 = ((f32[32,4,128]{2,1,0:T(4,128)}), f32[32,4,128]{2,1,0:T(4,128)S(1)}, u32[]{:S(2)}, u32[]{:S(2)}) async-start(f32[32,4,128]{2,1,0:T(4,128)} %get-tuple-element.402), calls=%async_computation.4 | async-start | bytes 131072 | tf_op jit(solution)/shard_map/all_to_all | solution.py:417
  (72 other events, 590.8 us)

commit v7 on v6

--- a/solution.py
+++ b/solution.py
@@ -1473,8 +1473,8 @@
 
     got = over_plane(*first_to)
     got, up_first = pin(got, up_got[0])
+    first_sums, back_out, down_got = pin(first_fold.column(*got), back_out, down_got)
     down_grad = total_of(down_sums[0], *down_got)
-    first_sums, back_out = pin(first_fold.column(*got), back_out)
 
     first_got = over_column(first_sums)
     up_grad = total_of(up_sums[0], up_first, *up_got[1:])

time: 316 us -> 317 us (level)
  starting transfers between devices: 95.3 us -> 100 us
  waiting for transfers between devices: 76.6 us -> 73.1 us
    ppermute x9, starting transfers between devices: 13 us -> 17.5 us  [over_column(): lax.ppermute(sums[k], 'dev', shifts(devices, k))]
    unnamed x122 -> x128, local copies, waits for them, and re-layouts: 8.03 us -> 8.07 us
  transfers between devices with their start and end apart: 76 -> 76, of which waited for: 30 -> 29; matrix products, arithmetic and copies ran while one was open for 4% -> 3% of each run, Pallas kernels for 34% -> 34%
where the time goes in v7:
time: 317 us; the launch traced here: 315 us
  Pallas kernels  113 us (36%)
  starting transfers between devices  100 us (32%)
  waiting for transfers between devices  73.1 us (23%)
  other arithmetic  14.8 us (5%)
  local copies, waits for them, and re-layouts  11.3 us (4%)
  between operations  3.26 us (1%)
    ppermute x52, waiting for transfers between devices, send(): return lax.ppermute(value, 'dev', flips(lax.axis_size('dev'), mask))  49.5 us
    ppermute x52, starting transfers between devices, send(): return lax.ppermute(value, 'dev', flips(lax.axis_size('dev'), mask))  38.3 us
    all_to_all x5, starting transfers between devices, exchange(): return lax.all_to_all(rows, 'dev', split_axis=0, concat_axis=0, tiled=True)  28.5 us
    pallas_call x1, Pallas kernels, feed_back(): pl.pallas_call(kernel, grid=(steps + 1,), out_shape=[shaped((count, featu...  19 us
    ppermute x9, starting transfers between devices, over_column(): lax.ppermute(sums[k], 'dev', shifts(devices, k))  17.5 us
    pallas_call x2, Pallas kernels, attend(): pl.pallas_call(kernel, grid=(pairs,), out_shape=[shaped((pairs * 128, cou...  16.2 us
    pallas_call x2, Pallas kernels, attend_back(): pl.pallas_call(kernel, grid=(pairs,), out_shape=[shaped((3, count, wide),...  16 us
    ppermute x9, starting transfers between devices, along_z(): lax.ppermute(block, 'dev', shifts(devices, k))  15.2 us
  transfers between devices with their start and end apart: 76, of which 29 were waited for; matrix products, arithmetic and copies ran while one was open for 3% of the time, Pallas kernels for 34%

profile of v7, /device:TPU:0, one launch (start us, length us, event | category | flops | bytes accessed | tf_op | source)
XLA Modules:
  0.0 315.5 jit_solution(12917041074720239093)
XLA Ops:
  4.2 3.0 collective-permute-start.1
  7.2 2.1 collective-permute-start.4
  10.3 2.8 shard_map.211
  13.9 9.5 %all-to-all-start = ((bf16[32,16,896]{2,1,0:T(8,128)(2,1)}), bf16[32,16,896]{2,1,0:T(8,128)(2,1)S(1)}, u32[]{:S(2)}, u32[]{:S(2)}) async-start(bf16[32,16,896]{2,1,0:T(8,128)(2,1)} %bitcast.12), calls=%async_computation | async-start | bytes 1835008 | tf_op jit(solution)/shard_map/all_to_all | solution.py:417
  23.5 1.8 collective-permute-start.7
  25.3 1.5 collective-permute-start.5
  27.7 13.6 %collective-permute-done.7.refs_5_ = bf16[2,48,1536]{2,1,0:T(8,128)(2,1)S(1)} collective-permute-done((bf16[2,48,1536]{2,1,0:T(8,128)(2,1)S(1)}, bf16[2,48,1536]{2,1,0:T(8,128)(2,1)S(1)}, u32[]{:S(2)}, u32[]{:S(2)}) %collective-permute-start.7) | collective-permute-done | bytes 294944 | tf_op jit(solution)/shard_map/ppermute | solution.py:339
  41.7 7.1 %collective-permute-done.6.refs_4_ = bf16[2,48,1536]{2,1,0:T(8,128)(2,1)S(1)} collective-permute-done((bf16[2,48,1536]{2,1,0:T(8,128)(2,1)S(1)}, bf16[2,48,1536]{2,1,0:T(8,128)(2,1)S(1)}, u32[]{:S(2)}, u32[]{:S(2)}) %collective-permute-start.6) | collective-permute-done | bytes 294944 | tf_op jit(solution)/shard_map/ppermute | solution.py:339
  49.3 1.4 collective-permute-start.8
  52.3 6.1 %collective-permute-done.8.refs_6_ = bf16[2,48,1536]{2,1,0:T(8,128)(2,1)} collective-permute-done((bf16[2,48,1536]{2,1,0:T(8,128)(2,1)S(1)}, bf16[2,48,1536]{2,1,0:T(8,128)(2,1)}, u32[]{:S(2)}, u32[]{:S(2)}) %collective-permute-start.8) | collective-permute-done | bytes 294944 | tf_op jit(solution)/shard_map/ppermute | solution.py:339
  58.4 1.9 collective-permute-done.9.refs_7_
  62.7 3.3 %collective-permute-start.20 = (bf16[48,1536]{1,0:T(8,128)(2,1)S(1)}, bf16[48,1536]{1,0:T(8,128)(2,1)S(1)}, u32[]{:S(2)}, u32[]{:S(2)}) collective-permute-start(bf16[48,1536]{1,0:T(8,128)(2,1)S(1)} %get-tuple-element.243), channel_id=1, source_target_pairs={{0,24},{1,25},{2,26},{3,27},{4,28},{5,29},{6,30},{7,31},{8,0},{9,1... | collective-permute-start | bytes 442376 | tf_op jit(solution)/shard_map/ppermute | solution.py:345
  67.2 9.2 %shard_map.212 = (bf16[768,512]{1,0:T(8,128)(2,1)}, bf16[512,2304]{1,0:T(8,128)(2,1)}, bf16[768,2304]{1,0:T(8,128)(2,1)}, bf16[768,768]{1,0:T(8,128)(2,1)}) custom-call(s32[4]{0:T(128)} %pad_add_fusion.where_ref, bf16[512,896]{1,0:T(8,128)(2,1)} %bitcast.128, f32[12,768]{1,0:T(8,128)} %refs_6_.1, bf16[2,48,1536]{2,1,0:T(8,128)(2,1)} %copy-done.38, ...), custom_call_target="tpu_custom_call" | custom-call | flops 1811939328 | bytes 7077888 | tf_op jit(solution)/shard_map/pallas_call | solution.py:619
  76.4 2.7 collective-permute-done.19
  79.8 1.5 collective-permute-start.21
  82.5 1.5 collective-permute-start.24
  84.0 2.0 collective-permute-start.23
  86.0 5.9 %shard_map.213 = (bf16[384,512]{1,0:T(8,128)(2,1)}, f32[3,8,512]{2,1,0:T(8,128)}, bf16[512,384]{1,0:T(8,128)(2,1)}) custom-call(bf16[512,2304]{1,0:T(8,128)(2,1)} %get-tuple-element.245.q_ref.k_ref.v_ref, bf16[512,2304]{1,0:T(8,128)(2,1)} %get-tuple-element.245.q_ref.k_ref.v_ref, bf16[512,2304]{1,0:T(8,128)(2,1)} %get-tuple-element.245.q_ref.k_ref.v_ref, ...), custom_call_target="tpu_custom_call" | custom-call | flops 805306368 | bytes 5505024 | tf_op jit(solution)/shard_map/pallas_call | solution.py:730
  92.0 4.3 %collective-permute-done.24 = bf16[96,768]{1,0:T(8,128)(2,1)S(1)} collective-permute-done((bf16[96,768]{1,0:T(8,128)(2,1)S(1)}, bf16[96,768]{1,0:T(8,128)(2,1)S(1)}, u32[]{:S(2)}, u32[]{:S(2)}) %collective-permute-start.24) | collective-permute-done | bytes 147488 | tf_op jit(solution)/shard_map/ppermute | solution.py:345
  97.0 2.8 all-to-all-start.1
  100.8 1.5 collective-permute-start.27
  102.3 1.5 collective-permute-start.26
  103.8 10.3 %shard_map.214 = (bf16[384,512]{1,0:T(8,128)(2,1)}, f32[3,8,512]{2,1,0:T(8,128)}, f32[512,768]{1,0:T(8,128)}, bf16[512,768]{1,0:T(8,128)(2,1)}) custom-call(bf16[512,2304]{1,0:T(8,128)(2,1)} %get-tuple-element.245.q_ref.k_ref.v_ref, bf16[512,2304]{1,0:T(8,128)(2,1)} %get-tuple-element.245.q_ref.k_ref.v_ref, ...), custom_call_target="tpu_custom_call" | custom-call | flops 805306368 | bytes 5505024 | tf_op jit(solution)/shard_map/pallas_call | solution.py:730
  114.1 1.9 collective-permute-done.27.refs_4_
  120.2 1.5 collective-permute-start.36
  122.8 10.9 %shard_map.215 = (bf16[512,3072]{1,0:T(8,128)(2,1)}, f32[512,3072]{1,0:T(8,128)}, bf16[768,3072]{1,0:T(8,128)(2,1)}) custom-call(s32[4]{0:T(128)} %pad_add_fusion.where_ref, bf16[512,768]{1,0:T(8,128)(2,1)} %get-tuple-element.263.low_ref, f32[1,3072]{1,0:T(1,128)} %bitcast.152, bf16[4,48,1536]{2,1,0:T(8,128)(2,1)} %copy-done.36, ...), custom_call_target="tpu_custom_call" | custom-call | flops 2415919104 | bytes 14155776 | tf_op jit(solution)/shard_map/pallas_call | solution.py:808
  142.7 6.0 %shard_map.216 = (bf16[4,4,96,768]{3,2,1,0:T(8,128)(2,1)S(1)}, bf16[4,4,96,768]{3,2,1,0:T(8,128)(2,1)S(1)}) custom-call(s32[4]{0:T(128)S(1)} %copy-done.26, bf16[512,3072]{1,0:T(8,128)(2,1)} %get-tuple-element.276.hidden_ref, bf16[512,768]{1,0:T(8,128)(2,1)S(1)} %bitcast.138), custom_call_target="tpu_custom_call" | custom-call | flops 2415919104 | bytes 7864320 | tf_op jit(solution)/shard_map/pallas_call | solution.py:854
  149.6 4.2 %collective-permute-done.45.refs_14_ = bf16[2,96,768]{2,1,0:T(8,128)(2,1)S(1)} collective-permute-done((bf16[2,96,768]{2,1,0:T(8,128)(2,1)}, bf16[2,96,768]{2,1,0:T(8,128)(2,1)S(1)}, u32[]{:S(2)}, u32[]{:S(2)}) %collective-permute-start.45) | collective-permute-done | bytes 294944 | tf_op jit(solution)/shard_map/ppermute | solution.py:339
  156.9 9.6 %shard_map.217 = (bf16[512,768]{1,0:T(8,128)(2,1)S(1)}, bf16[3072,768]{1,0:T(8,128)(2,1)}) custom-call(s32[4]{0:T(128)S(1)} %copy-done.26, bf16[512,3072]{1,0:T(8,128)(2,1)} %get-tuple-element.276.hidden_ref, f32[512,768]{1,0:T(8,128)} %get-tuple-element.292.resid_ref, f32[12,768]{1,0:T(8,128)S(1)} %copy-done.9, ...), custom_call_target="tpu_custom_call" | custom-call | flops 2415919104 | bytes 14155776 | tf_op jit(solution)/shard_map/pallas_call | solution.py:913
  167.9 5.7 %all-to-all-start.2 = ((bf16[32,16,768]{2,1,0:T(8,128)(2,1)}), bf16[32,16,768]{2,1,0:T(8,128)(2,1)S(1)}, u32[]{:S(2)}, u32[]{:S(2)}) async-start(bf16[32,16,768]{2,1,0:T(8,128)(2,1)} %bitcast.139), calls=%async_computation.2 | async-start | bytes 1572864 | tf_op jit(solution)/shard_map/all_to_all | solution.py:417
  173.6 1.6 collective-permute-start.50
  175.2 1.5 collective-permute-start.51
  176.7 19.0 %shard_map.218 = (f32[512,768]{1,0:T(8,128)}, bf16[512,768]{1,0:T(8,128)(2,1)}, f32[8,768]{1,0:T(8,128)}, f32[1,3072]{1,0:T(1,128)}, bf16[4,4,24,3840]{3,2,1,0:T(8,128)(2,1)}, /*index=5*/bf16[4,4,24,3840]{3,2,1,0:T(8,128)(2,1)}) custom-call(s32[4]{0:T(128)} %pad_add_fusion.where_ref, f32[512,3072]{1,0:T(8,128)} %get-tuple-element.291.slope_ref, ...), custom_call_target="tpu_custom_call" | custom-call | flops 7247757312 | bytes 34603008 | tf_op jit(solution)/shard_map/pallas_call | solution.py:991
  195.7 1.8 collective-permute-done.50
  197.6 1.9 fusion.29
  200.6 8.1 %shard_map.219 = (bf16[3,512,384]{2,1,0:T(8,128)(2,1)S(1)}, f32[8,384]{1,0:T(8,128)S(1)}) custom-call(bf16[512,2304]{1,0:T(8,128)(2,1)} %get-tuple-element.245.q_ref.k_ref.v_ref, bf16[512,2304]{1,0:T(8,128)(2,1)} %get-tuple-element.245.q_ref.k_ref.v_ref, bf16[512,2304]{1,0:T(8,128)(2,1)} %get-tuple-element.245.q_ref.k_ref.v_ref, ...), custom_call_target="tpu_custom_call" | custom-call | flops 1409286144 | bytes 6291456 | tf_op jit(solution)/shard_map/pallas_call | solution.py:1076
  209.1 1.4 collective-permute-start.53
  211.1 1.5 collective-permute-start.55
  212.6 2.4 collective-permute-start.56
  215.0 1.5 collective-permute-start.57
  216.4 7.9 %shard_map.220 = (bf16[3,512,384]{2,1,0:T(8,128)(2,1)S(1)}, f32[8,384]{1,0:T(8,128)S(1)}) custom-call(bf16[512,2304]{1,0:T(8,128)(2,1)} %get-tuple-element.245.q_ref.k_ref.v_ref, bf16[512,2304]{1,0:T(8,128)(2,1)} %get-tuple-element.245.q_ref.k_ref.v_ref, bf16[512,2304]{1,0:T(8,128)(2,1)} %get-tuple-element.245.q_ref.k_ref.v_ref, ...), custom_call_target="tpu_custom_call" | custom-call | flops 1409286144 | bytes 6291456 | tf_op jit(solution)/shard_map/pallas_call | solution.py:1076
  226.7 1.5 collective-permute-start.58
  228.9 8.5 %shard_map.221 = bf16[512,896]{1,0:T(8,128)(2,1)} custom-call(bf16[512,896]{1,0:T(8,128)(2,1)S(1)} %bitcast.134, bf16[3,512,384]{2,1,0:T(8,128)(2,1)S(1)} %get-tuple-element.334.d_ref, bf16[3,512,384]{2,1,0:T(8,128)(2,1)S(1)} %get-tuple-element.356.e_ref, f32[512,768]{1,0:T(8,128)S(1)} %copy-done.6, f32[12,768]{1,0:T(8,128)S(1)} %copy-done.10, ...), custom_call_target="tpu_custom_call" | custom-call | flops 1811939328 | bytes 3538944 | tf_op jit(solution)/shard_map/pallas_call | solution.py:1181
  237.4 6.1 %all-to-all-start.3 = ((bf16[32,16,896]{2,1,0:T(8,128)(2,1)}), bf16[32,16,896]{2,1,0:T(8,128)(2,1)S(1)}, u32[]{:S(2)}, u32[]{:S(2)}) async-start(bf16[32,16,896]{2,1,0:T(8,128)(2,1)} %bitcast.56), calls=%async_computation.3 | async-start | bytes 1835008 | tf_op jit(solution)/shard_map/all_to_all | solution.py:417
  243.4 6.1 %shard_map.222 = (bf16[4,4,24,2304]{3,2,1,0:T(8,128)(2,1)}, bf16[4,4,24,2304]{3,2,1,0:T(8,128)(2,1)}) custom-call(s32[4]{0:T(128)} %pad_add_fusion.where_ref, bf16[768,512]{1,0:T(8,128)(2,1)} %get-tuple-element.241.flipped_ref, bf16[3,512,384]{2,1,0:T(8,128)(2,1)} %copy-done.7, bf16[3,512,384]{2,1,0:T(8,128)(2,1)} %copy-done.8), custom_call_target="tpu_custom_call" | custom-call | flops 1811939328 | bytes 9437184 | tf_op jit(solution)/shard_map/pallas_call | solution.py:1120
  249.6 1.9 fusion.27
  253.8 1.6 collective-permute-start.61
  255.4 1.5 collective-permute-start.62
  256.8 6.1 %collective-permute-done.61 = bf16[2,24,2304]{2,1,0:T(8,128)(2,1)S(1)} collective-permute-done((bf16[2,24,2304]{2,1,0:T(8,128)(2,1)S(1)}, bf16[2,24,2304]{2,1,0:T(8,128)(2,1)S(1)}, u32[]{:S(2)}, u32[]{:S(2)}) %collective-permute-start.61) | collective-permute-done | bytes 221216 | tf_op jit(solution)/shard_map/ppermute | solution.py:339
  263.7 2.9 all-to-all-done.3.refs_3_
  266.6 1.5 collective-permute-start.63
  268.1 1.5 collective-permute-start.64
  271.6 1.8 collective-permute-start.70
  273.4 5.8 %collective-permute-done.65 = bf16[24,3840]{1,0:T(8,128)(2,1)S(1)} collective-permute-done((bf16[24,3840]{1,0:T(8,128)(2,1)}, bf16[24,3840]{1,0:T(8,128)(2,1)S(1)}, u32[]{:S(2)}, u32[]{:S(2)}) %collective-permute-start.65) | collective-permute-done | bytes 184352 | tf_op jit(solution)/shard_map/ppermute | solution.py:413
  283.2 4.3 %collective-permute-start.67 = (bf16[24,2304]{1,0:T(8,128)(2,1)S(1)}, bf16[24,2304]{1,0:T(8,128)(2,1)S(1)}, u32[]{:S(2)}, u32[]{:S(2)}) collective-permute-start(bf16[24,2304]{1,0:T(8,128)(2,1)S(1)} %get-tuple-element.389), channel_id=1, source_target_pairs={{0,16},{1,17},{2,18},{3,19},{4,20},{5,21},{6,22},{7,23},{8,24},{9,... | collective-permute-start | bytes 331784 | tf_op jit(solution)/shard_map/ppermute | solution.py:413
  287.5 2.9 collective-permute-start.68
  290.4 1.5 multiply_reduce_fusion
  291.9 1.4 multiply_reduce_fusion.1
  294.7 1.5 shard_map.223
  296.9 2.0 shard_map.225
  298.9 4.4 %all-to-all-start.4 = ((f32[32,4,128]{2,1,0:T(4,128)}), f32[32,4,128]{2,1,0:T(4,128)S(1)}, u32[]{:S(2)}, u32[]{:S(2)}) async-start(f32[32,4,128]{2,1,0:T(4,128)} %get-tuple-element.408), calls=%async_computation.4 | async-start | bytes 131072 | tf_op jit(solution)/shard_map/all_to_all | solution.py:417
  303.4 1.5 shard_map.224
  304.9 5.9 %all-to-all-done.4.packets_ref = f32[32,4,128]{2,1,0:T(4,128)S(1)} async-done(((f32[32,4,128]{2,1,0:T(4,128)}), f32[32,4,128]{2,1,0:T(4,128)S(1)}, u32[]{:S(2)}, u32[]{:S(2)}) %all-to-all-start.4) | async-done | bytes 65568 | tf_op jit(solution)/shard_map/all_to_all | solution.py:417
  311.4 3.8 %shard_map.226 = (f32[1,1]{1,0:T(1,128)}, f32[24,6144]{1,0:T(8,128)}, f32[24,6144]{1,0:T(8,128)}, f32[24,6144]{1,0:T(8,128)}, f32[96,768]{1,0:T(8,128)}, /*index...) custom-call(f32[32,4,128]{2,1,0:T(4,128)} %copy-done.39, ...), custom_call_target="tpu_custom_call" | custom-call | flops 2949120 | bytes 5898240 | tf_op jit(solution)/shard_map/pallas_call | solution.py:1300
  (270 shorter events, 50.7 us)
Async XLA Ops:
  4.2 9.7 %collective-permute-start.1 = (bf16[48,1536]{1,0:T(8,128)(2,1)S(1)}, bf16[48,1536]{1,0:T(8,128)(2,1)S(1)}, u32[]{:S(2)}, u32[]{:S(2)}) collective-permute-start(bf16[48,1536]{1,0:T(8,128)(2,1)S(1)} %get-tuple-element.462), channel_id=1, source_target_pairs={{0,8},{1,9},{2,10},{3,11},{4,12},{5,13},{6,14},{7,15},{8,16},{9,17... | collective-permute-start | bytes 442376 | tf_op jit(solution)/shard_map/ppermute | solution.py:345
  7.2 16.2 %collective-permute-start.4 = (bf16[48,1536]{1,0:T(8,128)(2,1)S(1)}, bf16[48,1536]{1,0:T(8,128)(2,1)S(1)}, u32[]{:S(2)}, u32[]{:S(2)}) collective-permute-start(bf16[48,1536]{1,0:T(8,128)(2,1)S(1)} %get-tuple-element.462), channel_id=1, source_target_pairs={{0,24},{1,25},{2,26},{3,27},{4,28},{5,29},{6,30},{7,31},{8,0},{9,1... | collective-permute-start | bytes 442376 | tf_op jit(solution)/shard_map/ppermute | solution.py:345
  9.3 14.1 %collective-permute-start.3 = (bf16[48,1536]{1,0:T(8,128)(2,1)S(1)}, bf16[48,1536]{1,0:T(8,128)(2,1)S(1)}, u32[]{:S(2)}, u32[]{:S(2)}) collective-permute-start(bf16[48,1536]{1,0:T(8,128)(2,1)S(1)} %get-tuple-element.462), channel_id=1, source_target_pairs={{0,16},{1,17},{2,18},{3,19},{4,20},{5,21},{6,22},{7,23},{8,24},{9,... | collective-permute-start | bytes 442376 | tf_op jit(solution)/shard_map/ppermute | solution.py:345
  13.9 48.8 %all-to-all-start = ((bf16[32,16,896]{2,1,0:T(8,128)(2,1)}), bf16[32,16,896]{2,1,0:T(8,128)(2,1)S(1)}, u32[]{:S(2)}, u32[]{:S(2)}) async-start(bf16[32,16,896]{2,1,0:T(8,128)(2,1)} %bitcast.12), calls=%async_computation | async-start | bytes 1835008 | tf_op jit(solution)/shard_map/all_to_all | solution.py:417
  23.5 17.9 %collective-permute-start.7 = (bf16[2,48,1536]{2,1,0:T(8,128)(2,1)S(1)}, bf16[2,48,1536]{2,1,0:T(8,128)(2,1)S(1)}, u32[]{:S(2)}, u32[]{:S(2)}) collective-permute-start(bf16[2,48,1536]{2,1,0:T(8,128)(2,1)S(1)} %pad_maximum_fusion.8.refs_1_), channel_id=1, source_target_pairs={{0,4},{1,5},{2,6},{3,7},{4,0},{5,1},{6,2},{7,3},{8,12},{9,13},{10,... | collective-permute-start | bytes 884744 | tf_op jit(solution)/shard_map/ppermute | solution.py:339
  25.3 16.4 %collective-permute-start.5 = (bf16[2,48,1536]{2,1,0:T(8,128)(2,1)S(1)}, bf16[2,48,1536]{2,1,0:T(8,128)(2,1)S(1)}, u32[]{:S(2)}, u32[]{:S(2)}) collective-permute-start(bf16[2,48,1536]{2,1,0:T(8,128)(2,1)S(1)} %pad_maximum_fusion.8.refs_1_), channel_id=1, source_target_pairs={{0,2},{1,3},{2,0},{3,1},{4,6},{5,7},{6,4},{7,5},{8,10},{9,11},{10,... | collective-permute-start | bytes 884744 | tf_op jit(solution)/shard_map/ppermute | solution.py:339
  26.8 21.9 %collective-permute-start.6 = (bf16[2,48,1536]{2,1,0:T(8,128)(2,1)S(1)}, bf16[2,48,1536]{2,1,0:T(8,128)(2,1)S(1)}, u32[]{:S(2)}, u32[]{:S(2)}) collective-permute-start(bf16[2,48,1536]{2,1,0:T(8,128)(2,1)S(1)} %pad_maximum_fusion.7.refs_0_), channel_id=1, source_target_pairs={{0,4},{1,5},{2,6},{3,7},{4,0},{5,1},{6,2},{7,3},{8,12},{9,13},{10,... | collective-permute-start | bytes 884744 | tf_op jit(solution)/shard_map/ppermute | solution.py:339
  27.5 21.3 %collective-permute-start.2 = (bf16[2,48,1536]{2,1,0:T(8,128)(2,1)S(1)}, bf16[2,48,1536]{2,1,0:T(8,128)(2,1)S(1)}, u32[]{:S(2)}, u32[]{:S(2)}) collective-permute-start(bf16[2,48,1536]{2,1,0:T(8,128)(2,1)S(1)} %pad_maximum_fusion.7.refs_0_), channel_id=1, source_target_pairs={{0,2},{1,3},{2,0},{3,1},{4,6},{5,7},{6,4},{7,5},{8,10},{9,11},{10,... | collective-permute-start | bytes 884744 | tf_op jit(solution)/shard_map/ppermute | solution.py:339
  27.7 23.0 %collective-permute-start.11 = (bf16[2,48,1536]{2,1,0:T(8,128)(2,1)S(1)}, bf16[2,48,1536]{2,1,0:T(8,128)(2,1)S(1)}, u32[]{:S(2)}, u32[]{:S(2)}) collective-permute-start(bf16[2,48,1536]{2,1,0:T(8,128)(2,1)S(1)} %pad_maximum_fusion.8.refs_1_), channel_id=1, source_target_pairs={{0,1},{1,0},{2,3},{3,2},{4,5},{5,4},{6,7},{7,6},{8,9},{9,8},{10,11... | collective-permute-start | bytes 884744 | tf_op jit(solution)/shard_map/ppermute | solution.py:339
  41.4 9.4 %collective-permute-start.10 = (bf16[2,48,1536]{2,1,0:T(8,128)(2,1)S(1)}, bf16[2,48,1536]{2,1,0:T(8,128)(2,1)S(1)}, u32[]{:S(2)}, u32[]{:S(2)}) collective-permute-start(bf16[2,48,1536]{2,1,0:T(8,128)(2,1)S(1)} %pad_maximum_fusion.7.refs_0_), channel_id=1, source_target_pairs={{0,1},{1,0},{2,3},{3,2},{4,5},{5,4},{6,7},{7,6},{8,9},{9,8},{10,11... | collective-permute-start | bytes 884744 | tf_op jit(solution)/shard_map/ppermute | solution.py:339
  49.3 9.1 %collective-permute-start.8 = (bf16[2,48,1536]{2,1,0:T(8,128)(2,1)S(1)}, bf16[2,48,1536]{2,1,0:T(8,128)(2,1)}, u32[]{:S(2)}, u32[]{:S(2)}) collective-permute-start(bf16[2,48,1536]{2,1,0:T(8,128)(2,1)S(1)} %collective-permute-done.2.refs_2_), channel_id=1, source_target_pairs={{0,4},{1,5},{2,6},{3,7},{4,0},{5,1},{6,2},{7,3},{8,12},{9,13},{10,... | collective-permute-start | bytes 884744 | tf_op jit(solution)/shard_map/ppermute | solution.py:339
  50.8 7.7 %collective-permute-start.15 = (bf16[2,48,1536]{2,1,0:T(8,128)(2,1)S(1)}, bf16[2,48,1536]{2,1,0:T(8,128)(2,1)S(1)}, u32[]{:S(2)}, u32[]{:S(2)}) collective-permute-start(bf16[2,48,1536]{2,1,0:T(8,128)(2,1)S(1)} %collective-permute-done.7.refs_5_), channel_id=1, source_target_pairs={{0,1},{1,0},{2,3},{3,2},{4,5},{5,4},{6,7},{7,6},{8,9},{9,8},{10,11... | collective-permute-start | bytes 884744 | tf_op jit(solution)/shard_map/ppermute | solution.py:339
  51.3 9.1 %collective-permute-start.9 = (bf16[2,48,1536]{2,1,0:T(8,128)(2,1)S(1)}, bf16[2,48,1536]{2,1,0:T(8,128)(2,1)}, u32[]{:S(2)}, u32[]{:S(2)}) collective-permute-start(bf16[2,48,1536]{2,1,0:T(8,128)(2,1)S(1)} %collective-permute-done.7.refs_5_), channel_id=1, source_target_pairs={{0,2},{1,3},{2,0},{3,1},{4,6},{5,7},{6,4},{7,5},{8,10},{9,11},{10,... | collective-permute-start | bytes 884744 | tf_op jit(solution)/shard_map/ppermute | solution.py:339
  62.7 13.6 %collective-permute-start.20 = (bf16[48,1536]{1,0:T(8,128)(2,1)S(1)}, bf16[48,1536]{1,0:T(8,128)(2,1)S(1)}, u32[]{:S(2)}, u32[]{:S(2)}) collective-permute-start(bf16[48,1536]{1,0:T(8,128)(2,1)S(1)} %get-tuple-element.243), channel_id=1, source_target_pairs={{0,24},{1,25},{2,26},{3,27},{4,28},{5,29},{6,30},{7,31},{8,0},{9,1... | collective-permute-start | bytes 442376 | tf_op jit(solution)/shard_map/ppermute | solution.py:345
  66.0 13.0 %collective-permute-start.19 = (bf16[48,1536]{1,0:T(8,128)(2,1)S(1)}, bf16[48,1536]{1,0:T(8,128)(2,1)S(1)}, u32[]{:S(2)}, u32[]{:S(2)}) collective-permute-start(bf16[48,1536]{1,0:T(8,128)(2,1)S(1)} %get-tuple-element.243), channel_id=1, source_target_pairs={{0,16},{1,17},{2,18},{3,19},{4,20},{5,21},{6,22},{7,23},{8,24},{9,... | collective-permute-start | bytes 442376 | tf_op jit(solution)/shard_map/ppermute | solution.py:345
  66.0 13.0 %collective-permute-start.18 = (bf16[48,1536]{1,0:T(8,128)(2,1)S(1)}, bf16[48,1536]{1,0:T(8,128)(2,1)S(1)}, u32[]{:S(2)}, u32[]{:S(2)}) collective-permute-start(bf16[48,1536]{1,0:T(8,128)(2,1)S(1)} %get-tuple-element.243), channel_id=1, source_target_pairs={{0,8},{1,9},{2,10},{3,11},{4,12},{5,13},{6,14},{7,15},{8,16},{9,17... | collective-permute-start | bytes 442376 | tf_op jit(solution)/shard_map/ppermute | solution.py:345
  79.1 17.2 %collective-permute-start.22 = (bf16[4,48,1536]{2,1,0:T(8,128)(2,1)S(1)}, bf16[4,48,1536]{2,1,0:T(8,128)(2,1)S(1)}, u32[]{:S(2)}, u32[]{:S(2)}) collective-permute-start(bf16[4,48,1536]{2,1,0:T(8,128)(2,1)S(1)} %pad_maximum_fusion.2.refs_0_), channel_id=1, source_target_pairs={{0,4},{1,5},{2,6},{3,7},{4,0},{5,1},{6,2},{7,3},{8,12},{9,13},{10,... | collective-permute-start | bytes 1769480 | tf_op jit(solution)/shard_map/ppermute | solution.py:339
  79.8 16.6 %collective-permute-start.21 = (bf16[4,48,1536]{2,1,0:T(8,128)(2,1)S(1)}, bf16[4,48,1536]{2,1,0:T(8,128)(2,1)}, u32[]{:S(2)}, u32[]{:S(2)}) collective-permute-start(bf16[4,48,1536]{2,1,0:T(8,128)(2,1)S(1)} %pad_maximum_fusion.2.refs_0_), channel_id=1, source_target_pairs={{0,2},{1,3},{2,0},{3,1},{4,6},{5,7},{6,4},{7,5},{8,10},{9,11},{10,... | collective-permute-start | bytes 1769480 | tf_op jit(solution)/shard_map/ppermute | solution.py:339
  81.3 10.6 %collective-permute-start.25 = (bf16[96,768]{1,0:T(8,128)(2,1)S(1)}, bf16[96,768]{1,0:T(8,128)(2,1)S(1)}, u32[]{:S(2)}, u32[]{:S(2)}) collective-permute-start(bf16[96,768]{1,0:T(8,128)(2,1)S(1)} %convert_element_type.355), channel_id=1, source_target_pairs={{0,24},{1,25},{2,26},{3,27},{4,28},{5,29},{6,30},{7,31},{8,0},{9,1... | collective-permute-start | bytes 442376 | tf_op jit(solution)/shard_map/ppermute | solution.py:345
  82.5 13.8 %collective-permute-start.24 = (bf16[96,768]{1,0:T(8,128)(2,1)S(1)}, bf16[96,768]{1,0:T(8,128)(2,1)S(1)}, u32[]{:S(2)}, u32[]{:S(2)}) collective-permute-start(bf16[96,768]{1,0:T(8,128)(2,1)S(1)} %convert_element_type.355), channel_id=1, source_target_pairs={{0,16},{1,17},{2,18},{3,19},{4,20},{5,21},{6,22},{7,23},{8,24},{9,... | collective-permute-start | bytes 442376 | tf_op jit(solution)/shard_map/ppermute | solution.py:345
  84.0 12.3 %collective-permute-start.23 = (bf16[96,768]{1,0:T(8,128)(2,1)S(1)}, bf16[96,768]{1,0:T(8,128)(2,1)S(1)}, u32[]{:S(2)}, u32[]{:S(2)}) collective-permute-start(bf16[96,768]{1,0:T(8,128)(2,1)S(1)} %convert_element_type.355), channel_id=1, source_target_pairs={{0,8},{1,9},{2,10},{3,11},{4,12},{5,13},{6,14},{7,15},{8,16},{9,17... | collective-permute-start | bytes 442376 | tf_op jit(solution)/shard_map/ppermute | solution.py:345
  91.9 22.2 %collective-permute-start.28 = (bf16[4,48,1536]{2,1,0:T(8,128)(2,1)S(1)}, bf16[4,48,1536]{2,1,0:T(8,128)(2,1)}, u32[]{:S(2)}, u32[]{:S(2)}) collective-permute-start(bf16[4,48,1536]{2,1,0:T(8,128)(2,1)S(1)} %pad_maximum_fusion.2.refs_0_), channel_id=1, source_target_pairs={{0,1},{1,0},{2,3},{3,2},{4,5},{5,4},{6,7},{7,6},{8,9},{9,8},{10,11... | collective-permute-start | bytes 1769480 | tf_op jit(solution)/shard_map/ppermute | solution.py:339
  96.4 19.7 %collective-permute-start.29 = (bf16[4,48,1536]{2,1,0:T(8,128)(2,1)}, bf16[4,48,1536]{2,1,0:T(8,128)(2,1)}, u32[]{:S(2)}, u32[]{:S(2)}) collective-permute-start(bf16[4,48,1536]{2,1,0:T(8,128)(2,1)} %collective-permute-done.21.refs_1_), channel_id=1, source_target_pairs={{0,1},{1,0},{2,3},{3,2},{4,5},{5,4},{6,7},{7,6},{8,9},{9,8},{10,11... | collective-permute-start | bytes 1769480 | tf_op jit(solution)/shard_map/ppermute | solution.py:339
  96.5 19.6 %collective-permute-start.30 = (bf16[4,48,1536]{2,1,0:T(8,128)(2,1)S(1)}, bf16[4,48,1536]{2,1,0:T(8,128)(2,1)}, u32[]{:S(2)}, u32[]{:S(2)}) collective-permute-start(bf16[4,48,1536]{2,1,0:T(8,128)(2,1)S(1)} %collective-permute-done.22.refs_2_), channel_id=1, source_target_pairs={{0,1},{1,0},{2,3},{3,2},{4,5},{5,4},{6,7},{7,6},{8,9},{9,8},{10,11... | collective-permute-start | bytes 1769480 | tf_op jit(solution)/shard_map/ppermute | solution.py:339
  97.0 43.7 %all-to-all-start.1 = ((bf16[32,16,768]{2,1,0:T(8,128)(2,1)}), bf16[32,16,768]{2,1,0:T(8,128)(2,1)S(1)}, u32[]{:S(2)}, u32[]{:S(2)}) async-start(bf16[32,16,768]{2,1,0:T(8,128)(2,1)} %bitcast.23), calls=%async_computation.1 | async-start | bytes 1572864 | tf_op jit(solution)/shard_map/all_to_all | solution.py:417
  100.8 15.2 %collective-permute-start.27 = (bf16[2,48,1536]{2,1,0:T(8,128)(2,1)S(1)}, bf16[2,48,1536]{2,1,0:T(8,128)(2,1)S(1)}, u32[]{:S(2)}, u32[]{:S(2)}) collective-permute-start(bf16[2,48,1536]{2,1,0:T(8,128)(2,1)S(1)} %slice.197), channel_id=1, source_target_pairs={{0,2},{1,3},{2,0},{3,1},{4,6},{5,7},{6,4},{7,5},{8,10},{9,11},{10,... | collective-permute-start | bytes 884744 | tf_op jit(solution)/shard_map/ppermute | solution.py:339
  102.3 13.7 %collective-permute-start.26 = (bf16[2,48,1536]{2,1,0:T(8,128)(2,1)S(1)}, bf16[2,48,1536]{2,1,0:T(8,128)(2,1)}, u32[]{:S(2)}, u32[]{:S(2)}) collective-permute-start(bf16[2,48,1536]{2,1,0:T(8,128)(2,1)S(1)} %slice.196), channel_id=1, source_target_pairs={{0,4},{1,5},{2,6},{3,7},{4,0},{5,1},{6,2},{7,3},{8,12},{9,13},{10,... | collective-permute-start | bytes 884744 | tf_op jit(solution)/shard_map/ppermute | solution.py:339
  118.1 15.7 %collective-permute-start.35 = (bf16[2,96,768]{2,1,0:T(8,128)(2,1)S(1)}, bf16[2,96,768]{2,1,0:T(8,128)(2,1)}, u32[]{:S(2)}, u32[]{:S(2)}) collective-permute-start(bf16[2,96,768]{2,1,0:T(8,128)(2,1)S(1)} %pad_maximum_fusion.9.refs_0_), channel_id=1, source_target_pairs={{0,4},{1,5},{2,6},{3,7},{4,0},{5,1},{6,2},{7,3},{8,12},{9,13},{10,... | collective-permute-start | bytes 884744 | tf_op jit(solution)/shard_map/ppermute | solution.py:339
  119.5 14.9 %collective-permute-start.33 = (bf16[2,96,768]{2,1,0:T(8,128)(2,1)S(1)}, bf16[2,96,768]{2,1,0:T(8,128)(2,1)}, u32[]{:S(2)}, u32[]{:S(2)}) collective-permute-start(bf16[2,96,768]{2,1,0:T(8,128)(2,1)S(1)} %pad_maximum_fusion.9.refs_0_), channel_id=1, source_target_pairs={{0,2},{1,3},{2,0},{3,1},{4,6},{5,7},{6,4},{7,5},{8,10},{9,11},{10,... | collective-permute-start | bytes 884744 | tf_op jit(solution)/shard_map/ppermute | solution.py:339
  120.2 14.2 %collective-permute-start.36 = (bf16[2,96,768]{2,1,0:T(8,128)(2,1)S(1)}, bf16[2,96,768]{2,1,0:T(8,128)(2,1)}, u32[]{:S(2)}, u32[]{:S(2)}) collective-permute-start(bf16[2,96,768]{2,1,0:T(8,128)(2,1)S(1)} %pad_maximum_fusion.10.refs_1_), channel_id=1, source_target_pairs={{0,4},{1,5},{2,6},{3,7},{4,0},{5,1},{6,2},{7,3},{8,12},{9,13},{10,... | collective-permute-start | bytes 884744 | tf_op jit(solution)/shard_map/ppermute | solution.py:339
  121.7 12.9 %collective-permute-start.34 = (bf16[2,96,768]{2,1,0:T(8,128)(2,1)S(1)}, bf16[2,96,768]{2,1,0:T(8,128)(2,1)S(1)}, u32[]{:S(2)}, u32[]{:S(2)}) collective-permute-start(bf16[2,96,768]{2,1,0:T(8,128)(2,1)S(1)} %pad_maximum_fusion.10.refs_1_), channel_id=1, source_target_pairs={{0,2},{1,3},{2,0},{3,1},{4,6},{5,7},{6,4},{7,5},{8,10},{9,11},{10,... | collective-permute-start | bytes 884744 | tf_op jit(solution)/shard_map/ppermute | solution.py:339
  122.8 14.2 %collective-permute-start.39 = (bf16[2,96,768]{2,1,0:T(8,128)(2,1)S(1)}, bf16[2,96,768]{2,1,0:T(8,128)(2,1)S(1)}, u32[]{:S(2)}, u32[]{:S(2)}) collective-permute-start(bf16[2,96,768]{2,1,0:T(8,128)(2,1)S(1)} %pad_maximum_fusion.9.refs_0_), channel_id=1, source_target_pairs={{0,1},{1,0},{2,3},{3,2},{4,5},{5,4},{6,7},{7,6},{8,9},{9,8},{10,11... | collective-permute-start | bytes 884744 | tf_op jit(solution)/shard_map/ppermute | solution.py:339
  135.3 13.4 %collective-permute-start.41 = (bf16[2,96,768]{2,1,0:T(8,128)(2,1)}, bf16[2,96,768]{2,1,0:T(8,128)(2,1)}, u32[]{:S(2)}, u32[]{:S(2)}) collective-permute-start(bf16[2,96,768]{2,1,0:T(8,128)(2,1)} %collective-permute-done.33.refs_2_), channel_id=1, source_target_pairs={{0,1},{1,0},{2,3},{3,2},{4,5},{5,4},{6,7},{7,6},{8,9},{9,8},{10,11... | collective-permute-start | bytes 884744 | tf_op jit(solution)/shard_map/ppermute | solution.py:339
  135.8 12.9 %collective-permute-start.37 = (bf16[2,96,768]{2,1,0:T(8,128)(2,1)}, bf16[2,96,768]{2,1,0:T(8,128)(2,1)}, u32[]{:S(2)}, u32[]{:S(2)}) collective-permute-start(bf16[2,96,768]{2,1,0:T(8,128)(2,1)} %collective-permute-done.33.refs_2_), channel_id=1, source_target_pairs={{0,4},{1,5},{2,6},{3,7},{4,0},{5,1},{6,2},{7,3},{8,12},{9,13},{10,... | collective-permute-start | bytes 884744 | tf_op jit(solution)/shard_map/ppermute | solution.py:339
  137.7 10.9 %collective-permute-start.43 = (bf16[2,96,768]{2,1,0:T(8,128)(2,1)}, bf16[2,96,768]{2,1,0:T(8,128)(2,1)}, u32[]{:S(2)}, u32[]{:S(2)}) collective-permute-start(bf16[2,96,768]{2,1,0:T(8,128)(2,1)} %collective-permute-done.35.refs_4_), channel_id=1, source_target_pairs={{0,1},{1,0},{2,3},{3,2},{4,5},{5,4},{6,7},{7,6},{8,9},{9,8},{10,11... | collective-permute-start | bytes 884744 | tf_op jit(solution)/shard_map/ppermute | solution.py:339
  138.4 10.2 %collective-permute-start.44 = (bf16[2,96,768]{2,1,0:T(8,128)(2,1)}, bf16[2,96,768]{2,1,0:T(8,128)(2,1)}, u32[]{:S(2)}, u32[]{:S(2)}) collective-permute-start(bf16[2,96,768]{2,1,0:T(8,128)(2,1)} %collective-permute-done.36.refs_5_), channel_id=1, source_target_pairs={{0,1},{1,0},{2,3},{3,2},{4,5},{5,4},{6,7},{7,6},{8,9},{9,8},{10,11... | collective-permute-start | bytes 884744 | tf_op jit(solution)/shard_map/ppermute | solution.py:339
  139.7 9.2 %collective-permute-start.38 = (bf16[2,96,768]{2,1,0:T(8,128)(2,1)}, bf16[2,96,768]{2,1,0:T(8,128)(2,1)}, u32[]{:S(2)}, u32[]{:S(2)}) collective-permute-start(bf16[2,96,768]{2,1,0:T(8,128)(2,1)} %collective-permute-done.36.refs_5_), channel_id=1, source_target_pairs={{0,2},{1,3},{2,0},{3,1},{4,6},{5,7},{6,4},{7,5},{8,10},{9,11},{10,... | collective-permute-start | bytes 884744 | tf_op jit(solution)/shard_map/ppermute | solution.py:339
  148.9 5.4 %collective-permute-start.47 = (bf16[4,4,96,768]{3,2,1,0:T(8,128)(2,1)S(1)}, bf16[4,4,96,768]{3,2,1,0:T(8,128)(2,1)S(1)}, u32[]{:S(2)}, u32[]{:S(2)}) collective-permute-start(bf16[4,4,96,768]{3,2,1,0:T(8,128)(2,1)S(1)} %get-tuple-element.289), channel_id=1, source_target_pairs={{0,1},{1,0},{2,3},{3,2},{4,5},{5,4},{6,7},{7,6},{8,9},{9,8},{10,11... | collective-permute-start | bytes 7077896 | tf_op jit(solution)/shard_map/ppermute | solution.py:339
  149.0 4.8 %collective-permute-start.45 = (bf16[2,96,768]{2,1,0:T(8,128)(2,1)}, bf16[2,96,768]{2,1,0:T(8,128)(2,1)S(1)}, u32[]{:S(2)}, u32[]{:S(2)}) collective-permute-start(bf16[2,96,768]{2,1,0:T(8,128)(2,1)} %collective-permute-done.37.refs_6_), channel_id=1, source_target_pairs={{0,1},{1,0},{2,3},{3,2},{4,5},{5,4},{6,7},{7,6},{8,9},{9,8},{10,11... | collective-permute-start | bytes 884744 | tf_op jit(solution)/shard_map/ppermute | solution.py:339
  154.7 11.9 %collective-permute-start.48 = (bf16[2,96,768]{2,1,0:T(8,128)(2,1)S(1)}, bf16[2,96,768]{2,1,0:T(8,128)(2,1)S(1)}, u32[]{:S(2)}, u32[]{:S(2)}) collective-permute-start(bf16[2,96,768]{2,1,0:T(8,128)(2,1)S(1)} %get-tuple-element.312), channel_id=1, source_target_pairs={{0,4},{1,5},{2,6},{3,7},{4,0},{5,1},{6,2},{7,3},{8,12},{9,13},{10,... | collective-permute-start | bytes 884744 | tf_op jit(solution)/shard_map/ppermute | solution.py:339
  155.7 10.8 %collective-permute-start.49 = (bf16[2,96,768]{2,1,0:T(8,128)(2,1)S(1)}, bf16[2,96,768]{2,1,0:T(8,128)(2,1)S(1)}, u32[]{:S(2)}, u32[]{:S(2)}) collective-permute-start(bf16[2,96,768]{2,1,0:T(8,128)(2,1)S(1)} %get-tuple-element.313), channel_id=1, source_target_pairs={{0,2},{1,3},{2,0},{3,1},{4,6},{5,7},{6,4},{7,5},{8,10},{9,11},{10,... | collective-permute-start | bytes 884744 | tf_op jit(solution)/shard_map/ppermute | solution.py:339
  167.9 29.6 %all-to-all-start.2 = ((bf16[32,16,768]{2,1,0:T(8,128)(2,1)}), bf16[32,16,768]{2,1,0:T(8,128)(2,1)S(1)}, u32[]{:S(2)}, u32[]{:S(2)}) async-start(bf16[32,16,768]{2,1,0:T(8,128)(2,1)} %bitcast.139), calls=%async_computation.2 | async-start | bytes 1572864 | tf_op jit(solution)/shard_map/all_to_all | solution.py:417
  173.6 23.8 %collective-permute-start.50 = (bf16[4,96,768]{2,1,0:T(8,128)(2,1)}, bf16[4,96,768]{2,1,0:T(8,128)(2,1)}, u32[]{:S(2)}, u32[]{:S(2)}) collective-permute-start(bf16[4,96,768]{2,1,0:T(8,128)(2,1)} %get-tuple-element.321), channel_id=1, source_target_pairs={{0,2},{1,3},{2,0},{3,1},{4,6},{5,7},{6,4},{7,5},{8,10},{9,11},{10,... | collective-permute-start | bytes 1769480 | tf_op jit(solution)/shard_map/ppermute | solution.py:339
  175.2 22.3 %collective-permute-start.51 = (bf16[4,96,768]{2,1,0:T(8,128)(2,1)}, bf16[4,96,768]{2,1,0:T(8,128)(2,1)}, u32[]{:S(2)}, u32[]{:S(2)}) collective-permute-start(bf16[4,96,768]{2,1,0:T(8,128)(2,1)} %get-tuple-element.322), channel_id=1, source_target_pairs={{0,4},{1,5},{2,6},{3,7},{4,0},{5,1},{6,2},{7,3},{8,12},{9,13},{10,... | collective-permute-start | bytes 1769480 | tf_op jit(solution)/shard_map/ppermute | solution.py:339
  199.5 9.3 %collective-permute-start.52 = (bf16[4,4,24,3840]{3,2,1,0:T(8,128)(2,1)}, bf16[4,4,24,3840]{3,2,1,0:T(8,128)(2,1)S(1)}, u32[]{:S(2)}, u32[]{:S(2)}) collective-permute-start(bf16[4,4,24,3840]{3,2,1,0:T(8,128)(2,1)} %get-tuple-element.330), channel_id=1, source_target_pairs={{0,1},{1,0},{2,3},{3,2},{4,5},{5,4},{6,7},{7,6},{8,9},{9,8},{10,11... | collective-permute-start | bytes 8847368 | tf_op jit(solution)/shard_map/ppermute | solution.py:339
  209.1 15.3 %collective-permute-start.53 = (bf16[2,24,3840]{2,1,0:T(8,128)(2,1)S(1)}, bf16[2,24,3840]{2,1,0:T(8,128)(2,1)S(1)}, u32[]{:S(2)}, u32[]{:S(2)}) collective-permute-start(bf16[2,24,3840]{2,1,0:T(8,128)(2,1)S(1)} %get-tuple-element.338), channel_id=1, source_target_pairs={{0,4},{1,5},{2,6},{3,7},{4,0},{5,1},{6,2},{7,3},{8,12},{9,13},{10,... | collective-permute-start | bytes 1105928 | tf_op jit(solution)/shard_map/ppermute | solution.py:339
  210.6 13.9 %collective-permute-start.54 = (bf16[2,24,3840]{2,1,0:T(8,128)(2,1)S(1)}, bf16[2,24,3840]{2,1,0:T(8,128)(2,1)S(1)}, u32[]{:S(2)}, u32[]{:S(2)}) collective-permute-start(bf16[2,24,3840]{2,1,0:T(8,128)(2,1)S(1)} %get-tuple-element.339), channel_id=1, source_target_pairs={{0,2},{1,3},{2,0},{3,1},{4,6},{5,7},{6,4},{7,5},{8,10},{9,11},{10,... | collective-permute-start | bytes 1105928 | tf_op jit(solution)/shard_map/ppermute | solution.py:339
  211.1 13.3 %collective-permute-start.55 = (bf16[96,768]{1,0:T(8,128)(2,1)S(1)}, bf16[96,768]{1,0:T(8,128)(2,1)S(1)}, u32[]{:S(2)}, u32[]{:S(2)}) collective-permute-start(bf16[96,768]{1,0:T(8,128)(2,1)S(1)} %get-tuple-element.343), channel_id=1, source_target_pairs={{0,8},{1,9},{2,10},{3,11},{4,12},{5,13},{6,14},{7,15},{8,16},{9,17... | collective-permute-start | bytes 442376 | tf_op jit(solution)/shard_map/ppermute | solution.py:413
  212.6 11.8 %collective-permute-start.56 = (bf16[96,768]{1,0:T(8,128)(2,1)S(1)}, bf16[96,768]{1,0:T(8,128)(2,1)S(1)}, u32[]{:S(2)}, u32[]{:S(2)}) collective-permute-start(bf16[96,768]{1,0:T(8,128)(2,1)S(1)} %get-tuple-element.344), channel_id=1, source_target_pairs={{0,16},{1,17},{2,18},{3,19},{4,20},{5,21},{6,22},{7,23},{8,24},{9,... | collective-permute-start | bytes 442376 | tf_op jit(solution)/shard_map/ppermute | solution.py:413
  215.0 9.5 %collective-permute-start.57 = (bf16[96,768]{1,0:T(8,128)(2,1)S(1)}, bf16[96,768]{1,0:T(8,128)(2,1)S(1)}, u32[]{:S(2)}, u32[]{:S(2)}) collective-permute-start(bf16[96,768]{1,0:T(8,128)(2,1)S(1)} %get-tuple-element.345), channel_id=1, source_target_pairs={{0,24},{1,25},{2,26},{3,27},{4,28},{5,29},{6,30},{7,31},{8,0},{9,1... | collective-permute-start | bytes 442376 | tf_op jit(solution)/shard_map/ppermute | solution.py:413
  226.7 22.8 %collective-permute-start.58 = (bf16[4,24,3840]{2,1,0:T(8,128)(2,1)}, bf16[4,24,3840]{2,1,0:T(8,128)(2,1)S(1)}, u32[]{:S(2)}, u32[]{:S(2)}) collective-permute-start(bf16[4,24,3840]{2,1,0:T(8,128)(2,1)} %pad_maximum_fusion), channel_id=1, source_target_pairs={{0,2},{1,3},{2,0},{3,1},{4,6},{5,7},{6,4},{7,5},{8,10},{9,11},{10,... | collective-permute-start | bytes 2211848 | tf_op jit(solution)/shard_map/ppermute | solution.py:339
  228.2 21.3 %collective-permute-start.59 = (bf16[4,24,3840]{2,1,0:T(8,128)(2,1)}, bf16[4,24,3840]{2,1,0:T(8,128)(2,1)}, u32[]{:S(2)}, u32[]{:S(2)}) collective-permute-start(bf16[4,24,3840]{2,1,0:T(8,128)(2,1)} %pad_maximum_fusion.1), channel_id=1, source_target_pairs={{0,4},{1,5},{2,6},{3,7},{4,0},{5,1},{6,2},{7,3},{8,12},{9,13},{10,... | collective-permute-start | bytes 2211848 | tf_op jit(solution)/shard_map/ppermute | solution.py:339
  237.4 29.3 %all-to-all-start.3 = ((bf16[32,16,896]{2,1,0:T(8,128)(2,1)}), bf16[32,16,896]{2,1,0:T(8,128)(2,1)S(1)}, u32[]{:S(2)}, u32[]{:S(2)}) async-start(bf16[32,16,896]{2,1,0:T(8,128)(2,1)} %bitcast.56), calls=%async_computation.3 | async-start | bytes 1835008 | tf_op jit(solution)/shard_map/all_to_all | solution.py:417
  253.8 9.2 %collective-permute-start.61 = (bf16[2,24,2304]{2,1,0:T(8,128)(2,1)S(1)}, bf16[2,24,2304]{2,1,0:T(8,128)(2,1)S(1)}, u32[]{:S(2)}, u32[]{:S(2)}) collective-permute-start(bf16[2,24,2304]{2,1,0:T(8,128)(2,1)S(1)} %get-tuple-element.370), channel_id=1, source_target_pairs={{0,4},{1,5},{2,6},{3,7},{4,0},{5,1},{6,2},{7,3},{8,12},{9,13},{10,... | collective-permute-start | bytes 663560 | tf_op jit(solution)/shard_map/ppermute | solution.py:339
  255.4 8.0 %collective-permute-start.62 = (bf16[2,24,2304]{2,1,0:T(8,128)(2,1)S(1)}, bf16[2,24,2304]{2,1,0:T(8,128)(2,1)S(1)}, u32[]{:S(2)}, u32[]{:S(2)}) collective-permute-start(bf16[2,24,2304]{2,1,0:T(8,128)(2,1)S(1)} %get-tuple-element.371), channel_id=1, source_target_pairs={{0,2},{1,3},{2,0},{3,1},{4,6},{5,7},{6,4},{7,5},{8,10},{9,11},{10,... | collective-permute-start | bytes 663560 | tf_op jit(solution)/shard_map/ppermute | solution.py:339
  266.6 12.6 %collective-permute-start.63 = (bf16[4,24,2304]{2,1,0:T(8,128)(2,1)S(1)}, bf16[4,24,2304]{2,1,0:T(8,128)(2,1)S(1)}, u32[]{:S(2)}, u32[]{:S(2)}) collective-permute-start(bf16[4,24,2304]{2,1,0:T(8,128)(2,1)S(1)} %pad_maximum_fusion.5), channel_id=1, source_target_pairs={{0,2},{1,3},{2,0},{3,1},{4,6},{5,7},{6,4},{7,5},{8,10},{9,11},{10,... | collective-permute-start | bytes 1327112 | tf_op jit(solution)/shard_map/ppermute | solution.py:339
  268.1 11.8 %collective-permute-start.64 = (bf16[4,24,2304]{2,1,0:T(8,128)(2,1)S(1)}, bf16[4,24,2304]{2,1,0:T(8,128)(2,1)S(1)}, u32[]{:S(2)}, u32[]{:S(2)}) collective-permute-start(bf16[4,24,2304]{2,1,0:T(8,128)(2,1)S(1)} %pad_maximum_fusion.6), channel_id=1, source_target_pairs={{0,4},{1,5},{2,6},{3,7},{4,0},{5,1},{6,2},{7,3},{8,12},{9,13},{10,... | collective-permute-start | bytes 1327112 | tf_op jit(solution)/shard_map/ppermute | solution.py:339
  269.6 9.7 %collective-permute-start.65 = (bf16[24,3840]{1,0:T(8,128)(2,1)}, bf16[24,3840]{1,0:T(8,128)(2,1)S(1)}, u32[]{:S(2)}, u32[]{:S(2)}) collective-permute-start(bf16[24,3840]{1,0:T(8,128)(2,1)} %get-tuple-element.381), channel_id=1, source_target_pairs={{0,8},{1,9},{2,10},{3,11},{4,12},{5,13},{6,14},{7,15},{8,16},{9,17... | collective-permute-start | bytes 552968 | tf_op jit(solution)/shard_map/ppermute | solution.py:413
  270.9 19.5 %collective-permute-start.69 = (bf16[24,3840]{1,0:T(8,128)(2,1)}, bf16[24,3840]{1,0:T(8,128)(2,1)S(1)}, u32[]{:S(2)}, u32[]{:S(2)}) collective-permute-start(bf16[24,3840]{1,0:T(8,128)(2,1)} %get-tuple-element.393), channel_id=1, source_target_pairs={{0,16},{1,17},{2,18},{3,19},{4,20},{5,21},{6,22},{7,23},{8,24},{9,... | collective-permute-start | bytes 552968 | tf_op jit(solution)/shard_map/ppermute | solution.py:413
  271.6 18.8 %collective-permute-start.70 = (bf16[24,3840]{1,0:T(8,128)(2,1)}, bf16[24,3840]{1,0:T(8,128)(2,1)S(1)}, u32[]{:S(2)}, u32[]{:S(2)}) collective-permute-start(bf16[24,3840]{1,0:T(8,128)(2,1)} %get-tuple-element.394), channel_id=1, source_target_pairs={{0,24},{1,25},{2,26},{3,27},{4,28},{5,29},{6,30},{7,31},{8,0},{9,1... | collective-permute-start | bytes 552968 | tf_op jit(solution)/shard_map/ppermute | solution.py:413
  282.0 14.2 %collective-permute-start.66 = (bf16[24,2304]{1,0:T(8,128)(2,1)S(1)}, bf16[24,2304]{1,0:T(8,128)(2,1)S(1)}, u32[]{:S(2)}, u32[]{:S(2)}) collective-permute-start(bf16[24,2304]{1,0:T(8,128)(2,1)S(1)} %get-tuple-element.388), channel_id=1, source_target_pairs={{0,8},{1,9},{2,10},{3,11},{4,12},{5,13},{6,14},{7,15},{8,16},{9,17... | collective-permute-start | bytes 331784 | tf_op jit(solution)/shard_map/ppermute | solution.py:413
  283.2 13.0 %collective-permute-start.67 = (bf16[24,2304]{1,0:T(8,128)(2,1)S(1)}, bf16[24,2304]{1,0:T(8,128)(2,1)S(1)}, u32[]{:S(2)}, u32[]{:S(2)}) collective-permute-start(bf16[24,2304]{1,0:T(8,128)(2,1)S(1)} %get-tuple-element.389), channel_id=1, source_target_pairs={{0,16},{1,17},{2,18},{3,19},{4,20},{5,21},{6,22},{7,23},{8,24},{9,... | collective-permute-start | bytes 331784 | tf_op jit(solution)/shard_map/ppermute | solution.py:413
  287.5 8.7 %collective-permute-start.68 = (bf16[24,2304]{1,0:T(8,128)(2,1)S(1)}, bf16[24,2304]{1,0:T(8,128)(2,1)S(1)}, u32[]{:S(2)}, u32[]{:S(2)}) collective-permute-start(bf16[24,2304]{1,0:T(8,128)(2,1)S(1)} %get-tuple-element.390), channel_id=1, source_target_pairs={{0,24},{1,25},{2,26},{3,27},{4,28},{5,29},{6,30},{7,31},{8,0},{9,1... | collective-permute-start | bytes 331784 | tf_op jit(solution)/shard_map/ppermute | solution.py:413
  298.9 11.9 %all-to-all-start.4 = ((f32[32,4,128]{2,1,0:T(4,128)}), f32[32,4,128]{2,1,0:T(4,128)S(1)}, u32[]{:S(2)}, u32[]{:S(2)}) async-start(f32[32,4,128]{2,1,0:T(4,128)} %get-tuple-element.408), calls=%async_computation.4 | async-start | bytes 131072 | tf_op jit(solution)/shard_map/all_to_all | solution.py:417
  (75 other events, 611.6 us)
